TPU v7x, 32 devices: a whole 2x2x4 slice. The times are simulated.
32 devices in a mesh: parts: 2 (over x), leaf: 16 (over z, y, core).
Axes of the slice: x: 2, y: 2, z: 4, core: 2. Of those that a mesh axis runs over, the one named last changes fastest.
Arguments:
- right_side: float32 [32, 65536], P(None, ('parts', 'leaf')), parts along dimension 1, may hold values from -16 to 16
- near_pairs: int32 [2, 2048], P(None, ('parts', 'leaf')), parts along dimension 1, may hold values from 0 to 15, as said below
- near_count: int32 [32], P(('parts', 'leaf')), parts along dimension 0, may hold values from 8 to 64, as said below
- near_blocks: bfloat16 [2048, 256, 256], P(('parts', 'leaf')), parts along dimension 0, may hold values from -1 to 2
- far_pairs: int32 [2, 4096], P(None, ('parts', 'leaf')), parts along dimension 1, may hold values from 0 to 127, as said below
- coupling: bfloat16 [4096, 1024], P(('parts', 'leaf')), parts along dimension 0, may hold values from -0.21875 to 0.21875
- cluster_basis: bfloat16 [256, 32, 256], P(('parts', 'leaf')), parts along dimension 0, may hold values from -0.375 to 0.375
- cluster_slot: int32 [256], P('parts'), parts along dimension 0, may hold values from 0 to 127, as said below
Outputs:
- solution_field: float32 [32, 65536], P(None, ('parts', 'leaf')), parts along dimension 1
- residual: float32 [32, 65536], P(None, ('parts', 'leaf')), parts along dimension 1
- hessenberg: float32 [128, 32], P('parts'), parts along dimension 0
There are 2 independent parts, one for each index of `parts`. A program takes and returns all parts, laid end to end along the dimension named above; each array names one. Nothing has to cross between parts.
Inputs may be any that keep to these rules, and one draw needn't show every extreme that they name: `near_pairs`: A device's first 8 slots pair each of its clusters with itself; in every other slot the second entry exceeds the first. Entries below 8 name the device's own clusters, higher ones the next device's clusters, which the last device never names. `near_count`: some device has exactly 64 live slots. `far_pairs`: the first number of a pair is smaller than the second. Through cluster_slot, exactly one end of each of a device's far pairs is a cluster stored on that device and the other end is stored on another device; of one device's far pairs at most 9 have their other end on any one given device, and exactly 9 for some. `cluster_slot`: each number appears once.
All inputs are finite; a program needn't handle non-finite values.
Results may differ from a plain program's by a relative error of at most 0.0078.
Values may be sent and summed in bfloat16 or wider, within the bound.
No kernel may reach another device: no remote copies, remote signals or barrier semaphores. Data moves between devices by JAX's collectives and lax.ppermute only.
A program may use at most 64 MiB of HBM per device.

v0:
```python
import functools

import jax
import jax.numpy as jnp
from jax import lax
from jax.experimental import pallas as pl
from jax.experimental.pallas import tpu as pltpu
from jax.sharding import PartitionSpec as P

PANEL = 256
R = 32
K = 32
GROUP = 8
highest = lax.Precision.HIGHEST
VMEM = pltpu.VMEM
SMEM = pltpu.SMEM
TN = (((0,), (0,)), ((), ()))
NT = (((1,), (1,)), ((), ()))
f32 = jnp.float32
bf16 = jnp.bfloat16


def spec(space):
    return pl.BlockSpec(memory_space=space)


def call(kernel, outs, ins, spaces, scratch=(), limit=40, flops=10**8, moved=10**6):
    return pl.pallas_call(
        kernel,
        out_shape=outs,
        in_specs=[spec(s) for s in spaces],
        out_specs=jax.tree.map(lambda _: spec(VMEM), outs),
        scratch_shapes=list(scratch),
        compiler_params=pltpu.CompilerParams(vmem_limit_bytes=limit << 20),
        cost_estimate=pl.CostEstimate(flops=flops, bytes_accessed=moved, transcendentals=0),
    )(*ins)


def dot(x, y):
    return jnp.dot(x, y, preferred_element_type=f32)


def dot_nt(x, y):
    return lax.dot_general(x, y, NT, preferred_element_type=f32)


def exact_nt(x, y):
    return lax.dot_general(x, y, NT, precision=highest, preferred_element_type=f32)


def split_rows(x):
    high = x.astype(bf16)
    low = (x - high.astype(f32)).astype(bf16)
    return jnp.concatenate([high, low], axis=0)


def join_rows(x):
    return x[:R] + x[R:]


def lane_group(shape):
    return lax.broadcasted_iota(jnp.int32, shape, 1) // K


def project(fields, basis, clusters):
    group = lane_group((2 * R, clusters * K))
    total = jnp.zeros((2 * R, clusters * K), f32)
    for c in range(clusters):
        total = total + jnp.where(group == c, dot_nt(fields[c], basis), 0.0)
    return split_rows(join_rows(total))


def start_kernel(right_ref, basis_ref, field_ref, proj_ref):
    clusters = field_ref.shape[0]
    fields = []
    for c in range(clusters):
        field = split_rows(right_ref[:, c * PANEL : (c + 1) * PANEL])
        field_ref[c] = field
        fields.append(field)
    proj_ref[...] = project(fields, basis_ref[...], clusters)


def couple_kernel(bits, pairs_ref, slots_ref, me_ref, coupling_ref, out_ref):
    clusters = out_ref.shape[2] // K
    me = me_ref[0]
    out_ref[...] = jnp.zeros_like(out_ref)
    group = lane_group((K, clusters * K))

    def one(f, carry):
        first = slots_ref[pairs_ref[0, f]]
        second = slots_ref[pairs_ref[1, f]]
        first_home, second_home = first // clusters, second // clusters
        own = (first_home == me).astype(jnp.int32)
        apart = (first_home + second_home - me) ^ me
        place = jnp.int32(0)
        for b in range(bits):
            place = place + (((apart >> b) & 1) << (bits - 1 - b))
        block = jnp.concatenate([coupling_ref[f]] * clusters, axis=1)
        block = jnp.where(group == second % clusters, block.astype(f32), 0.0).astype(bf16)
        rows = pl.ds(pl.multiple_of((first % clusters) * K, K), K)
        where = own * (1 << bits) + place
        out_ref[where, rows, :] = out_ref[where, rows, :] + block
        return carry

    lax.fori_loop(0, pairs_ref.shape[1], one, 0)


def send_kernel(coupled_ref, proj_ref, out_ref):
    devices = out_ref.shape[0]
    proj = proj_ref[...]
    for d in range(devices):
        value = dot(proj, coupled_ref[devices + d]) + dot_nt(proj, coupled_ref[d])
        out_ref[d] = join_rows(value)


def near_specs(nb, group):
    return pl.BlockSpec((group, PANEL, PANEL), lambda g, pairs, count: (jnp.minimum(g, (count[0] - 1) // group), 0, 0))


def whole(shape):
    return pl.BlockSpec(shape, lambda g, pairs, count: (0,) * len(shape))


def near_cols_kernel(pairs_ref, count_ref, blocks_ref, field_ref, own_ref, next_ref, total):
    g = pl.program_id(0)
    clusters = field_ref.shape[0]

    @pl.when(g == 0)
    def _():
        total[...] = jnp.zeros_like(total)

    @pl.when(g * GROUP < count_ref[0])
    def _():
        for u in range(GROUP):
            s = g * GROUP + u
            i = pairs_ref[0, s]
            j = jnp.where(s < count_ref[0], pairs_ref[1, s], 2 * clusters)
            total[j] = total[j] + join_rows(dot(field_ref[i], blocks_ref[u]))

    @pl.when(g == pl.num_programs(0) - 1)
    def _():
        own_ref[...] = total[:clusters]
        next_ref[...] = total[clusters : 2 * clusters]


def near_rows_kernel(pairs_ref, count_ref, blocks_ref, field_ref, after_ref, begun_ref, out_ref, window, total):
    g = pl.program_id(0)
    clusters = field_ref.shape[0]

    @pl.when(g == 0)
    def _():
        window[:clusters] = field_ref[...]
        window[clusters:] = after_ref[...]
        total[:clusters] = begun_ref[...]

    @pl.when(g * GROUP < count_ref[0])
    def _():
        for u in range(GROUP):
            s = g * GROUP + u
            i = jnp.where(s < count_ref[0], pairs_ref[0, s], clusters)
            j = pairs_ref[1, s]
            total[i] = total[i] + join_rows(dot_nt(window[j], blocks_ref[u]))

    @pl.when(g == pl.num_programs(0) - 1)
    def _():
        out_ref[...] = total[:clusters]


def near_call(kernel, outs, near_pairs, near_count, near_blocks, arrays, scratch):
    nb = near_blocks.shape[0]
    return pl.pallas_call(
        kernel,
        out_shape=outs,
        grid_spec=pltpu.PrefetchScalarGridSpec(
            num_scalar_prefetch=2,
            grid=(nb // GROUP,),
            in_specs=[near_specs(nb, GROUP)] + [whole(a.shape) for a in arrays],
            out_specs=jax.tree.map(lambda o: whole(o.shape), outs),
            scratch_shapes=scratch,
        ),
        compiler_params=pltpu.CompilerParams(
            vmem_limit_bytes=24 << 20, dimension_semantics=("arbitrary",)
        ),
        cost_estimate=pl.CostEstimate(
            flops=nb * 64 * PANEL * PANEL * 2, bytes_accessed=nb * PANEL * PANEL * 2, transcendentals=0
        ),
    )(near_pairs, near_count, near_blocks, *arrays)


def far_fields(coupled_ref, gathered_refs, reduced_refs, basis):
    devices = coupled_ref.shape[0] // 2
    total = jnp.zeros((2 * R, basis.shape[0]), f32)
    place = 0
    for ref in gathered_refs:
        for d in range(ref.shape[0]):
            proj = ref[d]
            total = total + dot(proj, coupled_ref[place]) + dot_nt(proj, coupled_ref[devices + place])
            place += 1
    sums = join_rows(total)
    for ref in reduced_refs:
        sums = sums + ref[0]
    sums = split_rows(sums)
    group = lane_group(sums.shape)
    zero = jnp.zeros_like(sums)
    return lambda c: join_rows(dot(jnp.where(group == c, sums, zero), basis))


def finish_one_kernel(coupled_ref, near_ref, back_ref, low_ref, high_ref, kept_ref, got_ref, basis_ref,
                      image_ref, field_ref, proj_ref):
    clusters = near_ref.shape[0]
    basis = basis_ref[...]
    far = far_fields(coupled_ref, (low_ref, high_ref), (kept_ref, got_ref), basis)
    fields = []
    for c in range(clusters):
        image = near_ref[c] + back_ref[c] + far(c)
        image_ref[c] = image
        field = split_rows(image)
        field_ref[c] = field
        fields.append(field)
    proj_ref[...] = project(fields, basis, clusters)


def finish_two_kernel(coupled_ref, near_ref, back_ref, low_ref, high_ref, kept_ref, got_ref, basis_ref,
                      right_ref, image_ref, second_ref, gram_ref):
    clusters = near_ref.shape[0]
    basis = basis_ref[...]
    far = far_fields(coupled_ref, (low_ref, high_ref), (kept_ref, got_ref), basis)
    gram = jnp.zeros((4 * R, 4 * R), f32)
    for c in range(clusters):
        second = near_ref[c] + back_ref[c] + far(c)
        second_ref[c] = second
        right = right_ref[:, c * PANEL : (c + 1) * PANEL]
        rows = jnp.concatenate([right, image_ref[c], second, jnp.zeros_like(second)], axis=0)
        gram = gram + exact_nt(rows, rows)
    gram_ref[...] = gram[: 3 * R]


def column(x, k):
    return jnp.broadcast_to(x[:, k : k + 1], x.shape)


def last_kernel(kept_ref, got_ref, right_ref, image_ref, second_ref, field_ref, residual_ref, hessenberg_ref):
    clusters = image_ref.shape[0]
    gram = kept_ref[...] + got_ref[...]
    lanes = lax.broadcasted_iota(jnp.int32, (2 * R, 4 * R), 1)
    rows = lax.broadcasted_iota(jnp.int32, (2 * R, 4 * R), 0)
    system = gram[R : 3 * R]
    lower = gram[: 2 * R]
    lower = jnp.where(lanes < 2 * R, lower, jnp.where(lanes - 2 * R == rows, 1.0, 0.0))
    for k in range(2 * R):
        pivot = system[k : k + 1]
        inverse = 1.0 / pivot[:, R + k : R + k + 1]
        pivot = pivot * inverse
        factor = column(system, R + k)
        system = jnp.where(rows == k, pivot, system - factor * pivot)
        top = lower[k : k + 1]
        top = top * lax.rsqrt(top[:, k : k + 1])
        down = column(lower, k)
        scaled = lower - (down / top[:, k : k + 1]) * top
        lower = jnp.where(rows == k, top, jnp.where(rows > k, scaled, lower))
    weights = system[:, :R]
    inverse_zero = lower[:R, 2 * R : 3 * R]
    cross = lower[:R, R : 2 * R]
    corner = lower[R:, R : 2 * R]
    hessenberg_ref[:R] = exact_nt(cross, inverse_zero)
    hessenberg_ref[R:] = exact_nt(inverse_zero, corner)
    for c in range(clusters):
        right = right_ref[:, c * PANEL : (c + 1) * PANEL]
        image = image_ref[c]
        second = second_ref[c]

        def combine(x, y):
            stacked = jnp.concatenate([x, y], axis=0)
            return lax.dot_general(weights, stacked, TN, precision=highest, preferred_element_type=f32)

        field_ref[:, c * PANEL : (c + 1) * PANEL] = combine(right, image)
        residual_ref[:, c * PANEL : (c + 1) * PANEL] = right - combine(image, second)


def body(right_side, near_pairs, near_count, near_blocks, far_pairs, coupling, cluster_basis, cluster_slot):
    devices = lax.axis_size("leaf")
    bits = devices.bit_length() - 1
    clusters = cluster_basis.shape[0]
    me = lax.axis_index("leaf").astype(jnp.int32).reshape(1)
    basis = cluster_basis.reshape(clusters * K, PANEL)
    sds = jax.ShapeDtypeStruct

    def across(x, bit):
        return lax.ppermute(x, "leaf", [(i, i ^ bit) for i in range(devices)])

    def shift(x, by):
        return lax.ppermute(x, "leaf", [(i, i + by) for i in range(devices) if 0 <= i + by < devices])

    panels = sds((clusters, R, PANEL), f32)
    split = sds((clusters, 2 * R, PANEL), bf16)
    rank = sds((2 * R, clusters * K), bf16)

    field, proj = call(start_kernel, (split, rank), (right_side, basis), (VMEM, VMEM))
    coupled = call(
        functools.partial(couple_kernel, bits),
        sds((2 * devices, clusters * K, clusters * K), bf16),
        (far_pairs, cluster_slot, me, coupling.reshape(-1, K, K)),
        (SMEM, SMEM, SMEM, VMEM),
    )

    def exchange(field, proj):
        gathered = proj[None]
        after = shift(field, -1)
        sent = call(send_kernel, sds((devices, R, clusters * K), f32), (coupled, proj), (VMEM, VMEM))
        own, following = near_call(
            near_cols_kernel, (panels, panels), near_pairs, near_count, near_blocks, (field,),
            [pltpu.VMEM((2 * clusters + 1, R, PANEL), f32)],
        )
        back = shift(following, 1)
        got_gather = got_sent = None
        for b in range(bits):
            if b > 0:
                gathered = jnp.concatenate([gathered, got_gather], axis=0)
                sent = sent[: devices >> b] + got_sent
            got_gather = across(gathered, devices >> (b + 1))
            got_sent = across(sent[devices >> (b + 1) :], 1 << b)
        near = near_call(
            near_rows_kernel, panels, near_pairs, near_count, near_blocks, (field, after, own),
            [pltpu.VMEM((2 * clusters, 2 * R, PANEL), bf16), pltpu.VMEM((clusters + 1, R, PANEL), f32)],
        )
        return (coupled, near, back, gathered, got_gather, sent[:1], got_sent, basis)

    parts = exchange(field, proj)
    image, field, proj = call(finish_one_kernel, (panels, split, rank), parts, [VMEM] * 8)
    parts = exchange(field, proj)
    second, gram = call(
        finish_two_kernel, (panels, sds((3 * R, 4 * R), f32)), parts + (right_side, image), [VMEM] * 10
    )
    got = None
    for b in range(bits):
        if b > 0:
            gram = gram + got
        got = across(gram, 1 << b)
    wide = sds(right_side.shape, f32)
    return call(
        last_kernel, (wide, wide, sds((2 * R, R), f32)), (gram, got, right_side, image, second), [VMEM] * 5
    )


def solution(mesh):
    in_specs = (
        P(None, ("parts", "leaf")),
        P(None, ("parts", "leaf")),
        P(("parts", "leaf")),
        P(("parts", "leaf"), None, None),
        P(None, ("parts", "leaf")),
        P(("parts", "leaf"), None),
        P(("parts", "leaf"), None, None),
        P("parts"),
    )
    out_specs = (P(None, ("parts", "leaf")), P(None, ("parts", "leaf")), P("parts", None))
    return jax.shard_map(body, mesh=mesh, in_specs=in_specs, out_specs=out_specs, check_vma=False)
```

profile of v0, /device:TPU:0, one launch (start us, length us, event | category | flops | bytes accessed | tf_op | source)
XLA Modules:
  0.0 115.2 jit_solution(14344683944796305132)
XLA Ops:
  1.8 1.5 %copy.13.coupling_ref = bf16[128,32,32]{2,1,0:T(8,128)(2,1)S(1)} copy(bf16[128,32,32]{0,2,1:T(8,128)(2,1)S(1)} %bitcast.16) | data formatting | bytes 524288 | tf_op jit(solution)/shard_map/reshape | solution.py:302
  7.3 10.9 %shard_map.103.coupled_ref = bf16[32,256,256]{2,1,0:T(8,128)(2,1)S(1)} custom-call(s32[2,128]{1,0:T(2,128)S(1)} %copy-done.5, s32[128]{0:T(128)S(1)} %copy-done.6, s32[1]{0:T(128)} %bitcast.me_ref, bf16[128,32,32]{2,1,0:T(8,128)(2,1)S(1)} %copy.13.coupling_ref), custom_call_target="tpu_custom_call" | custom-call | flops 100000000 | bytes 1000000 | tf_op jit(solution)/shard_map/pallas_call | solution.py:28
  19.8 3.7 %collective-permute-start.2 = (bf16[1,64,256]{2,1,0:T(8,128)(2,1)S(1)}, bf16[1,64,256]{2,1,0:T(8,128)(2,1)S(1)}, u32[]{:S(2)}, u32[]{:S(2)}) collective-permute-start(bf16[1,64,256]{2,1,0:T(8,128)(2,1)S(1)} %bitcast.12), channel_id=1, source_target_pairs={{0,8},{1,9},{2,10},{3,11},{4,12},{5,13},{6,14},{7,15},{8,0},{9,1},... | collective-permute-start | bytes 98312 | tf_op jit(solution)/shard_map/ppermute | solution.py:289
  23.5 1.3 %collective-permute-start = (bf16[8,64,256]{2,1,0:T(8,128)(2,1)S(1)}, bf16[8,64,256]{2,1,0:T(8,128)(2,1)S(1)}, u32[]{:S(2)}, u32[]{:S(2)}) collective-permute-start(bf16[8,64,256]{2,1,0:T(8,128)(2,1)S(1)} %get-tuple-element.14.field_ref), channel_id=1, source_target_pairs={{1,0},{2,1},{3,2},{4,3},{5,4},{6,5},{7,6},{8,7},{9,8},{10,9},{11,1... | collective-permute-start | bytes 786440 | tf_op jit(solution)/shard_map/ppermute | solution.py:292
  25.4 3.4 %collective-permute-start.3 = (bf16[2,64,256]{2,1,0:T(8,128)(2,1)S(1)}, bf16[2,64,256]{2,1,0:T(8,128)(2,1)S(1)}, u32[]{:S(2)}, u32[]{:S(2)}) collective-permute-start(bf16[2,64,256]{2,1,0:T(8,128)(2,1)S(1)} %pad_maximum_fusion.4), channel_id=1, source_target_pairs={{0,4},{1,5},{2,6},{3,7},{4,0},{5,1},{6,2},{7,3},{8,12},{9,13},{10,... | collective-permute-start | bytes 196616 | tf_op jit(solution)/shard_map/ppermute | solution.py:289
  29.6 1.8 %shard_map.105 = (f32[8,32,256]{2,1,0:T(8,128)S(1)}, f32[8,32,256]{2,1,0:T(8,128)S(1)}) custom-call(s32[2,64]{1,0:T(2,128)S(1)} %copy-done.4, s32[1]{0:T(128)S(6)} %copy.15.count_ref, bf16[64,256,256]{2,1,0:T(8,128)(2,1)S(1)} %copy-done, bf16[8,64,256]{2,1,0:T(8,128)(2,1)S(1)} %get-tuple-element.14.field_ref), custom_call_target="tpu_custom_call" | custom-call | flops 536870912 | bytes 8388608 | tf_op jit(solution)/shard_map/pallas_call | solution.py:171
  31.4 1.3 %collective-permute-start.1 = (f32[8,32,256]{2,1,0:T(8,128)S(1)}, f32[8,32,256]{2,1,0:T(8,128)S(1)}, u32[]{:S(2)}, u32[]{:S(2)}) collective-permute-start(f32[8,32,256]{2,1,0:T(8,128)S(1)} %get-tuple-element.16), channel_id=1, source_target_pairs={{0,1},{1,2},{2,3},{3,4},{4,5},{5,6},{6,7},{7,8},{8,9},{9,10},{10,1... | collective-permute-start | bytes 786440 | tf_op jit(solution)/shard_map/ppermute | solution.py:292
  33.5 2.3 %collective-permute-start.4 = (bf16[4,64,256]{2,1,0:T(8,128)(2,1)S(1)}, bf16[4,64,256]{2,1,0:T(8,128)(2,1)S(1)}, u32[]{:S(2)}, u32[]{:S(2)}) collective-permute-start(bf16[4,64,256]{2,1,0:T(8,128)(2,1)S(1)} %pad_maximum_fusion.2), channel_id=1, source_target_pairs={{0,2},{1,3},{2,0},{3,1},{4,6},{5,7},{6,4},{7,5},{8,10},{9,11},{10,... | collective-permute-start | bytes 393224 | tf_op jit(solution)/shard_map/ppermute | solution.py:289
  36.0 3.6 %collective-permute-done.4 = bf16[4,64,256]{2,1,0:T(8,128)(2,1)S(1)} collective-permute-done((bf16[4,64,256]{2,1,0:T(8,128)(2,1)S(1)}, bf16[4,64,256]{2,1,0:T(8,128)(2,1)S(1)}, u32[]{:S(2)}, u32[]{:S(2)}) %collective-permute-start.4) | collective-permute-done | bytes 131104 | tf_op jit(solution)/shard_map/ppermute | solution.py:289
  39.6 2.3 %collective-permute-start.5 = (bf16[8,64,256]{2,1,0:T(8,128)(2,1)S(1)}, bf16[8,64,256]{2,1,0:T(8,128)(2,1)S(1)}, u32[]{:S(2)}, u32[]{:S(2)}) collective-permute-start(bf16[8,64,256]{2,1,0:T(8,128)(2,1)S(1)} %pad_maximum_fusion.low_ref), channel_id=1, source_target_pairs={{0,1},{1,0},{2,3},{3,2},{4,5},{5,4},{6,7},{7,6},{8,9},{9,8},{10,11... | collective-permute-start | bytes 786440 | tf_op jit(solution)/shard_map/ppermute | solution.py:289
  42.0 3.5 %collective-permute-start.9 = (f32[1,32,256]{2,1,0:T(8,128)S(1)}, f32[1,32,256]{2,1,0:T(8,128)S(1)}, u32[]{:S(2)}, u32[]{:S(2)}) collective-permute-start(f32[1,32,256]{2,1,0:T(8,128)S(1)} %get-tuple-element.33), channel_id=1, source_target_pairs={{0,8},{1,9},{2,10},{3,11},{4,12},{5,13},{6,14},{7,15},{8,0},{9,1},... | collective-permute-start | bytes 98312 | tf_op jit(solution)/shard_map/ppermute | solution.py:289
  45.5 2.2 %shard_map.106.near_ref = f32[8,32,256]{2,1,0:T(8,128)S(1)} custom-call(s32[2,64]{1,0:T(2,128)S(1)} %copy-done.4, s32[1]{0:T(128)S(6)} %copy.15.count_ref, bf16[64,256,256]{2,1,0:T(8,128)(2,1)S(1)} %copy-done, bf16[8,64,256]{2,1,0:T(8,128)(2,1)S(1)} %get-tuple-element.14.field_ref, bf16[8,64,256]{2,1,0:T(8,128)(2,1)S(1)} %collective-permute-done.after_ref, ...), custom_call_target="tpu_custom_call" | custom-call | flops 536870912 | bytes 8388608 | tf_op jit(solution)/shard_map/pallas_call | solution.py:171
  47.7 2.4 %shard_map.108 = (f32[8,32,256]{2,1,0:T(8,128)S(1)}, bf16[8,64,256]{2,1,0:T(8,128)(2,1)S(1)}, bf16[64,256]{1,0:T(8,128)(2,1)S(1)}) custom-call(bf16[32,256,256]{2,1,0:T(8,128)(2,1)S(1)} %shard_map.103.coupled_ref, f32[8,32,256]{2,1,0:T(8,128)S(1)} %shard_map.106.near_ref, f32[8,32,256]{2,1,0:T(8,128)S(1)} %collective-permute-done.1.back_ref, ...), custom_call_target="tpu_custom_call" | custom-call | flops 100000000 | bytes 1000000 | tf_op jit(solution)/shard_map/pallas_call | solution.py:28
  51.4 2.6 %collective-permute-start.12 = (bf16[1,64,256]{2,1,0:T(8,128)(2,1)S(1)}, bf16[1,64,256]{2,1,0:T(8,128)(2,1)S(1)}, u32[]{:S(2)}, u32[]{:S(2)}) collective-permute-start(bf16[1,64,256]{2,1,0:T(8,128)(2,1)S(1)} %bitcast.8), channel_id=1, source_target_pairs={{0,8},{1,9},{2,10},{3,11},{4,12},{5,13},{6,14},{7,15},{8,0},{9,1},... | collective-permute-start | bytes 98312 | tf_op jit(solution)/shard_map/ppermute | solution.py:289
  54.0 2.2 %collective-permute-done.12 = bf16[1,64,256]{2,1,0:T(8,128)(2,1)S(1)} collective-permute-done((bf16[1,64,256]{2,1,0:T(8,128)(2,1)S(1)}, bf16[1,64,256]{2,1,0:T(8,128)(2,1)S(1)}, u32[]{:S(2)}, u32[]{:S(2)}) %collective-permute-start.12) | collective-permute-done | bytes 32800 | tf_op jit(solution)/shard_map/ppermute | solution.py:289
  56.3 3.1 %collective-permute-start.13 = (bf16[2,64,256]{2,1,0:T(8,128)(2,1)S(1)}, bf16[2,64,256]{2,1,0:T(8,128)(2,1)S(1)}, u32[]{:S(2)}, u32[]{:S(2)}) collective-permute-start(bf16[2,64,256]{2,1,0:T(8,128)(2,1)S(1)} %pad_maximum_fusion.5), channel_id=1, source_target_pairs={{0,4},{1,5},{2,6},{3,7},{4,0},{5,1},{6,2},{7,3},{8,12},{9,13},{10,... | collective-permute-start | bytes 196616 | tf_op jit(solution)/shard_map/ppermute | solution.py:289
  59.5 1.8 %shard_map.109 = (f32[8,32,256]{2,1,0:T(8,128)S(1)}, f32[8,32,256]{2,1,0:T(8,128)S(1)}) custom-call(s32[2,64]{1,0:T(2,128)S(1)} %copy-done.4, s32[1]{0:T(128)S(6)} %copy.15.count_ref, bf16[64,256,256]{2,1,0:T(8,128)(2,1)S(1)} %copy-done, bf16[8,64,256]{2,1,0:T(8,128)(2,1)S(1)} %get-tuple-element.18.field_ref), custom_call_target="tpu_custom_call" | custom-call | flops 536870912 | bytes 8388608 | tf_op jit(solution)/shard_map/pallas_call | solution.py:171
  61.3 1.3 %collective-permute-start.10 = (bf16[8,64,256]{2,1,0:T(8,128)(2,1)S(1)}, bf16[8,64,256]{2,1,0:T(8,128)(2,1)S(1)}, u32[]{:S(2)}, u32[]{:S(2)}) collective-permute-start(bf16[8,64,256]{2,1,0:T(8,128)(2,1)S(1)} %get-tuple-element.18.field_ref), channel_id=1, source_target_pairs={{1,0},{2,1},{3,2},{4,3},{5,4},{6,5},{7,6},{8,7},{9,8},{10,9},{11,1... | collective-permute-start | bytes 786440 | tf_op jit(solution)/shard_map/ppermute | solution.py:292
  62.6 3.2 %collective-permute-start.11 = (f32[8,32,256]{2,1,0:T(8,128)S(1)}, f32[8,32,256]{2,1,0:T(8,128)S(1)}, u32[]{:S(2)}, u32[]{:S(2)}) collective-permute-start(f32[8,32,256]{2,1,0:T(8,128)S(1)} %get-tuple-element.20), channel_id=1, source_target_pairs={{0,1},{1,2},{2,3},{3,4},{4,5},{5,6},{6,7},{7,8},{8,9},{9,10},{10,1... | collective-permute-start | bytes 786440 | tf_op jit(solution)/shard_map/ppermute | solution.py:292
  65.9 2.9 %collective-permute-start.14 = (bf16[4,64,256]{2,1,0:T(8,128)(2,1)S(1)}, bf16[4,64,256]{2,1,0:T(8,128)(2,1)S(1)}, u32[]{:S(2)}, u32[]{:S(2)}) collective-permute-start(bf16[4,64,256]{2,1,0:T(8,128)(2,1)S(1)} %pad_maximum_fusion.3), channel_id=1, source_target_pairs={{0,2},{1,3},{2,0},{3,1},{4,6},{5,7},{6,4},{7,5},{8,10},{9,11},{10,... | collective-permute-start | bytes 393224 | tf_op jit(solution)/shard_map/ppermute | solution.py:289
  68.9 3.8 %collective-permute-done.14 = bf16[4,64,256]{2,1,0:T(8,128)(2,1)S(1)} collective-permute-done((bf16[4,64,256]{2,1,0:T(8,128)(2,1)S(1)}, bf16[4,64,256]{2,1,0:T(8,128)(2,1)S(1)}, u32[]{:S(2)}, u32[]{:S(2)}) %collective-permute-start.14) | collective-permute-done | bytes 131104 | tf_op jit(solution)/shard_map/ppermute | solution.py:289
  72.8 1.7 %collective-permute-start.15 = (bf16[8,64,256]{2,1,0:T(8,128)(2,1)S(1)}, bf16[8,64,256]{2,1,0:T(8,128)(2,1)S(1)}, u32[]{:S(2)}, u32[]{:S(2)}) collective-permute-start(bf16[8,64,256]{2,1,0:T(8,128)(2,1)S(1)} %pad_maximum_fusion.1.low_ref), channel_id=1, source_target_pairs={{0,1},{1,0},{2,3},{3,2},{4,5},{5,4},{6,7},{7,6},{8,9},{9,8},{10,11... | collective-permute-start | bytes 786440 | tf_op jit(solution)/shard_map/ppermute | solution.py:289
  74.5 3.0 %collective-permute-start.19 = (f32[1,32,256]{2,1,0:T(8,128)S(1)}, f32[1,32,256]{2,1,0:T(8,128)S(1)}, u32[]{:S(2)}, u32[]{:S(2)}) collective-permute-start(f32[1,32,256]{2,1,0:T(8,128)S(1)} %get-tuple-element.31), channel_id=1, source_target_pairs={{0,8},{1,9},{2,10},{3,11},{4,12},{5,13},{6,14},{7,15},{8,0},{9,1},... | collective-permute-start | bytes 98312 | tf_op jit(solution)/shard_map/ppermute | solution.py:289
  77.6 2.2 %shard_map.110.near_ref = f32[8,32,256]{2,1,0:T(8,128)S(1)} custom-call(s32[2,64]{1,0:T(2,128)S(1)} %copy-done.4, s32[1]{0:T(128)S(6)} %copy.15.count_ref, bf16[64,256,256]{2,1,0:T(8,128)(2,1)S(1)} %copy-done, bf16[8,64,256]{2,1,0:T(8,128)(2,1)S(1)} %get-tuple-element.18.field_ref, bf16[8,64,256]{2,1,0:T(8,128)(2,1)S(1)} %collective-permute-done.10.after_ref, ...), custom_call_target="tpu_custom_call" | custom-call | flops 536870912 | bytes 8388608 | tf_op jit(solution)/shard_map/pallas_call | solution.py:171
  79.8 4.6 %shard_map.112 = (f32[8,32,256]{2,1,0:T(8,128)S(1)}, f32[96,128]{1,0:T(8,128)S(1)}) custom-call(bf16[32,256,256]{2,1,0:T(8,128)(2,1)S(1)} %shard_map.103.coupled_ref, f32[8,32,256]{2,1,0:T(8,128)S(1)} %shard_map.110.near_ref, f32[8,32,256]{2,1,0:T(8,128)S(1)} %collective-permute-done.11.back_ref, bf16[8,64,256]{2,1,0:T(8,128)(2,1)S(1)} %pad_maximum_fusion.1.low_ref, ...), custom_call_target="tpu_custom_call" | custom-call | flops 100000000 | bytes 1000000 | tf_op jit(solution)/shard_map/pallas_call | solution.py:28
  85.7 2.7 %collective-permute-start.21 = (f32[96,128]{1,0:T(8,128)S(1)}, f32[96,128]{1,0:T(8,128)S(1)}, u32[]{:S(2)}, u32[]{:S(2)}) collective-permute-start(f32[96,128]{1,0:T(8,128)S(1)} %add.33), channel_id=1, source_target_pairs={{0,2},{1,3},{2,0},{3,1},{4,6},{5,7},{6,4},{7,5},{8,10},{9,11},{10,... | collective-permute-start | bytes 147464 | tf_op jit(solution)/shard_map/ppermute | solution.py:289
  88.4 2.1 %collective-permute-done.21 = f32[96,128]{1,0:T(8,128)S(1)} collective-permute-done((f32[96,128]{1,0:T(8,128)S(1)}, f32[96,128]{1,0:T(8,128)S(1)}, u32[]{:S(2)}, u32[]{:S(2)}) %collective-permute-start.21) | collective-permute-done | bytes 49184 | tf_op jit(solution)/shard_map/ppermute | solution.py:289
  90.5 2.2 %collective-permute-start.22 = (f32[96,128]{1,0:T(8,128)S(1)}, f32[96,128]{1,0:T(8,128)S(1)}, u32[]{:S(2)}, u32[]{:S(2)}) collective-permute-start(f32[96,128]{1,0:T(8,128)S(1)} %add.34), channel_id=1, source_target_pairs={{0,4},{1,5},{2,6},{3,7},{4,0},{5,1},{6,2},{7,3},{8,12},{9,13},{10,... | collective-permute-start | bytes 147464 | tf_op jit(solution)/shard_map/ppermute | solution.py:289
  92.7 2.1 %collective-permute-done.22 = f32[96,128]{1,0:T(8,128)S(1)} collective-permute-done((f32[96,128]{1,0:T(8,128)S(1)}, f32[96,128]{1,0:T(8,128)S(1)}, u32[]{:S(2)}, u32[]{:S(2)}) %collective-permute-start.22) | collective-permute-done | bytes 49184 | tf_op jit(solution)/shard_map/ppermute | solution.py:289
  94.7 1.9 %collective-permute-start.23 = (f32[96,128]{1,0:T(8,128)S(1)}, f32[96,128]{1,0:T(8,128)S(1)}, u32[]{:S(2)}, u32[]{:S(2)}) collective-permute-start(f32[96,128]{1,0:T(8,128)S(1)} %add.35.kept_ref), channel_id=1, source_target_pairs={{0,8},{1,9},{2,10},{3,11},{4,12},{5,13},{6,14},{7,15},{8,0},{9,1},... | collective-permute-start | bytes 147464 | tf_op jit(solution)/shard_map/ppermute | solution.py:289
  96.6 3.2 %collective-permute-done.23.got_ref = f32[96,128]{1,0:T(8,128)S(1)} collective-permute-done((f32[96,128]{1,0:T(8,128)S(1)}, f32[96,128]{1,0:T(8,128)S(1)}, u32[]{:S(2)}, u32[]{:S(2)}) %collective-permute-start.23) | collective-permute-done | bytes 49184 | tf_op jit(solution)/shard_map/ppermute | solution.py:289
  99.8 14.7 %shard_map.113 = (f32[32,2048]{1,0:T(8,128)}, f32[32,2048]{1,0:T(8,128)}, f32[64,32]{1,0:T(8,128)S(1)}) custom-call(f32[96,128]{1,0:T(8,128)S(1)} %add.35.kept_ref, f32[96,128]{1,0:T(8,128)S(1)} %collective-permute-done.23.got_ref, f32[32,2048]{1,0:T(8,128)S(1)} %copy-done.2, f32[8,32,256]{2,1,0:T(8,128)S(1)} %get-tuple-element.22.image_ref, ...), custom_call_target="tpu_custom_call" | custom-call | flops 100000000 | bytes 1000000 | tf_op jit(solution)/shard_map/pallas_call | solution.py:28
  (67 shorter events, 12.1 us)
Async XLA Ops:
  0.6 29.0 %copy-start.4 = (s32[2,64]{1,0:T(2,128)S(1)}, s32[2,64]{1,0:T(2,128)}, u32[]{:S(2)}) copy-start(s32[2,64]{1,0:T(2,128)} %pairs_ref.9) | copy-start | bytes 1540
  3.2 26.4 %copy-start = (bf16[64,256,256]{2,1,0:T(8,128)(2,1)S(1)}, bf16[64,256,256]{2,1,0:T(8,128)(2,1)}, u32[]{:S(2)}) copy-start(bf16[64,256,256]{2,1,0:T(8,128)(2,1)} %blocks_ref.7) | copy-start | bytes 25165828
  3.3 1.1 copy-start.1
  4.4 1.1 copy-start.3
  5.9 0.7 copy-start.5
  6.6 0.7 copy-start.6
  19.3 9.6 %collective-permute-start.6 = (f32[8,32,256]{2,1,0:T(8,128)S(1)}, f32[8,32,256]{2,1,0:T(8,128)S(1)}, u32[]{:S(2)}, u32[]{:S(2)}) collective-permute-start(f32[8,32,256]{2,1,0:T(8,128)S(1)} %slice.65), channel_id=1, source_target_pairs={{0,1},{1,0},{2,3},{3,2},{4,5},{5,4},{6,7},{7,6},{8,9},{9,8},{10,11... | collective-permute-start | bytes 786440 | tf_op jit(solution)/shard_map/ppermute | solution.py:289
  19.8 5.6 %collective-permute-start.2 = (bf16[1,64,256]{2,1,0:T(8,128)(2,1)S(1)}, bf16[1,64,256]{2,1,0:T(8,128)(2,1)S(1)}, u32[]{:S(2)}, u32[]{:S(2)}) collective-permute-start(bf16[1,64,256]{2,1,0:T(8,128)(2,1)S(1)} %bitcast.12), channel_id=1, source_target_pairs={{0,8},{1,9},{2,10},{3,11},{4,12},{5,13},{6,14},{7,15},{8,0},{9,1},... | collective-permute-start | bytes 98312 | tf_op jit(solution)/shard_map/ppermute | solution.py:289
  23.5 22.0 %collective-permute-start = (bf16[8,64,256]{2,1,0:T(8,128)(2,1)S(1)}, bf16[8,64,256]{2,1,0:T(8,128)(2,1)S(1)}, u32[]{:S(2)}, u32[]{:S(2)}) collective-permute-start(bf16[8,64,256]{2,1,0:T(8,128)(2,1)S(1)} %get-tuple-element.14.field_ref), channel_id=1, source_target_pairs={{1,0},{2,1},{3,2},{4,3},{5,4},{6,5},{7,6},{8,7},{9,8},{10,9},{11,1... | collective-permute-start | bytes 786440 | tf_op jit(solution)/shard_map/ppermute | solution.py:292
  25.4 8.0 %collective-permute-start.3 = (bf16[2,64,256]{2,1,0:T(8,128)(2,1)S(1)}, bf16[2,64,256]{2,1,0:T(8,128)(2,1)S(1)}, u32[]{:S(2)}, u32[]{:S(2)}) collective-permute-start(bf16[2,64,256]{2,1,0:T(8,128)(2,1)S(1)} %pad_maximum_fusion.4), channel_id=1, source_target_pairs={{0,4},{1,5},{2,6},{3,7},{4,0},{5,1},{6,2},{7,3},{8,12},{9,13},{10,... | collective-permute-start | bytes 196616 | tf_op jit(solution)/shard_map/ppermute | solution.py:289
  28.9 6.8 %collective-permute-start.7 = (f32[4,32,256]{2,1,0:T(8,128)S(1)}, f32[4,32,256]{2,1,0:T(8,128)S(1)}, u32[]{:S(2)}, u32[]{:S(2)}) collective-permute-start(f32[4,32,256]{2,1,0:T(8,128)S(1)} %slice.67), channel_id=1, source_target_pairs={{0,2},{1,3},{2,0},{3,1},{4,6},{5,7},{6,4},{7,5},{8,10},{9,11},{10,... | collective-permute-start | bytes 393224 | tf_op jit(solution)/shard_map/ppermute | solution.py:289
  31.4 16.3 %collective-permute-start.1 = (f32[8,32,256]{2,1,0:T(8,128)S(1)}, f32[8,32,256]{2,1,0:T(8,128)S(1)}, u32[]{:S(2)}, u32[]{:S(2)}) collective-permute-start(f32[8,32,256]{2,1,0:T(8,128)S(1)} %get-tuple-element.16), channel_id=1, source_target_pairs={{0,1},{1,2},{2,3},{3,4},{4,5},{5,6},{6,7},{7,8},{8,9},{9,10},{10,1... | collective-permute-start | bytes 786440 | tf_op jit(solution)/shard_map/ppermute | solution.py:292
  33.5 6.1 %collective-permute-start.4 = (bf16[4,64,256]{2,1,0:T(8,128)(2,1)S(1)}, bf16[4,64,256]{2,1,0:T(8,128)(2,1)S(1)}, u32[]{:S(2)}, u32[]{:S(2)}) collective-permute-start(bf16[4,64,256]{2,1,0:T(8,128)(2,1)S(1)} %pad_maximum_fusion.2), channel_id=1, source_target_pairs={{0,2},{1,3},{2,0},{3,1},{4,6},{5,7},{6,4},{7,5},{8,10},{9,11},{10,... | collective-permute-start | bytes 393224 | tf_op jit(solution)/shard_map/ppermute | solution.py:289
  35.8 6.2 %collective-permute-start.8 = (f32[2,32,256]{2,1,0:T(8,128)S(1)}, f32[2,32,256]{2,1,0:T(8,128)S(1)}, u32[]{:S(2)}, u32[]{:S(2)}) collective-permute-start(f32[2,32,256]{2,1,0:T(8,128)S(1)} %slice.69), channel_id=1, source_target_pairs={{0,4},{1,5},{2,6},{3,7},{4,0},{5,1},{6,2},{7,3},{8,12},{9,13},{10,... | collective-permute-start | bytes 196616 | tf_op jit(solution)/shard_map/ppermute | solution.py:289
  39.6 8.1 %collective-permute-start.5 = (bf16[8,64,256]{2,1,0:T(8,128)(2,1)S(1)}, bf16[8,64,256]{2,1,0:T(8,128)(2,1)S(1)}, u32[]{:S(2)}, u32[]{:S(2)}) collective-permute-start(bf16[8,64,256]{2,1,0:T(8,128)(2,1)S(1)} %pad_maximum_fusion.low_ref), channel_id=1, source_target_pairs={{0,1},{1,0},{2,3},{3,2},{4,5},{5,4},{6,7},{7,6},{8,9},{9,8},{10,11... | collective-permute-start | bytes 786440 | tf_op jit(solution)/shard_map/ppermute | solution.py:289
  42.0 5.7 %collective-permute-start.9 = (f32[1,32,256]{2,1,0:T(8,128)S(1)}, f32[1,32,256]{2,1,0:T(8,128)S(1)}, u32[]{:S(2)}, u32[]{:S(2)}) collective-permute-start(f32[1,32,256]{2,1,0:T(8,128)S(1)} %get-tuple-element.33), channel_id=1, source_target_pairs={{0,8},{1,9},{2,10},{3,11},{4,12},{5,13},{6,14},{7,15},{8,0},{9,1},... | collective-permute-start | bytes 98312 | tf_op jit(solution)/shard_map/ppermute | solution.py:289
  51.3 8.0 %collective-permute-start.16 = (f32[8,32,256]{2,1,0:T(8,128)S(1)}, f32[8,32,256]{2,1,0:T(8,128)S(1)}, u32[]{:S(2)}, u32[]{:S(2)}) collective-permute-start(f32[8,32,256]{2,1,0:T(8,128)S(1)} %slice.73), channel_id=1, source_target_pairs={{0,1},{1,0},{2,3},{3,2},{4,5},{5,4},{6,7},{7,6},{8,9},{9,8},{10,11... | collective-permute-start | bytes 786440 | tf_op jit(solution)/shard_map/ppermute | solution.py:289
  51.4 4.9 %collective-permute-start.12 = (bf16[1,64,256]{2,1,0:T(8,128)(2,1)S(1)}, bf16[1,64,256]{2,1,0:T(8,128)(2,1)S(1)}, u32[]{:S(2)}, u32[]{:S(2)}) collective-permute-start(bf16[1,64,256]{2,1,0:T(8,128)(2,1)S(1)} %bitcast.8), channel_id=1, source_target_pairs={{0,8},{1,9},{2,10},{3,11},{4,12},{5,13},{6,14},{7,15},{8,0},{9,1},... | collective-permute-start | bytes 98312 | tf_op jit(solution)/shard_map/ppermute | solution.py:289
  56.3 9.6 %collective-permute-start.13 = (bf16[2,64,256]{2,1,0:T(8,128)(2,1)S(1)}, bf16[2,64,256]{2,1,0:T(8,128)(2,1)S(1)}, u32[]{:S(2)}, u32[]{:S(2)}) collective-permute-start(bf16[2,64,256]{2,1,0:T(8,128)(2,1)S(1)} %pad_maximum_fusion.5), channel_id=1, source_target_pairs={{0,4},{1,5},{2,6},{3,7},{4,0},{5,1},{6,2},{7,3},{8,12},{9,13},{10,... | collective-permute-start | bytes 196616 | tf_op jit(solution)/shard_map/ppermute | solution.py:289
  59.4 9.4 %collective-permute-start.17 = (f32[4,32,256]{2,1,0:T(8,128)S(1)}, f32[4,32,256]{2,1,0:T(8,128)S(1)}, u32[]{:S(2)}, u32[]{:S(2)}) collective-permute-start(f32[4,32,256]{2,1,0:T(8,128)S(1)} %slice.75), channel_id=1, source_target_pairs={{0,2},{1,3},{2,0},{3,1},{4,6},{5,7},{6,4},{7,5},{8,10},{9,11},{10,... | collective-permute-start | bytes 393224 | tf_op jit(solution)/shard_map/ppermute | solution.py:289
  59.5 20.3 %copy-start.2 = (f32[32,2048]{1,0:T(8,128)S(1)}, f32[32,2048]{1,0:T(8,128)}, u32[]{:S(2)}) copy-start(f32[32,2048]{1,0:T(8,128)} %right_ref.5) | copy-start | bytes 786436
  61.3 16.3 %collective-permute-start.10 = (bf16[8,64,256]{2,1,0:T(8,128)(2,1)S(1)}, bf16[8,64,256]{2,1,0:T(8,128)(2,1)S(1)}, u32[]{:S(2)}, u32[]{:S(2)}) collective-permute-start(bf16[8,64,256]{2,1,0:T(8,128)(2,1)S(1)} %get-tuple-element.18.field_ref), channel_id=1, source_target_pairs={{1,0},{2,1},{3,2},{4,3},{5,4},{6,5},{7,6},{8,7},{9,8},{10,9},{11,1... | collective-permute-start | bytes 786440 | tf_op jit(solution)/shard_map/ppermute | solution.py:292
  62.6 17.2 %collective-permute-start.11 = (f32[8,32,256]{2,1,0:T(8,128)S(1)}, f32[8,32,256]{2,1,0:T(8,128)S(1)}, u32[]{:S(2)}, u32[]{:S(2)}) collective-permute-start(f32[8,32,256]{2,1,0:T(8,128)S(1)} %get-tuple-element.20), channel_id=1, source_target_pairs={{0,1},{1,2},{2,3},{3,4},{4,5},{5,6},{6,7},{7,8},{8,9},{9,10},{10,1... | collective-permute-start | bytes 786440 | tf_op jit(solution)/shard_map/ppermute | solution.py:292
  65.9 6.9 %collective-permute-start.14 = (bf16[4,64,256]{2,1,0:T(8,128)(2,1)S(1)}, bf16[4,64,256]{2,1,0:T(8,128)(2,1)S(1)}, u32[]{:S(2)}, u32[]{:S(2)}) collective-permute-start(bf16[4,64,256]{2,1,0:T(8,128)(2,1)S(1)} %pad_maximum_fusion.3), channel_id=1, source_target_pairs={{0,2},{1,3},{2,0},{3,1},{4,6},{5,7},{6,4},{7,5},{8,10},{9,11},{10,... | collective-permute-start | bytes 393224 | tf_op jit(solution)/shard_map/ppermute | solution.py:289
  68.8 5.7 %collective-permute-start.18 = (f32[2,32,256]{2,1,0:T(8,128)S(1)}, f32[2,32,256]{2,1,0:T(8,128)S(1)}, u32[]{:S(2)}, u32[]{:S(2)}) collective-permute-start(f32[2,32,256]{2,1,0:T(8,128)S(1)} %slice.77), channel_id=1, source_target_pairs={{0,4},{1,5},{2,6},{3,7},{4,0},{5,1},{6,2},{7,3},{8,12},{9,13},{10,... | collective-permute-start | bytes 196616 | tf_op jit(solution)/shard_map/ppermute | solution.py:289
  72.8 7.0 %collective-permute-start.15 = (bf16[8,64,256]{2,1,0:T(8,128)(2,1)S(1)}, bf16[8,64,256]{2,1,0:T(8,128)(2,1)S(1)}, u32[]{:S(2)}, u32[]{:S(2)}) collective-permute-start(bf16[8,64,256]{2,1,0:T(8,128)(2,1)S(1)} %pad_maximum_fusion.1.low_ref), channel_id=1, source_target_pairs={{0,1},{1,0},{2,3},{3,2},{4,5},{5,4},{6,7},{7,6},{8,9},{9,8},{10,11... | collective-permute-start | bytes 786440 | tf_op jit(solution)/shard_map/ppermute | solution.py:289
  74.5 5.2 %collective-permute-start.19 = (f32[1,32,256]{2,1,0:T(8,128)S(1)}, f32[1,32,256]{2,1,0:T(8,128)S(1)}, u32[]{:S(2)}, u32[]{:S(2)}) collective-permute-start(f32[1,32,256]{2,1,0:T(8,128)S(1)} %get-tuple-element.31), channel_id=1, source_target_pairs={{0,8},{1,9},{2,10},{3,11},{4,12},{5,13},{6,14},{7,15},{8,0},{9,1},... | collective-permute-start | bytes 98312 | tf_op jit(solution)/shard_map/ppermute | solution.py:289
  84.4 1.3 %collective-permute-start.20 = (f32[96,128]{1,0:T(8,128)S(1)}, f32[96,128]{1,0:T(8,128)S(1)}, u32[]{:S(2)}, u32[]{:S(2)}) collective-permute-start(f32[96,128]{1,0:T(8,128)S(1)} %get-tuple-element.23), channel_id=1, source_target_pairs={{0,1},{1,0},{2,3},{3,2},{4,5},{5,4},{6,7},{7,6},{8,9},{9,8},{10,11... | collective-permute-start | bytes 147464 | tf_op jit(solution)/shard_map/ppermute | solution.py:289
  85.7 4.8 %collective-permute-start.21 = (f32[96,128]{1,0:T(8,128)S(1)}, f32[96,128]{1,0:T(8,128)S(1)}, u32[]{:S(2)}, u32[]{:S(2)}) collective-permute-start(f32[96,128]{1,0:T(8,128)S(1)} %add.33), channel_id=1, source_target_pairs={{0,2},{1,3},{2,0},{3,1},{4,6},{5,7},{6,4},{7,5},{8,10},{9,11},{10,... | collective-permute-start | bytes 147464 | tf_op jit(solution)/shard_map/ppermute | solution.py:289
  90.5 4.2 %collective-permute-start.22 = (f32[96,128]{1,0:T(8,128)S(1)}, f32[96,128]{1,0:T(8,128)S(1)}, u32[]{:S(2)}, u32[]{:S(2)}) collective-permute-start(f32[96,128]{1,0:T(8,128)S(1)} %add.34), channel_id=1, source_target_pairs={{0,4},{1,5},{2,6},{3,7},{4,0},{5,1},{6,2},{7,3},{8,12},{9,13},{10,... | collective-permute-start | bytes 147464 | tf_op jit(solution)/shard_map/ppermute | solution.py:289
  94.7 5.0 %collective-permute-start.23 = (f32[96,128]{1,0:T(8,128)S(1)}, f32[96,128]{1,0:T(8,128)S(1)}, u32[]{:S(2)}, u32[]{:S(2)}) collective-permute-start(f32[96,128]{1,0:T(8,128)S(1)} %add.35.kept_ref), channel_id=1, source_target_pairs={{0,8},{1,9},{2,10},{3,11},{4,12},{5,13},{6,14},{7,15},{8,0},{9,1},... | collective-permute-start | bytes 147464 | tf_op jit(solution)/shard_map/ppermute | solution.py:289
where the time goes:
time: 115 us
  starting transfers between devices  44.1 us (38%)
  Pallas kernels  43.2 us (38%)
  waiting for transfers between devices  19 us (17%)
  local copies, waits for them, and re-layouts  6.93 us (6%)
  between operations  1.65 us (1%)
    ppermute x20, starting transfers between devices, across(): return lax.ppermute(x, 'leaf', [(i, i ^ bit) for i in range(devices)])  37 us
    pallas_call x7, Pallas kernels, call(): pl.pallas_call(kernel, out_shape=outs, in_specs=[spec(s) for s in spaces]...  35.2 us
    ppermute x20, waiting for transfers between devices, across(): return lax.ppermute(x, 'leaf', [(i, i ^ bit) for i in range(devices)])  19 us
    pallas_call x4, Pallas kernels, near_call(): pl.pallas_call(kernel, out_shape=outs, grid_spec=pltpu.PrefetchScalarGrid...  7.99 us
    ppermute x4, starting transfers between devices, shift(): lax.ppermute(x, 'leaf', [(i, i + by) for i in range(devices) if 0 <= i +...  7.1 us
    unnamed x15, local copies, waits for them, and re-layouts  4.68 us
  transfers between devices with their start and end apart: 24, of which 8 were waited for; matrix products, arithmetic and copies ran while one was open for 0% of the time, Pallas kernels for 7%

commit v1 on v0

v1 whole, which is shorter than its diff:
```python
import functools

import jax
import jax.numpy as jnp
from jax import lax
from jax.experimental import pallas as pl
from jax.experimental.pallas import tpu as pltpu
from jax.sharding import PartitionSpec as P

PANEL = 256
R = 32
K = 32
GROUP = 8
highest = lax.Precision.HIGHEST
VMEM = pltpu.VMEM
SMEM = pltpu.SMEM
TN = (((0,), (0,)), ((), ()))
NT = (((1,), (1,)), ((), ()))
f32 = jnp.float32
bf16 = jnp.bfloat16


def spec(space):
    return pl.BlockSpec(memory_space=space)


def call(kernel, outs, ins, spaces, scratch=(), limit=40, flops=10**8, moved=10**6):
    return pl.pallas_call(
        kernel,
        out_shape=outs,
        in_specs=[spec(s) for s in spaces],
        out_specs=jax.tree.map(lambda _: spec(VMEM), outs),
        scratch_shapes=list(scratch),
        compiler_params=pltpu.CompilerParams(vmem_limit_bytes=limit << 20),
        cost_estimate=pl.CostEstimate(flops=flops, bytes_accessed=moved, transcendentals=0),
    )(*ins)


def dot(x, y):
    return jnp.dot(x, y, preferred_element_type=f32)


def dot_nt(x, y):
    return lax.dot_general(x, y, NT, preferred_element_type=f32)


def exact_nt(x, y):
    return lax.dot_general(x, y, NT, precision=highest, preferred_element_type=f32)


def split_rows(x):
    high = x.astype(bf16)
    low = (x - high.astype(f32)).astype(bf16)
    return jnp.concatenate([high, low], axis=0)


def join_rows(x):
    return x[:R] + x[R:]


def lane_group(shape):
    return lax.broadcasted_iota(jnp.int32, shape, 1) // K


def project(fields, basis, clusters):
    group = lane_group((2 * R, clusters * K))
    total = jnp.zeros((2 * R, clusters * K), f32)
    for c in range(clusters):
        total = total + jnp.where(group == c, dot_nt(fields[c], basis), 0.0)
    return join_rows(total).astype(bf16)


def start_kernel(right_ref, basis_ref, field_ref, proj_ref):
    clusters = field_ref.shape[0]
    fields = []
    for c in range(clusters):
        field = split_rows(right_ref[:, c * PANEL : (c + 1) * PANEL])
        field_ref[c] = field
        fields.append(field)
    proj_ref[...] = project(fields, basis_ref[...], clusters)


def places(devices):
    bits = devices.bit_length() - 1
    order = [0] + list(range(bits - 1, 0, -1))
    place = [sum(((d >> b) & 1) << (bits - 1 - t) for t, b in enumerate(order)) for d in range(devices)]
    return order, place


def couple_kernel(order, me_ref, pairs_hbm, slots_hbm, coupling_ref, out_ref, wide, pairs_ref, slots_ref, sems):
    clusters = out_ref.shape[2] // K
    pairs = coupling_ref.shape[0] // K
    me = me_ref[0]
    copies = [
        pltpu.make_async_copy(pairs_hbm, pairs_ref, sems.at[0]),
        pltpu.make_async_copy(slots_hbm, slots_ref, sems.at[1]),
    ]
    for copy in copies:
        copy.start()
    out_ref[...] = jnp.zeros_like(out_ref)
    rows = lax.broadcasted_iota(jnp.int32, (K, clusters * K), 0)
    lanes = lax.broadcasted_iota(jnp.int32, (K, clusters * K), 1)
    spread = jnp.where(lanes % K == rows, 1.0, 0.0).astype(bf16)
    wide[...] = dot(coupling_ref[...], spread).astype(bf16)
    group = lanes // K
    for copy in copies:
        copy.wait()

    def one(f):
        first = slots_ref[pairs_ref[0, f]]
        second = slots_ref[pairs_ref[1, f]]
        first_home, second_home = first // clusters, second // clusters
        own = (first_home == me).astype(jnp.int32)
        apart = (first_home + second_home - me) ^ me
        place = jnp.int32(0)
        for t, b in enumerate(order):
            place = place + (((apart >> b) & 1) << (len(order) - 1 - t))
        block = wide[pl.ds(pl.multiple_of(f * K, K), K), :]
        block = jnp.where(group == second % clusters, block, jnp.zeros_like(block))
        here = pl.ds(pl.multiple_of((first % clusters) * K, K), K)
        where = own * (1 << len(order)) + place
        out_ref[where, here, :] = out_ref[where, here, :] + block

    def some(step, carry):
        for u in range(4):
            one(step * 4 + u)
        return carry

    lax.fori_loop(0, pairs // 4, some, 0)


def send_kernel(coupled_ref, proj_ref, out_ref):
    devices = out_ref.shape[0]
    proj = proj_ref[...]
    for d in range(devices):
        out_ref[d] = dot(proj, coupled_ref[devices + d]) + dot_nt(proj, coupled_ref[d])


def near_specs(nb, group):
    return pl.BlockSpec((group, PANEL, PANEL), lambda g, pairs, count: (jnp.minimum(g, (count[0] - 1) // group), 0, 0))


def whole(shape):
    return pl.BlockSpec(shape, lambda g, pairs, count: (0,) * len(shape))


def near_cols_kernel(pairs_ref, count_ref, blocks_ref, field_ref, own_ref, next_ref, total):
    g = pl.program_id(0)
    clusters = field_ref.shape[0]

    @pl.when(g == 0)
    def _():
        total[...] = jnp.zeros_like(total)

    @pl.when(g * GROUP < count_ref[0])
    def _():
        for u in range(GROUP):
            s = g * GROUP + u
            i = pairs_ref[0, s]
            j = jnp.where(s < count_ref[0], pairs_ref[1, s], 2 * clusters)
            total[j] = total[j] + join_rows(dot(field_ref[i], blocks_ref[u]))

    @pl.when(g == pl.num_programs(0) - 1)
    def _():
        own_ref[...] = total[:clusters]
        next_ref[...] = total[clusters : 2 * clusters].astype(bf16)


def near_rows_kernel(pairs_ref, count_ref, blocks_ref, field_ref, after_ref, begun_ref, out_ref, window, total):
    g = pl.program_id(0)
    clusters = field_ref.shape[0]

    @pl.when(g == 0)
    def _():
        window[:clusters] = field_ref[...]
        window[clusters:] = after_ref[...]
        total[:clusters] = begun_ref[...]

    @pl.when(g * GROUP < count_ref[0])
    def _():
        for u in range(GROUP):
            s = g * GROUP + u
            i = jnp.where(s < count_ref[0], pairs_ref[0, s], clusters)
            j = pairs_ref[1, s]
            total[i] = total[i] + join_rows(dot_nt(window[j], blocks_ref[u]))

    @pl.when(g == pl.num_programs(0) - 1)
    def _():
        out_ref[...] = total[:clusters]


def near_call(kernel, outs, near_pairs, near_count, near_blocks, arrays, scratch):
    nb = near_blocks.shape[0]
    return pl.pallas_call(
        kernel,
        out_shape=outs,
        grid_spec=pltpu.PrefetchScalarGridSpec(
            num_scalar_prefetch=2,
            grid=(nb // GROUP,),
            in_specs=[near_specs(nb, GROUP)] + [whole(a.shape) for a in arrays],
            out_specs=jax.tree.map(lambda o: whole(o.shape), outs),
            scratch_shapes=scratch,
        ),
        compiler_params=pltpu.CompilerParams(
            vmem_limit_bytes=24 << 20, dimension_semantics=("arbitrary",)
        ),
        cost_estimate=pl.CostEstimate(
            flops=nb * 64 * PANEL * PANEL * 2, bytes_accessed=nb * PANEL * PANEL * 2, transcendentals=0
        ),
    )(near_pairs, near_count, near_blocks, *arrays)


def far_fields(place, coupled_ref, low_ref, high_ref, kept_ref, got_ref, basis):
    devices = coupled_ref.shape[0] // 2
    sums = kept_ref[0] + got_ref[0].astype(f32)
    order = places(devices)[0]
    for g in range(devices):
        proj = low_ref[g] if g < devices // 2 else high_ref[g - devices // 2]
        apart = sum(((g >> t) & 1) << b for t, b in enumerate(order))
        sums = sums + dot(proj, coupled_ref[place[apart]]) + dot_nt(proj, coupled_ref[devices + place[apart]])
    sums = split_rows(sums)
    group = lane_group(sums.shape)
    zero = jnp.zeros_like(sums)
    return lambda c: join_rows(dot(jnp.where(group == c, sums, zero), basis))


def finish_one_kernel(place, coupled_ref, near_ref, back_ref, low_ref, high_ref, kept_ref, got_ref, basis_ref,
                      image_ref, field_ref, proj_ref):
    clusters = near_ref.shape[0]
    basis = basis_ref[...]
    far = far_fields(place, coupled_ref, low_ref, high_ref, kept_ref, got_ref, basis)
    fields = []
    for c in range(clusters):
        image = near_ref[c] + back_ref[c].astype(f32) + far(c)
        image_ref[c] = image
        field = split_rows(image)
        field_ref[c] = field
        fields.append(field)
    proj_ref[...] = project(fields, basis, clusters)


def finish_two_kernel(place, coupled_ref, near_ref, back_ref, low_ref, high_ref, kept_ref, got_ref, basis_ref,
                      right_ref, image_ref, second_ref, gram_ref):
    clusters = near_ref.shape[0]
    basis = basis_ref[...]
    far = far_fields(place, coupled_ref, low_ref, high_ref, kept_ref, got_ref, basis)
    gram = jnp.zeros((2 * R, 4 * R), f32)
    corner = jnp.zeros((R, 4 * R), f32)
    zero = jnp.zeros((R, PANEL), f32)
    for c in range(clusters):
        second = near_ref[c] + back_ref[c].astype(f32) + far(c)
        second_ref[c] = second
        right = right_ref[:, c * PANEL : (c + 1) * PANEL]
        image = image_ref[c]
        gram = gram + exact_nt(
            jnp.concatenate([image, second], axis=0), jnp.concatenate([right, image, second, zero], axis=0)
        )
        corner = corner + exact_nt(right, jnp.concatenate([zero, zero, right, zero], axis=0))
    lanes = lax.broadcasted_iota(jnp.int32, (R, 4 * R), 1)
    gram_ref[:R] = jnp.where(lanes // R == 2, corner, gram[:R])
    gram_ref[R:] = gram[R:]


def lane(x, k):
    return jnp.broadcast_to(x[:, k : k + 1], x.shape)


def last_kernel(kept_ref, got_ref, right_ref, image_ref, second_ref, field_ref, residual_ref, hessenberg_ref):
    clusters = image_ref.shape[0]
    gram = kept_ref[...] + got_ref[...]
    top, bottom = gram[:R], gram[R:]
    lanes = lax.broadcasted_iota(jnp.int32, (2 * R, 4 * R), 1)
    rows = lax.broadcasted_iota(jnp.int32, (2 * R, 4 * R), 0)
    wide = jnp.zeros((R, R), f32)
    first_first, image_first = top[:, 2 * R : 3 * R], top[:, :R]
    image_image, second_first, second_image = top[:, R : 2 * R], bottom[:, :R], bottom[:, R : 2 * R]
    second_second = bottom[:, 2 * R : 3 * R]
    system = jnp.concatenate(
        [
            jnp.concatenate([image_image, second_image.T, image_first, wide], axis=1),
            jnp.concatenate([second_image, second_second, second_first, wide], axis=1),
        ],
        axis=0,
    )
    lower = jnp.concatenate(
        [
            jnp.concatenate([first_first, image_first.T, wide, wide], axis=1),
            jnp.concatenate([image_first, image_image, wide, wide], axis=1),
        ],
        axis=0,
    )
    lower = jnp.where(lanes - 2 * R == rows, 1.0, lower)

    def two(matrix, k):
        p, q = matrix[k : k + 1], matrix[k + 1 : k + 2]
        a, b, c, d = lane(p, k), lane(p, k + 1), lane(q, k), lane(q, k + 1)
        scale = 1.0 / (a * d - b * c)
        p_new, q_new = (d * p - b * q) * scale, (a * q - c * p) * scale
        rest = matrix - lane(matrix, k) * p_new - lane(matrix, k + 1) * q_new
        return p, q, a, c, p_new, q_new, rest

    for k in range(0, 2 * R, 2):
        p, q, a, c, p_new, q_new, rest = two(system, k)
        system = jnp.where(rows == k, p_new, jnp.where(rows == k + 1, q_new, rest))
        p, q, a, c, p_new, q_new, rest = two(lower, k)
        lower = jnp.where(rows > k + 1, rest, jnp.where(rows == k + 1, q - c / a * p, lower))
    diagonal = jnp.sum(jnp.where(lanes == rows, lower, 0.0), axis=1, keepdims=True)
    lower = lower * lax.rsqrt(diagonal)
    weights = system.T[2 * R : 3 * R, : 2 * R]
    inverse_zero = lower[:R, 2 * R : 3 * R]
    hessenberg_ref[:R] = exact_nt(lower[:R, R : 2 * R], inverse_zero)
    hessenberg_ref[R:] = exact_nt(inverse_zero, lower[R:, R : 2 * R])
    for c in range(clusters):
        here = slice(c * PANEL, (c + 1) * PANEL)
        right, image, second = right_ref[:, here], image_ref[c], second_ref[c]

        def combine(x, y):
            return jnp.dot(
                weights, jnp.concatenate([x, y], axis=0), precision=highest, preferred_element_type=f32
            )

        field_ref[:, here] = combine(right, image)
        residual_ref[:, here] = right - combine(image, second)


def body(right_side, near_pairs, near_count, near_blocks, far_pairs, coupling, cluster_basis, cluster_slot):
    devices = lax.axis_size("leaf")
    order, place = places(devices)
    clusters = cluster_basis.shape[0]
    me = lax.axis_index("leaf").astype(jnp.int32).reshape(1)
    basis = cluster_basis.reshape(clusters * K, PANEL)
    sds = jax.ShapeDtypeStruct

    def across(x, b):
        return lax.ppermute(x, "leaf", [(i, i ^ (1 << b)) for i in range(devices)])

    def shift(x, by):
        return lax.ppermute(x, "leaf", [(i, i + by) for i in range(devices) if 0 <= i + by < devices])

    panels = sds((clusters, R, PANEL), f32)
    split = sds((clusters, 2 * R, PANEL), bf16)
    rank = sds((R, clusters * K), bf16)

    field, proj = call(start_kernel, (split, rank), (right_side, basis), (VMEM, VMEM))
    coupled = call(
        functools.partial(couple_kernel, order),
        sds((2 * devices, clusters * K, clusters * K), bf16),
        (me, far_pairs, cluster_slot, coupling.reshape(-1, K)),
        (SMEM, pl.ANY, pl.ANY, VMEM),
        [
            pltpu.VMEM((coupling.shape[0] * K, clusters * K), bf16),
            pltpu.SMEM(far_pairs.shape, jnp.int32),
            pltpu.SMEM(cluster_slot.shape, jnp.int32),
            pltpu.SemaphoreType.DMA((2,)),
        ],
    )

    def exchange(field, proj):
        after = shift(field, -1)
        sums = call(send_kernel, sds((devices, R, clusters * K), f32), (coupled, proj), (VMEM, VMEM))
        own, following = near_call(
            near_cols_kernel, (panels, sds(panels.shape, bf16)), near_pairs, near_count, near_blocks, (field,),
            [pltpu.VMEM((2 * clusters + 1, R, PANEL), f32)],
        )
        back = shift(following, 1)
        gathered = proj[None]
        for t, b in enumerate(order):
            held, half = gathered.shape[0], sums.shape[0] // 2
            got = across(jnp.concatenate([gathered, sums[half:].astype(bf16)], axis=0), b)
            sums, got_gathered, got_sums = sums[:half], got[:held], got[held:]
            if t < len(order) - 1:
                gathered = jnp.concatenate([gathered, got_gathered], axis=0)
                sums = sums + got_sums.astype(f32)
        near = near_call(
            near_rows_kernel, panels, near_pairs, near_count, near_blocks, (field, after, own),
            [pltpu.VMEM((2 * clusters, 2 * R, PANEL), bf16), pltpu.VMEM((clusters + 1, R, PANEL), f32)],
        )
        return (coupled, near, back, gathered, got_gathered, sums, got_sums, basis)

    parts = exchange(field, proj)
    image, field, proj = call(
        functools.partial(finish_one_kernel, place), (panels, split, rank), parts, [VMEM] * 8
    )
    parts = exchange(field, proj)
    second, gram = call(
        functools.partial(finish_two_kernel, place), (panels, sds((2 * R, 4 * R), f32)), parts + (right_side, image),
        [VMEM] * 10,
    )
    got = None
    for t, b in enumerate(order):
        if t > 0:
            gram = gram + got
        got = across(gram, b)
    wide = sds(right_side.shape, f32)
    return call(
        last_kernel, (wide, wide, sds((2 * R, R), f32)), (gram, got, right_side, image, second), [VMEM] * 5
    )


def solution(mesh):
    in_specs = (
        P(None, ("parts", "leaf")),
        P(None, ("parts", "leaf")),
        P(("parts", "leaf")),
        P(("parts", "leaf"), None, None),
        P(None, ("parts", "leaf")),
        P(("parts", "leaf"), None),
        P(("parts", "leaf"), None, None),
        P("parts"),
    )
    out_specs = (P(None, ("parts", "leaf")), P(None, ("parts", "leaf")), P("parts", None))
    return jax.shard_map(body, mesh=mesh, in_specs=in_specs, out_specs=out_specs, check_vma=False)
```

time: 115 us -> 91.3 us (0.79); the launches traced: 115 us -> 90.2 us
  Pallas kernels: 43.2 us -> 24.5 us
  starting transfers between devices: 44.1 us -> 27 us
  waiting for transfers between devices: 19 us -> 30.5 us
    ppermute x20 -> x12, starting transfers between devices: 37 us -> 16.5 us  [across(): return lax.ppermute(x, 'leaf', [(i, i ^ 1 << b) for i in range(devices)])]
    pallas_call x7, Pallas kernels: 35.2 us -> 17.9 us  [call(): pl.pallas_call(kernel, out_shape=outs, in_specs=[spec(s) for s in spaces]...]
    ppermute x20 -> x12, waiting for transfers between devices: 19 us -> 30.5 us  [across(): return lax.ppermute(x, 'leaf', [(i, i ^ 1 << b) for i in range(devices)])]
    ppermute x4, starting transfers between devices: 7.1 us -> 10.5 us  [shift(): lax.ppermute(x, 'leaf', [(i, i + by) for i in range(devices) if 0 <= i +...]
    pallas_call x4, Pallas kernels: 7.99 us -> 6.54 us  [near_call(): pl.pallas_call(kernel, out_shape=outs, grid_spec=pltpu.PrefetchScalarGrid...]
    unnamed x15 -> x22, local copies, waits for them, and re-layouts: 4.68 us -> 3.61 us
  transfers between devices with their start and end apart: 24 -> 16, of which waited for: 8 -> 10; matrix products, arithmetic and copies ran while one was open for 0% -> 0% of each run, Pallas kernels for 7% -> 7%
where the time goes in v1:
time: 91.3 us; the launch traced here: 90.2 us
  waiting for transfers between devices  30.5 us (33%)
  starting transfers between devices  27 us (30%)
  Pallas kernels  24.5 us (27%)
  local copies, waits for them, and re-layouts  6.24 us (7%)
  between operations  1.73 us (2%)
    ppermute x12, waiting for transfers between devices, across(): return lax.ppermute(x, 'leaf', [(i, i ^ 1 << b) for i in range(devices)])  30.5 us
    pallas_call x7, Pallas kernels, call(): pl.pallas_call(kernel, out_shape=outs, in_specs=[spec(s) for s in spaces]...  17.9 us
    ppermute x12, starting transfers between devices, across(): return lax.ppermute(x, 'leaf', [(i, i ^ 1 << b) for i in range(devices)])  16.5 us
    ppermute x4, starting transfers between devices, shift(): lax.ppermute(x, 'leaf', [(i, i + by) for i in range(devices) if 0 <= i +...  10.5 us
    pallas_call x4, Pallas kernels, near_call(): pl.pallas_call(kernel, out_shape=outs, grid_spec=pltpu.PrefetchScalarGrid...  6.54 us
    unnamed x22, local copies, waits for them, and re-layouts  3.61 us
    reshape x1, local copies, waits for them, and re-layouts, body(): coupling.reshape(-1, K)  1.84 us
  transfers between devices with their start and end apart: 16, of which 10 were waited for; matrix products, arithmetic and copies ran while one was open for 0% of the time, Pallas kernels for 7%

profile of v1, /device:TPU:0, one launch (start us, length us, event | category | flops | bytes accessed | tf_op | source)
XLA Modules:
  0.0 90.2 jit_solution(15540616664130768626)
XLA Ops:
  0.6 1.8 %reshape.16.coupling_ref = bf16[4096,32]{1,0:T(8,128)(2,1)S(1)} reshape(bf16[128,1024]{1,0:T(8,128)(2,1)} %param.13) | data formatting | bytes 524288 | tf_op jit(solution)/shard_map/reshape | solution.py:348
  2.5 1.1 %copy-done.1 = f32[32,2048]{1,0:T(8,128)S(1)} copy-done((f32[32,2048]{1,0:T(8,128)S(1)}, f32[32,2048]{1,0:T(8,128)}, u32[]{:S(2)}) %copy-start.1) | copy-done | bytes 262168
  3.6 1.1 %copy-done.3 = bf16[8,32,256]{2,1,0:T(8,128)(2,1)S(1)} copy-done((bf16[8,32,256]{2,1,0:T(8,128)(2,1)S(1)}, bf16[8,32,256]{2,1,0:T(8,128)(2,1)}, u32[]{:S(2)}) %copy-start.3) | copy-done | bytes 131096
  6.5 3.7 %shard_map.103.coupled_ref = bf16[32,256,256]{2,1,0:T(8,128)(2,1)S(1)} custom-call(s32[1]{0:T(128)} %bitcast.me_ref, s32[2,128]{1,0:T(2,128)S(1)} %copy-done.5, s32[128]{0:T(128)S(1)} %copy-done.6, bf16[4096,32]{1,0:T(8,128)(2,1)S(1)} %reshape.16.coupling_ref), custom_call_target="tpu_custom_call" | custom-call | flops 100000000 | bytes 1000000 | tf_op jit(solution)/shard_map/pallas_call | solution.py:28
  10.2 1.1 %shard_map.107 = f32[16,32,256]{2,1,0:T(8,128)S(1)} custom-call(bf16[32,256,256]{2,1,0:T(8,128)(2,1)S(1)} %shard_map.103.coupled_ref, bf16[32,256]{1,0:T(8,128)(2,1)S(1)} %get-tuple-element.17.proj_ref), custom_call_target="tpu_custom_call" | custom-call | flops 100000000 | bytes 1000000 | tf_op jit(solution)/shard_map/pallas_call | solution.py:28
  11.8 1.0 %collective-permute-done.2 = bf16[9,32,256]{2,1,0:T(8,128)(2,1)S(1)} collective-permute-done((bf16[9,32,256]{2,1,0:T(8,128)(2,1)S(1)}, bf16[9,32,256]{2,1,0:T(8,128)(2,1)S(1)}, u32[]{:S(2)}, u32[]{:S(2)}) %collective-permute-start.2) | collective-permute-done | bytes 147488 | tf_op jit(solution)/shard_map/ppermute | solution.py:335
  12.9 4.0 %collective-permute-start.3 = (bf16[6,32,256]{2,1,0:T(8,128)(2,1)S(1)}, bf16[6,32,256]{2,1,0:T(8,128)(2,1)S(1)}, u32[]{:S(2)}, u32[]{:S(2)}) collective-permute-start(bf16[6,32,256]{2,1,0:T(8,128)(2,1)S(1)} %pad_maximum_fusion.4), channel_id=1, source_target_pairs={{0,8},{1,9},{2,10},{3,11},{4,12},{5,13},{6,14},{7,15},{8,0},{9,1},... | collective-permute-start | bytes 294920 | tf_op jit(solution)/shard_map/ppermute | solution.py:335
  16.9 5.2 %collective-permute-done.3 = bf16[6,32,256]{2,1,0:T(8,128)(2,1)S(1)} collective-permute-done((bf16[6,32,256]{2,1,0:T(8,128)(2,1)S(1)}, bf16[6,32,256]{2,1,0:T(8,128)(2,1)S(1)}, u32[]{:S(2)}, u32[]{:S(2)}) %collective-permute-start.3) | collective-permute-done | bytes 98336 | tf_op jit(solution)/shard_map/ppermute | solution.py:335
  23.0 1.3 %collective-permute-start = (bf16[8,64,256]{2,1,0:T(8,128)(2,1)S(1)}, bf16[8,64,256]{2,1,0:T(8,128)(2,1)S(1)}, u32[]{:S(2)}, u32[]{:S(2)}) collective-permute-start(bf16[8,64,256]{2,1,0:T(8,128)(2,1)S(1)} %get-tuple-element.14.field_ref), channel_id=1, source_target_pairs={{1,0},{2,1},{3,2},{4,3},{5,4},{6,5},{7,6},{8,7},{9,8},{10,9},{11,1... | collective-permute-start | bytes 786440 | tf_op jit(solution)/shard_map/ppermute | solution.py:338
  25.0 1.5 %shard_map.105 = (f32[8,32,256]{2,1,0:T(8,128)S(1)}, bf16[8,32,256]{2,1,0:T(8,128)(2,1)S(1)}) custom-call(s32[2,64]{1,0:T(2,128)S(1)} %copy-done.4, s32[1]{0:T(128)S(6)} %copy.21.count_ref, bf16[64,256,256]{2,1,0:T(8,128)(2,1)S(1)} %copy-done, bf16[8,64,256]{2,1,0:T(8,128)(2,1)S(1)} %get-tuple-element.14.field_ref), custom_call_target="tpu_custom_call" | custom-call | flops 536870912 | bytes 8388608 | tf_op jit(solution)/shard_map/pallas_call | solution.py:194
  26.5 3.9 %collective-permute-start.1 = (bf16[8,32,256]{2,1,0:T(8,128)(2,1)S(1)}, bf16[8,32,256]{2,1,0:T(8,128)(2,1)S(1)}, u32[]{:S(2)}, u32[]{:S(2)}) collective-permute-start(bf16[8,32,256]{2,1,0:T(8,128)(2,1)S(1)} %get-tuple-element.16), channel_id=1, source_target_pairs={{0,1},{1,2},{2,3},{3,4},{4,5},{5,6},{6,7},{7,8},{8,9},{9,10},{10,1... | collective-permute-start | bytes 393224 | tf_op jit(solution)/shard_map/ppermute | solution.py:338
  31.3 1.8 %shard_map.106.near_ref = f32[8,32,256]{2,1,0:T(8,128)S(1)} custom-call(s32[2,64]{1,0:T(2,128)S(1)} %copy-done.4, s32[1]{0:T(128)S(6)} %copy.21.count_ref, bf16[64,256,256]{2,1,0:T(8,128)(2,1)S(1)} %copy-done, bf16[8,64,256]{2,1,0:T(8,128)(2,1)S(1)} %get-tuple-element.14.field_ref, bf16[8,64,256]{2,1,0:T(8,128)(2,1)S(1)} %collective-permute-done.after_ref, ...), custom_call_target="tpu_custom_call" | custom-call | flops 536870912 | bytes 8388608 | tf_op jit(solution)/shard_map/pallas_call | solution.py:194
  33.1 4.0 %collective-permute-done.5 = bf16[9,32,256]{2,1,0:T(8,128)(2,1)S(1)} collective-permute-done((bf16[9,32,256]{2,1,0:T(8,128)(2,1)S(1)}, bf16[9,32,256]{2,1,0:T(8,128)(2,1)S(1)}, u32[]{:S(2)}, u32[]{:S(2)}) %collective-permute-start.5) | collective-permute-done | bytes 147488 | tf_op jit(solution)/shard_map/ppermute | solution.py:335
  37.2 2.4 %shard_map.108 = (f32[8,32,256]{2,1,0:T(8,128)S(1)}, bf16[8,64,256]{2,1,0:T(8,128)(2,1)S(1)}, bf16[32,256]{1,0:T(8,128)(2,1)S(1)}) custom-call(bf16[32,256,256]{2,1,0:T(8,128)(2,1)S(1)} %shard_map.103.coupled_ref, f32[8,32,256]{2,1,0:T(8,128)S(1)} %shard_map.106.near_ref, bf16[8,32,256]{2,1,0:T(8,128)(2,1)S(1)} %collective-permute-done.1.back_ref, ...), custom_call_target="tpu_custom_call" | custom-call | flops 100000000 | bytes 1000000 | tf_op jit(solution)/shard_map/pallas_call | solution.py:28
  39.5 1.1 %shard_map.111 = f32[16,32,256]{2,1,0:T(8,128)S(1)} custom-call(bf16[32,256,256]{2,1,0:T(8,128)(2,1)S(1)} %shard_map.103.coupled_ref, bf16[32,256]{1,0:T(8,128)(2,1)S(1)} %get-tuple-element.21.proj_ref), custom_call_target="tpu_custom_call" | custom-call | flops 100000000 | bytes 1000000 | tf_op jit(solution)/shard_map/pallas_call | solution.py:28
  40.8 1.3 %collective-permute-done.8 = bf16[9,32,256]{2,1,0:T(8,128)(2,1)S(1)} collective-permute-done((bf16[9,32,256]{2,1,0:T(8,128)(2,1)S(1)}, bf16[9,32,256]{2,1,0:T(8,128)(2,1)S(1)}, u32[]{:S(2)}, u32[]{:S(2)}) %collective-permute-start.8) | collective-permute-done | bytes 147488 | tf_op jit(solution)/shard_map/ppermute | solution.py:335
  42.2 3.2 %collective-permute-start.9 = (bf16[6,32,256]{2,1,0:T(8,128)(2,1)S(1)}, bf16[6,32,256]{2,1,0:T(8,128)(2,1)S(1)}, u32[]{:S(2)}, u32[]{:S(2)}) collective-permute-start(bf16[6,32,256]{2,1,0:T(8,128)(2,1)S(1)} %pad_maximum_fusion.7), channel_id=1, source_target_pairs={{0,8},{1,9},{2,10},{3,11},{4,12},{5,13},{6,14},{7,15},{8,0},{9,1},... | collective-permute-start | bytes 294920 | tf_op jit(solution)/shard_map/ppermute | solution.py:335
  45.4 5.4 %collective-permute-done.9 = bf16[6,32,256]{2,1,0:T(8,128)(2,1)S(1)} collective-permute-done((bf16[6,32,256]{2,1,0:T(8,128)(2,1)S(1)}, bf16[6,32,256]{2,1,0:T(8,128)(2,1)S(1)}, u32[]{:S(2)}, u32[]{:S(2)}) %collective-permute-start.9) | collective-permute-done | bytes 98336 | tf_op jit(solution)/shard_map/ppermute | solution.py:335
  51.7 1.4 %collective-permute-start.6 = (bf16[8,64,256]{2,1,0:T(8,128)(2,1)S(1)}, bf16[8,64,256]{2,1,0:T(8,128)(2,1)S(1)}, u32[]{:S(2)}, u32[]{:S(2)}) collective-permute-start(bf16[8,64,256]{2,1,0:T(8,128)(2,1)S(1)} %get-tuple-element.18.field_ref), channel_id=1, source_target_pairs={{1,0},{2,1},{3,2},{4,3},{5,4},{6,5},{7,6},{8,7},{9,8},{10,9},{11,1... | collective-permute-start | bytes 786440 | tf_op jit(solution)/shard_map/ppermute | solution.py:338
  53.1 1.5 %shard_map.109 = (f32[8,32,256]{2,1,0:T(8,128)S(1)}, bf16[8,32,256]{2,1,0:T(8,128)(2,1)S(1)}) custom-call(s32[2,64]{1,0:T(2,128)S(1)} %copy-done.4, s32[1]{0:T(128)S(6)} %copy.21.count_ref, bf16[64,256,256]{2,1,0:T(8,128)(2,1)S(1)} %copy-done, bf16[8,64,256]{2,1,0:T(8,128)(2,1)S(1)} %get-tuple-element.18.field_ref), custom_call_target="tpu_custom_call" | custom-call | flops 536870912 | bytes 8388608 | tf_op jit(solution)/shard_map/pallas_call | solution.py:194
  54.6 3.9 %collective-permute-start.7 = (bf16[8,32,256]{2,1,0:T(8,128)(2,1)S(1)}, bf16[8,32,256]{2,1,0:T(8,128)(2,1)S(1)}, u32[]{:S(2)}, u32[]{:S(2)}) collective-permute-start(bf16[8,32,256]{2,1,0:T(8,128)(2,1)S(1)} %get-tuple-element.20), channel_id=1, source_target_pairs={{0,1},{1,2},{2,3},{3,4},{4,5},{5,6},{6,7},{7,8},{8,9},{9,10},{10,1... | collective-permute-start | bytes 393224 | tf_op jit(solution)/shard_map/ppermute | solution.py:338
  59.3 1.8 %shard_map.110.near_ref = f32[8,32,256]{2,1,0:T(8,128)S(1)} custom-call(s32[2,64]{1,0:T(2,128)S(1)} %copy-done.4, s32[1]{0:T(128)S(6)} %copy.21.count_ref, bf16[64,256,256]{2,1,0:T(8,128)(2,1)S(1)} %copy-done, bf16[8,64,256]{2,1,0:T(8,128)(2,1)S(1)} %get-tuple-element.18.field_ref, bf16[8,64,256]{2,1,0:T(8,128)(2,1)S(1)} %collective-permute-done.6.after_ref, ...), custom_call_target="tpu_custom_call" | custom-call | flops 536870912 | bytes 8388608 | tf_op jit(solution)/shard_map/pallas_call | solution.py:194
  61.1 4.0 %collective-permute-done.11 = bf16[9,32,256]{2,1,0:T(8,128)(2,1)S(1)} collective-permute-done((bf16[9,32,256]{2,1,0:T(8,128)(2,1)S(1)}, bf16[9,32,256]{2,1,0:T(8,128)(2,1)S(1)}, u32[]{:S(2)}, u32[]{:S(2)}) %collective-permute-start.11) | collective-permute-done | bytes 147488 | tf_op jit(solution)/shard_map/ppermute | solution.py:335
  65.2 4.3 %shard_map.112 = (f32[8,32,256]{2,1,0:T(8,128)S(1)}, f32[64,128]{1,0:T(8,128)S(1)}) custom-call(bf16[32,256,256]{2,1,0:T(8,128)(2,1)S(1)} %shard_map.103.coupled_ref, f32[8,32,256]{2,1,0:T(8,128)S(1)} %shard_map.110.near_ref, bf16[8,32,256]{2,1,0:T(8,128)(2,1)S(1)} %collective-permute-done.7.back_ref, bf16[8,32,256]{2,1,0:T(8,128)(2,1)S(1)} %pad_maximum_fusion.3.low_ref, ...), custom_call_target="tpu_custom_call" | custom-call | flops 100000000 | bytes 1000000 | tf_op jit(solution)/shard_map/pallas_call | solution.py:28
  69.5 1.2 %collective-permute-done.12 = f32[64,128]{1,0:T(8,128)S(1)} collective-permute-done((f32[64,128]{1,0:T(8,128)S(1)}, f32[64,128]{1,0:T(8,128)S(1)}, u32[]{:S(2)}, u32[]{:S(2)}) %collective-permute-start.12) | collective-permute-done | bytes 32800 | tf_op jit(solution)/shard_map/ppermute | solution.py:335
  70.7 3.8 %collective-permute-start.13 = (f32[64,128]{1,0:T(8,128)S(1)}, f32[64,128]{1,0:T(8,128)S(1)}, u32[]{:S(2)}, u32[]{:S(2)}) collective-permute-start(f32[64,128]{1,0:T(8,128)S(1)} %add.33), channel_id=1, source_target_pairs={{0,8},{1,9},{2,10},{3,11},{4,12},{5,13},{6,14},{7,15},{8,0},{9,1},... | collective-permute-start | bytes 98312 | tf_op jit(solution)/shard_map/ppermute | solution.py:335
  74.5 2.1 %collective-permute-done.13 = f32[64,128]{1,0:T(8,128)S(1)} collective-permute-done((f32[64,128]{1,0:T(8,128)S(1)}, f32[64,128]{1,0:T(8,128)S(1)}, u32[]{:S(2)}, u32[]{:S(2)}) %collective-permute-start.13) | collective-permute-done | bytes 32800 | tf_op jit(solution)/shard_map/ppermute | solution.py:335
  76.7 0.9 %collective-permute-start.14 = (f32[64,128]{1,0:T(8,128)S(1)}, f32[64,128]{1,0:T(8,128)S(1)}, u32[]{:S(2)}, u32[]{:S(2)}) collective-permute-start(f32[64,128]{1,0:T(8,128)S(1)} %add.34), channel_id=1, source_target_pairs={{0,4},{1,5},{2,6},{3,7},{4,0},{5,1},{6,2},{7,3},{8,12},{9,13},{10,... | collective-permute-start | bytes 98312 | tf_op jit(solution)/shard_map/ppermute | solution.py:335
  77.6 3.0 %collective-permute-done.14 = f32[64,128]{1,0:T(8,128)S(1)} collective-permute-done((f32[64,128]{1,0:T(8,128)S(1)}, f32[64,128]{1,0:T(8,128)S(1)}, u32[]{:S(2)}, u32[]{:S(2)}) %collective-permute-start.14) | collective-permute-done | bytes 32800 | tf_op jit(solution)/shard_map/ppermute | solution.py:335
  80.6 0.8 collective-permute-start.15
  81.4 3.1 %collective-permute-done.15.got_ref = f32[64,128]{1,0:T(8,128)S(1)} collective-permute-done((f32[64,128]{1,0:T(8,128)S(1)}, f32[64,128]{1,0:T(8,128)S(1)}, u32[]{:S(2)}, u32[]{:S(2)}) %collective-permute-start.15) | collective-permute-done | bytes 32800 | tf_op jit(solution)/shard_map/ppermute | solution.py:335
  84.5 5.0 %shard_map.113 = (f32[32,2048]{1,0:T(8,128)}, f32[32,2048]{1,0:T(8,128)}, f32[64,32]{1,0:T(8,128)S(1)}) custom-call(f32[64,128]{1,0:T(8,128)S(1)} %add.35.kept_ref, f32[64,128]{1,0:T(8,128)S(1)} %collective-permute-done.15.got_ref, f32[32,2048]{1,0:T(8,128)S(1)} %copy-done.2, f32[8,32,256]{2,1,0:T(8,128)S(1)} %get-tuple-element.22.image_ref, ...), custom_call_target="tpu_custom_call" | custom-call | flops 100000000 | bytes 1000000 | tf_op jit(solution)/shard_map/pallas_call | solution.py:28
  (66 shorter events, 6.5 us)
Async XLA Ops:
  0.6 24.3 %copy-start.4 = (s32[2,64]{1,0:T(2,128)S(1)}, s32[2,64]{1,0:T(2,128)}, u32[]{:S(2)}) copy-start(s32[2,64]{1,0:T(2,128)} %pairs_ref.7) | copy-start | bytes 1540
  2.5 22.5 %copy-start = (bf16[64,256,256]{2,1,0:T(8,128)(2,1)S(1)}, bf16[64,256,256]{2,1,0:T(8,128)(2,1)}, u32[]{:S(2)}) copy-start(bf16[64,256,256]{2,1,0:T(8,128)(2,1)} %blocks_ref.7) | copy-start | bytes 25165828
  2.5 1.1 %copy-start.1 = (f32[32,2048]{1,0:T(8,128)S(1)}, f32[32,2048]{1,0:T(8,128)}, u32[]{:S(2)}) copy-start(f32[32,2048]{1,0:T(8,128)} %right_ref.5) | copy-start | bytes 786436
  3.6 1.1 %copy-start.3 = (bf16[8,32,256]{2,1,0:T(8,128)(2,1)S(1)}, bf16[8,32,256]{2,1,0:T(8,128)(2,1)}, u32[]{:S(2)}) copy-start(bf16[8,32,256]{2,1,0:T(8,128)(2,1)} %param.14) | copy-start | bytes 393220
  5.2 0.7 copy-start.5
  5.8 0.7 copy-start.6
  11.3 1.5 %collective-permute-start.2 = (bf16[9,32,256]{2,1,0:T(8,128)(2,1)S(1)}, bf16[9,32,256]{2,1,0:T(8,128)(2,1)S(1)}, u32[]{:S(2)}, u32[]{:S(2)}) collective-permute-start(bf16[9,32,256]{2,1,0:T(8,128)(2,1)S(1)} %pad_maximum_fusion), channel_id=1, source_target_pairs={{0,1},{1,0},{2,3},{3,2},{4,5},{5,4},{6,7},{7,6},{8,9},{9,8},{10,11... | collective-permute-start | bytes 442376 | tf_op jit(solution)/shard_map/ppermute | solution.py:335
  12.9 9.2 %collective-permute-start.3 = (bf16[6,32,256]{2,1,0:T(8,128)(2,1)S(1)}, bf16[6,32,256]{2,1,0:T(8,128)(2,1)S(1)}, u32[]{:S(2)}, u32[]{:S(2)}) collective-permute-start(bf16[6,32,256]{2,1,0:T(8,128)(2,1)S(1)} %pad_maximum_fusion.4), channel_id=1, source_target_pairs={{0,8},{1,9},{2,10},{3,11},{4,12},{5,13},{6,14},{7,15},{8,0},{9,1},... | collective-permute-start | bytes 294920 | tf_op jit(solution)/shard_map/ppermute | solution.py:335
  22.2 8.2 %collective-permute-start.4 = (bf16[6,32,256]{2,1,0:T(8,128)(2,1)S(1)}, bf16[6,32,256]{2,1,0:T(8,128)(2,1)S(1)}, u32[]{:S(2)}, u32[]{:S(2)}) collective-permute-start(bf16[6,32,256]{2,1,0:T(8,128)(2,1)S(1)} %pad_maximum_fusion.6), channel_id=1, source_target_pairs={{0,4},{1,5},{2,6},{3,7},{4,0},{5,1},{6,2},{7,3},{8,12},{9,13},{10,... | collective-permute-start | bytes 294920 | tf_op jit(solution)/shard_map/ppermute | solution.py:335
  23.0 8.3 %collective-permute-start = (bf16[8,64,256]{2,1,0:T(8,128)(2,1)S(1)}, bf16[8,64,256]{2,1,0:T(8,128)(2,1)S(1)}, u32[]{:S(2)}, u32[]{:S(2)}) collective-permute-start(bf16[8,64,256]{2,1,0:T(8,128)(2,1)S(1)} %get-tuple-element.14.field_ref), channel_id=1, source_target_pairs={{1,0},{2,1},{3,2},{4,3},{5,4},{6,5},{7,6},{8,7},{9,8},{10,9},{11,1... | collective-permute-start | bytes 786440 | tf_op jit(solution)/shard_map/ppermute | solution.py:338
  26.5 10.7 %collective-permute-start.1 = (bf16[8,32,256]{2,1,0:T(8,128)(2,1)S(1)}, bf16[8,32,256]{2,1,0:T(8,128)(2,1)S(1)}, u32[]{:S(2)}, u32[]{:S(2)}) collective-permute-start(bf16[8,32,256]{2,1,0:T(8,128)(2,1)S(1)} %get-tuple-element.16), channel_id=1, source_target_pairs={{0,1},{1,2},{2,3},{3,4},{4,5},{5,6},{6,7},{7,8},{8,9},{9,10},{10,1... | collective-permute-start | bytes 393224 | tf_op jit(solution)/shard_map/ppermute | solution.py:338
  30.5 6.7 %collective-permute-start.5 = (bf16[9,32,256]{2,1,0:T(8,128)(2,1)S(1)}, bf16[9,32,256]{2,1,0:T(8,128)(2,1)S(1)}, u32[]{:S(2)}, u32[]{:S(2)}) collective-permute-start(bf16[9,32,256]{2,1,0:T(8,128)(2,1)S(1)} %constant_dynamic-update-slice_fusion), channel_id=1, source_target_pairs={{0,2},{1,3},{2,0},{3,1},{4,6},{5,7},{6,4},{7,5},{8,10},{9,11},{10,... | collective-permute-start | bytes 442376 | tf_op jit(solution)/shard_map/ppermute | solution.py:335
  40.7 1.4 %collective-permute-start.8 = (bf16[9,32,256]{2,1,0:T(8,128)(2,1)S(1)}, bf16[9,32,256]{2,1,0:T(8,128)(2,1)S(1)}, u32[]{:S(2)}, u32[]{:S(2)}) collective-permute-start(bf16[9,32,256]{2,1,0:T(8,128)(2,1)S(1)} %pad_maximum_fusion.1), channel_id=1, source_target_pairs={{0,1},{1,0},{2,3},{3,2},{4,5},{5,4},{6,7},{7,6},{8,9},{9,8},{10,11... | collective-permute-start | bytes 442376 | tf_op jit(solution)/shard_map/ppermute | solution.py:335
  42.2 8.7 %collective-permute-start.9 = (bf16[6,32,256]{2,1,0:T(8,128)(2,1)S(1)}, bf16[6,32,256]{2,1,0:T(8,128)(2,1)S(1)}, u32[]{:S(2)}, u32[]{:S(2)}) collective-permute-start(bf16[6,32,256]{2,1,0:T(8,128)(2,1)S(1)} %pad_maximum_fusion.7), channel_id=1, source_target_pairs={{0,8},{1,9},{2,10},{3,11},{4,12},{5,13},{6,14},{7,15},{8,0},{9,1},... | collective-permute-start | bytes 294920 | tf_op jit(solution)/shard_map/ppermute | solution.py:335
  50.9 7.7 %collective-permute-start.10 = (bf16[6,32,256]{2,1,0:T(8,128)(2,1)S(1)}, bf16[6,32,256]{2,1,0:T(8,128)(2,1)S(1)}, u32[]{:S(2)}, u32[]{:S(2)}) collective-permute-start(bf16[6,32,256]{2,1,0:T(8,128)(2,1)S(1)} %pad_maximum_fusion.9), channel_id=1, source_target_pairs={{0,4},{1,5},{2,6},{3,7},{4,0},{5,1},{6,2},{7,3},{8,12},{9,13},{10,... | collective-permute-start | bytes 294920 | tf_op jit(solution)/shard_map/ppermute | solution.py:335
  51.7 13.5 %copy-start.2 = (f32[32,2048]{1,0:T(8,128)S(1)}, f32[32,2048]{1,0:T(8,128)}, u32[]{:S(2)}) copy-start(f32[32,2048]{1,0:T(8,128)} %right_ref.5) | copy-start | bytes 786436
  51.7 7.6 %collective-permute-start.6 = (bf16[8,64,256]{2,1,0:T(8,128)(2,1)S(1)}, bf16[8,64,256]{2,1,0:T(8,128)(2,1)S(1)}, u32[]{:S(2)}, u32[]{:S(2)}) collective-permute-start(bf16[8,64,256]{2,1,0:T(8,128)(2,1)S(1)} %get-tuple-element.18.field_ref), channel_id=1, source_target_pairs={{1,0},{2,1},{3,2},{4,3},{5,4},{6,5},{7,6},{8,7},{9,8},{10,9},{11,1... | collective-permute-start | bytes 786440 | tf_op jit(solution)/shard_map/ppermute | solution.py:338
  54.6 10.5 %collective-permute-start.7 = (bf16[8,32,256]{2,1,0:T(8,128)(2,1)S(1)}, bf16[8,32,256]{2,1,0:T(8,128)(2,1)S(1)}, u32[]{:S(2)}, u32[]{:S(2)}) collective-permute-start(bf16[8,32,256]{2,1,0:T(8,128)(2,1)S(1)} %get-tuple-element.20), channel_id=1, source_target_pairs={{0,1},{1,2},{2,3},{3,4},{4,5},{5,6},{6,7},{7,8},{8,9},{9,10},{10,1... | collective-permute-start | bytes 393224 | tf_op jit(solution)/shard_map/ppermute | solution.py:338
  58.6 6.5 %collective-permute-start.11 = (bf16[9,32,256]{2,1,0:T(8,128)(2,1)S(1)}, bf16[9,32,256]{2,1,0:T(8,128)(2,1)S(1)}, u32[]{:S(2)}, u32[]{:S(2)}) collective-permute-start(bf16[9,32,256]{2,1,0:T(8,128)(2,1)S(1)} %constant_dynamic-update-slice_fusion.5), channel_id=1, source_target_pairs={{0,2},{1,3},{2,0},{3,1},{4,6},{5,7},{6,4},{7,5},{8,10},{9,11},{10,... | collective-permute-start | bytes 442376 | tf_op jit(solution)/shard_map/ppermute | solution.py:335
  69.5 1.2 %collective-permute-start.12 = (f32[64,128]{1,0:T(8,128)S(1)}, f32[64,128]{1,0:T(8,128)S(1)}, u32[]{:S(2)}, u32[]{:S(2)}) collective-permute-start(f32[64,128]{1,0:T(8,128)S(1)} %get-tuple-element.23), channel_id=1, source_target_pairs={{0,1},{1,0},{2,3},{3,2},{4,5},{5,4},{6,7},{7,6},{8,9},{9,8},{10,11... | collective-permute-start | bytes 98312 | tf_op jit(solution)/shard_map/ppermute | solution.py:335
  70.7 6.0 %collective-permute-start.13 = (f32[64,128]{1,0:T(8,128)S(1)}, f32[64,128]{1,0:T(8,128)S(1)}, u32[]{:S(2)}, u32[]{:S(2)}) collective-permute-start(f32[64,128]{1,0:T(8,128)S(1)} %add.33), channel_id=1, source_target_pairs={{0,8},{1,9},{2,10},{3,11},{4,12},{5,13},{6,14},{7,15},{8,0},{9,1},... | collective-permute-start | bytes 98312 | tf_op jit(solution)/shard_map/ppermute | solution.py:335
  76.7 3.9 %collective-permute-start.14 = (f32[64,128]{1,0:T(8,128)S(1)}, f32[64,128]{1,0:T(8,128)S(1)}, u32[]{:S(2)}, u32[]{:S(2)}) collective-permute-start(f32[64,128]{1,0:T(8,128)S(1)} %add.34), channel_id=1, source_target_pairs={{0,4},{1,5},{2,6},{3,7},{4,0},{5,1},{6,2},{7,3},{8,12},{9,13},{10,... | collective-permute-start | bytes 98312 | tf_op jit(solution)/shard_map/ppermute | solution.py:335
  80.6 3.9 %collective-permute-start.15 = (f32[64,128]{1,0:T(8,128)S(1)}, f32[64,128]{1,0:T(8,128)S(1)}, u32[]{:S(2)}, u32[]{:S(2)}) collective-permute-start(f32[64,128]{1,0:T(8,128)S(1)} %add.35.kept_ref), channel_id=1, source_target_pairs={{0,2},{1,3},{2,0},{3,1},{4,6},{5,7},{6,4},{7,5},{8,10},{9,11},{10,... | collective-permute-start | bytes 98312 | tf_op jit(solution)/shard_map/ppermute | solution.py:335

commit v2 on v1

--- a/solution.py
+++ b/solution.py
@@ -62,22 +62,42 @@
     return lax.broadcasted_iota(jnp.int32, shape, 1) // K
 
 
-def project(fields, basis, clusters):
+def project(fields, basis):
+    clusters = fields.shape[0] // (2 * R)
+    all_pairs = dot_nt(fields, basis)
     group = lane_group((2 * R, clusters * K))
     total = jnp.zeros((2 * R, clusters * K), f32)
     for c in range(clusters):
-        total = total + jnp.where(group == c, dot_nt(fields[c], basis), 0.0)
-    return join_rows(total).astype(bf16)
-
-
-def start_kernel(right_ref, basis_ref, field_ref, proj_ref):
+        total = total + jnp.where(group == c, all_pairs[c * 2 * R : (c + 1) * 2 * R], 0.0)
+    return join_rows(total)
+
+
+def expand(sums, basis):
+    group = lane_group(sums.shape)
+    zero = jnp.zeros_like(sums)
+    spread = [jnp.where(group == c, sums, zero) for c in range(sums.shape[1] // K)]
+    return dot(jnp.concatenate(spread, axis=0), basis)
+
+
+def start_kernel(right_hbm, basis_hbm, field_ref, proj_ref, near_proj_ref, cross_ref, right_ref, basis_ref, sems):
     clusters = field_ref.shape[0]
-    fields = []
+    copies = [
+        pltpu.make_async_copy(basis_hbm, basis_ref, sems.at[0]),
+        pltpu.make_async_copy(right_hbm, right_ref, sems.at[1]),
+    ]
+    for copy in copies:
+        copy.start()
+    copies[0].wait()
+    basis = basis_ref[...]
+    cross = dot_nt(basis, basis)
+    same = lane_group(cross.shape) == lax.broadcasted_iota(jnp.int32, cross.shape, 0) // K
+    cross_ref[...] = jnp.where(same, cross, 0.0)
+    copies[1].wait()
     for c in range(clusters):
-        field = split_rows(right_ref[:, c * PANEL : (c + 1) * PANEL])
-        field_ref[c] = field
-        fields.append(field)
-    proj_ref[...] = project(fields, basis_ref[...], clusters)
+        field_ref[c] = split_rows(right_ref[:, c * PANEL : (c + 1) * PANEL])
+    proj = project(field_ref[...].reshape(clusters * 2 * R, PANEL), basis)
+    proj_ref[...] = proj.astype(bf16)
+    near_proj_ref[...] = proj
 
 
 def places(devices):
@@ -129,11 +149,19 @@
     lax.fori_loop(0, pairs // 4, some, 0)
 
 
-def send_kernel(coupled_ref, proj_ref, out_ref):
-    devices = out_ref.shape[0]
-    proj = proj_ref[...]
-    for d in range(devices):
-        out_ref[d] = dot(proj, coupled_ref[devices + d]) + dot_nt(proj, coupled_ref[d])
+def send(coupled_ref, proj, payload_ref, kept_ref):
+    half = kept_ref.shape[0]
+    payload_ref[0] = proj
+    for d in range(2 * half):
+        value = dot(proj, coupled_ref[2 * half + d]) + dot_nt(proj, coupled_ref[d])
+        if d < half:
+            kept_ref[d] = value
+        else:
+            payload_ref[1 + d - half] = value.astype(bf16)
+
+
+def send_kernel(coupled_ref, proj_ref, payload_ref, kept_ref):
+    send(coupled_ref, proj_ref[...], payload_ref, kept_ref)
 
 
 def near_specs(nb, group):
@@ -166,7 +194,8 @@
         next_ref[...] = total[clusters : 2 * clusters].astype(bf16)
 
 
-def near_rows_kernel(pairs_ref, count_ref, blocks_ref, field_ref, after_ref, begun_ref, out_ref, window, total):
+def near_rows_kernel(pairs_ref, count_ref, blocks_ref, field_ref, after_ref, begun_ref, back_ref, basis_ref,
+                     out_ref, proj_ref, window, total):
     g = pl.program_id(0)
     clusters = field_ref.shape[0]
 
@@ -174,7 +203,7 @@
     def _():
         window[:clusters] = field_ref[...]
         window[clusters:] = after_ref[...]
-        total[:clusters] = begun_ref[...]
+        total[:clusters] = begun_ref[...] + back_ref[...].astype(f32)
 
     @pl.when(g * GROUP < count_ref[0])
     def _():
@@ -186,7 +215,10 @@
 
     @pl.when(g == pl.num_programs(0) - 1)
     def _():
-        out_ref[...] = total[:clusters]
+        near = total[:clusters]
+        out_ref[...] = near
+        split = jnp.concatenate([split_rows(near[c]) for c in range(clusters)], axis=0)
+        proj_ref[...] = project(split, basis_ref[...])
 
 
 def near_call(kernel, outs, near_pairs, near_count, near_blocks, arrays, scratch):
@@ -210,55 +242,77 @@
     )(near_pairs, near_count, near_blocks, *arrays)
 
 
-def far_fields(place, coupled_ref, low_ref, high_ref, kept_ref, got_ref, basis):
+def far_sums(place, coupled_ref, low_ref, high_ref, kept_ref, got_ref):
     devices = coupled_ref.shape[0] // 2
-    sums = kept_ref[0] + got_ref[0].astype(f32)
+    sums = kept_ref[0]
+    for piece in range(got_ref.shape[0]):
+        sums = sums + got_ref[piece].astype(f32)
     order = places(devices)[0]
     for g in range(devices):
         proj = low_ref[g] if g < devices // 2 else high_ref[g - devices // 2]
         apart = sum(((g >> t) & 1) << b for t, b in enumerate(order))
         sums = sums + dot(proj, coupled_ref[place[apart]]) + dot_nt(proj, coupled_ref[devices + place[apart]])
-    sums = split_rows(sums)
-    group = lane_group(sums.shape)
-    zero = jnp.zeros_like(sums)
-    return lambda c: join_rows(dot(jnp.where(group == c, sums, zero), basis))
-
-
-def finish_one_kernel(place, coupled_ref, near_ref, back_ref, low_ref, high_ref, kept_ref, got_ref, basis_ref,
-                      image_ref, field_ref, proj_ref):
-    clusters = near_ref.shape[0]
-    basis = basis_ref[...]
-    far = far_fields(place, coupled_ref, low_ref, high_ref, kept_ref, got_ref, basis)
-    fields = []
-    for c in range(clusters):
-        image = near_ref[c] + back_ref[c].astype(f32) + far(c)
+    return split_rows(sums)
+
+
+def exact(x, y):
+    return jnp.dot(x, y, precision=highest, preferred_element_type=f32)
+
+
+def turn_kernel(place, coupled_ref, low_ref, high_ref, kept_ref, got_ref, near_proj_ref, cross_ref,
+                sums_ref, proj_ref, payload_ref, next_ref):
+    sums = far_sums(place, coupled_ref, low_ref, high_ref, kept_ref, got_ref)
+    sums_ref[...] = sums
+    proj = near_proj_ref[...] + exact(join_rows(sums.astype(f32)), cross_ref[...])
+    proj_ref[...] = proj
+    send(coupled_ref, proj.astype(bf16), payload_ref, next_ref)
+
+
+def image_kernel(near_ref, sums_ref, basis_ref, image_ref, field_ref):
+    far = expand(sums_ref[...], basis_ref[...])
+    for c in range(near_ref.shape[0]):
+        image = near_ref[c] + join_rows(far[c * 2 * R : (c + 1) * 2 * R])
         image_ref[c] = image
-        field = split_rows(image)
-        field_ref[c] = field
-        fields.append(field)
-    proj_ref[...] = project(fields, basis, clusters)
-
-
-def finish_two_kernel(place, coupled_ref, near_ref, back_ref, low_ref, high_ref, kept_ref, got_ref, basis_ref,
-                      right_ref, image_ref, second_ref, gram_ref):
-    clusters = near_ref.shape[0]
-    basis = basis_ref[...]
-    far = far_fields(place, coupled_ref, low_ref, high_ref, kept_ref, got_ref, basis)
-    gram = jnp.zeros((2 * R, 4 * R), f32)
+        field_ref[c] = split_rows(image)
+
+
+def second_kernel(near_ref, sums_ref, basis_ref, image_ref):
+    far = expand(sums_ref[...], basis_ref[...])
+    for c in range(near_ref.shape[0]):
+        image_ref[c] = near_ref[c] + join_rows(far[c * 2 * R : (c + 1) * 2 * R])
+
+
+def gram_one_kernel(right_ref, image_ref, gram_ref):
+    gram = jnp.zeros((R, 4 * R), f32)
     corner = jnp.zeros((R, 4 * R), f32)
     zero = jnp.zeros((R, PANEL), f32)
-    for c in range(clusters):
-        second = near_ref[c] + back_ref[c].astype(f32) + far(c)
-        second_ref[c] = second
-        right = right_ref[:, c * PANEL : (c + 1) * PANEL]
-        image = image_ref[c]
-        gram = gram + exact_nt(
-            jnp.concatenate([image, second], axis=0), jnp.concatenate([right, image, second, zero], axis=0)
-        )
+    for c in range(image_ref.shape[0]):
+        right, image = right_ref[:, c * PANEL : (c + 1) * PANEL], image_ref[c]
+        gram = gram + exact_nt(image, jnp.concatenate([right, image, zero, zero], axis=0))
         corner = corner + exact_nt(right, jnp.concatenate([zero, zero, right, zero], axis=0))
-    lanes = lax.broadcasted_iota(jnp.int32, (R, 4 * R), 1)
-    gram_ref[:R] = jnp.where(lanes // R == 2, corner, gram[:R])
-    gram_ref[R:] = gram[R:]
+    gram_ref[...] = gram + corner
+
+
+def gram_two_kernel(right_ref, image_ref, near_ref, gram_ref):
+    gram = jnp.zeros((R, 4 * R), f32)
+    zero = jnp.zeros((R, PANEL), f32)
+    for c in range(image_ref.shape[0]):
+        right, near = right_ref[:, c * PANEL : (c + 1) * PANEL], near_ref[c]
+        gram = gram + exact_nt(near, jnp.concatenate([right, image_ref[c], near, zero], axis=0))
+    gram_ref[...] = gram
+
+
+def tail_kernel(place, coupled_ref, low_ref, high_ref, kept_ref, got_ref, near_proj_ref, cross_ref,
+                right_proj_ref, image_proj_ref, early_ref, gram_ref, sums_ref, out_ref):
+    sums = far_sums(place, coupled_ref, low_ref, high_ref, kept_ref, got_ref)
+    sums_ref[...] = sums
+    sums = join_rows(sums.astype(f32))
+    half = near_proj_ref[...] + 0.5 * exact(sums, cross_ref[...])
+    known = jnp.concatenate([right_proj_ref[...], image_proj_ref[...], half, jnp.zeros_like(half)], axis=0)
+    out_ref[:R] = early_ref[...]
+    added = exact_nt(sums, known)
+    mirror = exact_nt(half, jnp.concatenate([jnp.zeros_like(sums)] * 2 + [sums, jnp.zeros_like(sums)], axis=0))
+    out_ref[R:] = gram_ref[...] + added + mirror
 
 
 def lane(x, k):
@@ -338,15 +392,26 @@
         return lax.ppermute(x, "leaf", [(i, i + by) for i in range(devices) if 0 <= i + by < devices])
 
     panels = sds((clusters, R, PANEL), f32)
+    narrow = sds((clusters, R, PANEL), bf16)
     split = sds((clusters, 2 * R, PANEL), bf16)
     rank = sds((R, clusters * K), bf16)
-
-    field, proj = call(start_kernel, (split, rank), (right_side, basis), (VMEM, VMEM))
+    rank_wide = sds((R, clusters * K), f32)
+    rank_split = sds((2 * R, clusters * K), bf16)
+    square = sds((clusters * K, clusters * K), f32)
+    half = devices // 2
+    payload_out = sds((1 + half, R, clusters * K), bf16)
+    kept_out = sds((half, R, clusters * K), f32)
+    barrier = lax.optimization_barrier
+
+    field, proj, right_proj, cross = call(
+        start_kernel, (split, rank, rank_wide, square), (right_side, basis), (pltpu.HBM, pltpu.HBM),
+        [pltpu.VMEM(right_side.shape, f32), pltpu.VMEM(basis.shape, bf16), pltpu.SemaphoreType.DMA((2,))],
+    )
     coupled = call(
         functools.partial(couple_kernel, order),
         sds((2 * devices, clusters * K, clusters * K), bf16),
         (me, far_pairs, cluster_slot, coupling.reshape(-1, K)),
-        (SMEM, pl.ANY, pl.ANY, VMEM),
+        (SMEM, pltpu.HBM, pltpu.HBM, VMEM),
         [
             pltpu.VMEM((coupling.shape[0] * K, clusters * K), bf16),
             pltpu.SMEM(far_pairs.shape, jnp.int32),
@@ -355,42 +420,69 @@
         ],
     )
 
-    def exchange(field, proj):
-        after = shift(field, -1)
-        sums = call(send_kernel, sds((devices, R, clusters * K), f32), (coupled, proj), (VMEM, VMEM))
-        own, following = near_call(
-            near_cols_kernel, (panels, sds(panels.shape, bf16)), near_pairs, near_count, near_blocks, (field,),
-            [pltpu.VMEM((2 * clusters + 1, R, PANEL), f32)],
-        )
-        back = shift(following, 1)
-        gathered = proj[None]
+    def exchange(make_field, payload, sums):
         for t, b in enumerate(order):
-            held, half = gathered.shape[0], sums.shape[0] // 2
-            got = across(jnp.concatenate([gathered, sums[half:].astype(bf16)], axis=0), b)
-            sums, got_gathered, got_sums = sums[:half], got[:held], got[held:]
+            if t > 0:
+                held, half = gathered.shape[0], sums.shape[0] // 2
+                payload = jnp.concatenate([gathered, sums[half:].astype(bf16)], axis=0)
+                sums = sums[:half]
+            else:
+                gathered, held = payload[:1], 1
+            if t == 2:
+                payload, own = barrier((payload, own))
+            got = across(payload, b)
+            if t == 0:
+                image, field, got = make_field(got)
+                after = shift(field, -1)
+                own, following = near_call(
+                    near_cols_kernel, (panels, narrow), near_pairs, near_count, near_blocks, (field,),
+                    [pltpu.VMEM((2 * clusters + 1, R, PANEL), f32)],
+                )
+                back = shift(following, 1)
+            if t == len(order) - 2:
+                after, got = barrier((after, got))
+            got_gathered, got_sums = got[:held], got[held:]
             if t < len(order) - 1:
                 gathered = jnp.concatenate([gathered, got_gathered], axis=0)
                 sums = sums + got_sums.astype(f32)
-        near = near_call(
-            near_rows_kernel, panels, near_pairs, near_count, near_blocks, (field, after, own),
+        near, near_proj = near_call(
+            near_rows_kernel, (panels, rank_wide), near_pairs, near_count, near_blocks,
+            (field, after, own, back, basis),
             [pltpu.VMEM((2 * clusters, 2 * R, PANEL), bf16), pltpu.VMEM((clusters + 1, R, PANEL), f32)],
         )
-        return (coupled, near, back, gathered, got_gathered, sums, got_sums, basis)
-
-    parts = exchange(field, proj)
-    image, field, proj = call(
-        functools.partial(finish_one_kernel, place), (panels, split, rank), parts, [VMEM] * 8
-    )
-    parts = exchange(field, proj)
-    second, gram = call(
-        functools.partial(finish_two_kernel, place), (panels, sds((2 * R, 4 * R), f32)), parts + (right_side, image),
-        [VMEM] * 10,
+        return image, near, (coupled, gathered, got_gathered, sums, got_sums, near_proj, cross)
+
+    def first_field(got):
+        ready, got = barrier((field, got))
+        return right_side, ready, got
+
+    payload, sums = call(send_kernel, (payload_out, kept_out), (coupled, proj), (VMEM, VMEM))
+    unused, near, parts = exchange(first_field, payload, sums)
+    far, image_proj, payload, sums = call(
+        functools.partial(turn_kernel, place), (rank_split, rank_wide, payload_out, kept_out), parts, [VMEM] * 7
+    )
+
+    def second_field(got):
+        ready, got = barrier((far, got))
+        return *call(image_kernel, (panels, split), (near, ready, basis), [VMEM] * 3), got
+
+    image, near_two, parts = exchange(second_field, payload, sums)
+    early = call(gram_one_kernel, sds((R, 4 * R), f32), (right_side, image), [VMEM] * 2)
+    gram = call(gram_two_kernel, sds((R, 4 * R), f32), (right_side, image, near_two), [VMEM] * 3)
+    far, gram = call(
+        functools.partial(tail_kernel, place), (rank_split, sds((2 * R, 4 * R), f32)),
+        parts + (right_proj, image_proj, early, gram), [VMEM] * 11,
     )
     got = None
     for t, b in enumerate(order):
         if t > 0:
             gram = gram + got
+        if t == 2:
+            gram, second = barrier((gram, second))
         got = across(gram, b)
+        if t == 0:
+            far, got = barrier((far, got))
+            second = call(second_kernel, panels, (near_two, far, basis), [VMEM] * 3)
     wide = sds(right_side.shape, f32)
     return call(
         last_kernel, (wide, wide, sds((2 * R, R), f32)), (gram, got, right_side, image, second), [VMEM] * 5

time: 91.3 us -> 82 us (0.90); the launches traced: 90.2 us -> 82.5 us
  waiting for transfers between devices: 30.5 us -> 21.1 us
  Pallas kernels: 24.5 us -> 28.4 us
  starting transfers between devices: 27 us -> 24.9 us
    ppermute x12, waiting for transfers between devices: 30.5 us -> 21.1 us  [across(): return lax.ppermute(x, 'leaf', [(i, i ^ 1 << b) for i in range(devices)])]
    pallas_call x4, Pallas kernels: 6.54 us -> 9.94 us  [near_call(): pl.pallas_call(kernel, out_shape=outs, grid_spec=pltpu.PrefetchScalarGrid...]
    ppermute x4, starting transfers between devices: 10.5 us -> 8.1 us  [shift(): lax.ppermute(x, 'leaf', [(i, i + by) for i in range(devices) if 0 <= i +...]
    pallas_call x7 -> x10, Pallas kernels: 17.9 us -> 18.4 us  [call(): pl.pallas_call(kernel, out_shape=outs, in_specs=[spec(s) for s in spaces]...]
    unnamed x22 -> x24, local copies, waits for them, and re-layouts: 3.61 us -> 3.62 us
  transfers between devices with their start and end apart: 16 -> 16, of which waited for: 10 -> 12; matrix products, arithmetic and copies ran while one was open for 0% -> 0% of each run, Pallas kernels for 7% -> 15%
where the time goes in v2:
time: 82 us; the launch traced here: 82.5 us
  Pallas kernels  28.4 us (35%)
  starting transfers between devices  24.9 us (30%)
  waiting for transfers between devices  21.1 us (26%)
  local copies, waits for them, and re-layouts  6.21 us (8%)
  between operations  1.73 us (2%)
    ppermute x12, waiting for transfers between devices, across(): return lax.ppermute(x, 'leaf', [(i, i ^ 1 << b) for i in range(devices)])  21.1 us
    pallas_call x10, Pallas kernels, call(): pl.pallas_call(kernel, out_shape=outs, in_specs=[spec(s) for s in spaces]...  18.4 us
    ppermute x12, starting transfers between devices, across(): return lax.ppermute(x, 'leaf', [(i, i ^ 1 << b) for i in range(devices)])  16.8 us
    pallas_call x4, Pallas kernels, near_call(): pl.pallas_call(kernel, out_shape=outs, grid_spec=pltpu.PrefetchScalarGrid...  9.94 us
    ppermute x4, starting transfers between devices, shift(): lax.ppermute(x, 'leaf', [(i, i + by) for i in range(devices) if 0 <= i +...  8.1 us
    unnamed x24, local copies, waits for them, and re-layouts  3.62 us
    reshape x1, local copies, waits for them, and re-layouts, body(): coupling.reshape(-1, K)  1.84 us
  transfers between devices with their start and end apart: 16, of which 12 were waited for; matrix products, arithmetic and copies ran while one was open for 0% of the time, Pallas kernels for 15%

profile of v2, /device:TPU:0, one launch (start us, length us, event | category | flops | bytes accessed | tf_op | source)
XLA Modules:
  0.0 82.5 jit_solution(9424613438652079549)
XLA Ops:
  0.6 1.8 %reshape.16.coupling_ref = bf16[4096,32]{1,0:T(8,128)(2,1)S(1)} reshape(bf16[128,1024]{1,0:T(8,128)(2,1)} %param.13) | data formatting | bytes 524288 | tf_op jit(solution)/shard_map/reshape | solution.py:413
  2.5 1.1 %copy-done.1 = f32[32,2048]{1,0:T(8,128)S(1)} copy-done((f32[32,2048]{1,0:T(8,128)S(1)}, f32[32,2048]{1,0:T(8,128)}, u32[]{:S(2)}) %copy-start.1) | copy-done | bytes 262168
  3.6 1.1 %copy-done.3 = bf16[8,32,256]{2,1,0:T(8,128)(2,1)S(1)} copy-done((bf16[8,32,256]{2,1,0:T(8,128)(2,1)S(1)}, bf16[8,32,256]{2,1,0:T(8,128)(2,1)}, u32[]{:S(2)}) %copy-start.3) | copy-done | bytes 131096
  6.8 3.7 %shard_map.103.coupled_ref = bf16[32,256,256]{2,1,0:T(8,128)(2,1)S(1)} custom-call(s32[1]{0:T(128)} %bitcast.me_ref, s32[2,128]{1,0:T(2,128)S(1)} %copy-done.6, s32[128]{0:T(128)S(1)} %copy-done.7, bf16[4096,32]{1,0:T(8,128)(2,1)S(1)} %reshape.16.coupling_ref), custom_call_target="tpu_custom_call" | custom-call | flops 100000000 | bytes 1000000 | tf_op jit(solution)/shard_map/pallas_call | solution.py:28
  10.5 1.1 %shard_map.105 = (bf16[9,32,256]{2,1,0:T(8,128)(2,1)S(1)}, f32[8,32,256]{2,1,0:T(8,128)S(1)}) custom-call(bf16[32,256,256]{2,1,0:T(8,128)(2,1)S(1)} %shard_map.103.coupled_ref, bf16[32,256]{1,0:T(8,128)(2,1)S(1)} %get-tuple-element.41.proj_ref), custom_call_target="tpu_custom_call" | custom-call | flops 100000000 | bytes 1000000 | tf_op jit(solution)/shard_map/pallas_call | solution.py:28
  12.1 1.0 %collective-permute-done = bf16[9,32,256]{2,1,0:T(8,128)(2,1)S(1)} collective-permute-done((bf16[9,32,256]{2,1,0:T(8,128)(2,1)S(1)}, bf16[9,32,256]{2,1,0:T(8,128)(2,1)S(1)}, u32[]{:S(2)}, u32[]{:S(2)}) %collective-permute-start) | collective-permute-done | bytes 147488 | tf_op jit(solution)/shard_map/ppermute | solution.py:389
  13.1 4.0 %collective-permute-start.1 = (bf16[6,32,256]{2,1,0:T(8,128)(2,1)S(1)}, bf16[6,32,256]{2,1,0:T(8,128)(2,1)S(1)}, u32[]{:S(2)}, u32[]{:S(2)}) collective-permute-start(bf16[6,32,256]{2,1,0:T(8,128)(2,1)S(1)} %pad_maximum_fusion.2), channel_id=1, source_target_pairs={{0,8},{1,9},{2,10},{3,11},{4,12},{5,13},{6,14},{7,15},{8,0},{9,1},... | collective-permute-start | bytes 294920 | tf_op jit(solution)/shard_map/ppermute | solution.py:389
  17.8 1.3 %collective-permute-start.2 = (bf16[8,64,256]{2,1,0:T(8,128)(2,1)S(1)}, bf16[8,64,256]{2,1,0:T(8,128)(2,1)S(1)}, u32[]{:S(2)}, u32[]{:S(2)}) collective-permute-start(bf16[8,64,256]{2,1,0:T(8,128)(2,1)S(1)} %get-tuple-element.46.field_ref), channel_id=1, source_target_pairs={{1,0},{2,1},{3,2},{4,3},{5,4},{6,5},{7,6},{8,7},{9,8},{10,9},{11,1... | collective-permute-start | bytes 786440 | tf_op jit(solution)/shard_map/ppermute | solution.py:392
  19.1 2.1 %shard_map.106 = (f32[8,32,256]{2,1,0:T(8,128)S(1)}, bf16[8,32,256]{2,1,0:T(8,128)(2,1)S(1)}) custom-call(s32[2,64]{1,0:T(2,128)S(1)} %copy-done.5, s32[1]{0:T(128)S(6)} %copy.21.count_ref, bf16[64,256,256]{2,1,0:T(8,128)(2,1)S(1)} %copy-done, bf16[8,64,256]{2,1,0:T(8,128)(2,1)S(1)} %get-tuple-element.46.field_ref), custom_call_target="tpu_custom_call" | custom-call | flops 536870912 | bytes 8388608 | tf_op jit(solution)/shard_map/pallas_call | solution.py:226
  21.2 1.1 %collective-permute-done.1 = bf16[6,32,256]{2,1,0:T(8,128)(2,1)S(1)} collective-permute-done((bf16[6,32,256]{2,1,0:T(8,128)(2,1)S(1)}, bf16[6,32,256]{2,1,0:T(8,128)(2,1)S(1)}, u32[]{:S(2)}, u32[]{:S(2)}) %collective-permute-start.1) | collective-permute-done | bytes 98336 | tf_op jit(solution)/shard_map/ppermute | solution.py:389
  22.4 1.4 %collective-permute-start.3 = (bf16[6,32,256]{2,1,0:T(8,128)(2,1)S(1)}, bf16[6,32,256]{2,1,0:T(8,128)(2,1)S(1)}, u32[]{:S(2)}, u32[]{:S(2)}) collective-permute-start(bf16[6,32,256]{2,1,0:T(8,128)(2,1)S(1)} %pad_maximum_fusion.4), channel_id=1, source_target_pairs={{0,4},{1,5},{2,6},{3,7},{4,0},{5,1},{6,2},{7,3},{8,12},{9,13},{10,... | collective-permute-start | bytes 294920 | tf_op jit(solution)/shard_map/ppermute | solution.py:389
  23.9 2.2 %collective-permute-start.5 = (bf16[8,32,256]{2,1,0:T(8,128)(2,1)S(1)}, bf16[8,32,256]{2,1,0:T(8,128)(2,1)S(1)}, u32[]{:S(2)}, u32[]{:S(2)}) collective-permute-start(bf16[8,32,256]{2,1,0:T(8,128)(2,1)S(1)} %get-tuple-element.52), channel_id=1, source_target_pairs={{0,1},{1,2},{2,3},{3,4},{4,5},{5,6},{6,7},{7,8},{8,9},{9,10},{10,1... | collective-permute-start | bytes 393224 | tf_op jit(solution)/shard_map/ppermute | solution.py:392
  26.0 2.6 %collective-permute-done.3 = bf16[6,32,256]{2,1,0:T(8,128)(2,1)S(1)} collective-permute-done((bf16[6,32,256]{2,1,0:T(8,128)(2,1)S(1)}, bf16[6,32,256]{2,1,0:T(8,128)(2,1)S(1)}, u32[]{:S(2)}, u32[]{:S(2)}) %collective-permute-start.3) | collective-permute-done | bytes 98336 | tf_op jit(solution)/shard_map/ppermute | solution.py:389
  28.7 1.1 %collective-permute-start.4 = (bf16[9,32,256]{2,1,0:T(8,128)(2,1)S(1)}, bf16[9,32,256]{2,1,0:T(8,128)(2,1)S(1)}, u32[]{:S(2)}, u32[]{:S(2)}) collective-permute-start(bf16[9,32,256]{2,1,0:T(8,128)(2,1)S(1)} %constant_dynamic-update-slice_fusion), channel_id=1, source_target_pairs={{0,2},{1,3},{2,0},{3,1},{4,6},{5,7},{6,4},{7,5},{8,10},{9,11},{10,... | collective-permute-start | bytes 442376 | tf_op jit(solution)/shard_map/ppermute | solution.py:389
  29.7 2.9 %shard_map.107 = (f32[8,32,256]{2,1,0:T(8,128)S(1)}, f32[32,256]{1,0:T(8,128)S(1)}) custom-call(s32[2,64]{1,0:T(2,128)S(1)} %copy-done.5, s32[1]{0:T(128)S(6)} %copy.21.count_ref, bf16[64,256,256]{2,1,0:T(8,128)(2,1)S(1)} %copy-done, bf16[8,64,256]{2,1,0:T(8,128)(2,1)S(1)} %get-tuple-element.46.field_ref, ...), custom_call_target="tpu_custom_call" | custom-call | flops 536870912 | bytes 8388608 | tf_op jit(solution)/shard_map/pallas_call | solution.py:226
  32.7 1.2 %collective-permute-done.4 = bf16[9,32,256]{2,1,0:T(8,128)(2,1)S(1)} collective-permute-done((bf16[9,32,256]{2,1,0:T(8,128)(2,1)S(1)}, bf16[9,32,256]{2,1,0:T(8,128)(2,1)S(1)}, u32[]{:S(2)}, u32[]{:S(2)}) %collective-permute-start.4) | collective-permute-done | bytes 147488 | tf_op jit(solution)/shard_map/ppermute | solution.py:389
  33.9 3.7 %shard_map.108 = (bf16[64,256]{1,0:T(8,128)(2,1)S(1)}, f32[32,256]{1,0:T(8,128)S(1)}, bf16[9,32,256]{2,1,0:T(8,128)(2,1)S(1)}, f32[8,32,256]{2,1,0:T(8,128)S(1)}) custom-call(bf16[32,256,256]{2,1,0:T(8,128)(2,1)S(1)} %shard_map.103.coupled_ref, bf16[8,32,256]{2,1,0:T(8,128)(2,1)S(1)} %pad_maximum_fusion.low_ref, bf16[8,32,256]{2,1,0:T(8,128)(2,1)S(1)} %slice.133.high_ref, ...), custom_call_target="tpu_custom_call" | custom-call | flops 100000000 | bytes 1000000 | tf_op jit(solution)/shard_map/pallas_call | solution.py:28
  37.6 1.4 %collective-permute-done.6 = bf16[9,32,256]{2,1,0:T(8,128)(2,1)S(1)} collective-permute-done((bf16[9,32,256]{2,1,0:T(8,128)(2,1)S(1)}, bf16[9,32,256]{2,1,0:T(8,128)(2,1)S(1)}, u32[]{:S(2)}, u32[]{:S(2)}) %collective-permute-start.6) | collective-permute-done | bytes 147488 | tf_op jit(solution)/shard_map/ppermute | solution.py:389
  39.0 4.8 %collective-permute-start.7 = (bf16[6,32,256]{2,1,0:T(8,128)(2,1)S(1)}, bf16[6,32,256]{2,1,0:T(8,128)(2,1)S(1)}, u32[]{:S(2)}, u32[]{:S(2)}) collective-permute-start(bf16[6,32,256]{2,1,0:T(8,128)(2,1)S(1)} %pad_maximum_fusion.5), channel_id=1, source_target_pairs={{0,8},{1,9},{2,10},{3,11},{4,12},{5,13},{6,14},{7,15},{8,0},{9,1},... | collective-permute-start | bytes 294920 | tf_op jit(solution)/shard_map/ppermute | solution.py:389
  44.1 1.3 %collective-permute-start.8 = (bf16[8,64,256]{2,1,0:T(8,128)(2,1)S(1)}, bf16[8,64,256]{2,1,0:T(8,128)(2,1)S(1)}, u32[]{:S(2)}, u32[]{:S(2)}) collective-permute-start(bf16[8,64,256]{2,1,0:T(8,128)(2,1)S(1)} %get-tuple-element.61.field_ref), channel_id=1, source_target_pairs={{1,0},{2,1},{3,2},{4,3},{5,4},{6,5},{7,6},{8,7},{9,8},{10,9},{11,1... | collective-permute-start | bytes 786440 | tf_op jit(solution)/shard_map/ppermute | solution.py:392
  45.4 2.1 %shard_map.110 = (f32[8,32,256]{2,1,0:T(8,128)S(1)}, bf16[8,32,256]{2,1,0:T(8,128)(2,1)S(1)}) custom-call(s32[2,64]{1,0:T(2,128)S(1)} %copy-done.5, s32[1]{0:T(128)S(6)} %copy.21.count_ref, bf16[64,256,256]{2,1,0:T(8,128)(2,1)S(1)} %copy-done, bf16[8,64,256]{2,1,0:T(8,128)(2,1)S(1)} %get-tuple-element.61.field_ref), custom_call_target="tpu_custom_call" | custom-call | flops 536870912 | bytes 8388608 | tf_op jit(solution)/shard_map/pallas_call | solution.py:226
  48.1 3.4 %collective-permute-start.11 = (bf16[8,32,256]{2,1,0:T(8,128)(2,1)S(1)}, bf16[8,32,256]{2,1,0:T(8,128)(2,1)S(1)}, u32[]{:S(2)}, u32[]{:S(2)}) collective-permute-start(bf16[8,32,256]{2,1,0:T(8,128)(2,1)S(1)} %get-tuple-element.67), channel_id=1, source_target_pairs={{0,1},{1,2},{2,3},{3,4},{4,5},{5,6},{6,7},{7,8},{8,9},{9,10},{10,1... | collective-permute-start | bytes 393224 | tf_op jit(solution)/shard_map/ppermute | solution.py:392
  51.5 1.1 %shard_map.112.early_ref = f32[32,128]{1,0:T(8,128)S(1)} custom-call(f32[32,2048]{1,0:T(8,128)S(1)} %copy-done.2, f32[8,32,256]{2,1,0:T(8,128)S(1)} %get-tuple-element.71.image_ref), custom_call_target="tpu_custom_call" | custom-call | flops 100000000 | bytes 1000000 | tf_op jit(solution)/shard_map/pallas_call | solution.py:28
  53.9 2.9 %shard_map.111 = (f32[8,32,256]{2,1,0:T(8,128)S(1)}, f32[32,256]{1,0:T(8,128)S(1)}) custom-call(s32[2,64]{1,0:T(2,128)S(1)} %copy-done.5, s32[1]{0:T(128)S(6)} %copy.21.count_ref, bf16[64,256,256]{2,1,0:T(8,128)(2,1)S(1)} %copy-done, bf16[8,64,256]{2,1,0:T(8,128)(2,1)S(1)} %get-tuple-element.61.field_ref, ...), custom_call_target="tpu_custom_call" | custom-call | flops 536870912 | bytes 8388608 | tf_op jit(solution)/shard_map/pallas_call | solution.py:226
  57.6 1.8 %collective-permute-done.10 = bf16[9,32,256]{2,1,0:T(8,128)(2,1)S(1)} collective-permute-done((bf16[9,32,256]{2,1,0:T(8,128)(2,1)S(1)}, bf16[9,32,256]{2,1,0:T(8,128)(2,1)S(1)}, u32[]{:S(2)}, u32[]{:S(2)}) %collective-permute-start.10) | collective-permute-done | bytes 147488 | tf_op jit(solution)/shard_map/ppermute | solution.py:389
  59.5 2.0 %shard_map.114 = (bf16[64,256]{1,0:T(8,128)(2,1)S(1)}, f32[64,128]{1,0:T(8,128)S(1)}) custom-call(bf16[32,256,256]{2,1,0:T(8,128)(2,1)S(1)} %shard_map.103.coupled_ref, bf16[8,32,256]{2,1,0:T(8,128)(2,1)S(1)} %pad_maximum_fusion.1.low_ref, bf16[8,32,256]{2,1,0:T(8,128)(2,1)S(1)} %slice.143.high_ref, f32[1,32,256]{2,1,0:T(8,128)S(1)} %slice.144.kept_ref, ...), custom_call_target="tpu_custom_call" | custom-call | flops 100000000 | bytes 1000000 | tf_op jit(solution)/shard_map/pallas_call | solution.py:28
  61.4 1.2 %collective-permute-done.12 = f32[64,128]{1,0:T(8,128)S(1)} collective-permute-done((f32[64,128]{1,0:T(8,128)S(1)}, f32[64,128]{1,0:T(8,128)S(1)}, u32[]{:S(2)}, u32[]{:S(2)}) %collective-permute-start.12) | collective-permute-done | bytes 32800 | tf_op jit(solution)/shard_map/ppermute | solution.py:389
  62.7 4.5 %collective-permute-start.13 = (f32[64,128]{1,0:T(8,128)S(1)}, f32[64,128]{1,0:T(8,128)S(1)}, u32[]{:S(2)}, u32[]{:S(2)}) collective-permute-start(f32[64,128]{1,0:T(8,128)S(1)} %add.33), channel_id=1, source_target_pairs={{0,8},{1,9},{2,10},{3,11},{4,12},{5,13},{6,14},{7,15},{8,0},{9,1},... | collective-permute-start | bytes 98312 | tf_op jit(solution)/shard_map/ppermute | solution.py:389
  67.3 1.7 %collective-permute-done.13 = f32[64,128]{1,0:T(8,128)S(1)} collective-permute-done((f32[64,128]{1,0:T(8,128)S(1)}, f32[64,128]{1,0:T(8,128)S(1)}, u32[]{:S(2)}, u32[]{:S(2)}) %collective-permute-start.13) | collective-permute-done | bytes 32800 | tf_op jit(solution)/shard_map/ppermute | solution.py:389
  69.0 3.9 %collective-permute-done.14 = f32[64,128]{1,0:T(8,128)S(1)} collective-permute-done((f32[64,128]{1,0:T(8,128)S(1)}, f32[64,128]{1,0:T(8,128)S(1)}, u32[]{:S(2)}, u32[]{:S(2)}) %collective-permute-start.14) | collective-permute-done | bytes 32800 | tf_op jit(solution)/shard_map/ppermute | solution.py:389
  72.9 3.9 %collective-permute-done.15.got_ref = f32[64,128]{1,0:T(8,128)S(1)} collective-permute-done((f32[64,128]{1,0:T(8,128)S(1)}, f32[64,128]{1,0:T(8,128)S(1)}, u32[]{:S(2)}, u32[]{:S(2)}) %collective-permute-start.15) | collective-permute-done | bytes 32800 | tf_op jit(solution)/shard_map/ppermute | solution.py:389
  76.9 5.0 %shard_map.116 = (f32[32,2048]{1,0:T(8,128)}, f32[32,2048]{1,0:T(8,128)}, f32[64,32]{1,0:T(8,128)S(1)}) custom-call(f32[64,128]{1,0:T(8,128)S(1)} %add.35.kept_ref, f32[64,128]{1,0:T(8,128)S(1)} %collective-permute-done.15.got_ref, f32[32,2048]{1,0:T(8,128)S(1)} %copy-done.2, f32[8,32,256]{2,1,0:T(8,128)S(1)} %get-tuple-element.71.image_ref, ...), custom_call_target="tpu_custom_call" | custom-call | flops 100000000 | bytes 1000000 | tf_op jit(solution)/shard_map/pallas_call | solution.py:28
  (67 shorter events, 6.6 us)
Async XLA Ops:
  0.6 18.5 %copy-start.5 = (s32[2,64]{1,0:T(2,128)S(1)}, s32[2,64]{1,0:T(2,128)}, u32[]{:S(2)}) copy-start(s32[2,64]{1,0:T(2,128)} %pairs_ref.7) | copy-start | bytes 1540
  2.5 16.6 %copy-start = (bf16[64,256,256]{2,1,0:T(8,128)(2,1)S(1)}, bf16[64,256,256]{2,1,0:T(8,128)(2,1)}, u32[]{:S(2)}) copy-start(bf16[64,256,256]{2,1,0:T(8,128)(2,1)} %blocks_ref.7) | copy-start | bytes 25165828
  2.5 1.1 %copy-start.1 = (f32[32,2048]{1,0:T(8,128)S(1)}, f32[32,2048]{1,0:T(8,128)}, u32[]{:S(2)}) copy-start(f32[32,2048]{1,0:T(8,128)} %right_ref.5) | copy-start | bytes 786436
  3.6 1.1 %copy-start.3 = (bf16[8,32,256]{2,1,0:T(8,128)(2,1)S(1)}, bf16[8,32,256]{2,1,0:T(8,128)(2,1)}, u32[]{:S(2)}) copy-start(bf16[8,32,256]{2,1,0:T(8,128)(2,1)} %param.14) | copy-start | bytes 393220
  5.5 0.7 copy-start.6
  6.1 0.7 copy-start.7
  11.6 1.5 %collective-permute-start = (bf16[9,32,256]{2,1,0:T(8,128)(2,1)S(1)}, bf16[9,32,256]{2,1,0:T(8,128)(2,1)S(1)}, u32[]{:S(2)}, u32[]{:S(2)}) collective-permute-start(bf16[9,32,256]{2,1,0:T(8,128)(2,1)S(1)} %get-tuple-element.42), channel_id=1, source_target_pairs={{0,1},{1,0},{2,3},{3,2},{4,5},{5,4},{6,7},{7,6},{8,9},{9,8},{10,11... | collective-permute-start | bytes 442376 | tf_op jit(solution)/shard_map/ppermute | solution.py:389
  13.1 9.2 %collective-permute-start.1 = (bf16[6,32,256]{2,1,0:T(8,128)(2,1)S(1)}, bf16[6,32,256]{2,1,0:T(8,128)(2,1)S(1)}, u32[]{:S(2)}, u32[]{:S(2)}) collective-permute-start(bf16[6,32,256]{2,1,0:T(8,128)(2,1)S(1)} %pad_maximum_fusion.2), channel_id=1, source_target_pairs={{0,8},{1,9},{2,10},{3,11},{4,12},{5,13},{6,14},{7,15},{8,0},{9,1},... | collective-permute-start | bytes 294920 | tf_op jit(solution)/shard_map/ppermute | solution.py:389
  17.8 10.8 %collective-permute-start.2 = (bf16[8,64,256]{2,1,0:T(8,128)(2,1)S(1)}, bf16[8,64,256]{2,1,0:T(8,128)(2,1)S(1)}, u32[]{:S(2)}, u32[]{:S(2)}) collective-permute-start(bf16[8,64,256]{2,1,0:T(8,128)(2,1)S(1)} %get-tuple-element.46.field_ref), channel_id=1, source_target_pairs={{1,0},{2,1},{3,2},{4,3},{5,4},{6,5},{7,6},{8,7},{9,8},{10,9},{11,1... | collective-permute-start | bytes 786440 | tf_op jit(solution)/shard_map/ppermute | solution.py:392
  22.4 21.5 %copy-start.4 = (bf16[8,32,256]{2,1,0:T(8,128)(2,1)S(1)}, bf16[8,32,256]{2,1,0:T(8,128)(2,1)}, u32[]{:S(2)}) copy-start(bf16[8,32,256]{2,1,0:T(8,128)(2,1)} %param.14) | copy-start | bytes 393220
  22.4 6.1 %collective-permute-start.3 = (bf16[6,32,256]{2,1,0:T(8,128)(2,1)S(1)}, bf16[6,32,256]{2,1,0:T(8,128)(2,1)S(1)}, u32[]{:S(2)}, u32[]{:S(2)}) collective-permute-start(bf16[6,32,256]{2,1,0:T(8,128)(2,1)S(1)} %pad_maximum_fusion.4), channel_id=1, source_target_pairs={{0,4},{1,5},{2,6},{3,7},{4,0},{5,1},{6,2},{7,3},{8,12},{9,13},{10,... | collective-permute-start | bytes 294920 | tf_op jit(solution)/shard_map/ppermute | solution.py:389
  23.9 5.9 %collective-permute-start.5 = (bf16[8,32,256]{2,1,0:T(8,128)(2,1)S(1)}, bf16[8,32,256]{2,1,0:T(8,128)(2,1)S(1)}, u32[]{:S(2)}, u32[]{:S(2)}) collective-permute-start(bf16[8,32,256]{2,1,0:T(8,128)(2,1)S(1)} %get-tuple-element.52), channel_id=1, source_target_pairs={{0,1},{1,2},{2,3},{3,4},{4,5},{5,6},{6,7},{7,8},{8,9},{9,10},{10,1... | collective-permute-start | bytes 393224 | tf_op jit(solution)/shard_map/ppermute | solution.py:392
  28.7 5.2 %collective-permute-start.4 = (bf16[9,32,256]{2,1,0:T(8,128)(2,1)S(1)}, bf16[9,32,256]{2,1,0:T(8,128)(2,1)S(1)}, u32[]{:S(2)}, u32[]{:S(2)}) collective-permute-start(bf16[9,32,256]{2,1,0:T(8,128)(2,1)S(1)} %constant_dynamic-update-slice_fusion), channel_id=1, source_target_pairs={{0,2},{1,3},{2,0},{3,1},{4,6},{5,7},{6,4},{7,5},{8,10},{9,11},{10,... | collective-permute-start | bytes 442376 | tf_op jit(solution)/shard_map/ppermute | solution.py:389
  32.6 18.8 %copy-start.2 = (f32[32,2048]{1,0:T(8,128)S(1)}, f32[32,2048]{1,0:T(8,128)}, u32[]{:S(2)}) copy-start(f32[32,2048]{1,0:T(8,128)} %right_ref.5) | copy-start | bytes 786436
  37.6 1.4 %collective-permute-start.6 = (bf16[9,32,256]{2,1,0:T(8,128)(2,1)S(1)}, bf16[9,32,256]{2,1,0:T(8,128)(2,1)S(1)}, u32[]{:S(2)}, u32[]{:S(2)}) collective-permute-start(bf16[9,32,256]{2,1,0:T(8,128)(2,1)S(1)} %get-tuple-element.55), channel_id=1, source_target_pairs={{0,1},{1,0},{2,3},{3,2},{4,5},{5,4},{6,7},{7,6},{8,9},{9,8},{10,11... | collective-permute-start | bytes 442376 | tf_op jit(solution)/shard_map/ppermute | solution.py:389
  39.0 8.9 %collective-permute-start.7 = (bf16[6,32,256]{2,1,0:T(8,128)(2,1)S(1)}, bf16[6,32,256]{2,1,0:T(8,128)(2,1)S(1)}, u32[]{:S(2)}, u32[]{:S(2)}) collective-permute-start(bf16[6,32,256]{2,1,0:T(8,128)(2,1)S(1)} %pad_maximum_fusion.5), channel_id=1, source_target_pairs={{0,8},{1,9},{2,10},{3,11},{4,12},{5,13},{6,14},{7,15},{8,0},{9,1},... | collective-permute-start | bytes 294920 | tf_op jit(solution)/shard_map/ppermute | solution.py:389
  44.1 9.4 %collective-permute-start.8 = (bf16[8,64,256]{2,1,0:T(8,128)(2,1)S(1)}, bf16[8,64,256]{2,1,0:T(8,128)(2,1)S(1)}, u32[]{:S(2)}, u32[]{:S(2)}) collective-permute-start(bf16[8,64,256]{2,1,0:T(8,128)(2,1)S(1)} %get-tuple-element.61.field_ref), channel_id=1, source_target_pairs={{1,0},{2,1},{3,2},{4,3},{5,4},{6,5},{7,6},{8,7},{9,8},{10,9},{11,1... | collective-permute-start | bytes 786440 | tf_op jit(solution)/shard_map/ppermute | solution.py:392
  48.0 5.4 %collective-permute-start.9 = (bf16[6,32,256]{2,1,0:T(8,128)(2,1)S(1)}, bf16[6,32,256]{2,1,0:T(8,128)(2,1)S(1)}, u32[]{:S(2)}, u32[]{:S(2)}) collective-permute-start(bf16[6,32,256]{2,1,0:T(8,128)(2,1)S(1)} %pad_maximum_fusion.7), channel_id=1, source_target_pairs={{0,4},{1,5},{2,6},{3,7},{4,0},{5,1},{6,2},{7,3},{8,12},{9,13},{10,... | collective-permute-start | bytes 294920 | tf_op jit(solution)/shard_map/ppermute | solution.py:389
  48.1 5.8 %collective-permute-start.11 = (bf16[8,32,256]{2,1,0:T(8,128)(2,1)S(1)}, bf16[8,32,256]{2,1,0:T(8,128)(2,1)S(1)}, u32[]{:S(2)}, u32[]{:S(2)}) collective-permute-start(bf16[8,32,256]{2,1,0:T(8,128)(2,1)S(1)} %get-tuple-element.67), channel_id=1, source_target_pairs={{0,1},{1,2},{2,3},{3,4},{4,5},{5,6},{6,7},{7,8},{8,9},{9,10},{10,1... | collective-permute-start | bytes 393224 | tf_op jit(solution)/shard_map/ppermute | solution.py:392
  53.5 5.9 %collective-permute-start.10 = (bf16[9,32,256]{2,1,0:T(8,128)(2,1)S(1)}, bf16[9,32,256]{2,1,0:T(8,128)(2,1)S(1)}, u32[]{:S(2)}, u32[]{:S(2)}) collective-permute-start(bf16[9,32,256]{2,1,0:T(8,128)(2,1)S(1)} %constant_dynamic-update-slice_fusion.5), channel_id=1, source_target_pairs={{0,2},{1,3},{2,0},{3,1},{4,6},{5,7},{6,4},{7,5},{8,10},{9,11},{10,... | collective-permute-start | bytes 442376 | tf_op jit(solution)/shard_map/ppermute | solution.py:389
  61.4 1.2 %collective-permute-start.12 = (f32[64,128]{1,0:T(8,128)S(1)}, f32[64,128]{1,0:T(8,128)S(1)}, u32[]{:S(2)}, u32[]{:S(2)}) collective-permute-start(f32[64,128]{1,0:T(8,128)S(1)} %get-tuple-element.73), channel_id=1, source_target_pairs={{0,1},{1,0},{2,3},{3,2},{4,5},{5,4},{6,7},{7,6},{8,9},{9,8},{10,11... | collective-permute-start | bytes 98312 | tf_op jit(solution)/shard_map/ppermute | solution.py:389
  62.7 6.4 %collective-permute-start.13 = (f32[64,128]{1,0:T(8,128)S(1)}, f32[64,128]{1,0:T(8,128)S(1)}, u32[]{:S(2)}, u32[]{:S(2)}) collective-permute-start(f32[64,128]{1,0:T(8,128)S(1)} %add.33), channel_id=1, source_target_pairs={{0,8},{1,9},{2,10},{3,11},{4,12},{5,13},{6,14},{7,15},{8,0},{9,1},... | collective-permute-start | bytes 98312 | tf_op jit(solution)/shard_map/ppermute | solution.py:389
  69.0 3.9 %collective-permute-start.14 = (f32[64,128]{1,0:T(8,128)S(1)}, f32[64,128]{1,0:T(8,128)S(1)}, u32[]{:S(2)}, u32[]{:S(2)}) collective-permute-start(f32[64,128]{1,0:T(8,128)S(1)} %add.34), channel_id=1, source_target_pairs={{0,4},{1,5},{2,6},{3,7},{4,0},{5,1},{6,2},{7,3},{8,12},{9,13},{10,... | collective-permute-start | bytes 98312 | tf_op jit(solution)/shard_map/ppermute | solution.py:389
  72.9 3.9 %collective-permute-start.15 = (f32[64,128]{1,0:T(8,128)S(1)}, f32[64,128]{1,0:T(8,128)S(1)}, u32[]{:S(2)}, u32[]{:S(2)}) collective-permute-start(f32[64,128]{1,0:T(8,128)S(1)} %add.35.kept_ref), channel_id=1, source_target_pairs={{0,2},{1,3},{2,0},{3,1},{4,6},{5,7},{6,4},{7,5},{8,10},{9,11},{10,... | collective-permute-start | bytes 98312 | tf_op jit(solution)/shard_map/ppermute | solution.py:389

commit v3 on v2

--- a/solution.py
+++ b/solution.py
@@ -24,12 +24,12 @@
     return pl.BlockSpec(memory_space=space)
 
 
-def call(kernel, outs, ins, spaces, scratch=(), limit=40, flops=10**8, moved=10**6):
+def call(kernel, outs, ins, spaces, scratch=(), limit=40, flops=10**8, moved=10**6, placed=None):
     return pl.pallas_call(
         kernel,
         out_shape=outs,
         in_specs=[spec(s) for s in spaces],
-        out_specs=jax.tree.map(lambda _: spec(VMEM), outs),
+        out_specs=jax.tree.map(lambda _: spec(VMEM), outs) if placed is None else tuple(map(spec, placed)),
         scratch_shapes=list(scratch),
         compiler_params=pltpu.CompilerParams(vmem_limit_bytes=limit << 20),
         cost_estimate=pl.CostEstimate(flops=flops, bytes_accessed=moved, transcendentals=0),
@@ -79,27 +79,6 @@
     return dot(jnp.concatenate(spread, axis=0), basis)
 
 
-def start_kernel(right_hbm, basis_hbm, field_ref, proj_ref, near_proj_ref, cross_ref, right_ref, basis_ref, sems):
-    clusters = field_ref.shape[0]
-    copies = [
-        pltpu.make_async_copy(basis_hbm, basis_ref, sems.at[0]),
-        pltpu.make_async_copy(right_hbm, right_ref, sems.at[1]),
-    ]
-    for copy in copies:
-        copy.start()
-    copies[0].wait()
-    basis = basis_ref[...]
-    cross = dot_nt(basis, basis)
-    same = lane_group(cross.shape) == lax.broadcasted_iota(jnp.int32, cross.shape, 0) // K
-    cross_ref[...] = jnp.where(same, cross, 0.0)
-    copies[1].wait()
-    for c in range(clusters):
-        field_ref[c] = split_rows(right_ref[:, c * PANEL : (c + 1) * PANEL])
-    proj = project(field_ref[...].reshape(clusters * 2 * R, PANEL), basis)
-    proj_ref[...] = proj.astype(bf16)
-    near_proj_ref[...] = proj
-
-
 def places(devices):
     bits = devices.bit_length() - 1
     order = [0] + list(range(bits - 1, 0, -1))
@@ -107,24 +86,10 @@
     return order, place
 
 
-def couple_kernel(order, me_ref, pairs_hbm, slots_hbm, coupling_ref, out_ref, wide, pairs_ref, slots_ref, sems):
+def couple(order, me, pairs_ref, slots_ref, wide_ref, out_ref):
     clusters = out_ref.shape[2] // K
-    pairs = coupling_ref.shape[0] // K
-    me = me_ref[0]
-    copies = [
-        pltpu.make_async_copy(pairs_hbm, pairs_ref, sems.at[0]),
-        pltpu.make_async_copy(slots_hbm, slots_ref, sems.at[1]),
-    ]
-    for copy in copies:
-        copy.start()
-    out_ref[...] = jnp.zeros_like(out_ref)
-    rows = lax.broadcasted_iota(jnp.int32, (K, clusters * K), 0)
-    lanes = lax.broadcasted_iota(jnp.int32, (K, clusters * K), 1)
-    spread = jnp.where(lanes % K == rows, 1.0, 0.0).astype(bf16)
-    wide[...] = dot(coupling_ref[...], spread).astype(bf16)
-    group = lanes // K
-    for copy in copies:
-        copy.wait()
+    pairs = wide_ref.shape[0] // K
+    group = lane_group((K, clusters * K))
 
     def one(f):
         first = slots_ref[pairs_ref[0, f]]
@@ -135,33 +100,77 @@
         place = jnp.int32(0)
         for t, b in enumerate(order):
             place = place + (((apart >> b) & 1) << (len(order) - 1 - t))
-        block = wide[pl.ds(pl.multiple_of(f * K, K), K), :]
-        block = jnp.where(group == second % clusters, block, jnp.zeros_like(block))
+        block = wide_ref[pl.ds(f, K, stride=pairs), :]
+        block = jnp.concatenate([block] * (clusters * K // block.shape[1]), axis=1)
+        block = jnp.where(group == second % clusters, block, 0.0).astype(bf16)
         here = pl.ds(pl.multiple_of((first % clusters) * K, K), K)
         where = own * (1 << len(order)) + place
         out_ref[where, here, :] = out_ref[where, here, :] + block
 
     def some(step, carry):
-        for u in range(4):
-            one(step * 4 + u)
+        for u in range(8):
+            one(step * 8 + u)
         return carry
 
-    lax.fori_loop(0, pairs // 4, some, 0)
-
-
-def send(coupled_ref, proj, payload_ref, kept_ref):
+    lax.fori_loop(0, pairs // 8, some, 0)
+
+
+def open_kernel(order, me_ref, pairs_hbm, slots_hbm, coupling_hbm, right_hbm, basis_hbm, near_hbm, blocks_hbm,
+                near_pairs_ref, blocks_ref, field_ref, near_proj_ref, cross_ref, coupled_ref, payload_ref, kept_ref,
+                pairs_ref, slots_ref, coupling_ref, right_ref, basis_ref, wide_ref, sems):
+    clusters = field_ref.shape[0]
+    moves = [(coupling_hbm, coupling_ref), (basis_hbm, basis_ref), (right_hbm, right_ref),
+             (pairs_hbm, pairs_ref), (slots_hbm, slots_ref), (near_hbm, near_pairs_ref), (blocks_hbm, blocks_ref)]
+    copies = [pltpu.make_async_copy(*move, sems.at[i]) for i, move in enumerate(moves)]
+    for copy in copies:
+        copy.start()
+    coupled_ref[...] = jnp.zeros_like(coupled_ref)
+    copies[0].wait()
+    pairs = coupling_ref.shape[0]
+    lanes_held = 128
+    rows = lax.broadcasted_iota(jnp.int32, (lanes_held, lanes_held), 0)
+    lanes = lax.broadcasted_iota(jnp.int32, (lanes_held, lanes_held), 1)
+    tiles = coupling_ref.shape[1] // lanes_held
+    flat = jnp.concatenate(
+        [coupling_ref[:, t * lanes_held : (t + 1) * lanes_held] for t in range(tiles)], axis=0
+    )
+    each = lanes_held // K
+    for u in range(each):
+        spread = jnp.where((lanes % K == rows % K) & (rows // K == u), 1.0, 0.0).astype(bf16)
+        value = dot(flat, spread)
+        for t in range(tiles):
+            wide_ref[(t * each + u) * pairs : (t * each + u + 1) * pairs] = value[t * pairs : (t + 1) * pairs]
+    copies[1].wait()
+    basis = basis_ref[...]
+    cross = dot_nt(basis, basis)
+    same = lane_group(cross.shape) == lax.broadcasted_iota(jnp.int32, cross.shape, 0) // K
+    cross = jnp.where(same, cross, 0.0)
+    high = cross.astype(bf16)
+    cross_ref[0] = high
+    cross_ref[1] = (cross - high.astype(f32)).astype(bf16)
+    copies[2].wait()
+    for c in range(clusters):
+        field_ref[c] = split_rows(right_ref[:, c * PANEL : (c + 1) * PANEL])
+    proj = project(field_ref[...].reshape(clusters * 2 * R, PANEL), basis)
+    near_proj_ref[...] = proj
+    copies[3].wait()
+    copies[4].wait()
+    copies[5].wait()
+    couple(order, me_ref[0], pairs_ref, slots_ref, wide_ref, coupled_ref)
+    proj = proj.astype(bf16)
+    devices = coupled_ref.shape[0] // 2
+    send(lambda d: dot(proj, coupled_ref[devices + d]) + dot_nt(proj, coupled_ref[d]), payload_ref, kept_ref, proj)
+    copies[6].wait()
+
+
+def send(products, payload_ref, kept_ref, proj):
     half = kept_ref.shape[0]
     payload_ref[0] = proj
     for d in range(2 * half):
-        value = dot(proj, coupled_ref[2 * half + d]) + dot_nt(proj, coupled_ref[d])
         if d < half:
-            kept_ref[d] = value
+            kept_ref[d] = products(d)
         else:
-            payload_ref[1 + d - half] = value.astype(bf16)
-
-
-def send_kernel(coupled_ref, proj_ref, payload_ref, kept_ref):
-    send(coupled_ref, proj_ref[...], payload_ref, kept_ref)
+            payload_ref[1 + d - half] = products(d).astype(bf16)
 
 
 def near_specs(nb, group):
@@ -242,8 +251,14 @@
     )(near_pairs, near_count, near_blocks, *arrays)
 
 
-def far_sums(place, coupled_ref, low_ref, high_ref, kept_ref, got_ref):
-    devices = coupled_ref.shape[0] // 2
+def merge_kernel(coupled_ref, out_ref):
+    devices = out_ref.shape[0]
+    for d in range(devices):
+        out_ref[d] = coupled_ref[d] + coupled_ref[devices + d].T
+
+
+def far_sums(place, merged_ref, low_ref, high_ref, kept_ref, got_ref):
+    devices = merged_ref.shape[0]
     sums = kept_ref[0]
     for piece in range(got_ref.shape[0]):
         sums = sums + got_ref[piece].astype(f32)
@@ -251,21 +266,22 @@
     for g in range(devices):
         proj = low_ref[g] if g < devices // 2 else high_ref[g - devices // 2]
         apart = sum(((g >> t) & 1) << b for t, b in enumerate(order))
-        sums = sums + dot(proj, coupled_ref[place[apart]]) + dot_nt(proj, coupled_ref[devices + place[apart]])
+        sums = sums + dot(proj, merged_ref[place[apart]])
     return split_rows(sums)
 
 
-def exact(x, y):
-    return jnp.dot(x, y, precision=highest, preferred_element_type=f32)
-
-
-def turn_kernel(place, coupled_ref, low_ref, high_ref, kept_ref, got_ref, near_proj_ref, cross_ref,
+def across_clusters(sums, cross_ref):
+    return join_rows(dot(sums, cross_ref[0])) + dot(sums[:R], cross_ref[1])
+
+
+def turn_kernel(place, merged_ref, low_ref, high_ref, kept_ref, got_ref, near_proj_ref, cross_ref,
                 sums_ref, proj_ref, payload_ref, next_ref):
-    sums = far_sums(place, coupled_ref, low_ref, high_ref, kept_ref, got_ref)
+    sums = far_sums(place, merged_ref, low_ref, high_ref, kept_ref, got_ref)
     sums_ref[...] = sums
-    proj = near_proj_ref[...] + exact(join_rows(sums.astype(f32)), cross_ref[...])
+    proj = near_proj_ref[...] + across_clusters(sums, cross_ref)
     proj_ref[...] = proj
-    send(coupled_ref, proj.astype(bf16), payload_ref, next_ref)
+    proj = proj.astype(bf16)
+    send(lambda d: dot_nt(proj, merged_ref[d]), payload_ref, next_ref, proj)
 
 
 def image_kernel(near_ref, sums_ref, basis_ref, image_ref, field_ref):
@@ -302,12 +318,12 @@
     gram_ref[...] = gram
 
 
-def tail_kernel(place, coupled_ref, low_ref, high_ref, kept_ref, got_ref, near_proj_ref, cross_ref,
+def tail_kernel(place, merged_ref, low_ref, high_ref, kept_ref, got_ref, near_proj_ref, cross_ref,
                 right_proj_ref, image_proj_ref, early_ref, gram_ref, sums_ref, out_ref):
-    sums = far_sums(place, coupled_ref, low_ref, high_ref, kept_ref, got_ref)
+    sums = far_sums(place, merged_ref, low_ref, high_ref, kept_ref, got_ref)
     sums_ref[...] = sums
+    half = near_proj_ref[...] + 0.5 * across_clusters(sums, cross_ref)
     sums = join_rows(sums.astype(f32))
-    half = near_proj_ref[...] + 0.5 * exact(sums, cross_ref[...])
     known = jnp.concatenate([right_proj_ref[...], image_proj_ref[...], half, jnp.zeros_like(half)], axis=0)
     out_ref[:R] = early_ref[...]
     added = exact_nt(sums, known)
@@ -315,8 +331,44 @@
     out_ref[R:] = gram_ref[...] + added + mirror
 
 
+TALL = 8
+
+
 def lane(x, k):
     return jnp.broadcast_to(x[:, k : k + 1], x.shape)
+
+
+def eliminate(wide, late, k):
+    block, at = k // TALL, k % TALL
+    rows = lax.broadcasted_iota(jnp.int32, wide[block].shape, 0)
+    both = [wide] if late is None or block < len(wide) // 2 else [wide, late]
+    columns = [[lane(x, k + j) for x in wide[block:]] for j in range(4)]
+    m = [[columns[j][0][at + i : at + i + 1] for j in range(4)] for i in range(4)]
+    scale = 1.0 / (m[0][0] * m[1][1] - m[0][1] * m[1][0])
+    first = {j: (m[1][1] * m[0][j] - m[0][1] * m[1][j]) * scale for j in (2, 3)}
+    second = {j: (m[0][0] * m[1][j] - m[1][0] * m[0][j]) * scale for j in (2, 3)}
+    s = {(i, j): m[i][j] - (m[i][0] * first[j] + m[i][1] * second[j]) for i in (2, 3) for j in (2, 3)}
+    after = 1.0 / (s[2, 2] * s[3, 3] - s[2, 3] * s[3, 2])
+    ratio, last_ratio = m[1][0] / m[0][0], s[3, 2] / s[2, 2]
+    for part in both:
+        p = [part[block][at + i : at + i + 1] for i in range(4)]
+        y0 = (m[1][1] * p[0] - m[0][1] * p[1]) * scale
+        y1 = (m[0][0] * p[1] - m[1][0] * p[0]) * scale
+        r2 = p[2] - (m[2][0] * y0 + m[2][1] * y1)
+        r3 = p[3] - (m[3][0] * y0 + m[3][1] * y1)
+        x2 = (s[3, 3] * r2 - s[2, 3] * r3) * after
+        x3 = (s[2, 2] * r3 - s[3, 2] * r2) * after
+        x0 = y0 - (first[2] * x2 + first[3] * x3)
+        x1 = y1 - (second[2] * x2 + second[3] * x3)
+        own = [p[0], p[1] - ratio * p[0], r2, r3 - last_ratio * r2]
+        for i in range(block, len(wide)):
+            c = [column[i - block] for column in columns]
+            rest = part[i] - ((c[0] * x0 + c[1] * x1) + (c[2] * x2 + c[3] * x3))
+            if i == block:
+                rest = jnp.where(rows > at + 3, rest, part[i])
+                for t in range(1, 4):
+                    rest = jnp.where(rows == at + t, own[t], rest)
+            part[i] = rest
 
 
 def last_kernel(kept_ref, got_ref, right_ref, image_ref, second_ref, field_ref, residual_ref, hessenberg_ref):
@@ -344,37 +396,46 @@
         axis=0,
     )
     lower = jnp.where(lanes - 2 * R == rows, 1.0, lower)
-
-    def two(matrix, k):
-        p, q = matrix[k : k + 1], matrix[k + 1 : k + 2]
-        a, b, c, d = lane(p, k), lane(p, k + 1), lane(q, k), lane(q, k + 1)
-        scale = 1.0 / (a * d - b * c)
-        p_new, q_new = (d * p - b * q) * scale, (a * q - c * p) * scale
-        rest = matrix - lane(matrix, k) * p_new - lane(matrix, k + 1) * q_new
-        return p, q, a, c, p_new, q_new, rest
-
-    for k in range(0, 2 * R, 2):
-        p, q, a, c, p_new, q_new, rest = two(system, k)
-        system = jnp.where(rows == k, p_new, jnp.where(rows == k + 1, q_new, rest))
-        p, q, a, c, p_new, q_new, rest = two(lower, k)
-        lower = jnp.where(rows > k + 1, rest, jnp.where(rows == k + 1, q - c / a * p, lower))
-    diagonal = jnp.sum(jnp.where(lanes == rows, lower, 0.0), axis=1, keepdims=True)
-    lower = lower * lax.rsqrt(diagonal)
-    weights = system.T[2 * R : 3 * R, : 2 * R]
+    system = jnp.where(lanes - 3 * R == rows, 1.0, system)
+    late = jnp.where(lanes + R == rows, 1.0, 0.0)
+
+    def blocks(x):
+        return [x[i : i + TALL] for i in range(0, 2 * R, TALL)]
+
+    system, lower, late = blocks(system), blocks(lower), blocks(late)
+    for k in range(0, 2 * R, 4):
+        eliminate(system, late, k)
+        eliminate(lower, None, k)
+    system, lower, late = (jnp.concatenate(x, axis=0) for x in (system, lower, late))
+
+    def diagonal(x):
+        return jnp.sum(jnp.where(lanes == rows, x, 0.0), axis=1, keepdims=True)
+
+    lower = lower * lax.rsqrt(diagonal(lower))
+    scaled = system[:, 2 * R : 3 * R] / diagonal(system)
+    inverse = jnp.concatenate([system[:, 3 * R :], late[:, :R]], axis=1)
+    weights = lax.dot_general(scaled, inverse, TN, precision=highest, preferred_element_type=f32)
     inverse_zero = lower[:R, 2 * R : 3 * R]
-    hessenberg_ref[:R] = exact_nt(lower[:R, R : 2 * R], inverse_zero)
-    hessenberg_ref[R:] = exact_nt(inverse_zero, lower[R:, R : 2 * R])
+    hessenberg_ref[:, :R] = exact_nt(inverse_zero, lower[:R, R : 2 * R])
+    hessenberg_ref[:, R:] = lax.dot_general(
+        lower[R:, R : 2 * R], inverse_zero, NT, precision=highest, preferred_element_type=f32
+    )
+    none = jnp.zeros((R, R), f32)
+    mix = jnp.concatenate(
+        [jnp.concatenate([weights, none], axis=1), jnp.concatenate([none, weights], axis=1)], axis=0
+    )
+    mix_high = mix.astype(bf16)
+    mix_both = jnp.concatenate([mix_high, (mix - mix_high.astype(f32)).astype(bf16)], axis=0)
     for c in range(clusters):
         here = slice(c * PANEL, (c + 1) * PANEL)
-        right, image, second = right_ref[:, here], image_ref[c], second_ref[c]
-
-        def combine(x, y):
-            return jnp.dot(
-                weights, jnp.concatenate([x, y], axis=0), precision=highest, preferred_element_type=f32
-            )
-
-        field_ref[:, here] = combine(right, image)
-        residual_ref[:, here] = right - combine(image, second)
+        right = right_ref[:, here]
+        stacked = jnp.concatenate([right, image_ref[c], second_ref[c]], axis=0)
+        high = stacked.astype(bf16)
+        low = (stacked - high.astype(f32)).astype(bf16)
+        both = dot(mix_both, high)
+        value = both[: 2 * R] + both[2 * R :] + dot(mix_high, low)
+        field_ref[:, here] = value[:R]
+        residual_ref[:, here] = right - value[R:]
 
 
 def body(right_side, near_pairs, near_count, near_blocks, far_pairs, coupling, cluster_basis, cluster_slot):
@@ -394,33 +455,36 @@
     panels = sds((clusters, R, PANEL), f32)
     narrow = sds((clusters, R, PANEL), bf16)
     split = sds((clusters, 2 * R, PANEL), bf16)
-    rank = sds((R, clusters * K), bf16)
     rank_wide = sds((R, clusters * K), f32)
     rank_split = sds((2 * R, clusters * K), bf16)
-    square = sds((clusters * K, clusters * K), f32)
     half = devices // 2
     payload_out = sds((1 + half, R, clusters * K), bf16)
     kept_out = sds((half, R, clusters * K), f32)
     barrier = lax.optimization_barrier
 
-    field, proj, right_proj, cross = call(
-        start_kernel, (split, rank, rank_wide, square), (right_side, basis), (pltpu.HBM, pltpu.HBM),
-        [pltpu.VMEM(right_side.shape, f32), pltpu.VMEM(basis.shape, bf16), pltpu.SemaphoreType.DMA((2,))],
-    )
-    coupled = call(
-        functools.partial(couple_kernel, order),
-        sds((2 * devices, clusters * K, clusters * K), bf16),
-        (me, far_pairs, cluster_slot, coupling.reshape(-1, K)),
-        (SMEM, pltpu.HBM, pltpu.HBM, VMEM),
+    def in_hbm(x):
+        return pltpu.with_memory_space_constraint(x, pltpu.HBM)
+
+    near_pairs, near_blocks, field, right_proj, cross, coupled, payload, sums = call(
+        functools.partial(open_kernel, order),
+        (sds(near_pairs.shape, jnp.int32), sds(near_blocks.shape, bf16), split, rank_wide, sds((2, clusters * K, clusters * K), bf16),
+         sds((2 * devices, clusters * K, clusters * K), bf16), payload_out, kept_out),
+        (me, in_hbm(far_pairs), in_hbm(cluster_slot), in_hbm(coupling), in_hbm(right_side), in_hbm(basis),
+         in_hbm(near_pairs), in_hbm(near_blocks)),
+        [SMEM] + [pltpu.HBM] * 7,
         [
-            pltpu.VMEM((coupling.shape[0] * K, clusters * K), bf16),
             pltpu.SMEM(far_pairs.shape, jnp.int32),
             pltpu.SMEM(cluster_slot.shape, jnp.int32),
-            pltpu.SemaphoreType.DMA((2,)),
+            pltpu.VMEM(coupling.shape, bf16),
+            pltpu.VMEM(right_side.shape, f32),
+            pltpu.VMEM(basis.shape, bf16),
+            pltpu.VMEM((coupling.shape[0] * K, 128), f32),
+            pltpu.SemaphoreType.DMA((7,)),
         ],
-    )
-
-    def exchange(make_field, payload, sums):
+        placed=[SMEM] + [VMEM] * 7,
+    )
+
+    def exchange(make_field, payload, sums, merged):
         for t, b in enumerate(order):
             if t > 0:
                 held, half = gathered.shape[0], sums.shape[0] // 2
@@ -430,6 +494,8 @@
                 gathered, held = payload[:1], 1
             if t == 2:
                 payload, own = barrier((payload, own))
+            if t == 3 and merged is None:
+                payload, merged = barrier((payload, made))
             got = across(payload, b)
             if t == 0:
                 image, field, got = make_field(got)
@@ -439,6 +505,11 @@
                     [pltpu.VMEM((2 * clusters + 1, R, PANEL), f32)],
                 )
                 back = shift(following, 1)
+            if t == 1 and merged is None:
+                ready, got = barrier((coupled, got))
+                made = call(
+                    merge_kernel, sds((devices, clusters * K, clusters * K), bf16), (ready,), [VMEM]
+                )
             if t == len(order) - 2:
                 after, got = barrier((after, got))
             got_gathered, got_sums = got[:held], got[held:]
@@ -450,14 +521,13 @@
             (field, after, own, back, basis),
             [pltpu.VMEM((2 * clusters, 2 * R, PANEL), bf16), pltpu.VMEM((clusters + 1, R, PANEL), f32)],
         )
-        return image, near, (coupled, gathered, got_gathered, sums, got_sums, near_proj, cross)
+        return image, near, (merged, gathered, got_gathered, sums, got_sums, near_proj, cross)
 
     def first_field(got):
         ready, got = barrier((field, got))
         return right_side, ready, got
 
-    payload, sums = call(send_kernel, (payload_out, kept_out), (coupled, proj), (VMEM, VMEM))
-    unused, near, parts = exchange(first_field, payload, sums)
+    unused, near, parts = exchange(first_field, payload, sums, None)
     far, image_proj, payload, sums = call(
         functools.partial(turn_kernel, place), (rank_split, rank_wide, payload_out, kept_out), parts, [VMEM] * 7
     )
@@ -466,7 +536,7 @@
         ready, got = barrier((far, got))
         return *call(image_kernel, (panels, split), (near, ready, basis), [VMEM] * 3), got
 
-    image, near_two, parts = exchange(second_field, payload, sums)
+    image, near_two, parts = exchange(second_field, payload, sums, parts[0])
     early = call(gram_one_kernel, sds((R, 4 * R), f32), (right_side, image), [VMEM] * 2)
     gram = call(gram_two_kernel, sds((R, 4 * R), f32), (right_side, image, near_two), [VMEM] * 3)
     far, gram = call(
@@ -484,9 +554,10 @@
             far, got = barrier((far, got))
             second = call(second_kernel, panels, (near_two, far, basis), [VMEM] * 3)
     wide = sds(right_side.shape, f32)
-    return call(
-        last_kernel, (wide, wide, sds((2 * R, R), f32)), (gram, got, right_side, image, second), [VMEM] * 5
-    )
+    solution_field, residual, hessenberg = call(
+        last_kernel, (wide, wide, sds((R, 2 * R), f32)), (gram, got, right_side, image, second), [VMEM] * 5
+    )
+    return solution_field, residual, hessenberg.T
 
 
 def solution(mesh):

time: 82 us -> 73.1 us (0.89)
  waiting for transfers between devices: 21.1 us -> 13.4 us
  local copies, waits for them, and re-layouts: 6.21 us -> 0.14 us
  Pallas kernels: 28.4 us -> 32.3 us
    ppermute x12, waiting for transfers between devices: 21.1 us -> 13.4 us  [across(): return lax.ppermute(x, 'leaf', [(i, i ^ 1 << b) for i in range(devices)])]
    pallas_call x4, Pallas kernels: 9.94 us -> 15.9 us  [near_call(): pl.pallas_call(kernel, out_shape=outs, grid_spec=pltpu.PrefetchScalarGrid...]
    unnamed x24 -> x8, local copies, waits for them, and re-layouts: 3.62 us -> 0.04 us
    ppermute x12, starting transfers between devices: 16.8 us -> 20 us  [across(): return lax.ppermute(x, 'leaf', [(i, i ^ 1 << b) for i in range(devices)])]
    ppermute x4, starting transfers between devices: 8.1 us -> 5.15 us  [shift(): lax.ppermute(x, 'leaf', [(i, i + by) for i in range(devices) if 0 <= i +...]
    pallas_call x10 -> x9, Pallas kernels: 18.4 us -> 16.4 us  [call(): pl.pallas_call(kernel, out_shape=outs, in_specs=[spec(s) for s in spaces]...]
    reshape x1 -> x0, local copies, waits for them, and re-layouts: 1.84 us -> none  [body(): coupling.reshape(-1, K)]
  transfers between devices with their start and end apart: 16 -> 16, of which waited for: 12 -> 9; matrix products, arithmetic and copies ran while one was open for 0% -> 0% of each run, Pallas kernels for 15% -> 26%
where the time goes in v3:
time: 73.1 us; the launch traced here: 72.9 us
  Pallas kernels  32.3 us (44%)
  starting transfers between devices  25.2 us (34%)
  waiting for transfers between devices  13.4 us (18%)
  between operations  1.67 us (2%)
    ppermute x12, starting transfers between devices, across(): return lax.ppermute(x, 'leaf', [(i, i ^ 1 << b) for i in range(devices)])  20 us
    pallas_call x9, Pallas kernels, call(): pl.pallas_call(kernel, out_shape=outs, in_specs=[spec(s) for s in spaces]...  16.4 us
    pallas_call x4, Pallas kernels, near_call(): pl.pallas_call(kernel, out_shape=outs, grid_spec=pltpu.PrefetchScalarGrid...  15.9 us
    ppermute x12, waiting for transfers between devices, across(): return lax.ppermute(x, 'leaf', [(i, i ^ 1 << b) for i in range(devices)])  13.4 us
    ppermute x4, starting transfers between devices, shift(): lax.ppermute(x, 'leaf', [(i, i + by) for i in range(devices) if 0 <= i +...  5.15 us
  transfers between devices with their start and end apart: 16, of which 9 were waited for; matrix products, arithmetic and copies ran while one was open for 0% of the time, Pallas kernels for 26%

profile of v3, /device:TPU:0, one launch (start us, length us, event | category | flops | bytes accessed | tf_op | source)
XLA Modules:
  0.0 72.9 jit_solution(8740492462882223213)
XLA Ops:
  0.6 6.5 %shard_map.103 = (s32[2,64]{1,0:T(2,128)S(1)}, bf16[64,256,256]{2,1,0:T(8,128)(2,1)S(1)}, bf16[8,64,256]{2,1,0:T(8,128)(2,1)S(1)}, f32[32,256]{1,0:T(8,128)S(1)}...) custom-call(s32[1]{0:T(128)} %bitcast.me_ref, ...), custom_call_target="tpu_custom_call" | custom-call | flops 100000000 | bytes 1000000 | tf_op jit(solution)/shard_map/pallas_call | solution.py:28
  7.1 0.5 collective-permute-start
  7.6 1.0 %collective-permute-done = bf16[9,32,256]{2,1,0:T(8,128)(2,1)S(1)} collective-permute-done((bf16[9,32,256]{2,1,0:T(8,128)(2,1)S(1)}, bf16[9,32,256]{2,1,0:T(8,128)(2,1)S(1)}, u32[]{:S(2)}, u32[]{:S(2)}) %collective-permute-start) | collective-permute-done | bytes 147488 | tf_op jit(solution)/shard_map/ppermute | solution.py:450
  8.7 4.0 %collective-permute-start.1 = (bf16[6,32,256]{2,1,0:T(8,128)(2,1)S(1)}, bf16[6,32,256]{2,1,0:T(8,128)(2,1)S(1)}, u32[]{:S(2)}, u32[]{:S(2)}) collective-permute-start(bf16[6,32,256]{2,1,0:T(8,128)(2,1)S(1)} %pad_maximum_fusion.2), channel_id=1, source_target_pairs={{0,8},{1,9},{2,10},{3,11},{4,12},{5,13},{6,14},{7,15},{8,0},{9,1},... | collective-permute-start | bytes 294920 | tf_op jit(solution)/shard_map/ppermute | solution.py:450
  13.4 1.3 %collective-permute-start.2 = (bf16[8,64,256]{2,1,0:T(8,128)(2,1)S(1)}, bf16[8,64,256]{2,1,0:T(8,128)(2,1)S(1)}, u32[]{:S(2)}, u32[]{:S(2)}) collective-permute-start(bf16[8,64,256]{2,1,0:T(8,128)(2,1)S(1)} %get-tuple-element.56.field_ref), channel_id=1, source_target_pairs={{1,0},{2,1},{3,2},{4,3},{5,4},{6,5},{7,6},{8,7},{9,8},{10,9},{11,1... | collective-permute-start | bytes 786440 | tf_op jit(solution)/shard_map/ppermute | solution.py:453
  14.7 3.3 %shard_map.104 = (f32[8,32,256]{2,1,0:T(8,128)S(1)}, bf16[8,32,256]{2,1,0:T(8,128)(2,1)S(1)}) custom-call(s32[2,64]{1,0:T(2,128)S(1)} %get-tuple-element.57.pairs_ref, s32[1]{0:T(128)S(6)} %copy.19.count_ref, bf16[64,256,256]{2,1,0:T(8,128)(2,1)S(1)} %get-tuple-element.58.blocks_ref, bf16[8,64,256]{2,1,0:T(8,128)(2,1)S(1)} %get-tuple-element.56.field_ref), custom_call_target="tpu_custom_call" | custom-call | flops 536870912 | bytes 8388608 | tf_op jit(solution)/shard_map/pallas_call | solution.py:235
  18.1 3.1 %collective-permute-start.3 = (bf16[6,32,256]{2,1,0:T(8,128)(2,1)S(1)}, bf16[6,32,256]{2,1,0:T(8,128)(2,1)S(1)}, u32[]{:S(2)}, u32[]{:S(2)}) collective-permute-start(bf16[6,32,256]{2,1,0:T(8,128)(2,1)S(1)} %pad_maximum_fusion.4), channel_id=1, source_target_pairs={{0,4},{1,5},{2,6},{3,7},{4,0},{5,1},{6,2},{7,3},{8,12},{9,13},{10,... | collective-permute-start | bytes 294920 | tf_op jit(solution)/shard_map/ppermute | solution.py:450
  21.2 1.3 %collective-permute-start.5 = (bf16[8,32,256]{2,1,0:T(8,128)(2,1)S(1)}, bf16[8,32,256]{2,1,0:T(8,128)(2,1)S(1)}, u32[]{:S(2)}, u32[]{:S(2)}) collective-permute-start(bf16[8,32,256]{2,1,0:T(8,128)(2,1)S(1)} %get-tuple-element.67), channel_id=1, source_target_pairs={{0,1},{1,2},{2,3},{3,4},{4,5},{5,6},{6,7},{7,8},{8,9},{9,10},{10,1... | collective-permute-start | bytes 393224 | tf_op jit(solution)/shard_map/ppermute | solution.py:453
  22.5 0.6 shard_map.105.merged_ref
  23.1 1.1 %collective-permute-done.3 = bf16[6,32,256]{2,1,0:T(8,128)(2,1)S(1)} collective-permute-done((bf16[6,32,256]{2,1,0:T(8,128)(2,1)S(1)}, bf16[6,32,256]{2,1,0:T(8,128)(2,1)S(1)}, u32[]{:S(2)}, u32[]{:S(2)}) %collective-permute-start.3) | collective-permute-done | bytes 98336 | tf_op jit(solution)/shard_map/ppermute | solution.py:450
  24.4 4.6 %shard_map.106 = (f32[8,32,256]{2,1,0:T(8,128)S(1)}, f32[32,256]{1,0:T(8,128)S(1)}) custom-call(s32[2,64]{1,0:T(2,128)S(1)} %get-tuple-element.57.pairs_ref, s32[1]{0:T(128)S(6)} %copy.19.count_ref, bf16[64,256,256]{2,1,0:T(8,128)(2,1)S(1)} %get-tuple-element.58.blocks_ref, bf16[8,64,256]{2,1,0:T(8,128)(2,1)S(1)} %get-tuple-element.56.field_ref, ...), custom_call_target="tpu_custom_call" | custom-call | flops 536870912 | bytes 8388608 | tf_op jit(solution)/shard_map/pallas_call | solution.py:235
  29.1 0.7 %collective-permute-done.4 = bf16[9,32,256]{2,1,0:T(8,128)(2,1)S(1)} collective-permute-done((bf16[9,32,256]{2,1,0:T(8,128)(2,1)S(1)}, bf16[9,32,256]{2,1,0:T(8,128)(2,1)S(1)}, u32[]{:S(2)}, u32[]{:S(2)}) %collective-permute-start.4) | collective-permute-done | bytes 147488 | tf_op jit(solution)/shard_map/ppermute | solution.py:450
  29.8 1.6 %shard_map.107 = (bf16[64,256]{1,0:T(8,128)(2,1)S(1)}, f32[32,256]{1,0:T(8,128)S(1)}, bf16[9,32,256]{2,1,0:T(8,128)(2,1)S(1)}, f32[8,32,256]{2,1,0:T(8,128)S(1)}) custom-call(bf16[16,256,256]{2,1,0:T(8,128)(2,1)S(1)} %shard_map.105.merged_ref, bf16[8,32,256]{2,1,0:T(8,128)(2,1)S(1)} %pad_maximum_fusion.low_ref, bf16[8,32,256]{2,1,0:T(8,128)(2,1)S(1)} %slice.131.high_ref, ...), custom_call_target="tpu_custom_call" | custom-call | flops 100000000 | bytes 1000000 | tf_op jit(solution)/shard_map/pallas_call | solution.py:28
  31.5 1.3 %collective-permute-done.6 = bf16[9,32,256]{2,1,0:T(8,128)(2,1)S(1)} collective-permute-done((bf16[9,32,256]{2,1,0:T(8,128)(2,1)S(1)}, bf16[9,32,256]{2,1,0:T(8,128)(2,1)S(1)}, u32[]{:S(2)}, u32[]{:S(2)}) %collective-permute-start.6) | collective-permute-done | bytes 147488 | tf_op jit(solution)/shard_map/ppermute | solution.py:450
  32.9 2.8 %collective-permute-start.7 = (bf16[6,32,256]{2,1,0:T(8,128)(2,1)S(1)}, bf16[6,32,256]{2,1,0:T(8,128)(2,1)S(1)}, u32[]{:S(2)}, u32[]{:S(2)}) collective-permute-start(bf16[6,32,256]{2,1,0:T(8,128)(2,1)S(1)} %pad_maximum_fusion.5), channel_id=1, source_target_pairs={{0,8},{1,9},{2,10},{3,11},{4,12},{5,13},{6,14},{7,15},{8,0},{9,1},... | collective-permute-start | bytes 294920 | tf_op jit(solution)/shard_map/ppermute | solution.py:450
  36.0 1.3 %collective-permute-start.8 = (bf16[8,64,256]{2,1,0:T(8,128)(2,1)S(1)}, bf16[8,64,256]{2,1,0:T(8,128)(2,1)S(1)}, u32[]{:S(2)}, u32[]{:S(2)}) collective-permute-start(bf16[8,64,256]{2,1,0:T(8,128)(2,1)S(1)} %get-tuple-element.76.field_ref), channel_id=1, source_target_pairs={{1,0},{2,1},{3,2},{4,3},{5,4},{6,5},{7,6},{8,7},{9,8},{10,9},{11,1... | collective-permute-start | bytes 786440 | tf_op jit(solution)/shard_map/ppermute | solution.py:453
  37.3 3.3 %shard_map.109 = (f32[8,32,256]{2,1,0:T(8,128)S(1)}, bf16[8,32,256]{2,1,0:T(8,128)(2,1)S(1)}) custom-call(s32[2,64]{1,0:T(2,128)S(1)} %get-tuple-element.57.pairs_ref, s32[1]{0:T(128)S(6)} %copy.19.count_ref, bf16[64,256,256]{2,1,0:T(8,128)(2,1)S(1)} %get-tuple-element.58.blocks_ref, bf16[8,64,256]{2,1,0:T(8,128)(2,1)S(1)} %get-tuple-element.76.field_ref), custom_call_target="tpu_custom_call" | custom-call | flops 536870912 | bytes 8388608 | tf_op jit(solution)/shard_map/pallas_call | solution.py:235
  40.7 2.2 %collective-permute-start.9 = (bf16[6,32,256]{2,1,0:T(8,128)(2,1)S(1)}, bf16[6,32,256]{2,1,0:T(8,128)(2,1)S(1)}, u32[]{:S(2)}, u32[]{:S(2)}) collective-permute-start(bf16[6,32,256]{2,1,0:T(8,128)(2,1)S(1)} %pad_maximum_fusion.7), channel_id=1, source_target_pairs={{0,4},{1,5},{2,6},{3,7},{4,0},{5,1},{6,2},{7,3},{8,12},{9,13},{10,... | collective-permute-start | bytes 294920 | tf_op jit(solution)/shard_map/ppermute | solution.py:450
  42.9 1.3 %collective-permute-start.11 = (bf16[8,32,256]{2,1,0:T(8,128)(2,1)S(1)}, bf16[8,32,256]{2,1,0:T(8,128)(2,1)S(1)}, u32[]{:S(2)}, u32[]{:S(2)}) collective-permute-start(bf16[8,32,256]{2,1,0:T(8,128)(2,1)S(1)} %get-tuple-element.82), channel_id=1, source_target_pairs={{0,1},{1,2},{2,3},{3,4},{4,5},{5,6},{6,7},{7,8},{8,9},{9,10},{10,1... | collective-permute-start | bytes 393224 | tf_op jit(solution)/shard_map/ppermute | solution.py:453
  44.2 1.1 %shard_map.111.early_ref = f32[32,128]{1,0:T(8,128)S(1)} custom-call(f32[32,2048]{1,0:T(8,128)S(1)} %copy-done, f32[8,32,256]{2,1,0:T(8,128)S(1)} %get-tuple-element.86.image_ref), custom_call_target="tpu_custom_call" | custom-call | flops 100000000 | bytes 1000000 | tf_op jit(solution)/shard_map/pallas_call | solution.py:28
  45.4 0.9 %collective-permute-done.9 = bf16[6,32,256]{2,1,0:T(8,128)(2,1)S(1)} collective-permute-done((bf16[6,32,256]{2,1,0:T(8,128)(2,1)S(1)}, bf16[6,32,256]{2,1,0:T(8,128)(2,1)S(1)}, u32[]{:S(2)}, u32[]{:S(2)}) %collective-permute-start.9) | collective-permute-done | bytes 98336 | tf_op jit(solution)/shard_map/ppermute | solution.py:450
  46.3 0.6 collective-permute-start.10
  46.9 4.6 %shard_map.110 = (f32[8,32,256]{2,1,0:T(8,128)S(1)}, f32[32,256]{1,0:T(8,128)S(1)}) custom-call(s32[2,64]{1,0:T(2,128)S(1)} %get-tuple-element.57.pairs_ref, s32[1]{0:T(128)S(6)} %copy.19.count_ref, bf16[64,256,256]{2,1,0:T(8,128)(2,1)S(1)} %get-tuple-element.58.blocks_ref, bf16[8,64,256]{2,1,0:T(8,128)(2,1)S(1)} %get-tuple-element.76.field_ref, ...), custom_call_target="tpu_custom_call" | custom-call | flops 536870912 | bytes 8388608 | tf_op jit(solution)/shard_map/pallas_call | solution.py:235
  51.5 0.7 %shard_map.112.gram_ref = f32[32,128]{1,0:T(8,128)S(1)} custom-call(f32[32,2048]{1,0:T(8,128)S(1)} %copy-done, f32[8,32,256]{2,1,0:T(8,128)S(1)} %get-tuple-element.86.image_ref, f32[8,32,256]{2,1,0:T(8,128)S(1)} %get-tuple-element.87.near_ref), custom_call_target="tpu_custom_call" | custom-call | flops 100000000 | bytes 1000000 | tf_op jit(solution)/shard_map/pallas_call | solution.py:28
  52.3 1.1 %shard_map.113 = (bf16[64,256]{1,0:T(8,128)(2,1)S(1)}, f32[64,128]{1,0:T(8,128)S(1)}) custom-call(bf16[16,256,256]{2,1,0:T(8,128)(2,1)S(1)} %shard_map.105.merged_ref, bf16[8,32,256]{2,1,0:T(8,128)(2,1)S(1)} %pad_maximum_fusion.1.low_ref, bf16[8,32,256]{2,1,0:T(8,128)(2,1)S(1)} %slice.141.high_ref, f32[1,32,256]{2,1,0:T(8,128)S(1)} %slice.142.kept_ref, ...), custom_call_target="tpu_custom_call" | custom-call | flops 100000000 | bytes 1000000 | tf_op jit(solution)/shard_map/pallas_call | solution.py:28
  53.6 1.1 %collective-permute-done.12 = f32[64,128]{1,0:T(8,128)S(1)} collective-permute-done((f32[64,128]{1,0:T(8,128)S(1)}, f32[64,128]{1,0:T(8,128)S(1)}, u32[]{:S(2)}, u32[]{:S(2)}) %collective-permute-start.12) | collective-permute-done | bytes 32800 | tf_op jit(solution)/shard_map/ppermute | solution.py:450
  54.7 3.3 %collective-permute-start.13 = (f32[64,128]{1,0:T(8,128)S(1)}, f32[64,128]{1,0:T(8,128)S(1)}, u32[]{:S(2)}, u32[]{:S(2)}) collective-permute-start(f32[64,128]{1,0:T(8,128)S(1)} %add.33), channel_id=1, source_target_pairs={{0,8},{1,9},{2,10},{3,11},{4,12},{5,13},{6,14},{7,15},{8,0},{9,1},... | collective-permute-start | bytes 98312 | tf_op jit(solution)/shard_map/ppermute | solution.py:450
  58.2 1.7 %collective-permute-done.13 = f32[64,128]{1,0:T(8,128)S(1)} collective-permute-done((f32[64,128]{1,0:T(8,128)S(1)}, f32[64,128]{1,0:T(8,128)S(1)}, u32[]{:S(2)}, u32[]{:S(2)}) %collective-permute-start.13) | collective-permute-done | bytes 32800 | tf_op jit(solution)/shard_map/ppermute | solution.py:450
  59.9 2.8 %collective-permute-start.14 = (f32[64,128]{1,0:T(8,128)S(1)}, f32[64,128]{1,0:T(8,128)S(1)}, u32[]{:S(2)}, u32[]{:S(2)}) collective-permute-start(f32[64,128]{1,0:T(8,128)S(1)} %add.34), channel_id=1, source_target_pairs={{0,4},{1,5},{2,6},{3,7},{4,0},{5,1},{6,2},{7,3},{8,12},{9,13},{10,... | collective-permute-start | bytes 98312 | tf_op jit(solution)/shard_map/ppermute | solution.py:450
  62.8 1.9 %collective-permute-done.14 = f32[64,128]{1,0:T(8,128)S(1)} collective-permute-done((f32[64,128]{1,0:T(8,128)S(1)}, f32[64,128]{1,0:T(8,128)S(1)}, u32[]{:S(2)}, u32[]{:S(2)}) %collective-permute-start.14) | collective-permute-done | bytes 32800 | tf_op jit(solution)/shard_map/ppermute | solution.py:450
  65.0 3.6 %collective-permute-done.15.got_ref = f32[64,128]{1,0:T(8,128)S(1)} collective-permute-done((f32[64,128]{1,0:T(8,128)S(1)}, f32[64,128]{1,0:T(8,128)S(1)}, u32[]{:S(2)}, u32[]{:S(2)}) %collective-permute-start.15) | collective-permute-done | bytes 32800 | tf_op jit(solution)/shard_map/ppermute | solution.py:450
  68.6 4.3 %shard_map.115 = (f32[32,2048]{1,0:T(8,128)}, f32[32,2048]{1,0:T(8,128)}, f32[32,64]{1,0:T(8,128)}) custom-call(f32[64,128]{1,0:T(8,128)S(1)} %add.35.kept_ref, f32[64,128]{1,0:T(8,128)S(1)} %collective-permute-done.15.got_ref, f32[32,2048]{1,0:T(8,128)S(1)} %copy-done, f32[8,32,256]{2,1,0:T(8,128)S(1)} %get-tuple-element.86.image_ref, ...), custom_call_target="tpu_custom_call" | custom-call | flops 100000000 | bytes 1000000 | tf_op jit(solution)/shard_map/pallas_call | solution.py:28
  (52 shorter events, 1.4 us)
Async XLA Ops:
  7.1 1.5 %collective-permute-start = (bf16[9,32,256]{2,1,0:T(8,128)(2,1)S(1)}, bf16[9,32,256]{2,1,0:T(8,128)(2,1)S(1)}, u32[]{:S(2)}, u32[]{:S(2)}) collective-permute-start(bf16[9,32,256]{2,1,0:T(8,128)(2,1)S(1)} %get-tuple-element.50), channel_id=1, source_target_pairs={{0,1},{1,0},{2,3},{3,2},{4,5},{5,4},{6,7},{7,6},{8,9},{9,8},{10,11... | collective-permute-start | bytes 442376 | tf_op jit(solution)/shard_map/ppermute | solution.py:450
  8.7 15.7 %copy-start.1 = (bf16[8,32,256]{2,1,0:T(8,128)(2,1)S(1)}, bf16[8,32,256]{2,1,0:T(8,128)(2,1)}, u32[]{:S(2)}) copy-start(bf16[8,32,256]{2,1,0:T(8,128)(2,1)} %param.14) | copy-start | bytes 393220
  8.7 9.3 %collective-permute-start.1 = (bf16[6,32,256]{2,1,0:T(8,128)(2,1)S(1)}, bf16[6,32,256]{2,1,0:T(8,128)(2,1)S(1)}, u32[]{:S(2)}, u32[]{:S(2)}) collective-permute-start(bf16[6,32,256]{2,1,0:T(8,128)(2,1)S(1)} %pad_maximum_fusion.2), channel_id=1, source_target_pairs={{0,8},{1,9},{2,10},{3,11},{4,12},{5,13},{6,14},{7,15},{8,0},{9,1},... | collective-permute-start | bytes 294920 | tf_op jit(solution)/shard_map/ppermute | solution.py:450
  13.4 10.8 %collective-permute-start.2 = (bf16[8,64,256]{2,1,0:T(8,128)(2,1)S(1)}, bf16[8,64,256]{2,1,0:T(8,128)(2,1)S(1)}, u32[]{:S(2)}, u32[]{:S(2)}) collective-permute-start(bf16[8,64,256]{2,1,0:T(8,128)(2,1)S(1)} %get-tuple-element.56.field_ref), channel_id=1, source_target_pairs={{1,0},{2,1},{3,2},{4,3},{5,4},{6,5},{7,6},{8,7},{9,8},{10,9},{11,1... | collective-permute-start | bytes 786440 | tf_op jit(solution)/shard_map/ppermute | solution.py:453
  18.1 6.1 %collective-permute-start.3 = (bf16[6,32,256]{2,1,0:T(8,128)(2,1)S(1)}, bf16[6,32,256]{2,1,0:T(8,128)(2,1)S(1)}, u32[]{:S(2)}, u32[]{:S(2)}) collective-permute-start(bf16[6,32,256]{2,1,0:T(8,128)(2,1)S(1)} %pad_maximum_fusion.4), channel_id=1, source_target_pairs={{0,4},{1,5},{2,6},{3,7},{4,0},{5,1},{6,2},{7,3},{8,12},{9,13},{10,... | collective-permute-start | bytes 294920 | tf_op jit(solution)/shard_map/ppermute | solution.py:450
  21.2 3.2 %collective-permute-start.5 = (bf16[8,32,256]{2,1,0:T(8,128)(2,1)S(1)}, bf16[8,32,256]{2,1,0:T(8,128)(2,1)S(1)}, u32[]{:S(2)}, u32[]{:S(2)}) collective-permute-start(bf16[8,32,256]{2,1,0:T(8,128)(2,1)S(1)} %get-tuple-element.67), channel_id=1, source_target_pairs={{0,1},{1,2},{2,3},{3,4},{4,5},{5,6},{6,7},{7,8},{8,9},{9,10},{10,1... | collective-permute-start | bytes 393224 | tf_op jit(solution)/shard_map/ppermute | solution.py:453
  24.3 5.6 %collective-permute-start.4 = (bf16[9,32,256]{2,1,0:T(8,128)(2,1)S(1)}, bf16[9,32,256]{2,1,0:T(8,128)(2,1)S(1)}, u32[]{:S(2)}, u32[]{:S(2)}) collective-permute-start(bf16[9,32,256]{2,1,0:T(8,128)(2,1)S(1)} %constant_dynamic-update-slice_fusion), channel_id=1, source_target_pairs={{0,2},{1,3},{2,0},{3,1},{4,6},{5,7},{6,4},{7,5},{8,10},{9,11},{10,... | collective-permute-start | bytes 442376 | tf_op jit(solution)/shard_map/ppermute | solution.py:450
  29.0 15.2 %copy-start = (f32[32,2048]{1,0:T(8,128)S(1)}, f32[32,2048]{1,0:T(8,128)}, u32[]{:S(2)}) copy-start(f32[32,2048]{1,0:T(8,128)} %right_ref.5) | copy-start | bytes 786436
  31.5 1.4 %collective-permute-start.6 = (bf16[9,32,256]{2,1,0:T(8,128)(2,1)S(1)}, bf16[9,32,256]{2,1,0:T(8,128)(2,1)S(1)}, u32[]{:S(2)}, u32[]{:S(2)}) collective-permute-start(bf16[9,32,256]{2,1,0:T(8,128)(2,1)S(1)} %get-tuple-element.70), channel_id=1, source_target_pairs={{0,1},{1,0},{2,3},{3,2},{4,5},{5,4},{6,7},{7,6},{8,9},{9,8},{10,11... | collective-permute-start | bytes 442376 | tf_op jit(solution)/shard_map/ppermute | solution.py:450
  32.9 7.7 %collective-permute-start.7 = (bf16[6,32,256]{2,1,0:T(8,128)(2,1)S(1)}, bf16[6,32,256]{2,1,0:T(8,128)(2,1)S(1)}, u32[]{:S(2)}, u32[]{:S(2)}) collective-permute-start(bf16[6,32,256]{2,1,0:T(8,128)(2,1)S(1)} %pad_maximum_fusion.5), channel_id=1, source_target_pairs={{0,8},{1,9},{2,10},{3,11},{4,12},{5,13},{6,14},{7,15},{8,0},{9,1},... | collective-permute-start | bytes 294920 | tf_op jit(solution)/shard_map/ppermute | solution.py:450
  36.0 10.3 %collective-permute-start.8 = (bf16[8,64,256]{2,1,0:T(8,128)(2,1)S(1)}, bf16[8,64,256]{2,1,0:T(8,128)(2,1)S(1)}, u32[]{:S(2)}, u32[]{:S(2)}) collective-permute-start(bf16[8,64,256]{2,1,0:T(8,128)(2,1)S(1)} %get-tuple-element.76.field_ref), channel_id=1, source_target_pairs={{1,0},{2,1},{3,2},{4,3},{5,4},{6,5},{7,6},{8,7},{9,8},{10,9},{11,1... | collective-permute-start | bytes 786440 | tf_op jit(solution)/shard_map/ppermute | solution.py:453
  40.7 5.6 %collective-permute-start.9 = (bf16[6,32,256]{2,1,0:T(8,128)(2,1)S(1)}, bf16[6,32,256]{2,1,0:T(8,128)(2,1)S(1)}, u32[]{:S(2)}, u32[]{:S(2)}) collective-permute-start(bf16[6,32,256]{2,1,0:T(8,128)(2,1)S(1)} %pad_maximum_fusion.7), channel_id=1, source_target_pairs={{0,4},{1,5},{2,6},{3,7},{4,0},{5,1},{6,2},{7,3},{8,12},{9,13},{10,... | collective-permute-start | bytes 294920 | tf_op jit(solution)/shard_map/ppermute | solution.py:450
  42.9 4.0 %collective-permute-start.11 = (bf16[8,32,256]{2,1,0:T(8,128)(2,1)S(1)}, bf16[8,32,256]{2,1,0:T(8,128)(2,1)S(1)}, u32[]{:S(2)}, u32[]{:S(2)}) collective-permute-start(bf16[8,32,256]{2,1,0:T(8,128)(2,1)S(1)} %get-tuple-element.82), channel_id=1, source_target_pairs={{0,1},{1,2},{2,3},{3,4},{4,5},{5,6},{6,7},{7,8},{8,9},{9,10},{10,1... | collective-permute-start | bytes 393224 | tf_op jit(solution)/shard_map/ppermute | solution.py:453
  46.3 6.0 %collective-permute-start.10 = (bf16[9,32,256]{2,1,0:T(8,128)(2,1)S(1)}, bf16[9,32,256]{2,1,0:T(8,128)(2,1)S(1)}, u32[]{:S(2)}, u32[]{:S(2)}) collective-permute-start(bf16[9,32,256]{2,1,0:T(8,128)(2,1)S(1)} %constant_dynamic-update-slice_fusion.5), channel_id=1, source_target_pairs={{0,2},{1,3},{2,0},{3,1},{4,6},{5,7},{6,4},{7,5},{8,10},{9,11},{10,... | collective-permute-start | bytes 442376 | tf_op jit(solution)/shard_map/ppermute | solution.py:450
  53.5 1.2 %collective-permute-start.12 = (f32[64,128]{1,0:T(8,128)S(1)}, f32[64,128]{1,0:T(8,128)S(1)}, u32[]{:S(2)}, u32[]{:S(2)}) collective-permute-start(f32[64,128]{1,0:T(8,128)S(1)} %get-tuple-element.88), channel_id=1, source_target_pairs={{0,1},{1,0},{2,3},{3,2},{4,5},{5,4},{6,7},{7,6},{8,9},{9,8},{10,11... | collective-permute-start | bytes 98312 | tf_op jit(solution)/shard_map/ppermute | solution.py:450
  54.7 5.2 %collective-permute-start.13 = (f32[64,128]{1,0:T(8,128)S(1)}, f32[64,128]{1,0:T(8,128)S(1)}, u32[]{:S(2)}, u32[]{:S(2)}) collective-permute-start(f32[64,128]{1,0:T(8,128)S(1)} %add.33), channel_id=1, source_target_pairs={{0,8},{1,9},{2,10},{3,11},{4,12},{5,13},{6,14},{7,15},{8,0},{9,1},... | collective-permute-start | bytes 98312 | tf_op jit(solution)/shard_map/ppermute | solution.py:450
  59.9 4.7 %collective-permute-start.14 = (f32[64,128]{1,0:T(8,128)S(1)}, f32[64,128]{1,0:T(8,128)S(1)}, u32[]{:S(2)}, u32[]{:S(2)}) collective-permute-start(f32[64,128]{1,0:T(8,128)S(1)} %add.34), channel_id=1, source_target_pairs={{0,4},{1,5},{2,6},{3,7},{4,0},{5,1},{6,2},{7,3},{8,12},{9,13},{10,... | collective-permute-start | bytes 98312 | tf_op jit(solution)/shard_map/ppermute | solution.py:450
  64.7 3.9 %collective-permute-start.15 = (f32[64,128]{1,0:T(8,128)S(1)}, f32[64,128]{1,0:T(8,128)S(1)}, u32[]{:S(2)}, u32[]{:S(2)}) collective-permute-start(f32[64,128]{1,0:T(8,128)S(1)} %add.35.kept_ref), channel_id=1, source_target_pairs={{0,2},{1,3},{2,0},{3,1},{4,6},{5,7},{6,4},{7,5},{8,10},{9,11},{10,... | collective-permute-start | bytes 98312 | tf_op jit(solution)/shard_map/ppermute | solution.py:450

commit v4 on v3

--- a/solution.py
+++ b/solution.py
@@ -10,7 +10,7 @@
 PANEL = 256
 R = 32
 K = 32
-GROUP = 8
+GROUP = 32
 highest = lax.Precision.HIGHEST
 VMEM = pltpu.VMEM
 SMEM = pltpu.SMEM
@@ -24,7 +24,7 @@
     return pl.BlockSpec(memory_space=space)
 
 
-def call(kernel, outs, ins, spaces, scratch=(), limit=40, flops=10**8, moved=10**6, placed=None):
+def call(kernel, outs, ins, spaces, scratch=(), limit=24, flops=10**8, moved=10**6, placed=None):
     return pl.pallas_call(
         kernel,
         out_shape=outs,
@@ -79,32 +79,52 @@
     return dot(jnp.concatenate(spread, axis=0), basis)
 
 
+def rounds(devices):
+    bits = devices.bit_length() - 1
+    return [1] + [(1 << b) | 1 for b in range(bits - 1, 0, -1)]
+
+
 def places(devices):
-    bits = devices.bit_length() - 1
-    order = [0] + list(range(bits - 1, 0, -1))
-    place = [sum(((d >> b) & 1) << (bits - 1 - t) for t, b in enumerate(order)) for d in range(devices)]
-    return order, place
-
-
-def couple(order, me, pairs_ref, slots_ref, wide_ref, out_ref):
+    steps = rounds(devices)
+    place = [0] * devices
+    for p in range(devices):
+        apart = 0
+        for t, step in enumerate(steps):
+            if (p >> (len(steps) - 1 - t)) & 1:
+                apart ^= step
+        place[apart] = p
+    return place
+
+
+def couple(me, pairs_ref, slots_ref, table_ref, wide_ref, out_ref):
     clusters = out_ref.shape[2] // K
-    pairs = wide_ref.shape[0] // K
+    devices = out_ref.shape[0] // 2
+    pairs = pairs_ref.shape[1]
     group = lane_group((K, clusters * K))
+    shift = clusters.bit_length() - 1
+    assert clusters == 1 << shift
+    steps = rounds(devices)
+    for home in range(devices):
+        apart = home ^ me
+        parity = apart
+        for b in range(1, len(steps)):
+            parity = parity ^ (apart >> b)
+        place = (parity & 1) << (len(steps) - 1)
+        for t, step in enumerate(steps[1:], 1):
+            bit = step.bit_length() - 1
+            place = place + (((apart >> bit) & 1) << (len(steps) - 1 - t))
+        table_ref[home] = place
 
     def one(f):
         first = slots_ref[pairs_ref[0, f]]
         second = slots_ref[pairs_ref[1, f]]
-        first_home, second_home = first // clusters, second // clusters
-        own = (first_home == me).astype(jnp.int32)
-        apart = (first_home + second_home - me) ^ me
-        place = jnp.int32(0)
-        for t, b in enumerate(order):
-            place = place + (((apart >> b) & 1) << (len(order) - 1 - t))
+        first_home, second_home = first >> shift, second >> shift
+        own = first_home == me
+        where = jnp.where(own, devices, 0) + table_ref[jnp.where(own, second_home, first_home)]
         block = wide_ref[pl.ds(f, K, stride=pairs), :]
         block = jnp.concatenate([block] * (clusters * K // block.shape[1]), axis=1)
-        block = jnp.where(group == second % clusters, block, 0.0).astype(bf16)
-        here = pl.ds(pl.multiple_of((first % clusters) * K, K), K)
-        where = own * (1 << len(order)) + place
+        block = jnp.where(group == (second & (clusters - 1)), block, 0.0).astype(bf16)
+        here = pl.ds(pl.multiple_of((first & (clusters - 1)) * K, K), K)
         out_ref[where, here, :] = out_ref[where, here, :] + block
 
     def some(step, carry):
@@ -115,9 +135,9 @@
     lax.fori_loop(0, pairs // 8, some, 0)
 
 
-def open_kernel(order, me_ref, pairs_hbm, slots_hbm, coupling_hbm, right_hbm, basis_hbm, near_hbm, blocks_hbm,
-                near_pairs_ref, blocks_ref, field_ref, near_proj_ref, cross_ref, coupled_ref, payload_ref, kept_ref,
-                pairs_ref, slots_ref, coupling_ref, right_ref, basis_ref, wide_ref, sems):
+def open_kernel(me_ref, pairs_hbm, slots_hbm, coupling_hbm, right_hbm, basis_hbm, near_hbm, blocks_hbm,
+                near_pairs_ref, blocks_ref, field_ref, near_proj_ref, coupled_ref, payload_ref,
+                pairs_ref, slots_ref, table_ref, coupling_ref, right_ref, basis_ref, wide_ref, sems):
     clusters = field_ref.shape[0]
     moves = [(coupling_hbm, coupling_ref), (basis_hbm, basis_ref), (right_hbm, right_ref),
              (pairs_hbm, pairs_ref), (slots_hbm, slots_ref), (near_hbm, near_pairs_ref), (blocks_hbm, blocks_ref)]
@@ -142,12 +162,6 @@
             wide_ref[(t * each + u) * pairs : (t * each + u + 1) * pairs] = value[t * pairs : (t + 1) * pairs]
     copies[1].wait()
     basis = basis_ref[...]
-    cross = dot_nt(basis, basis)
-    same = lane_group(cross.shape) == lax.broadcasted_iota(jnp.int32, cross.shape, 0) // K
-    cross = jnp.where(same, cross, 0.0)
-    high = cross.astype(bf16)
-    cross_ref[0] = high
-    cross_ref[1] = (cross - high.astype(f32)).astype(bf16)
     copies[2].wait()
     for c in range(clusters):
         field_ref[c] = split_rows(right_ref[:, c * PANEL : (c + 1) * PANEL])
@@ -156,105 +170,109 @@
     copies[3].wait()
     copies[4].wait()
     copies[5].wait()
-    couple(order, me_ref[0], pairs_ref, slots_ref, wide_ref, coupled_ref)
+    couple(me_ref[0], pairs_ref, slots_ref, table_ref, wide_ref, coupled_ref)
     proj = proj.astype(bf16)
     devices = coupled_ref.shape[0] // 2
-    send(lambda d: dot(proj, coupled_ref[devices + d]) + dot_nt(proj, coupled_ref[d]), payload_ref, kept_ref, proj)
+    send(
+        lambda d: dot(proj, coupled_ref[devices + d]) + dot_nt(proj, coupled_ref[d]),
+        payload_ref, proj, devices, True,
+    )
     copies[6].wait()
 
 
-def send(products, payload_ref, kept_ref, proj):
-    half = kept_ref.shape[0]
+def send(products, payload_ref, proj, devices, both):
     payload_ref[0] = proj
-    for d in range(2 * half):
-        if d < half:
-            kept_ref[d] = products(d)
-        else:
-            payload_ref[1 + d - half] = products(d).astype(bf16)
-
-
-def near_specs(nb, group):
-    return pl.BlockSpec((group, PANEL, PANEL), lambda g, pairs, count: (jnp.minimum(g, (count[0] - 1) // group), 0, 0))
-
-
-def whole(shape):
-    return pl.BlockSpec(shape, lambda g, pairs, count: (0,) * len(shape))
+    half = devices // 2
+    for d in range(half, devices):
+        value = products(d)
+        high = value.astype(bf16)
+        payload_ref[1 + d - half] = high
+        if both:
+            payload_ref[1 + d] = (value - high.astype(f32)).astype(bf16)
+
+
+def keep_one_kernel(coupled_ref, payload_ref, basis_ref, right_ref, kept_ref, cross_ref, corner_ref):
+    devices = coupled_ref.shape[0] // 2
+    proj = payload_ref[0]
+    for d in range(devices // 2):
+        kept_ref[d] = dot(proj, coupled_ref[devices + d]) + dot_nt(proj, coupled_ref[d])
+    basis = basis_ref[...]
+    cross = dot_nt(basis, basis)
+    same = lane_group(cross.shape) == lax.broadcasted_iota(jnp.int32, cross.shape, 0) // K
+    cross = jnp.where(same, cross, 0.0)
+    high = cross.astype(bf16)
+    cross_ref[0] = high
+    cross_ref[1] = (cross - high.astype(f32)).astype(bf16)
+    corner = jnp.zeros((R, 4 * R), f32)
+    zero = jnp.zeros((R, PANEL), f32)
+    for c in range(right_ref.shape[1] // PANEL):
+        right = right_ref[:, c * PANEL : (c + 1) * PANEL]
+        corner = corner + exact_nt(right, jnp.concatenate([zero, zero, right, zero], axis=0))
+    corner_ref[...] = corner
+
+
+def keep_two_kernel(turned_ref, payload_ref, kept_ref):
+    proj = payload_ref[0]
+    for d in range(kept_ref.shape[0]):
+        kept_ref[d] = dot(proj, turned_ref[d])
+
+
+def near_loop(count_ref, one):
+    def group(g, carry):
+        for u in range(GROUP):
+            one(g * GROUP + u)
+        return carry
+
+    lax.fori_loop(0, (count_ref[0] + GROUP - 1) // GROUP, group, 0)
 
 
 def near_cols_kernel(pairs_ref, count_ref, blocks_ref, field_ref, own_ref, next_ref, total):
-    g = pl.program_id(0)
     clusters = field_ref.shape[0]
-
-    @pl.when(g == 0)
-    def _():
-        total[...] = jnp.zeros_like(total)
-
-    @pl.when(g * GROUP < count_ref[0])
-    def _():
-        for u in range(GROUP):
-            s = g * GROUP + u
-            i = pairs_ref[0, s]
-            j = jnp.where(s < count_ref[0], pairs_ref[1, s], 2 * clusters)
-            total[j] = total[j] + join_rows(dot(field_ref[i], blocks_ref[u]))
-
-    @pl.when(g == pl.num_programs(0) - 1)
-    def _():
-        own_ref[...] = total[:clusters]
-        next_ref[...] = total[clusters : 2 * clusters].astype(bf16)
+    total[...] = jnp.zeros_like(total)
+
+    def one(s):
+        i = pairs_ref[0, s]
+        j = jnp.where(s < count_ref[0], pairs_ref[1, s], 2 * clusters)
+        total[j] = total[j] + join_rows(dot(field_ref[i], blocks_ref[s]))
+
+    near_loop(count_ref, one)
+    own_ref[...] = total[:clusters]
+    next_ref[...] = total[clusters : 2 * clusters].astype(bf16)
 
 
 def near_rows_kernel(pairs_ref, count_ref, blocks_ref, field_ref, after_ref, begun_ref, back_ref, basis_ref,
                      out_ref, proj_ref, window, total):
-    g = pl.program_id(0)
     clusters = field_ref.shape[0]
-
-    @pl.when(g == 0)
-    def _():
-        window[:clusters] = field_ref[...]
-        window[clusters:] = after_ref[...]
-        total[:clusters] = begun_ref[...] + back_ref[...].astype(f32)
-
-    @pl.when(g * GROUP < count_ref[0])
-    def _():
-        for u in range(GROUP):
-            s = g * GROUP + u
-            i = jnp.where(s < count_ref[0], pairs_ref[0, s], clusters)
-            j = pairs_ref[1, s]
-            total[i] = total[i] + join_rows(dot_nt(window[j], blocks_ref[u]))
-
-    @pl.when(g == pl.num_programs(0) - 1)
-    def _():
-        near = total[:clusters]
-        out_ref[...] = near
-        split = jnp.concatenate([split_rows(near[c]) for c in range(clusters)], axis=0)
-        proj_ref[...] = project(split, basis_ref[...])
-
-
-def near_call(kernel, outs, near_pairs, near_count, near_blocks, arrays, scratch):
-    nb = near_blocks.shape[0]
-    return pl.pallas_call(
-        kernel,
-        out_shape=outs,
-        grid_spec=pltpu.PrefetchScalarGridSpec(
-            num_scalar_prefetch=2,
-            grid=(nb // GROUP,),
-            in_specs=[near_specs(nb, GROUP)] + [whole(a.shape) for a in arrays],
-            out_specs=jax.tree.map(lambda o: whole(o.shape), outs),
-            scratch_shapes=scratch,
-        ),
-        compiler_params=pltpu.CompilerParams(
-            vmem_limit_bytes=24 << 20, dimension_semantics=("arbitrary",)
-        ),
-        cost_estimate=pl.CostEstimate(
-            flops=nb * 64 * PANEL * PANEL * 2, bytes_accessed=nb * PANEL * PANEL * 2, transcendentals=0
-        ),
-    )(near_pairs, near_count, near_blocks, *arrays)
-
-
-def merge_kernel(coupled_ref, out_ref):
+    window[:clusters] = field_ref[...]
+    window[clusters:] = after_ref[...]
+    total[:clusters] = begun_ref[...] + back_ref[...].astype(f32)
+    total[clusters] = jnp.zeros_like(total[clusters])
+
+    def one(s):
+        i = jnp.where(s < count_ref[0], pairs_ref[0, s], clusters)
+        j = pairs_ref[1, s]
+        total[i] = total[i] + join_rows(dot_nt(window[j], blocks_ref[s]))
+
+    near_loop(count_ref, one)
+    near = total[:clusters]
+    out_ref[...] = near
+    split = jnp.concatenate([split_rows(near[c]) for c in range(clusters)], axis=0)
+    proj_ref[...] = project(split, basis_ref[...])
+
+
+def rows_two_kernel(pairs_ref, count_ref, blocks_ref, field_ref, after_ref, begun_ref, back_ref, basis_ref,
+                    right_ref, image_ref, out_ref, proj_ref, gram_ref, window, total):
+    near_rows_kernel(pairs_ref, count_ref, blocks_ref, field_ref, after_ref, begun_ref, back_ref, basis_ref,
+                     out_ref, proj_ref, window, total)
+    gram_two(right_ref, image_ref, out_ref, gram_ref)
+
+
+def merge_kernel(coupled_ref, out_ref, turned_ref):
     devices = out_ref.shape[0]
     for d in range(devices):
-        out_ref[d] = coupled_ref[d] + coupled_ref[devices + d].T
+        near, away = coupled_ref[d], coupled_ref[devices + d]
+        out_ref[d] = near + away.T
+        turned_ref[d] = away + near.T
 
 
 def far_sums(place, merged_ref, low_ref, high_ref, kept_ref, got_ref):
@@ -262,10 +280,10 @@
     sums = kept_ref[0]
     for piece in range(got_ref.shape[0]):
         sums = sums + got_ref[piece].astype(f32)
-    order = places(devices)[0]
+    steps = rounds(devices)
     for g in range(devices):
         proj = low_ref[g] if g < devices // 2 else high_ref[g - devices // 2]
-        apart = sum(((g >> t) & 1) << b for t, b in enumerate(order))
+        apart = functools.reduce(lambda x, y: x ^ y, [step for t, step in enumerate(steps) if (g >> t) & 1], 0)
         sums = sums + dot(proj, merged_ref[place[apart]])
     return split_rows(sums)
 
@@ -275,13 +293,13 @@
 
 
 def turn_kernel(place, merged_ref, low_ref, high_ref, kept_ref, got_ref, near_proj_ref, cross_ref,
-                sums_ref, proj_ref, payload_ref, next_ref):
+                turned_ref, sums_ref, proj_ref, payload_ref):
     sums = far_sums(place, merged_ref, low_ref, high_ref, kept_ref, got_ref)
     sums_ref[...] = sums
     proj = near_proj_ref[...] + across_clusters(sums, cross_ref)
     proj_ref[...] = proj
     proj = proj.astype(bf16)
-    send(lambda d: dot_nt(proj, merged_ref[d]), payload_ref, next_ref, proj)
+    send(lambda d: dot(proj, turned_ref[d]), payload_ref, proj, turned_ref.shape[0], False)
 
 
 def image_kernel(near_ref, sums_ref, basis_ref, image_ref, field_ref):
@@ -298,18 +316,16 @@
         image_ref[c] = near_ref[c] + join_rows(far[c * 2 * R : (c + 1) * 2 * R])
 
 
-def gram_one_kernel(right_ref, image_ref, gram_ref):
-    gram = jnp.zeros((R, 4 * R), f32)
-    corner = jnp.zeros((R, 4 * R), f32)
+def gram_one_kernel(corner_ref, right_ref, image_ref, gram_ref):
+    gram = corner_ref[...]
     zero = jnp.zeros((R, PANEL), f32)
     for c in range(image_ref.shape[0]):
         right, image = right_ref[:, c * PANEL : (c + 1) * PANEL], image_ref[c]
         gram = gram + exact_nt(image, jnp.concatenate([right, image, zero, zero], axis=0))
-        corner = corner + exact_nt(right, jnp.concatenate([zero, zero, right, zero], axis=0))
-    gram_ref[...] = gram + corner
-
-
-def gram_two_kernel(right_ref, image_ref, near_ref, gram_ref):
+    gram_ref[...] = gram
+
+
+def gram_two(right_ref, image_ref, near_ref, gram_ref):
     gram = jnp.zeros((R, 4 * R), f32)
     zero = jnp.zeros((R, PANEL), f32)
     for c in range(image_ref.shape[0]):
@@ -325,10 +341,14 @@
     half = near_proj_ref[...] + 0.5 * across_clusters(sums, cross_ref)
     sums = join_rows(sums.astype(f32))
     known = jnp.concatenate([right_proj_ref[...], image_proj_ref[...], half, jnp.zeros_like(half)], axis=0)
-    out_ref[:R] = early_ref[...]
     added = exact_nt(sums, known)
     mirror = exact_nt(half, jnp.concatenate([jnp.zeros_like(sums)] * 2 + [sums, jnp.zeros_like(sums)], axis=0))
-    out_ref[R:] = gram_ref[...] + added + mirror
+    late = gram_ref[...] + added + mirror
+    lanes = lane_group(late.shape)
+    out_ref[:R] = jnp.where(lanes == 3, pltpu.roll(late, 3 * R, 1), early_ref[...])
+    rest = pltpu.roll(late, 3 * R, 1)
+    half_rows = R // 2
+    out_ref[R:] = jnp.where(lanes[:half_rows] < 2, rest[:half_rows], pltpu.roll(rest[half_rows:], 2 * R, 1))
 
 
 TALL = 8
@@ -374,13 +394,14 @@
 def last_kernel(kept_ref, got_ref, right_ref, image_ref, second_ref, field_ref, residual_ref, hessenberg_ref):
     clusters = image_ref.shape[0]
     gram = kept_ref[...] + got_ref[...]
-    top, bottom = gram[:R], gram[R:]
+    top, folded = gram[:R], gram[R:]
+    bottom = jnp.concatenate([folded[:, : 2 * R], folded[:, 2 * R :]], axis=0)
     lanes = lax.broadcasted_iota(jnp.int32, (2 * R, 4 * R), 1)
     rows = lax.broadcasted_iota(jnp.int32, (2 * R, 4 * R), 0)
     wide = jnp.zeros((R, R), f32)
     first_first, image_first = top[:, 2 * R : 3 * R], top[:, :R]
-    image_image, second_first, second_image = top[:, R : 2 * R], bottom[:, :R], bottom[:, R : 2 * R]
-    second_second = bottom[:, 2 * R : 3 * R]
+    image_image, second_first = top[:, R : 2 * R], top[:, 3 * R :]
+    second_image, second_second = bottom[:, :R], bottom[:, R:]
     system = jnp.concatenate(
         [
             jnp.concatenate([image_image, second_image.T, image_first, wide], axis=1),
@@ -440,14 +461,14 @@
 
 def body(right_side, near_pairs, near_count, near_blocks, far_pairs, coupling, cluster_basis, cluster_slot):
     devices = lax.axis_size("leaf")
-    order, place = places(devices)
+    order, place = rounds(devices), places(devices)
     clusters = cluster_basis.shape[0]
     me = lax.axis_index("leaf").astype(jnp.int32).reshape(1)
     basis = cluster_basis.reshape(clusters * K, PANEL)
     sds = jax.ShapeDtypeStruct
 
     def across(x, b):
-        return lax.ppermute(x, "leaf", [(i, i ^ (1 << b)) for i in range(devices)])
+        return lax.ppermute(x, "leaf", [(i, i ^ b) for i in range(devices)])
 
     def shift(x, by):
         return lax.ppermute(x, "leaf", [(i, i + by) for i in range(devices) if 0 <= i + by < devices])
@@ -458,33 +479,38 @@
     rank_wide = sds((R, clusters * K), f32)
     rank_split = sds((2 * R, clusters * K), bf16)
     half = devices // 2
+    merged_out = sds((devices, clusters * K, clusters * K), bf16)
     payload_out = sds((1 + half, R, clusters * K), bf16)
     kept_out = sds((half, R, clusters * K), f32)
     barrier = lax.optimization_barrier
+    near_spaces = [SMEM, SMEM, VMEM, VMEM]
 
     def in_hbm(x):
         return pltpu.with_memory_space_constraint(x, pltpu.HBM)
 
-    near_pairs, near_blocks, field, right_proj, cross, coupled, payload, sums = call(
-        functools.partial(open_kernel, order),
-        (sds(near_pairs.shape, jnp.int32), sds(near_blocks.shape, bf16), split, rank_wide, sds((2, clusters * K, clusters * K), bf16),
-         sds((2 * devices, clusters * K, clusters * K), bf16), payload_out, kept_out),
+    near_pairs, near_blocks, field, right_proj, coupled, payload = call(
+        open_kernel,
+        (sds(near_pairs.shape, jnp.int32), sds(near_blocks.shape, bf16), split, rank_wide,
+         sds((2 * devices, clusters * K, clusters * K), bf16),
+         sds((1 + devices, R, clusters * K), bf16)),
         (me, in_hbm(far_pairs), in_hbm(cluster_slot), in_hbm(coupling), in_hbm(right_side), in_hbm(basis),
          in_hbm(near_pairs), in_hbm(near_blocks)),
         [SMEM] + [pltpu.HBM] * 7,
         [
             pltpu.SMEM(far_pairs.shape, jnp.int32),
             pltpu.SMEM(cluster_slot.shape, jnp.int32),
+            pltpu.SMEM((devices,), jnp.int32),
             pltpu.VMEM(coupling.shape, bf16),
             pltpu.VMEM(right_side.shape, f32),
             pltpu.VMEM(basis.shape, bf16),
-            pltpu.VMEM((coupling.shape[0] * K, 128), f32),
+            pltpu.VMEM((coupling.shape[0] * (K + 1), 128), f32),
             pltpu.SemaphoreType.DMA((7,)),
         ],
-        placed=[SMEM] + [VMEM] * 7,
-    )
-
-    def exchange(make_field, payload, sums, merged):
+        placed=[SMEM] + [VMEM] * 5,
+    )
+
+    def exchange(make_field, beside, keep, payload, merged=None):
+        first = merged is None
         for t, b in enumerate(order):
             if t > 0:
                 held, half = gathered.shape[0], sums.shape[0] // 2
@@ -494,54 +520,74 @@
                 gathered, held = payload[:1], 1
             if t == 2:
                 payload, own = barrier((payload, own))
-            if t == 3 and merged is None:
-                payload, merged = barrier((payload, made))
+            if t == 3:
+                payload, made = barrier((payload, made))
             got = across(payload, b)
             if t == 0:
+                sums, cross, corner = keep(payload)
                 image, field, got = make_field(got)
                 after = shift(field, -1)
-                own, following = near_call(
-                    near_cols_kernel, (panels, narrow), near_pairs, near_count, near_blocks, (field,),
-                    [pltpu.VMEM((2 * clusters + 1, R, PANEL), f32)],
+                own, following = call(
+                    near_cols_kernel, (panels, narrow), (near_pairs, near_count, near_blocks, field), near_spaces,
+                    [pltpu.VMEM((2 * clusters + 1, R, PANEL), f32)], moved=12 << 20,
                 )
                 back = shift(following, 1)
-            if t == 1 and merged is None:
-                ready, got = barrier((coupled, got))
-                made = call(
-                    merge_kernel, sds((devices, clusters * K, clusters * K), bf16), (ready,), [VMEM]
-                )
+            if t == 1:
+                made, got = beside(image, corner, got)
             if t == len(order) - 2:
                 after, got = barrier((after, got))
             got_gathered, got_sums = got[:held], got[held:]
             if t < len(order) - 1:
                 gathered = jnp.concatenate([gathered, got_gathered], axis=0)
-                sums = sums + got_sums.astype(f32)
-        near, near_proj = near_call(
-            near_rows_kernel, (panels, rank_wide), near_pairs, near_count, near_blocks,
-            (field, after, own, back, basis),
+                for piece in range(0, got_sums.shape[0], sums.shape[0]):
+                    sums = sums + got_sums[piece : piece + sums.shape[0]].astype(f32)
+        kernel, ins, outs = near_rows_kernel, (near_blocks, field, after, own, back, basis), (panels, rank_wide)
+        if not first:
+            kernel, ins, outs = rows_two_kernel, ins + (right_side, image), outs + (sds((R, 4 * R), f32),)
+        near, near_proj, *gram = call(
+            kernel, outs, (near_pairs, near_count) + ins, [SMEM] * 2 + [VMEM] * len(ins),
             [pltpu.VMEM((2 * clusters, 2 * R, PANEL), bf16), pltpu.VMEM((clusters + 1, R, PANEL), f32)],
+            moved=12 << 20,
         )
-        return image, near, (merged, gathered, got_gathered, sums, got_sums, near_proj, cross)
+        merged = made if first else merged
+        return image, near, made, gram, cross, corner, (merged[0], gathered, got_gathered, sums, got_sums, near_proj, cross)
 
     def first_field(got):
         ready, got = barrier((field, got))
         return right_side, ready, got
 
-    unused, near, parts = exchange(first_field, payload, sums, None)
-    far, image_proj, payload, sums = call(
-        functools.partial(turn_kernel, place), (rank_split, rank_wide, payload_out, kept_out), parts, [VMEM] * 7
+    def keep_one(payload):
+        return call(
+            keep_one_kernel, (kept_out, sds((2, clusters * K, clusters * K), bf16), sds((R, 4 * R), f32)),
+            (coupled, payload, basis, right_side), [VMEM] * 4,
+        )
+
+    def merging(image, corner, got):
+        ready, got = barrier((coupled, got))
+        return call(merge_kernel, (merged_out, merged_out), (ready,), [VMEM]), got
+
+    def multiplying(image, corner, got):
+        ready, got = barrier((image, got))
+        return call(gram_one_kernel, sds((R, 4 * R), f32), (corner, right_side, ready), [VMEM] * 3), got
+
+    unused, near, merged, unused, cross, corner, parts = exchange(first_field, merging, keep_one, payload)
+    far, image_proj, payload = call(
+        functools.partial(turn_kernel, place), (rank_split, rank_wide, payload_out), parts + (merged[1],), [VMEM] * 8
     )
 
     def second_field(got):
         ready, got = barrier((far, got))
         return *call(image_kernel, (panels, split), (near, ready, basis), [VMEM] * 3), got
 
-    image, near_two, parts = exchange(second_field, payload, sums, parts[0])
-    early = call(gram_one_kernel, sds((R, 4 * R), f32), (right_side, image), [VMEM] * 2)
-    gram = call(gram_two_kernel, sds((R, 4 * R), f32), (right_side, image, near_two), [VMEM] * 3)
+    def keep_two(payload):
+        return call(keep_two_kernel, kept_out, (merged[1], payload), [VMEM] * 2), cross, corner
+
+    image, near_two, early, gram, unused, unused, parts = exchange(
+        second_field, multiplying, keep_two, payload, merged
+    )
     far, gram = call(
-        functools.partial(tail_kernel, place), (rank_split, sds((2 * R, 4 * R), f32)),
-        parts + (right_proj, image_proj, early, gram), [VMEM] * 11,
+        functools.partial(tail_kernel, place), (rank_split, sds((R + R // 2, 4 * R), f32)),
+        parts + (right_proj, image_proj, early, *gram), [VMEM] * 11,
     )
     got = None
     for t, b in enumerate(order):

time: 73.1 us -> 68.2 us (0.933); the launches traced: 72.9 us -> 67.2 us
  Pallas kernels: 32.3 us -> 28.2 us
  waiting for transfers between devices: 13.4 us -> 12.1 us
    pallas_call x4 -> x0, Pallas kernels: 15.9 us -> none  [near_call(): pl.pallas_call(kernel, out_shape=outs, grid_spec=pltpu.PrefetchScalarGrid...]
    pallas_call x9 -> x14, Pallas kernels: 16.4 us -> 28.2 us  [call(): pl.pallas_call(kernel, out_shape=outs, in_specs=[spec(s) for s in spaces]...]
    ppermute x12, starting transfers between devices: 20 us -> 16.5 us  [across(): return lax.ppermute(x, 'leaf', [(i, i ^ b) for i in range(devices)])]
    ppermute x4, starting transfers between devices: 5.15 us -> 8.35 us  [shift(): lax.ppermute(x, 'leaf', [(i, i + by) for i in range(devices) if 0 <= i +...]
    ppermute x12, waiting for transfers between devices: 13.4 us -> 12.1 us  [across(): return lax.ppermute(x, 'leaf', [(i, i ^ b) for i in range(devices)])]
  transfers between devices with their start and end apart: 16 -> 16, of which waited for: 9 -> 10; matrix products, arithmetic and copies ran while one was open for 0% -> 0% of each run, Pallas kernels for 26% -> 25%
where the time goes in v4:
time: 68.2 us; the launch traced here: 67.2 us
  Pallas kernels  28.2 us (41%)
  starting transfers between devices  24.9 us (37%)
  waiting for transfers between devices  12.1 us (18%)
  between operations  1.65 us (2%)
    pallas_call x14, Pallas kernels, call(): pl.pallas_call(kernel, out_shape=outs, in_specs=[spec(s) for s in spaces]...  28.2 us
    ppermute x12, starting transfers between devices, across(): return lax.ppermute(x, 'leaf', [(i, i ^ b) for i in range(devices)])  16.5 us
    ppermute x12, waiting for transfers between devices, across(): return lax.ppermute(x, 'leaf', [(i, i ^ b) for i in range(devices)])  12.1 us
    ppermute x4, starting transfers between devices, shift(): lax.ppermute(x, 'leaf', [(i, i + by) for i in range(devices) if 0 <= i +...  8.35 us
  transfers between devices with their start and end apart: 16, of which 10 were waited for; matrix products, arithmetic and copies ran while one was open for 0% of the time, Pallas kernels for 25%

profile of v4, /device:TPU:0, one launch (start us, length us, event | category | flops | bytes accessed | tf_op | source)
XLA Modules:
  0.0 67.2 jit_solution(6525852584142460916)
XLA Ops:
  0.7 5.0 %shard_map.103 = (s32[2,64]{1,0:T(2,128)S(1)}, bf16[64,256,256]{2,1,0:T(8,128)(2,1)S(1)}, bf16[8,64,256]{2,1,0:T(8,128)(2,1)S(1)}, f32[32,256]{1,0:T(8,128)S(1)}...) custom-call(s32[1]{0:T(128)} %bitcast.me_ref, s32[2,128]{1,0:T(2,128)} %pairs_hbm.1, s32[128]{0:T(128)} %slots_hbm.1, ...), custom_call_target="tpu_custom_call" | custom-call | flops 100000000 | bytes 1000000 | tf_op jit(solution)/shard_map/pallas_call | solution.py:28
  6.2 1.2 %shard_map.104 = (f32[8,32,256]{2,1,0:T(8,128)S(1)}, bf16[2,256,256]{2,1,0:T(8,128)(2,1)S(1)}, f32[32,128]{1,0:T(8,128)S(1)}) custom-call(bf16[32,256,256]{2,1,0:T(8,128)(2,1)S(1)} %get-tuple-element.70.coupled_ref, bf16[17,32,256]{2,1,0:T(8,128)(2,1)S(1)} %get-tuple-element.58.payload_ref, bf16[256,256]{1,0:T(8,128)(2,1)S(1)} %bitcast.4, f32[32,2048]{1,0:T(8,128)S(1)} %copy-done), custom_call_target="tpu_custom_call" | custom-call | flops 100000000 | bytes 1000000 | tf_op jit(solution)/shard_map/pallas_call | solution.py:28
  7.5 3.8 %collective-permute-start.1 = (bf16[6,32,256]{2,1,0:T(8,128)(2,1)S(1)}, bf16[6,32,256]{2,1,0:T(8,128)(2,1)S(1)}, u32[]{:S(2)}, u32[]{:S(2)}) collective-permute-start(bf16[6,32,256]{2,1,0:T(8,128)(2,1)S(1)} %pad_maximum_fusion.2), channel_id=1, source_target_pairs={{0,9},{1,8},{2,11},{3,10},{4,13},{5,12},{6,15},{7,14},{8,1},{9,0},... | collective-permute-start | bytes 294920 | tf_op jit(solution)/shard_map/ppermute | solution.py:471
  12.0 1.3 %collective-permute-start.2 = (bf16[8,64,256]{2,1,0:T(8,128)(2,1)S(1)}, bf16[8,64,256]{2,1,0:T(8,128)(2,1)S(1)}, u32[]{:S(2)}, u32[]{:S(2)}) collective-permute-start(bf16[8,64,256]{2,1,0:T(8,128)(2,1)S(1)} %get-tuple-element.64.field_ref), channel_id=1, source_target_pairs={{1,0},{2,1},{3,2},{4,3},{5,4},{6,5},{7,6},{8,7},{9,8},{10,9},{11,1... | collective-permute-start | bytes 786440 | tf_op jit(solution)/shard_map/ppermute | solution.py:474
  13.3 2.4 %shard_map.105 = (f32[8,32,256]{2,1,0:T(8,128)S(1)}, bf16[8,32,256]{2,1,0:T(8,128)(2,1)S(1)}) custom-call(s32[2,64]{1,0:T(2,128)S(1)} %get-tuple-element.65.pairs_ref, s32[1]{0:T(128)S(6)} %copy.19.count_ref, bf16[64,256,256]{2,1,0:T(8,128)(2,1)S(1)} %get-tuple-element.66.blocks_ref, bf16[8,64,256]{2,1,0:T(8,128)(2,1)S(1)} %get-tuple-element.64.field_ref), custom_call_target="tpu_custom_call" | custom-call | flops 100000000 | bytes 12582912 | tf_op jit(solution)/shard_map/pallas_call | solution.py:28
  15.7 0.7 %collective-permute-done.1 = bf16[6,32,256]{2,1,0:T(8,128)(2,1)S(1)} collective-permute-done((bf16[6,32,256]{2,1,0:T(8,128)(2,1)S(1)}, bf16[6,32,256]{2,1,0:T(8,128)(2,1)S(1)}, u32[]{:S(2)}, u32[]{:S(2)}) %collective-permute-start.1) | collective-permute-done | bytes 98336 | tf_op jit(solution)/shard_map/ppermute | solution.py:471
  16.4 1.1 %collective-permute-start.3 = (bf16[6,32,256]{2,1,0:T(8,128)(2,1)S(1)}, bf16[6,32,256]{2,1,0:T(8,128)(2,1)S(1)}, u32[]{:S(2)}, u32[]{:S(2)}) collective-permute-start(bf16[6,32,256]{2,1,0:T(8,128)(2,1)S(1)} %pad_maximum_fusion.4), channel_id=1, source_target_pairs={{0,5},{1,4},{2,7},{3,6},{4,1},{5,0},{6,3},{7,2},{8,13},{9,12},{10,... | collective-permute-start | bytes 294920 | tf_op jit(solution)/shard_map/ppermute | solution.py:471
  17.5 3.0 %collective-permute-start.5 = (bf16[8,32,256]{2,1,0:T(8,128)(2,1)S(1)}, bf16[8,32,256]{2,1,0:T(8,128)(2,1)S(1)}, u32[]{:S(2)}, u32[]{:S(2)}) collective-permute-start(bf16[8,32,256]{2,1,0:T(8,128)(2,1)S(1)} %get-tuple-element.77), channel_id=1, source_target_pairs={{0,1},{1,2},{2,3},{3,4},{4,5},{5,6},{6,7},{7,8},{8,9},{9,10},{10,1... | collective-permute-start | bytes 393224 | tf_op jit(solution)/shard_map/ppermute | solution.py:474
  20.5 1.1 %shard_map.106 = (bf16[16,256,256]{2,1,0:T(8,128)(2,1)S(1)}, bf16[16,256,256]{2,1,0:T(8,128)(2,1)S(1)}) custom-call(bf16[32,256,256]{2,1,0:T(8,128)(2,1)S(1)} %get-tuple-element.70.coupled_ref), custom_call_target="tpu_custom_call" | custom-call | flops 100000000 | bytes 1000000 | tf_op jit(solution)/shard_map/pallas_call | solution.py:28
  21.7 1.5 %collective-permute-start.4 = (bf16[9,32,256]{2,1,0:T(8,128)(2,1)S(1)}, bf16[9,32,256]{2,1,0:T(8,128)(2,1)S(1)}, u32[]{:S(2)}, u32[]{:S(2)}) collective-permute-start(bf16[9,32,256]{2,1,0:T(8,128)(2,1)S(1)} %constant_dynamic-update-slice_fusion), channel_id=1, source_target_pairs={{0,3},{1,2},{2,1},{3,0},{4,7},{5,6},{6,5},{7,4},{8,11},{9,10},{10,... | collective-permute-start | bytes 442376 | tf_op jit(solution)/shard_map/ppermute | solution.py:471
  23.1 3.7 %shard_map.107 = (f32[8,32,256]{2,1,0:T(8,128)S(1)}, f32[32,256]{1,0:T(8,128)S(1)}) custom-call(s32[2,64]{1,0:T(2,128)S(1)} %get-tuple-element.65.pairs_ref, s32[1]{0:T(128)S(6)} %copy.19.count_ref, bf16[64,256,256]{2,1,0:T(8,128)(2,1)S(1)} %get-tuple-element.66.blocks_ref, bf16[8,64,256]{2,1,0:T(8,128)(2,1)S(1)} %get-tuple-element.64.field_ref, ...), custom_call_target="tpu_custom_call" | custom-call | flops 100000000 | bytes 12582912 | tf_op jit(solution)/shard_map/pallas_call | solution.py:28
  26.9 1.1 %shard_map.108 = (bf16[64,256]{1,0:T(8,128)(2,1)S(1)}, f32[32,256]{1,0:T(8,128)S(1)}, bf16[9,32,256]{2,1,0:T(8,128)(2,1)S(1)}) custom-call(bf16[16,256,256]{2,1,0:T(8,128)(2,1)S(1)} %get-tuple-element.73.merged_ref, bf16[8,32,256]{2,1,0:T(8,128)(2,1)S(1)} %pad_maximum_fusion.low_ref, bf16[8,32,256]{2,1,0:T(8,128)(2,1)S(1)} %slice.138.high_ref, ...), custom_call_target="tpu_custom_call" | custom-call | flops 100000000 | bytes 1000000 | tf_op jit(solution)/shard_map/pallas_call | solution.py:28
  28.0 0.9 %collective-permute-start.6 = (bf16[9,32,256]{2,1,0:T(8,128)(2,1)S(1)}, bf16[9,32,256]{2,1,0:T(8,128)(2,1)S(1)}, u32[]{:S(2)}, u32[]{:S(2)}) collective-permute-start(bf16[9,32,256]{2,1,0:T(8,128)(2,1)S(1)} %get-tuple-element.81.payload_ref), channel_id=1, source_target_pairs={{0,1},{1,0},{2,3},{3,2},{4,5},{5,4},{6,7},{7,6},{8,9},{9,8},{10,11... | collective-permute-start | bytes 442376 | tf_op jit(solution)/shard_map/ppermute | solution.py:471
  29.2 0.7 %collective-permute-done.6 = bf16[9,32,256]{2,1,0:T(8,128)(2,1)S(1)} collective-permute-done((bf16[9,32,256]{2,1,0:T(8,128)(2,1)S(1)}, bf16[9,32,256]{2,1,0:T(8,128)(2,1)S(1)}, u32[]{:S(2)}, u32[]{:S(2)}) %collective-permute-start.6) | collective-permute-done | bytes 147488 | tf_op jit(solution)/shard_map/ppermute | solution.py:471
  30.0 3.3 %collective-permute-start.7 = (bf16[6,32,256]{2,1,0:T(8,128)(2,1)S(1)}, bf16[6,32,256]{2,1,0:T(8,128)(2,1)S(1)}, u32[]{:S(2)}, u32[]{:S(2)}) collective-permute-start(bf16[6,32,256]{2,1,0:T(8,128)(2,1)S(1)} %pad_maximum_fusion.5), channel_id=1, source_target_pairs={{0,9},{1,8},{2,11},{3,10},{4,13},{5,12},{6,15},{7,14},{8,1},{9,0},... | collective-permute-start | bytes 294920 | tf_op jit(solution)/shard_map/ppermute | solution.py:471
  33.6 1.3 %collective-permute-start.8 = (bf16[8,64,256]{2,1,0:T(8,128)(2,1)S(1)}, bf16[8,64,256]{2,1,0:T(8,128)(2,1)S(1)}, u32[]{:S(2)}, u32[]{:S(2)}) collective-permute-start(bf16[8,64,256]{2,1,0:T(8,128)(2,1)S(1)} %get-tuple-element.88.field_ref), channel_id=1, source_target_pairs={{1,0},{2,1},{3,2},{4,3},{5,4},{6,5},{7,6},{8,7},{9,8},{10,9},{11,1... | collective-permute-start | bytes 786440 | tf_op jit(solution)/shard_map/ppermute | solution.py:474
  34.9 2.4 %shard_map.111 = (f32[8,32,256]{2,1,0:T(8,128)S(1)}, bf16[8,32,256]{2,1,0:T(8,128)(2,1)S(1)}) custom-call(s32[2,64]{1,0:T(2,128)S(1)} %get-tuple-element.65.pairs_ref, s32[1]{0:T(128)S(6)} %copy.19.count_ref, bf16[64,256,256]{2,1,0:T(8,128)(2,1)S(1)} %get-tuple-element.66.blocks_ref, bf16[8,64,256]{2,1,0:T(8,128)(2,1)S(1)} %get-tuple-element.88.field_ref), custom_call_target="tpu_custom_call" | custom-call | flops 100000000 | bytes 12582912 | tf_op jit(solution)/shard_map/pallas_call | solution.py:28
  37.3 1.2 %collective-permute-done.7 = bf16[6,32,256]{2,1,0:T(8,128)(2,1)S(1)} collective-permute-done((bf16[6,32,256]{2,1,0:T(8,128)(2,1)S(1)}, bf16[6,32,256]{2,1,0:T(8,128)(2,1)S(1)}, u32[]{:S(2)}, u32[]{:S(2)}) %collective-permute-start.7) | collective-permute-done | bytes 98336 | tf_op jit(solution)/shard_map/ppermute | solution.py:471
  38.9 2.8 %collective-permute-start.11 = (bf16[8,32,256]{2,1,0:T(8,128)(2,1)S(1)}, bf16[8,32,256]{2,1,0:T(8,128)(2,1)S(1)}, u32[]{:S(2)}, u32[]{:S(2)}) collective-permute-start(bf16[8,32,256]{2,1,0:T(8,128)(2,1)S(1)} %get-tuple-element.97), channel_id=1, source_target_pairs={{0,1},{1,2},{2,3},{3,4},{4,5},{5,6},{6,7},{7,8},{8,9},{9,10},{10,1... | collective-permute-start | bytes 393224 | tf_op jit(solution)/shard_map/ppermute | solution.py:474
  41.7 0.5 shard_map.112.early_ref
  42.2 1.6 %collective-permute-done.9 = bf16[6,32,256]{2,1,0:T(8,128)(2,1)S(1)} collective-permute-done((bf16[6,32,256]{2,1,0:T(8,128)(2,1)S(1)}, bf16[6,32,256]{2,1,0:T(8,128)(2,1)S(1)}, u32[]{:S(2)}, u32[]{:S(2)}) %collective-permute-start.9) | collective-permute-done | bytes 98336 | tf_op jit(solution)/shard_map/ppermute | solution.py:471
  44.1 4.4 %shard_map.113 = (f32[8,32,256]{2,1,0:T(8,128)S(1)}, f32[32,256]{1,0:T(8,128)S(1)}, f32[32,128]{1,0:T(8,128)S(1)}) custom-call(s32[2,64]{1,0:T(2,128)S(1)} %get-tuple-element.65.pairs_ref, s32[1]{0:T(128)S(6)} %copy.19.count_ref, bf16[64,256,256]{2,1,0:T(8,128)(2,1)S(1)} %get-tuple-element.66.blocks_ref, ...), custom_call_target="tpu_custom_call" | custom-call | flops 100000000 | bytes 12582912 | tf_op jit(solution)/shard_map/pallas_call | solution.py:28
  48.6 0.8 %collective-permute-done.10 = bf16[9,32,256]{2,1,0:T(8,128)(2,1)S(1)} collective-permute-done((bf16[9,32,256]{2,1,0:T(8,128)(2,1)S(1)}, bf16[9,32,256]{2,1,0:T(8,128)(2,1)S(1)}, u32[]{:S(2)}, u32[]{:S(2)}) %collective-permute-start.10) | collective-permute-done | bytes 147488 | tf_op jit(solution)/shard_map/ppermute | solution.py:471
  49.4 1.3 %shard_map.114 = (bf16[64,256]{1,0:T(8,128)(2,1)S(1)}, f32[48,128]{1,0:T(8,128)S(1)}) custom-call(bf16[16,256,256]{2,1,0:T(8,128)(2,1)S(1)} %get-tuple-element.73.merged_ref, bf16[8,32,256]{2,1,0:T(8,128)(2,1)S(1)} %pad_maximum_fusion.1.low_ref, bf16[8,32,256]{2,1,0:T(8,128)(2,1)S(1)} %slice.146.high_ref, f32[1,32,256]{2,1,0:T(8,128)S(1)} %slice.147.kept_ref, ...), custom_call_target="tpu_custom_call" | custom-call | flops 100000000 | bytes 1000000 | tf_op jit(solution)/shard_map/pallas_call | solution.py:28
  51.1 0.8 %collective-permute-done.12 = f32[48,128]{1,0:T(8,128)S(1)} collective-permute-done((f32[48,128]{1,0:T(8,128)S(1)}, f32[48,128]{1,0:T(8,128)S(1)}, u32[]{:S(2)}, u32[]{:S(2)}) %collective-permute-start.12) | collective-permute-done | bytes 24608 | tf_op jit(solution)/shard_map/ppermute | solution.py:471
  52.0 2.9 %collective-permute-start.13 = (f32[48,128]{1,0:T(8,128)S(1)}, f32[48,128]{1,0:T(8,128)S(1)}, u32[]{:S(2)}, u32[]{:S(2)}) collective-permute-start(f32[48,128]{1,0:T(8,128)S(1)} %add.37), channel_id=1, source_target_pairs={{0,9},{1,8},{2,11},{3,10},{4,13},{5,12},{6,15},{7,14},{8,1},{9,0},... | collective-permute-start | bytes 73736 | tf_op jit(solution)/shard_map/ppermute | solution.py:471
  55.1 1.3 %collective-permute-done.13 = f32[48,128]{1,0:T(8,128)S(1)} collective-permute-done((f32[48,128]{1,0:T(8,128)S(1)}, f32[48,128]{1,0:T(8,128)S(1)}, u32[]{:S(2)}, u32[]{:S(2)}) %collective-permute-start.13) | collective-permute-done | bytes 24608 | tf_op jit(solution)/shard_map/ppermute | solution.py:471
  56.4 0.9 %collective-permute-start.14 = (f32[48,128]{1,0:T(8,128)S(1)}, f32[48,128]{1,0:T(8,128)S(1)}, u32[]{:S(2)}, u32[]{:S(2)}) collective-permute-start(f32[48,128]{1,0:T(8,128)S(1)} %add.38), channel_id=1, source_target_pairs={{0,5},{1,4},{2,7},{3,6},{4,1},{5,0},{6,3},{7,2},{8,13},{9,12},{10,... | collective-permute-start | bytes 73736 | tf_op jit(solution)/shard_map/ppermute | solution.py:471
  57.3 2.3 %collective-permute-done.14 = f32[48,128]{1,0:T(8,128)S(1)} collective-permute-done((f32[48,128]{1,0:T(8,128)S(1)}, f32[48,128]{1,0:T(8,128)S(1)}, u32[]{:S(2)}, u32[]{:S(2)}) %collective-permute-start.14) | collective-permute-done | bytes 24608 | tf_op jit(solution)/shard_map/ppermute | solution.py:471
  59.7 0.6 collective-permute-start.15
  60.3 2.7 %collective-permute-done.15.got_ref = f32[48,128]{1,0:T(8,128)S(1)} collective-permute-done((f32[48,128]{1,0:T(8,128)S(1)}, f32[48,128]{1,0:T(8,128)S(1)}, u32[]{:S(2)}, u32[]{:S(2)}) %collective-permute-start.15) | collective-permute-done | bytes 24608 | tf_op jit(solution)/shard_map/ppermute | solution.py:471
  62.9 4.3 %shard_map.116 = (f32[32,2048]{1,0:T(8,128)}, f32[32,2048]{1,0:T(8,128)}, f32[32,64]{1,0:T(8,128)}) custom-call(f32[48,128]{1,0:T(8,128)S(1)} %add.39.kept_ref, f32[48,128]{1,0:T(8,128)S(1)} %collective-permute-done.15.got_ref, f32[32,2048]{1,0:T(8,128)S(1)} %copy-done, f32[8,32,256]{2,1,0:T(8,128)S(1)} %get-tuple-element.93.image_ref, ...), custom_call_target="tpu_custom_call" | custom-call | flops 100000000 | bytes 1000000 | tf_op jit(solution)/shard_map/pallas_call | solution.py:28
  (53 shorter events, 2.8 us)
Async XLA Ops:
  0.6 5.5 %copy-start = (f32[32,2048]{1,0:T(8,128)S(1)}, f32[32,2048]{1,0:T(8,128)}, u32[]{:S(2)}) copy-start(f32[32,2048]{1,0:T(8,128)} %right_ref.7) | copy-start | bytes 786436
  0.6 5.5 %copy-start.1 = (bf16[8,32,256]{2,1,0:T(8,128)(2,1)S(1)}, bf16[8,32,256]{2,1,0:T(8,128)(2,1)}, u32[]{:S(2)}) copy-start(bf16[8,32,256]{2,1,0:T(8,128)(2,1)} %param.14) | copy-start | bytes 393220
  5.7 1.8 %collective-permute-start = (bf16[17,32,256]{2,1,0:T(8,128)(2,1)S(1)}, bf16[17,32,256]{2,1,0:T(8,128)(2,1)S(1)}, u32[]{:S(2)}, u32[]{:S(2)}) collective-permute-start(bf16[17,32,256]{2,1,0:T(8,128)(2,1)S(1)} %get-tuple-element.58.payload_ref), channel_id=1, source_target_pairs={{0,1},{1,0},{2,3},{3,2},{4,5},{5,4},{6,7},{7,6},{8,9},{9,8},{10,11... | collective-permute-start | bytes 835592 | tf_op jit(solution)/shard_map/ppermute | solution.py:471
  7.5 8.8 %collective-permute-start.1 = (bf16[6,32,256]{2,1,0:T(8,128)(2,1)S(1)}, bf16[6,32,256]{2,1,0:T(8,128)(2,1)S(1)}, u32[]{:S(2)}, u32[]{:S(2)}) collective-permute-start(bf16[6,32,256]{2,1,0:T(8,128)(2,1)S(1)} %pad_maximum_fusion.2), channel_id=1, source_target_pairs={{0,9},{1,8},{2,11},{3,10},{4,13},{5,12},{6,15},{7,14},{8,1},{9,0},... | collective-permute-start | bytes 294920 | tf_op jit(solution)/shard_map/ppermute | solution.py:471
  12.0 9.7 %collective-permute-start.2 = (bf16[8,64,256]{2,1,0:T(8,128)(2,1)S(1)}, bf16[8,64,256]{2,1,0:T(8,128)(2,1)S(1)}, u32[]{:S(2)}, u32[]{:S(2)}) collective-permute-start(bf16[8,64,256]{2,1,0:T(8,128)(2,1)S(1)} %get-tuple-element.64.field_ref), channel_id=1, source_target_pairs={{1,0},{2,1},{3,2},{4,3},{5,4},{6,5},{7,6},{8,7},{9,8},{10,9},{11,1... | collective-permute-start | bytes 786440 | tf_op jit(solution)/shard_map/ppermute | solution.py:474
  16.4 5.2 %collective-permute-start.3 = (bf16[6,32,256]{2,1,0:T(8,128)(2,1)S(1)}, bf16[6,32,256]{2,1,0:T(8,128)(2,1)S(1)}, u32[]{:S(2)}, u32[]{:S(2)}) collective-permute-start(bf16[6,32,256]{2,1,0:T(8,128)(2,1)S(1)} %pad_maximum_fusion.4), channel_id=1, source_target_pairs={{0,5},{1,4},{2,7},{3,6},{4,1},{5,0},{6,3},{7,2},{8,13},{9,12},{10,... | collective-permute-start | bytes 294920 | tf_op jit(solution)/shard_map/ppermute | solution.py:471
  17.5 5.7 %collective-permute-start.5 = (bf16[8,32,256]{2,1,0:T(8,128)(2,1)S(1)}, bf16[8,32,256]{2,1,0:T(8,128)(2,1)S(1)}, u32[]{:S(2)}, u32[]{:S(2)}) collective-permute-start(bf16[8,32,256]{2,1,0:T(8,128)(2,1)S(1)} %get-tuple-element.77), channel_id=1, source_target_pairs={{0,1},{1,2},{2,3},{3,4},{4,5},{5,6},{6,7},{7,8},{8,9},{9,10},{10,1... | collective-permute-start | bytes 393224 | tf_op jit(solution)/shard_map/ppermute | solution.py:474
  21.7 5.2 %collective-permute-start.4 = (bf16[9,32,256]{2,1,0:T(8,128)(2,1)S(1)}, bf16[9,32,256]{2,1,0:T(8,128)(2,1)S(1)}, u32[]{:S(2)}, u32[]{:S(2)}) collective-permute-start(bf16[9,32,256]{2,1,0:T(8,128)(2,1)S(1)} %constant_dynamic-update-slice_fusion), channel_id=1, source_target_pairs={{0,3},{1,2},{2,1},{3,0},{4,7},{5,6},{6,5},{7,4},{8,11},{9,10},{10,... | collective-permute-start | bytes 442376 | tf_op jit(solution)/shard_map/ppermute | solution.py:471
  28.0 1.9 %collective-permute-start.6 = (bf16[9,32,256]{2,1,0:T(8,128)(2,1)S(1)}, bf16[9,32,256]{2,1,0:T(8,128)(2,1)S(1)}, u32[]{:S(2)}, u32[]{:S(2)}) collective-permute-start(bf16[9,32,256]{2,1,0:T(8,128)(2,1)S(1)} %get-tuple-element.81.payload_ref), channel_id=1, source_target_pairs={{0,1},{1,0},{2,3},{3,2},{4,5},{5,4},{6,7},{7,6},{8,9},{9,8},{10,11... | collective-permute-start | bytes 442376 | tf_op jit(solution)/shard_map/ppermute | solution.py:471
  30.0 8.5 %collective-permute-start.7 = (bf16[6,32,256]{2,1,0:T(8,128)(2,1)S(1)}, bf16[6,32,256]{2,1,0:T(8,128)(2,1)S(1)}, u32[]{:S(2)}, u32[]{:S(2)}) collective-permute-start(bf16[6,32,256]{2,1,0:T(8,128)(2,1)S(1)} %pad_maximum_fusion.5), channel_id=1, source_target_pairs={{0,9},{1,8},{2,11},{3,10},{4,13},{5,12},{6,15},{7,14},{8,1},{9,0},... | collective-permute-start | bytes 294920 | tf_op jit(solution)/shard_map/ppermute | solution.py:471
  33.6 10.2 %collective-permute-start.8 = (bf16[8,64,256]{2,1,0:T(8,128)(2,1)S(1)}, bf16[8,64,256]{2,1,0:T(8,128)(2,1)S(1)}, u32[]{:S(2)}, u32[]{:S(2)}) collective-permute-start(bf16[8,64,256]{2,1,0:T(8,128)(2,1)S(1)} %get-tuple-element.88.field_ref), channel_id=1, source_target_pairs={{1,0},{2,1},{3,2},{4,3},{5,4},{6,5},{7,6},{8,7},{9,8},{10,9},{11,1... | collective-permute-start | bytes 786440 | tf_op jit(solution)/shard_map/ppermute | solution.py:474
  38.5 5.2 %collective-permute-start.9 = (bf16[6,32,256]{2,1,0:T(8,128)(2,1)S(1)}, bf16[6,32,256]{2,1,0:T(8,128)(2,1)S(1)}, u32[]{:S(2)}, u32[]{:S(2)}) collective-permute-start(bf16[6,32,256]{2,1,0:T(8,128)(2,1)S(1)} %pad_maximum_fusion.7), channel_id=1, source_target_pairs={{0,5},{1,4},{2,7},{3,6},{4,1},{5,0},{6,3},{7,2},{8,13},{9,12},{10,... | collective-permute-start | bytes 294920 | tf_op jit(solution)/shard_map/ppermute | solution.py:471
  38.9 5.3 %collective-permute-start.11 = (bf16[8,32,256]{2,1,0:T(8,128)(2,1)S(1)}, bf16[8,32,256]{2,1,0:T(8,128)(2,1)S(1)}, u32[]{:S(2)}, u32[]{:S(2)}) collective-permute-start(bf16[8,32,256]{2,1,0:T(8,128)(2,1)S(1)} %get-tuple-element.97), channel_id=1, source_target_pairs={{0,1},{1,2},{2,3},{3,4},{4,5},{5,6},{6,7},{7,8},{8,9},{9,10},{10,1... | collective-permute-start | bytes 393224 | tf_op jit(solution)/shard_map/ppermute | solution.py:474
  43.8 5.6 %collective-permute-start.10 = (bf16[9,32,256]{2,1,0:T(8,128)(2,1)S(1)}, bf16[9,32,256]{2,1,0:T(8,128)(2,1)S(1)}, u32[]{:S(2)}, u32[]{:S(2)}) collective-permute-start(bf16[9,32,256]{2,1,0:T(8,128)(2,1)S(1)} %constant_dynamic-update-slice_fusion.5), channel_id=1, source_target_pairs={{0,3},{1,2},{2,1},{3,0},{4,7},{5,6},{6,5},{7,4},{8,11},{9,10},{10,... | collective-permute-start | bytes 442376 | tf_op jit(solution)/shard_map/ppermute | solution.py:471
  50.7 1.3 %collective-permute-start.12 = (f32[48,128]{1,0:T(8,128)S(1)}, f32[48,128]{1,0:T(8,128)S(1)}, u32[]{:S(2)}, u32[]{:S(2)}) collective-permute-start(f32[48,128]{1,0:T(8,128)S(1)} %get-tuple-element.103), channel_id=1, source_target_pairs={{0,1},{1,0},{2,3},{3,2},{4,5},{5,4},{6,7},{7,6},{8,9},{9,8},{10,11... | collective-permute-start | bytes 73736 | tf_op jit(solution)/shard_map/ppermute | solution.py:471
  52.0 4.4 %collective-permute-start.13 = (f32[48,128]{1,0:T(8,128)S(1)}, f32[48,128]{1,0:T(8,128)S(1)}, u32[]{:S(2)}, u32[]{:S(2)}) collective-permute-start(f32[48,128]{1,0:T(8,128)S(1)} %add.37), channel_id=1, source_target_pairs={{0,9},{1,8},{2,11},{3,10},{4,13},{5,12},{6,15},{7,14},{8,1},{9,0},... | collective-permute-start | bytes 73736 | tf_op jit(solution)/shard_map/ppermute | solution.py:471
  56.4 3.3 %collective-permute-start.14 = (f32[48,128]{1,0:T(8,128)S(1)}, f32[48,128]{1,0:T(8,128)S(1)}, u32[]{:S(2)}, u32[]{:S(2)}) collective-permute-start(f32[48,128]{1,0:T(8,128)S(1)} %add.38), channel_id=1, source_target_pairs={{0,5},{1,4},{2,7},{3,6},{4,1},{5,0},{6,3},{7,2},{8,13},{9,12},{10,... | collective-permute-start | bytes 73736 | tf_op jit(solution)/shard_map/ppermute | solution.py:471
  59.7 3.3 %collective-permute-start.15 = (f32[48,128]{1,0:T(8,128)S(1)}, f32[48,128]{1,0:T(8,128)S(1)}, u32[]{:S(2)}, u32[]{:S(2)}) collective-permute-start(f32[48,128]{1,0:T(8,128)S(1)} %add.39.kept_ref), channel_id=1, source_target_pairs={{0,3},{1,2},{2,1},{3,0},{4,7},{5,6},{6,5},{7,4},{8,11},{9,10},{10,... | collective-permute-start | bytes 73736 | tf_op jit(solution)/shard_map/ppermute | solution.py:471

commit v5 on v4

--- a/solution.py
+++ b/solution.py
@@ -81,7 +81,7 @@
 
 def rounds(devices):
     bits = devices.bit_length() - 1
-    return [1] + [(1 << b) | 1 for b in range(bits - 1, 0, -1)]
+    return [1] + [(1 << b) | 1 for b in [bits - 1, 1] + list(range(bits - 2, 1, -1))]
 
 
 def places(devices):
@@ -121,18 +121,18 @@
         first_home, second_home = first >> shift, second >> shift
         own = first_home == me
         where = jnp.where(own, devices, 0) + table_ref[jnp.where(own, second_home, first_home)]
-        block = wide_ref[pl.ds(f, K, stride=pairs), :]
+        block = wide_ref[pl.ds(f, K, stride=pairs + 8), :]
         block = jnp.concatenate([block] * (clusters * K // block.shape[1]), axis=1)
         block = jnp.where(group == (second & (clusters - 1)), block, 0.0).astype(bf16)
         here = pl.ds(pl.multiple_of((first & (clusters - 1)) * K, K), K)
         out_ref[where, here, :] = out_ref[where, here, :] + block
 
     def some(step, carry):
-        for u in range(8):
-            one(step * 8 + u)
+        for u in range(16):
+            one(step * 16 + u)
         return carry
 
-    lax.fori_loop(0, pairs // 8, some, 0)
+    lax.fori_loop(0, pairs // 16, some, 0)
 
 
 def open_kernel(me_ref, pairs_hbm, slots_hbm, coupling_hbm, right_hbm, basis_hbm, near_hbm, blocks_hbm,
@@ -159,7 +159,8 @@
         spread = jnp.where((lanes % K == rows % K) & (rows // K == u), 1.0, 0.0).astype(bf16)
         value = dot(flat, spread)
         for t in range(tiles):
-            wide_ref[(t * each + u) * pairs : (t * each + u + 1) * pairs] = value[t * pairs : (t + 1) * pairs]
+            begin = (t * each + u) * (pairs + 8)
+            wide_ref[begin : begin + pairs] = value[t * pairs : (t + 1) * pairs]
     copies[1].wait()
     basis = basis_ref[...]
     copies[2].wait()
@@ -503,7 +504,7 @@
             pltpu.VMEM(coupling.shape, bf16),
             pltpu.VMEM(right_side.shape, f32),
             pltpu.VMEM(basis.shape, bf16),
-            pltpu.VMEM((coupling.shape[0] * (K + 1), 128), f32),
+            pltpu.VMEM(((coupling.shape[0] + 8) * (K + 1), 128), f32),
             pltpu.SemaphoreType.DMA((7,)),
         ],
         placed=[SMEM] + [VMEM] * 5,

time: 68.2 us -> 67.3 us (0.987); the launches traced: 67.2 us -> 67.3 us
  Pallas kernels: 28.2 us -> 22.9 us
  waiting for transfers between devices: 12.1 us -> 16.9 us
    pallas_call x14, Pallas kernels: 28.2 us -> 22.9 us  [call(): pl.pallas_call(kernel, out_shape=outs, in_specs=[spec(s) for s in spaces]...]
    ppermute x12, waiting for transfers between devices: 12.1 us -> 16.9 us  [across(): return lax.ppermute(x, 'leaf', [(i, i ^ b) for i in range(devices)])]
    ppermute x12, starting transfers between devices: 16.5 us -> 18.4 us  [across(): return lax.ppermute(x, 'leaf', [(i, i ^ b) for i in range(devices)])]
    ppermute x4, starting transfers between devices: 8.35 us -> 7.11 us  [shift(): lax.ppermute(x, 'leaf', [(i, i + by) for i in range(devices) if 0 <= i +...]
  transfers between devices with their start and end apart: 16 -> 16, of which waited for: 10 -> 11; matrix products, arithmetic and copies ran while one was open for 0% -> 0% of each run, Pallas kernels for 25% -> 18%
where the time goes in v5:
time: 67.3 us
  starting transfers between devices  25.5 us (38%)
  Pallas kernels  22.9 us (34%)
  waiting for transfers between devices  16.9 us (25%)
  between operations  1.63 us (2%)
    pallas_call x14, Pallas kernels, call(): pl.pallas_call(kernel, out_shape=outs, in_specs=[spec(s) for s in spaces]...  22.9 us
    ppermute x12, starting transfers between devices, across(): return lax.ppermute(x, 'leaf', [(i, i ^ b) for i in range(devices)])  18.4 us
    ppermute x12, waiting for transfers between devices, across(): return lax.ppermute(x, 'leaf', [(i, i ^ b) for i in range(devices)])  16.9 us
    ppermute x4, starting transfers between devices, shift(): lax.ppermute(x, 'leaf', [(i, i + by) for i in range(devices) if 0 <= i +...  7.11 us
  transfers between devices with their start and end apart: 16, of which 11 were waited for; matrix products, arithmetic and copies ran while one was open for 0% of the time, Pallas kernels for 18%

profile of v5, /device:TPU:0, one launch (start us, length us, event | category | flops | bytes accessed | tf_op | source)
XLA Modules:
  0.0 67.3 jit_solution(5830241591215797380)
XLA Ops:
  0.7 4.3 %shard_map.103 = (s32[2,64]{1,0:T(2,128)S(1)}, bf16[64,256,256]{2,1,0:T(8,128)(2,1)S(1)}, bf16[8,64,256]{2,1,0:T(8,128)(2,1)S(1)}, f32[32,256]{1,0:T(8,128)S(1)}...) custom-call(s32[1]{0:T(128)} %bitcast.me_ref, s32[2,128]{1,0:T(2,128)} %pairs_hbm.1, s32[128]{0:T(128)} %slots_hbm.1, ...), custom_call_target="tpu_custom_call" | custom-call | flops 100000000 | bytes 1000000 | tf_op jit(solution)/shard_map/pallas_call | solution.py:28
  5.5 1.2 %shard_map.104 = (f32[8,32,256]{2,1,0:T(8,128)S(1)}, bf16[2,256,256]{2,1,0:T(8,128)(2,1)S(1)}, f32[32,128]{1,0:T(8,128)S(1)}) custom-call(bf16[32,256,256]{2,1,0:T(8,128)(2,1)S(1)} %get-tuple-element.70.coupled_ref, bf16[17,32,256]{2,1,0:T(8,128)(2,1)S(1)} %get-tuple-element.58.payload_ref, bf16[256,256]{1,0:T(8,128)(2,1)S(1)} %bitcast.4, f32[32,2048]{1,0:T(8,128)S(1)} %copy-done), custom_call_target="tpu_custom_call" | custom-call | flops 100000000 | bytes 1000000 | tf_op jit(solution)/shard_map/pallas_call | solution.py:28
  6.9 3.8 %collective-permute-start.1 = (bf16[6,32,256]{2,1,0:T(8,128)(2,1)S(1)}, bf16[6,32,256]{2,1,0:T(8,128)(2,1)S(1)}, u32[]{:S(2)}, u32[]{:S(2)}) collective-permute-start(bf16[6,32,256]{2,1,0:T(8,128)(2,1)S(1)} %pad_maximum_fusion.2), channel_id=1, source_target_pairs={{0,9},{1,8},{2,11},{3,10},{4,13},{5,12},{6,15},{7,14},{8,1},{9,0},... | collective-permute-start | bytes 294920 | tf_op jit(solution)/shard_map/ppermute | solution.py:472
  11.3 1.3 %collective-permute-start.2 = (bf16[8,64,256]{2,1,0:T(8,128)(2,1)S(1)}, bf16[8,64,256]{2,1,0:T(8,128)(2,1)S(1)}, u32[]{:S(2)}, u32[]{:S(2)}) collective-permute-start(bf16[8,64,256]{2,1,0:T(8,128)(2,1)S(1)} %get-tuple-element.64.field_ref), channel_id=1, source_target_pairs={{1,0},{2,1},{3,2},{4,3},{5,4},{6,5},{7,6},{8,7},{9,8},{10,9},{11,1... | collective-permute-start | bytes 786440 | tf_op jit(solution)/shard_map/ppermute | solution.py:475
  12.6 1.5 %shard_map.105 = (f32[8,32,256]{2,1,0:T(8,128)S(1)}, bf16[8,32,256]{2,1,0:T(8,128)(2,1)S(1)}) custom-call(s32[2,64]{1,0:T(2,128)S(1)} %get-tuple-element.65.pairs_ref, s32[1]{0:T(128)S(6)} %copy.19.count_ref, bf16[64,256,256]{2,1,0:T(8,128)(2,1)S(1)} %get-tuple-element.66.blocks_ref, bf16[8,64,256]{2,1,0:T(8,128)(2,1)S(1)} %get-tuple-element.64.field_ref), custom_call_target="tpu_custom_call" | custom-call | flops 100000000 | bytes 12582912 | tf_op jit(solution)/shard_map/pallas_call | solution.py:28
  14.1 1.6 %collective-permute-done.1 = bf16[6,32,256]{2,1,0:T(8,128)(2,1)S(1)} collective-permute-done((bf16[6,32,256]{2,1,0:T(8,128)(2,1)S(1)}, bf16[6,32,256]{2,1,0:T(8,128)(2,1)S(1)}, u32[]{:S(2)}, u32[]{:S(2)}) %collective-permute-start.1) | collective-permute-done | bytes 98336 | tf_op jit(solution)/shard_map/ppermute | solution.py:472
  15.8 1.7 %collective-permute-start.3 = (bf16[6,32,256]{2,1,0:T(8,128)(2,1)S(1)}, bf16[6,32,256]{2,1,0:T(8,128)(2,1)S(1)}, u32[]{:S(2)}, u32[]{:S(2)}) collective-permute-start(bf16[6,32,256]{2,1,0:T(8,128)(2,1)S(1)} %pad_maximum_fusion.4), channel_id=1, source_target_pairs={{0,3},{1,2},{2,1},{3,0},{4,7},{5,6},{6,5},{7,4},{8,11},{9,10},{10,... | collective-permute-start | bytes 294920 | tf_op jit(solution)/shard_map/ppermute | solution.py:472
  17.4 2.3 %collective-permute-start.5 = (bf16[8,32,256]{2,1,0:T(8,128)(2,1)S(1)}, bf16[8,32,256]{2,1,0:T(8,128)(2,1)S(1)}, u32[]{:S(2)}, u32[]{:S(2)}) collective-permute-start(bf16[8,32,256]{2,1,0:T(8,128)(2,1)S(1)} %get-tuple-element.77), channel_id=1, source_target_pairs={{0,1},{1,2},{2,3},{3,4},{4,5},{5,6},{6,7},{7,8},{8,9},{9,10},{10,1... | collective-permute-start | bytes 393224 | tf_op jit(solution)/shard_map/ppermute | solution.py:475
  19.7 1.1 %shard_map.106 = (bf16[16,256,256]{2,1,0:T(8,128)(2,1)S(1)}, bf16[16,256,256]{2,1,0:T(8,128)(2,1)S(1)}) custom-call(bf16[32,256,256]{2,1,0:T(8,128)(2,1)S(1)} %get-tuple-element.70.coupled_ref), custom_call_target="tpu_custom_call" | custom-call | flops 100000000 | bytes 1000000 | tf_op jit(solution)/shard_map/pallas_call | solution.py:28
  21.6 1.4 %collective-permute-start.4 = (bf16[9,32,256]{2,1,0:T(8,128)(2,1)S(1)}, bf16[9,32,256]{2,1,0:T(8,128)(2,1)S(1)}, u32[]{:S(2)}, u32[]{:S(2)}) collective-permute-start(bf16[9,32,256]{2,1,0:T(8,128)(2,1)S(1)} %constant_dynamic-update-slice_fusion), channel_id=1, source_target_pairs={{0,5},{1,4},{2,7},{3,6},{4,1},{5,0},{6,3},{7,2},{8,13},{9,12},{10,... | collective-permute-start | bytes 442376 | tf_op jit(solution)/shard_map/ppermute | solution.py:472
  23.0 2.3 %shard_map.107 = (f32[8,32,256]{2,1,0:T(8,128)S(1)}, f32[32,256]{1,0:T(8,128)S(1)}) custom-call(s32[2,64]{1,0:T(2,128)S(1)} %get-tuple-element.65.pairs_ref, s32[1]{0:T(128)S(6)} %copy.19.count_ref, bf16[64,256,256]{2,1,0:T(8,128)(2,1)S(1)} %get-tuple-element.66.blocks_ref, bf16[8,64,256]{2,1,0:T(8,128)(2,1)S(1)} %get-tuple-element.64.field_ref, ...), custom_call_target="tpu_custom_call" | custom-call | flops 100000000 | bytes 12582912 | tf_op jit(solution)/shard_map/pallas_call | solution.py:28
  25.3 2.3 %collective-permute-done.4 = bf16[9,32,256]{2,1,0:T(8,128)(2,1)S(1)} collective-permute-done((bf16[9,32,256]{2,1,0:T(8,128)(2,1)S(1)}, bf16[9,32,256]{2,1,0:T(8,128)(2,1)S(1)}, u32[]{:S(2)}, u32[]{:S(2)}) %collective-permute-start.4) | collective-permute-done | bytes 147488 | tf_op jit(solution)/shard_map/ppermute | solution.py:472
  27.6 1.1 %shard_map.108 = (bf16[64,256]{1,0:T(8,128)(2,1)S(1)}, f32[32,256]{1,0:T(8,128)S(1)}, bf16[9,32,256]{2,1,0:T(8,128)(2,1)S(1)}) custom-call(bf16[16,256,256]{2,1,0:T(8,128)(2,1)S(1)} %get-tuple-element.73.merged_ref, bf16[8,32,256]{2,1,0:T(8,128)(2,1)S(1)} %pad_maximum_fusion.low_ref, bf16[8,32,256]{2,1,0:T(8,128)(2,1)S(1)} %slice.138.high_ref, ...), custom_call_target="tpu_custom_call" | custom-call | flops 100000000 | bytes 1000000 | tf_op jit(solution)/shard_map/pallas_call | solution.py:28
  29.1 1.0 %collective-permute-done.6 = bf16[9,32,256]{2,1,0:T(8,128)(2,1)S(1)} collective-permute-done((bf16[9,32,256]{2,1,0:T(8,128)(2,1)S(1)}, bf16[9,32,256]{2,1,0:T(8,128)(2,1)S(1)}, u32[]{:S(2)}, u32[]{:S(2)}) %collective-permute-start.6) | collective-permute-done | bytes 147488 | tf_op jit(solution)/shard_map/ppermute | solution.py:472
  30.2 2.9 %collective-permute-start.7 = (bf16[6,32,256]{2,1,0:T(8,128)(2,1)S(1)}, bf16[6,32,256]{2,1,0:T(8,128)(2,1)S(1)}, u32[]{:S(2)}, u32[]{:S(2)}) collective-permute-start(bf16[6,32,256]{2,1,0:T(8,128)(2,1)S(1)} %pad_maximum_fusion.5), channel_id=1, source_target_pairs={{0,9},{1,8},{2,11},{3,10},{4,13},{5,12},{6,15},{7,14},{8,1},{9,0},... | collective-permute-start | bytes 294920 | tf_op jit(solution)/shard_map/ppermute | solution.py:472
  33.3 1.3 %collective-permute-start.8 = (bf16[8,64,256]{2,1,0:T(8,128)(2,1)S(1)}, bf16[8,64,256]{2,1,0:T(8,128)(2,1)S(1)}, u32[]{:S(2)}, u32[]{:S(2)}) collective-permute-start(bf16[8,64,256]{2,1,0:T(8,128)(2,1)S(1)} %get-tuple-element.88.field_ref), channel_id=1, source_target_pairs={{1,0},{2,1},{3,2},{4,3},{5,4},{6,5},{7,6},{8,7},{9,8},{10,9},{11,1... | collective-permute-start | bytes 786440 | tf_op jit(solution)/shard_map/ppermute | solution.py:475
  34.6 1.5 %shard_map.111 = (f32[8,32,256]{2,1,0:T(8,128)S(1)}, bf16[8,32,256]{2,1,0:T(8,128)(2,1)S(1)}) custom-call(s32[2,64]{1,0:T(2,128)S(1)} %get-tuple-element.65.pairs_ref, s32[1]{0:T(128)S(6)} %copy.19.count_ref, bf16[64,256,256]{2,1,0:T(8,128)(2,1)S(1)} %get-tuple-element.66.blocks_ref, bf16[8,64,256]{2,1,0:T(8,128)(2,1)S(1)} %get-tuple-element.88.field_ref), custom_call_target="tpu_custom_call" | custom-call | flops 100000000 | bytes 12582912 | tf_op jit(solution)/shard_map/pallas_call | solution.py:28
  36.1 1.9 %collective-permute-done.7 = bf16[6,32,256]{2,1,0:T(8,128)(2,1)S(1)} collective-permute-done((bf16[6,32,256]{2,1,0:T(8,128)(2,1)S(1)}, bf16[6,32,256]{2,1,0:T(8,128)(2,1)S(1)}, u32[]{:S(2)}, u32[]{:S(2)}) %collective-permute-start.7) | collective-permute-done | bytes 98336 | tf_op jit(solution)/shard_map/ppermute | solution.py:472
  38.1 2.1 %collective-permute-start.9 = (bf16[6,32,256]{2,1,0:T(8,128)(2,1)S(1)}, bf16[6,32,256]{2,1,0:T(8,128)(2,1)S(1)}, u32[]{:S(2)}, u32[]{:S(2)}) collective-permute-start(bf16[6,32,256]{2,1,0:T(8,128)(2,1)S(1)} %pad_maximum_fusion.7), channel_id=1, source_target_pairs={{0,3},{1,2},{2,1},{3,0},{4,7},{5,6},{6,5},{7,4},{8,11},{9,10},{10,... | collective-permute-start | bytes 294920 | tf_op jit(solution)/shard_map/ppermute | solution.py:472
  40.2 2.2 %collective-permute-start.11 = (bf16[8,32,256]{2,1,0:T(8,128)(2,1)S(1)}, bf16[8,32,256]{2,1,0:T(8,128)(2,1)S(1)}, u32[]{:S(2)}, u32[]{:S(2)}) collective-permute-start(bf16[8,32,256]{2,1,0:T(8,128)(2,1)S(1)} %get-tuple-element.97), channel_id=1, source_target_pairs={{0,1},{1,2},{2,3},{3,4},{4,5},{5,6},{6,7},{7,8},{8,9},{9,10},{10,1... | collective-permute-start | bytes 393224 | tf_op jit(solution)/shard_map/ppermute | solution.py:475
  43.3 0.8 %collective-permute-start.10 = (bf16[9,32,256]{2,1,0:T(8,128)(2,1)S(1)}, bf16[9,32,256]{2,1,0:T(8,128)(2,1)S(1)}, u32[]{:S(2)}, u32[]{:S(2)}) collective-permute-start(bf16[9,32,256]{2,1,0:T(8,128)(2,1)S(1)} %constant_dynamic-update-slice_fusion.5), channel_id=1, source_target_pairs={{0,5},{1,4},{2,7},{3,6},{4,1},{5,0},{6,3},{7,2},{8,13},{9,12},{10,... | collective-permute-start | bytes 442376 | tf_op jit(solution)/shard_map/ppermute | solution.py:472
  44.0 3.0 %shard_map.113 = (f32[8,32,256]{2,1,0:T(8,128)S(1)}, f32[32,256]{1,0:T(8,128)S(1)}, f32[32,128]{1,0:T(8,128)S(1)}) custom-call(s32[2,64]{1,0:T(2,128)S(1)} %get-tuple-element.65.pairs_ref, s32[1]{0:T(128)S(6)} %copy.19.count_ref, bf16[64,256,256]{2,1,0:T(8,128)(2,1)S(1)} %get-tuple-element.66.blocks_ref, ...), custom_call_target="tpu_custom_call" | custom-call | flops 100000000 | bytes 12582912 | tf_op jit(solution)/shard_map/pallas_call | solution.py:28
  47.1 2.1 %collective-permute-done.10 = bf16[9,32,256]{2,1,0:T(8,128)(2,1)S(1)} collective-permute-done((bf16[9,32,256]{2,1,0:T(8,128)(2,1)S(1)}, bf16[9,32,256]{2,1,0:T(8,128)(2,1)S(1)}, u32[]{:S(2)}, u32[]{:S(2)}) %collective-permute-start.10) | collective-permute-done | bytes 147488 | tf_op jit(solution)/shard_map/ppermute | solution.py:472
  49.2 1.3 %shard_map.114 = (bf16[64,256]{1,0:T(8,128)(2,1)S(1)}, f32[48,128]{1,0:T(8,128)S(1)}) custom-call(bf16[16,256,256]{2,1,0:T(8,128)(2,1)S(1)} %get-tuple-element.73.merged_ref, bf16[8,32,256]{2,1,0:T(8,128)(2,1)S(1)} %pad_maximum_fusion.1.low_ref, bf16[8,32,256]{2,1,0:T(8,128)(2,1)S(1)} %slice.146.high_ref, f32[1,32,256]{2,1,0:T(8,128)S(1)} %slice.147.kept_ref, ...), custom_call_target="tpu_custom_call" | custom-call | flops 100000000 | bytes 1000000 | tf_op jit(solution)/shard_map/pallas_call | solution.py:28
  50.6 1.1 %collective-permute-done.12 = f32[48,128]{1,0:T(8,128)S(1)} collective-permute-done((f32[48,128]{1,0:T(8,128)S(1)}, f32[48,128]{1,0:T(8,128)S(1)}, u32[]{:S(2)}, u32[]{:S(2)}) %collective-permute-start.12) | collective-permute-done | bytes 24608 | tf_op jit(solution)/shard_map/ppermute | solution.py:472
  51.7 3.0 %collective-permute-start.13 = (f32[48,128]{1,0:T(8,128)S(1)}, f32[48,128]{1,0:T(8,128)S(1)}, u32[]{:S(2)}, u32[]{:S(2)}) collective-permute-start(f32[48,128]{1,0:T(8,128)S(1)} %add.37), channel_id=1, source_target_pairs={{0,9},{1,8},{2,11},{3,10},{4,13},{5,12},{6,15},{7,14},{8,1},{9,0},... | collective-permute-start | bytes 73736 | tf_op jit(solution)/shard_map/ppermute | solution.py:472
  55.0 1.5 %collective-permute-done.13 = f32[48,128]{1,0:T(8,128)S(1)} collective-permute-done((f32[48,128]{1,0:T(8,128)S(1)}, f32[48,128]{1,0:T(8,128)S(1)}, u32[]{:S(2)}, u32[]{:S(2)}) %collective-permute-start.13) | collective-permute-done | bytes 24608 | tf_op jit(solution)/shard_map/ppermute | solution.py:472
  56.5 1.1 %collective-permute-start.14 = (f32[48,128]{1,0:T(8,128)S(1)}, f32[48,128]{1,0:T(8,128)S(1)}, u32[]{:S(2)}, u32[]{:S(2)}) collective-permute-start(f32[48,128]{1,0:T(8,128)S(1)} %add.38), channel_id=1, source_target_pairs={{0,3},{1,2},{2,1},{3,0},{4,7},{5,6},{6,5},{7,4},{8,11},{9,10},{10,... | collective-permute-start | bytes 73736 | tf_op jit(solution)/shard_map/ppermute | solution.py:472
  57.7 2.1 %collective-permute-done.14 = f32[48,128]{1,0:T(8,128)S(1)} collective-permute-done((f32[48,128]{1,0:T(8,128)S(1)}, f32[48,128]{1,0:T(8,128)S(1)}, u32[]{:S(2)}, u32[]{:S(2)}) %collective-permute-start.14) | collective-permute-done | bytes 24608 | tf_op jit(solution)/shard_map/ppermute | solution.py:472
  59.8 0.8 %collective-permute-start.15 = (f32[48,128]{1,0:T(8,128)S(1)}, f32[48,128]{1,0:T(8,128)S(1)}, u32[]{:S(2)}, u32[]{:S(2)}) collective-permute-start(f32[48,128]{1,0:T(8,128)S(1)} %add.39.kept_ref), channel_id=1, source_target_pairs={{0,5},{1,4},{2,7},{3,6},{4,1},{5,0},{6,3},{7,2},{8,13},{9,12},{10,... | collective-permute-start | bytes 73736 | tf_op jit(solution)/shard_map/ppermute | solution.py:472
  60.6 2.5 %collective-permute-done.15.got_ref = f32[48,128]{1,0:T(8,128)S(1)} collective-permute-done((f32[48,128]{1,0:T(8,128)S(1)}, f32[48,128]{1,0:T(8,128)S(1)}, u32[]{:S(2)}, u32[]{:S(2)}) %collective-permute-start.15) | collective-permute-done | bytes 24608 | tf_op jit(solution)/shard_map/ppermute | solution.py:472
  63.0 4.3 %shard_map.116 = (f32[32,2048]{1,0:T(8,128)}, f32[32,2048]{1,0:T(8,128)}, f32[32,64]{1,0:T(8,128)}) custom-call(f32[48,128]{1,0:T(8,128)S(1)} %add.39.kept_ref, f32[48,128]{1,0:T(8,128)S(1)} %collective-permute-done.15.got_ref, f32[32,2048]{1,0:T(8,128)S(1)} %copy-done, f32[8,32,256]{2,1,0:T(8,128)S(1)} %get-tuple-element.93.image_ref, ...), custom_call_target="tpu_custom_call" | custom-call | flops 100000000 | bytes 1000000 | tf_op jit(solution)/shard_map/pallas_call | solution.py:28
  (53 shorter events, 3.4 us)
Async XLA Ops:
  0.6 4.9 %copy-start = (f32[32,2048]{1,0:T(8,128)S(1)}, f32[32,2048]{1,0:T(8,128)}, u32[]{:S(2)}) copy-start(f32[32,2048]{1,0:T(8,128)} %right_ref.7) | copy-start | bytes 786436
  0.6 4.9 %copy-start.1 = (bf16[8,32,256]{2,1,0:T(8,128)(2,1)S(1)}, bf16[8,32,256]{2,1,0:T(8,128)(2,1)}, u32[]{:S(2)}) copy-start(bf16[8,32,256]{2,1,0:T(8,128)(2,1)} %param.14) | copy-start | bytes 393220
  5.0 1.8 %collective-permute-start = (bf16[17,32,256]{2,1,0:T(8,128)(2,1)S(1)}, bf16[17,32,256]{2,1,0:T(8,128)(2,1)S(1)}, u32[]{:S(2)}, u32[]{:S(2)}) collective-permute-start(bf16[17,32,256]{2,1,0:T(8,128)(2,1)S(1)} %get-tuple-element.58.payload_ref), channel_id=1, source_target_pairs={{0,1},{1,0},{2,3},{3,2},{4,5},{5,4},{6,7},{7,6},{8,9},{9,8},{10,11... | collective-permute-start | bytes 835592 | tf_op jit(solution)/shard_map/ppermute | solution.py:472
  6.9 8.8 %collective-permute-start.1 = (bf16[6,32,256]{2,1,0:T(8,128)(2,1)S(1)}, bf16[6,32,256]{2,1,0:T(8,128)(2,1)S(1)}, u32[]{:S(2)}, u32[]{:S(2)}) collective-permute-start(bf16[6,32,256]{2,1,0:T(8,128)(2,1)S(1)} %pad_maximum_fusion.2), channel_id=1, source_target_pairs={{0,9},{1,8},{2,11},{3,10},{4,13},{5,12},{6,15},{7,14},{8,1},{9,0},... | collective-permute-start | bytes 294920 | tf_op jit(solution)/shard_map/ppermute | solution.py:472
  11.3 10.2 %collective-permute-start.2 = (bf16[8,64,256]{2,1,0:T(8,128)(2,1)S(1)}, bf16[8,64,256]{2,1,0:T(8,128)(2,1)S(1)}, u32[]{:S(2)}, u32[]{:S(2)}) collective-permute-start(bf16[8,64,256]{2,1,0:T(8,128)(2,1)S(1)} %get-tuple-element.64.field_ref), channel_id=1, source_target_pairs={{1,0},{2,1},{3,2},{4,3},{5,4},{6,5},{7,6},{8,7},{9,8},{10,9},{11,1... | collective-permute-start | bytes 786440 | tf_op jit(solution)/shard_map/ppermute | solution.py:475
  15.8 5.8 %collective-permute-start.3 = (bf16[6,32,256]{2,1,0:T(8,128)(2,1)S(1)}, bf16[6,32,256]{2,1,0:T(8,128)(2,1)S(1)}, u32[]{:S(2)}, u32[]{:S(2)}) collective-permute-start(bf16[6,32,256]{2,1,0:T(8,128)(2,1)S(1)} %pad_maximum_fusion.4), channel_id=1, source_target_pairs={{0,3},{1,2},{2,1},{3,0},{4,7},{5,6},{6,5},{7,4},{8,11},{9,10},{10,... | collective-permute-start | bytes 294920 | tf_op jit(solution)/shard_map/ppermute | solution.py:472
  17.4 5.5 %collective-permute-start.5 = (bf16[8,32,256]{2,1,0:T(8,128)(2,1)S(1)}, bf16[8,32,256]{2,1,0:T(8,128)(2,1)S(1)}, u32[]{:S(2)}, u32[]{:S(2)}) collective-permute-start(bf16[8,32,256]{2,1,0:T(8,128)(2,1)S(1)} %get-tuple-element.77), channel_id=1, source_target_pairs={{0,1},{1,2},{2,3},{3,4},{4,5},{5,6},{6,7},{7,8},{8,9},{9,10},{10,1... | collective-permute-start | bytes 393224 | tf_op jit(solution)/shard_map/ppermute | solution.py:475
  21.6 6.0 %collective-permute-start.4 = (bf16[9,32,256]{2,1,0:T(8,128)(2,1)S(1)}, bf16[9,32,256]{2,1,0:T(8,128)(2,1)S(1)}, u32[]{:S(2)}, u32[]{:S(2)}) collective-permute-start(bf16[9,32,256]{2,1,0:T(8,128)(2,1)S(1)} %constant_dynamic-update-slice_fusion), channel_id=1, source_target_pairs={{0,5},{1,4},{2,7},{3,6},{4,1},{5,0},{6,3},{7,2},{8,13},{9,12},{10,... | collective-permute-start | bytes 442376 | tf_op jit(solution)/shard_map/ppermute | solution.py:472
  28.6 1.4 %collective-permute-start.6 = (bf16[9,32,256]{2,1,0:T(8,128)(2,1)S(1)}, bf16[9,32,256]{2,1,0:T(8,128)(2,1)S(1)}, u32[]{:S(2)}, u32[]{:S(2)}) collective-permute-start(bf16[9,32,256]{2,1,0:T(8,128)(2,1)S(1)} %get-tuple-element.81.payload_ref), channel_id=1, source_target_pairs={{0,1},{1,0},{2,3},{3,2},{4,5},{5,4},{6,7},{7,6},{8,9},{9,8},{10,11... | collective-permute-start | bytes 442376 | tf_op jit(solution)/shard_map/ppermute | solution.py:472
  30.2 7.9 %collective-permute-start.7 = (bf16[6,32,256]{2,1,0:T(8,128)(2,1)S(1)}, bf16[6,32,256]{2,1,0:T(8,128)(2,1)S(1)}, u32[]{:S(2)}, u32[]{:S(2)}) collective-permute-start(bf16[6,32,256]{2,1,0:T(8,128)(2,1)S(1)} %pad_maximum_fusion.5), channel_id=1, source_target_pairs={{0,9},{1,8},{2,11},{3,10},{4,13},{5,12},{6,15},{7,14},{8,1},{9,0},... | collective-permute-start | bytes 294920 | tf_op jit(solution)/shard_map/ppermute | solution.py:472
  33.3 9.9 %collective-permute-start.8 = (bf16[8,64,256]{2,1,0:T(8,128)(2,1)S(1)}, bf16[8,64,256]{2,1,0:T(8,128)(2,1)S(1)}, u32[]{:S(2)}, u32[]{:S(2)}) collective-permute-start(bf16[8,64,256]{2,1,0:T(8,128)(2,1)S(1)} %get-tuple-element.88.field_ref), channel_id=1, source_target_pairs={{1,0},{2,1},{3,2},{4,3},{5,4},{6,5},{7,6},{8,7},{9,8},{10,9},{11,1... | collective-permute-start | bytes 786440 | tf_op jit(solution)/shard_map/ppermute | solution.py:475
  38.1 5.1 %collective-permute-start.9 = (bf16[6,32,256]{2,1,0:T(8,128)(2,1)S(1)}, bf16[6,32,256]{2,1,0:T(8,128)(2,1)S(1)}, u32[]{:S(2)}, u32[]{:S(2)}) collective-permute-start(bf16[6,32,256]{2,1,0:T(8,128)(2,1)S(1)} %pad_maximum_fusion.7), channel_id=1, source_target_pairs={{0,3},{1,2},{2,1},{3,0},{4,7},{5,6},{6,5},{7,4},{8,11},{9,10},{10,... | collective-permute-start | bytes 294920 | tf_op jit(solution)/shard_map/ppermute | solution.py:472
  40.2 3.8 %collective-permute-start.11 = (bf16[8,32,256]{2,1,0:T(8,128)(2,1)S(1)}, bf16[8,32,256]{2,1,0:T(8,128)(2,1)S(1)}, u32[]{:S(2)}, u32[]{:S(2)}) collective-permute-start(bf16[8,32,256]{2,1,0:T(8,128)(2,1)S(1)} %get-tuple-element.97), channel_id=1, source_target_pairs={{0,1},{1,2},{2,3},{3,4},{4,5},{5,6},{6,7},{7,8},{8,9},{9,10},{10,1... | collective-permute-start | bytes 393224 | tf_op jit(solution)/shard_map/ppermute | solution.py:475
  43.3 5.9 %collective-permute-start.10 = (bf16[9,32,256]{2,1,0:T(8,128)(2,1)S(1)}, bf16[9,32,256]{2,1,0:T(8,128)(2,1)S(1)}, u32[]{:S(2)}, u32[]{:S(2)}) collective-permute-start(bf16[9,32,256]{2,1,0:T(8,128)(2,1)S(1)} %constant_dynamic-update-slice_fusion.5), channel_id=1, source_target_pairs={{0,5},{1,4},{2,7},{3,6},{4,1},{5,0},{6,3},{7,2},{8,13},{9,12},{10,... | collective-permute-start | bytes 442376 | tf_op jit(solution)/shard_map/ppermute | solution.py:472
  50.5 1.2 %collective-permute-start.12 = (f32[48,128]{1,0:T(8,128)S(1)}, f32[48,128]{1,0:T(8,128)S(1)}, u32[]{:S(2)}, u32[]{:S(2)}) collective-permute-start(f32[48,128]{1,0:T(8,128)S(1)} %get-tuple-element.103), channel_id=1, source_target_pairs={{0,1},{1,0},{2,3},{3,2},{4,5},{5,4},{6,7},{7,6},{8,9},{9,8},{10,11... | collective-permute-start | bytes 73736 | tf_op jit(solution)/shard_map/ppermute | solution.py:472
  51.7 4.8 %collective-permute-start.13 = (f32[48,128]{1,0:T(8,128)S(1)}, f32[48,128]{1,0:T(8,128)S(1)}, u32[]{:S(2)}, u32[]{:S(2)}) collective-permute-start(f32[48,128]{1,0:T(8,128)S(1)} %add.37), channel_id=1, source_target_pairs={{0,9},{1,8},{2,11},{3,10},{4,13},{5,12},{6,15},{7,14},{8,1},{9,0},... | collective-permute-start | bytes 73736 | tf_op jit(solution)/shard_map/ppermute | solution.py:472
  56.5 3.3 %collective-permute-start.14 = (f32[48,128]{1,0:T(8,128)S(1)}, f32[48,128]{1,0:T(8,128)S(1)}, u32[]{:S(2)}, u32[]{:S(2)}) collective-permute-start(f32[48,128]{1,0:T(8,128)S(1)} %add.38), channel_id=1, source_target_pairs={{0,3},{1,2},{2,1},{3,0},{4,7},{5,6},{6,5},{7,4},{8,11},{9,10},{10,... | collective-permute-start | bytes 73736 | tf_op jit(solution)/shard_map/ppermute | solution.py:472
  59.8 3.3 %collective-permute-start.15 = (f32[48,128]{1,0:T(8,128)S(1)}, f32[48,128]{1,0:T(8,128)S(1)}, u32[]{:S(2)}, u32[]{:S(2)}) collective-permute-start(f32[48,128]{1,0:T(8,128)S(1)} %add.39.kept_ref), channel_id=1, source_target_pairs={{0,5},{1,4},{2,7},{3,6},{4,1},{5,0},{6,3},{7,2},{8,13},{9,12},{10,... | collective-permute-start | bytes 73736 | tf_op jit(solution)/shard_map/ppermute | solution.py:472

commit v6 on v5

--- a/solution.py
+++ b/solution.py
@@ -403,6 +403,17 @@
     first_first, image_first = top[:, 2 * R : 3 * R], top[:, :R]
     image_image, second_first = top[:, R : 2 * R], top[:, 3 * R :]
     second_image, second_second = bottom[:, :R], bottom[:, R:]
+    on_diagonal = lax.broadcasted_iota(jnp.int32, (R, R), 0) == lax.broadcasted_iota(jnp.int32, (R, R), 1)
+
+    def shrink(x):
+        trace = jnp.sum(jnp.where(on_diagonal, x, 0.0), axis=0, keepdims=True)
+        return lax.rsqrt(jnp.sum(trace, axis=1, keepdims=True) / R)
+
+    at_first, at_image, at_second = shrink(first_first), shrink(image_image), shrink(second_second)
+    stretch = at_first / at_image
+    first_first, image_first = first_first * at_first * at_first, image_first * at_image * at_first
+    image_image, second_second = image_image * at_image * at_image, second_second * at_second * at_second
+    second_image, second_first = second_image * at_second * at_image, second_first * at_second * at_first
     system = jnp.concatenate(
         [
             jnp.concatenate([image_image, second_image.T, image_first, wide], axis=1),
@@ -437,9 +448,10 @@
     scaled = system[:, 2 * R : 3 * R] / diagonal(system)
     inverse = jnp.concatenate([system[:, 3 * R :], late[:, :R]], axis=1)
     weights = lax.dot_general(scaled, inverse, TN, precision=highest, preferred_element_type=f32)
+    weights = weights * jnp.where(lanes[:R, : 2 * R] < R, at_image, at_second) / at_first
     inverse_zero = lower[:R, 2 * R : 3 * R]
-    hessenberg_ref[:, :R] = exact_nt(inverse_zero, lower[:R, R : 2 * R])
-    hessenberg_ref[:, R:] = lax.dot_general(
+    hessenberg_ref[:, :R] = stretch * exact_nt(inverse_zero, lower[:R, R : 2 * R])
+    hessenberg_ref[:, R:] = stretch * lax.dot_general(
         lower[R:, R : 2 * R], inverse_zero, NT, precision=highest, preferred_element_type=f32
     )
     none = jnp.zeros((R, R), f32)

time: 67.3 us -> 67.5 us (level)
  Pallas kernels: 22.9 us -> 27.7 us
  starting transfers between devices: 25.5 us -> 22.9 us
  waiting for transfers between devices: 16.9 us -> 14.5 us
    pallas_call x14, Pallas kernels: 22.9 us -> 27.7 us  [call(): pl.pallas_call(kernel, out_shape=outs, in_specs=[spec(s) for s in spaces]...]
    ppermute x12, starting transfers between devices: 18.4 us -> 15.8 us  [across(): return lax.ppermute(x, 'leaf', [(i, i ^ b) for i in range(devices)])]
    ppermute x12, waiting for transfers between devices: 16.9 us -> 14.5 us  [across(): return lax.ppermute(x, 'leaf', [(i, i ^ b) for i in range(devices)])]
  transfers between devices with their start and end apart: 16 -> 16, of which waited for: 11 -> 11; matrix products, arithmetic and copies ran while one was open for 0% -> 0% of each run, Pallas kernels for 18% -> 25%
where the time goes in v6:
time: 67.5 us; the launch traced here: 67.1 us
  Pallas kernels  27.7 us (41%)
  starting transfers between devices  22.9 us (34%)
  waiting for transfers between devices  14.5 us (21%)
  between operations  1.63 us (2%)
    pallas_call x14, Pallas kernels, call(): pl.pallas_call(kernel, out_shape=outs, in_specs=[spec(s) for s in spaces]...  27.7 us
    ppermute x12, starting transfers between devices, across(): return lax.ppermute(x, 'leaf', [(i, i ^ b) for i in range(devices)])  15.8 us
    ppermute x12, waiting for transfers between devices, across(): return lax.ppermute(x, 'leaf', [(i, i ^ b) for i in range(devices)])  14.5 us
    ppermute x4, starting transfers between devices, shift(): lax.ppermute(x, 'leaf', [(i, i + by) for i in range(devices) if 0 <= i +...  7.14 us
  transfers between devices with their start and end apart: 16, of which 11 were waited for; matrix products, arithmetic and copies ran while one was open for 0% of the time, Pallas kernels for 25%

profile of v6, /device:TPU:0, one launch (start us, length us, event | category | flops | bytes accessed | tf_op | source)
XLA Modules:
  0.0 67.1 jit_solution(11064793586667989988)
XLA Ops:
  0.7 4.3 %shard_map.103 = (s32[2,64]{1,0:T(2,128)S(1)}, bf16[64,256,256]{2,1,0:T(8,128)(2,1)S(1)}, bf16[8,64,256]{2,1,0:T(8,128)(2,1)S(1)}, f32[32,256]{1,0:T(8,128)S(1)}...) custom-call(s32[1]{0:T(128)} %bitcast.me_ref, s32[2,128]{1,0:T(2,128)} %pairs_hbm.1, s32[128]{0:T(128)} %slots_hbm.1, ...), custom_call_target="tpu_custom_call" | custom-call | flops 100000000 | bytes 1000000 | tf_op jit(solution)/shard_map/pallas_call | solution.py:28
  5.5 1.2 %shard_map.104 = (f32[8,32,256]{2,1,0:T(8,128)S(1)}, bf16[2,256,256]{2,1,0:T(8,128)(2,1)S(1)}, f32[32,128]{1,0:T(8,128)S(1)}) custom-call(bf16[32,256,256]{2,1,0:T(8,128)(2,1)S(1)} %get-tuple-element.70.coupled_ref, bf16[17,32,256]{2,1,0:T(8,128)(2,1)S(1)} %get-tuple-element.58.payload_ref, bf16[256,256]{1,0:T(8,128)(2,1)S(1)} %bitcast.4, f32[32,2048]{1,0:T(8,128)S(1)} %copy-done), custom_call_target="tpu_custom_call" | custom-call | flops 100000000 | bytes 1000000 | tf_op jit(solution)/shard_map/pallas_call | solution.py:28
  6.9 3.8 %collective-permute-start.1 = (bf16[6,32,256]{2,1,0:T(8,128)(2,1)S(1)}, bf16[6,32,256]{2,1,0:T(8,128)(2,1)S(1)}, u32[]{:S(2)}, u32[]{:S(2)}) collective-permute-start(bf16[6,32,256]{2,1,0:T(8,128)(2,1)S(1)} %pad_maximum_fusion.2), channel_id=1, source_target_pairs={{0,9},{1,8},{2,11},{3,10},{4,13},{5,12},{6,15},{7,14},{8,1},{9,0},... | collective-permute-start | bytes 294920 | tf_op jit(solution)/shard_map/ppermute | solution.py:484
  11.3 1.3 %collective-permute-start.2 = (bf16[8,64,256]{2,1,0:T(8,128)(2,1)S(1)}, bf16[8,64,256]{2,1,0:T(8,128)(2,1)S(1)}, u32[]{:S(2)}, u32[]{:S(2)}) collective-permute-start(bf16[8,64,256]{2,1,0:T(8,128)(2,1)S(1)} %get-tuple-element.64.field_ref), channel_id=1, source_target_pairs={{1,0},{2,1},{3,2},{4,3},{5,4},{6,5},{7,6},{8,7},{9,8},{10,9},{11,1... | collective-permute-start | bytes 786440 | tf_op jit(solution)/shard_map/ppermute | solution.py:487
  12.6 2.4 %shard_map.105 = (f32[8,32,256]{2,1,0:T(8,128)S(1)}, bf16[8,32,256]{2,1,0:T(8,128)(2,1)S(1)}) custom-call(s32[2,64]{1,0:T(2,128)S(1)} %get-tuple-element.65.pairs_ref, s32[1]{0:T(128)S(6)} %copy.19.count_ref, bf16[64,256,256]{2,1,0:T(8,128)(2,1)S(1)} %get-tuple-element.66.blocks_ref, bf16[8,64,256]{2,1,0:T(8,128)(2,1)S(1)} %get-tuple-element.64.field_ref), custom_call_target="tpu_custom_call" | custom-call | flops 100000000 | bytes 12582912 | tf_op jit(solution)/shard_map/pallas_call | solution.py:28
  15.0 0.7 %collective-permute-done.1 = bf16[6,32,256]{2,1,0:T(8,128)(2,1)S(1)} collective-permute-done((bf16[6,32,256]{2,1,0:T(8,128)(2,1)S(1)}, bf16[6,32,256]{2,1,0:T(8,128)(2,1)S(1)}, u32[]{:S(2)}, u32[]{:S(2)}) %collective-permute-start.1) | collective-permute-done | bytes 98336 | tf_op jit(solution)/shard_map/ppermute | solution.py:484
  15.8 1.7 %collective-permute-start.3 = (bf16[6,32,256]{2,1,0:T(8,128)(2,1)S(1)}, bf16[6,32,256]{2,1,0:T(8,128)(2,1)S(1)}, u32[]{:S(2)}, u32[]{:S(2)}) collective-permute-start(bf16[6,32,256]{2,1,0:T(8,128)(2,1)S(1)} %pad_maximum_fusion.4), channel_id=1, source_target_pairs={{0,3},{1,2},{2,1},{3,0},{4,7},{5,6},{6,5},{7,4},{8,11},{9,10},{10,... | collective-permute-start | bytes 294920 | tf_op jit(solution)/shard_map/ppermute | solution.py:484
  17.4 2.3 %collective-permute-start.5 = (bf16[8,32,256]{2,1,0:T(8,128)(2,1)S(1)}, bf16[8,32,256]{2,1,0:T(8,128)(2,1)S(1)}, u32[]{:S(2)}, u32[]{:S(2)}) collective-permute-start(bf16[8,32,256]{2,1,0:T(8,128)(2,1)S(1)} %get-tuple-element.77), channel_id=1, source_target_pairs={{0,1},{1,2},{2,3},{3,4},{4,5},{5,6},{6,7},{7,8},{8,9},{9,10},{10,1... | collective-permute-start | bytes 393224 | tf_op jit(solution)/shard_map/ppermute | solution.py:487
  19.7 1.1 %shard_map.106 = (bf16[16,256,256]{2,1,0:T(8,128)(2,1)S(1)}, bf16[16,256,256]{2,1,0:T(8,128)(2,1)S(1)}) custom-call(bf16[32,256,256]{2,1,0:T(8,128)(2,1)S(1)} %get-tuple-element.70.coupled_ref), custom_call_target="tpu_custom_call" | custom-call | flops 100000000 | bytes 1000000 | tf_op jit(solution)/shard_map/pallas_call | solution.py:28
  21.6 1.3 %collective-permute-start.4 = (bf16[9,32,256]{2,1,0:T(8,128)(2,1)S(1)}, bf16[9,32,256]{2,1,0:T(8,128)(2,1)S(1)}, u32[]{:S(2)}, u32[]{:S(2)}) collective-permute-start(bf16[9,32,256]{2,1,0:T(8,128)(2,1)S(1)} %constant_dynamic-update-slice_fusion), channel_id=1, source_target_pairs={{0,5},{1,4},{2,7},{3,6},{4,1},{5,0},{6,3},{7,2},{8,13},{9,12},{10,... | collective-permute-start | bytes 442376 | tf_op jit(solution)/shard_map/ppermute | solution.py:484
  22.8 3.7 %shard_map.107 = (f32[8,32,256]{2,1,0:T(8,128)S(1)}, f32[32,256]{1,0:T(8,128)S(1)}) custom-call(s32[2,64]{1,0:T(2,128)S(1)} %get-tuple-element.65.pairs_ref, s32[1]{0:T(128)S(6)} %copy.19.count_ref, bf16[64,256,256]{2,1,0:T(8,128)(2,1)S(1)} %get-tuple-element.66.blocks_ref, bf16[8,64,256]{2,1,0:T(8,128)(2,1)S(1)} %get-tuple-element.64.field_ref, ...), custom_call_target="tpu_custom_call" | custom-call | flops 100000000 | bytes 12582912 | tf_op jit(solution)/shard_map/pallas_call | solution.py:28
  26.6 1.0 %collective-permute-done.4 = bf16[9,32,256]{2,1,0:T(8,128)(2,1)S(1)} collective-permute-done((bf16[9,32,256]{2,1,0:T(8,128)(2,1)S(1)}, bf16[9,32,256]{2,1,0:T(8,128)(2,1)S(1)}, u32[]{:S(2)}, u32[]{:S(2)}) %collective-permute-start.4) | collective-permute-done | bytes 147488 | tf_op jit(solution)/shard_map/ppermute | solution.py:484
  27.6 1.1 %shard_map.108 = (bf16[64,256]{1,0:T(8,128)(2,1)S(1)}, f32[32,256]{1,0:T(8,128)S(1)}, bf16[9,32,256]{2,1,0:T(8,128)(2,1)S(1)}) custom-call(bf16[16,256,256]{2,1,0:T(8,128)(2,1)S(1)} %get-tuple-element.73.merged_ref, bf16[8,32,256]{2,1,0:T(8,128)(2,1)S(1)} %pad_maximum_fusion.low_ref, bf16[8,32,256]{2,1,0:T(8,128)(2,1)S(1)} %slice.138.high_ref, ...), custom_call_target="tpu_custom_call" | custom-call | flops 100000000 | bytes 1000000 | tf_op jit(solution)/shard_map/pallas_call | solution.py:28
  29.1 1.0 %collective-permute-done.6 = bf16[9,32,256]{2,1,0:T(8,128)(2,1)S(1)} collective-permute-done((bf16[9,32,256]{2,1,0:T(8,128)(2,1)S(1)}, bf16[9,32,256]{2,1,0:T(8,128)(2,1)S(1)}, u32[]{:S(2)}, u32[]{:S(2)}) %collective-permute-start.6) | collective-permute-done | bytes 147488 | tf_op jit(solution)/shard_map/ppermute | solution.py:484
  30.2 1.5 %collective-permute-start.7 = (bf16[6,32,256]{2,1,0:T(8,128)(2,1)S(1)}, bf16[6,32,256]{2,1,0:T(8,128)(2,1)S(1)}, u32[]{:S(2)}, u32[]{:S(2)}) collective-permute-start(bf16[6,32,256]{2,1,0:T(8,128)(2,1)S(1)} %pad_maximum_fusion.5), channel_id=1, source_target_pairs={{0,9},{1,8},{2,11},{3,10},{4,13},{5,12},{6,15},{7,14},{8,1},{9,0},... | collective-permute-start | bytes 294920 | tf_op jit(solution)/shard_map/ppermute | solution.py:484
  31.9 1.3 %collective-permute-start.8 = (bf16[8,64,256]{2,1,0:T(8,128)(2,1)S(1)}, bf16[8,64,256]{2,1,0:T(8,128)(2,1)S(1)}, u32[]{:S(2)}, u32[]{:S(2)}) collective-permute-start(bf16[8,64,256]{2,1,0:T(8,128)(2,1)S(1)} %get-tuple-element.88.field_ref), channel_id=1, source_target_pairs={{1,0},{2,1},{3,2},{4,3},{5,4},{6,5},{7,6},{8,7},{9,8},{10,9},{11,1... | collective-permute-start | bytes 786440 | tf_op jit(solution)/shard_map/ppermute | solution.py:487
  33.2 2.4 %shard_map.111 = (f32[8,32,256]{2,1,0:T(8,128)S(1)}, bf16[8,32,256]{2,1,0:T(8,128)(2,1)S(1)}) custom-call(s32[2,64]{1,0:T(2,128)S(1)} %get-tuple-element.65.pairs_ref, s32[1]{0:T(128)S(6)} %copy.19.count_ref, bf16[64,256,256]{2,1,0:T(8,128)(2,1)S(1)} %get-tuple-element.66.blocks_ref, bf16[8,64,256]{2,1,0:T(8,128)(2,1)S(1)} %get-tuple-element.88.field_ref), custom_call_target="tpu_custom_call" | custom-call | flops 100000000 | bytes 12582912 | tf_op jit(solution)/shard_map/pallas_call | solution.py:28
  35.6 2.4 %collective-permute-done.7 = bf16[6,32,256]{2,1,0:T(8,128)(2,1)S(1)} collective-permute-done((bf16[6,32,256]{2,1,0:T(8,128)(2,1)S(1)}, bf16[6,32,256]{2,1,0:T(8,128)(2,1)S(1)}, u32[]{:S(2)}, u32[]{:S(2)}) %collective-permute-start.7) | collective-permute-done | bytes 98336 | tf_op jit(solution)/shard_map/ppermute | solution.py:484
  38.1 2.2 %collective-permute-start.9 = (bf16[6,32,256]{2,1,0:T(8,128)(2,1)S(1)}, bf16[6,32,256]{2,1,0:T(8,128)(2,1)S(1)}, u32[]{:S(2)}, u32[]{:S(2)}) collective-permute-start(bf16[6,32,256]{2,1,0:T(8,128)(2,1)S(1)} %pad_maximum_fusion.7), channel_id=1, source_target_pairs={{0,3},{1,2},{2,1},{3,0},{4,7},{5,6},{6,5},{7,4},{8,11},{9,10},{10,... | collective-permute-start | bytes 294920 | tf_op jit(solution)/shard_map/ppermute | solution.py:484
  40.2 2.2 %collective-permute-start.11 = (bf16[8,32,256]{2,1,0:T(8,128)(2,1)S(1)}, bf16[8,32,256]{2,1,0:T(8,128)(2,1)S(1)}, u32[]{:S(2)}, u32[]{:S(2)}) collective-permute-start(bf16[8,32,256]{2,1,0:T(8,128)(2,1)S(1)} %get-tuple-element.97), channel_id=1, source_target_pairs={{0,1},{1,2},{2,3},{3,4},{4,5},{5,6},{6,7},{7,8},{8,9},{9,10},{10,1... | collective-permute-start | bytes 393224 | tf_op jit(solution)/shard_map/ppermute | solution.py:487
  43.2 0.7 %collective-permute-start.10 = (bf16[9,32,256]{2,1,0:T(8,128)(2,1)S(1)}, bf16[9,32,256]{2,1,0:T(8,128)(2,1)S(1)}, u32[]{:S(2)}, u32[]{:S(2)}) collective-permute-start(bf16[9,32,256]{2,1,0:T(8,128)(2,1)S(1)} %constant_dynamic-update-slice_fusion.5), channel_id=1, source_target_pairs={{0,5},{1,4},{2,7},{3,6},{4,1},{5,0},{6,3},{7,2},{8,13},{9,12},{10,... | collective-permute-start | bytes 442376 | tf_op jit(solution)/shard_map/ppermute | solution.py:484
  44.0 4.4 %shard_map.113 = (f32[8,32,256]{2,1,0:T(8,128)S(1)}, f32[32,256]{1,0:T(8,128)S(1)}, f32[32,128]{1,0:T(8,128)S(1)}) custom-call(s32[2,64]{1,0:T(2,128)S(1)} %get-tuple-element.65.pairs_ref, s32[1]{0:T(128)S(6)} %copy.19.count_ref, bf16[64,256,256]{2,1,0:T(8,128)(2,1)S(1)} %get-tuple-element.66.blocks_ref, ...), custom_call_target="tpu_custom_call" | custom-call | flops 100000000 | bytes 12582912 | tf_op jit(solution)/shard_map/pallas_call | solution.py:28
  48.4 0.7 %collective-permute-done.10 = bf16[9,32,256]{2,1,0:T(8,128)(2,1)S(1)} collective-permute-done((bf16[9,32,256]{2,1,0:T(8,128)(2,1)S(1)}, bf16[9,32,256]{2,1,0:T(8,128)(2,1)S(1)}, u32[]{:S(2)}, u32[]{:S(2)}) %collective-permute-start.10) | collective-permute-done | bytes 147488 | tf_op jit(solution)/shard_map/ppermute | solution.py:484
  49.2 1.3 %shard_map.114 = (bf16[64,256]{1,0:T(8,128)(2,1)S(1)}, f32[48,128]{1,0:T(8,128)S(1)}) custom-call(bf16[16,256,256]{2,1,0:T(8,128)(2,1)S(1)} %get-tuple-element.73.merged_ref, bf16[8,32,256]{2,1,0:T(8,128)(2,1)S(1)} %pad_maximum_fusion.1.low_ref, bf16[8,32,256]{2,1,0:T(8,128)(2,1)S(1)} %slice.146.high_ref, f32[1,32,256]{2,1,0:T(8,128)S(1)} %slice.147.kept_ref, ...), custom_call_target="tpu_custom_call" | custom-call | flops 100000000 | bytes 1000000 | tf_op jit(solution)/shard_map/pallas_call | solution.py:28
  50.6 1.1 %collective-permute-done.12 = f32[48,128]{1,0:T(8,128)S(1)} collective-permute-done((f32[48,128]{1,0:T(8,128)S(1)}, f32[48,128]{1,0:T(8,128)S(1)}, u32[]{:S(2)}, u32[]{:S(2)}) %collective-permute-start.12) | collective-permute-done | bytes 24608 | tf_op jit(solution)/shard_map/ppermute | solution.py:484
  51.7 0.8 %collective-permute-start.13 = (f32[48,128]{1,0:T(8,128)S(1)}, f32[48,128]{1,0:T(8,128)S(1)}, u32[]{:S(2)}, u32[]{:S(2)}) collective-permute-start(f32[48,128]{1,0:T(8,128)S(1)} %add.37), channel_id=1, source_target_pairs={{0,9},{1,8},{2,11},{3,10},{4,13},{5,12},{6,15},{7,14},{8,1},{9,0},... | collective-permute-start | bytes 73736 | tf_op jit(solution)/shard_map/ppermute | solution.py:484
  52.7 3.2 %collective-permute-done.13 = f32[48,128]{1,0:T(8,128)S(1)} collective-permute-done((f32[48,128]{1,0:T(8,128)S(1)}, f32[48,128]{1,0:T(8,128)S(1)}, u32[]{:S(2)}, u32[]{:S(2)}) %collective-permute-start.13) | collective-permute-done | bytes 24608 | tf_op jit(solution)/shard_map/ppermute | solution.py:484
  55.9 2.0 %collective-permute-start.14 = (f32[48,128]{1,0:T(8,128)S(1)}, f32[48,128]{1,0:T(8,128)S(1)}, u32[]{:S(2)}, u32[]{:S(2)}) collective-permute-start(f32[48,128]{1,0:T(8,128)S(1)} %add.38), channel_id=1, source_target_pairs={{0,3},{1,2},{2,1},{3,0},{4,7},{5,6},{6,5},{7,4},{8,11},{9,10},{10,... | collective-permute-start | bytes 73736 | tf_op jit(solution)/shard_map/ppermute | solution.py:484
  57.9 1.5 %collective-permute-done.14 = f32[48,128]{1,0:T(8,128)S(1)} collective-permute-done((f32[48,128]{1,0:T(8,128)S(1)}, f32[48,128]{1,0:T(8,128)S(1)}, u32[]{:S(2)}, u32[]{:S(2)}) %collective-permute-start.14) | collective-permute-done | bytes 24608 | tf_op jit(solution)/shard_map/ppermute | solution.py:484
  59.4 1.1 %collective-permute-start.15 = (f32[48,128]{1,0:T(8,128)S(1)}, f32[48,128]{1,0:T(8,128)S(1)}, u32[]{:S(2)}, u32[]{:S(2)}) collective-permute-start(f32[48,128]{1,0:T(8,128)S(1)} %add.39.kept_ref), channel_id=1, source_target_pairs={{0,5},{1,4},{2,7},{3,6},{4,1},{5,0},{6,3},{7,2},{8,13},{9,12},{10,... | collective-permute-start | bytes 73736 | tf_op jit(solution)/shard_map/ppermute | solution.py:484
  60.5 2.2 %collective-permute-done.15.got_ref = f32[48,128]{1,0:T(8,128)S(1)} collective-permute-done((f32[48,128]{1,0:T(8,128)S(1)}, f32[48,128]{1,0:T(8,128)S(1)}, u32[]{:S(2)}, u32[]{:S(2)}) %collective-permute-start.15) | collective-permute-done | bytes 24608 | tf_op jit(solution)/shard_map/ppermute | solution.py:484
  62.7 4.5 %shard_map.116 = (f32[32,2048]{1,0:T(8,128)}, f32[32,2048]{1,0:T(8,128)}, f32[32,64]{1,0:T(8,128)}) custom-call(f32[48,128]{1,0:T(8,128)S(1)} %add.39.kept_ref, f32[48,128]{1,0:T(8,128)S(1)} %collective-permute-done.15.got_ref, f32[32,2048]{1,0:T(8,128)S(1)} %copy-done, f32[8,32,256]{2,1,0:T(8,128)S(1)} %get-tuple-element.93.image_ref, ...), custom_call_target="tpu_custom_call" | custom-call | flops 100000000 | bytes 1000000 | tf_op jit(solution)/shard_map/pallas_call | solution.py:28
  (53 shorter events, 3.3 us)
Async XLA Ops:
  0.6 4.9 %copy-start = (f32[32,2048]{1,0:T(8,128)S(1)}, f32[32,2048]{1,0:T(8,128)}, u32[]{:S(2)}) copy-start(f32[32,2048]{1,0:T(8,128)} %right_ref.7) | copy-start | bytes 786436
  0.6 4.9 %copy-start.1 = (bf16[8,32,256]{2,1,0:T(8,128)(2,1)S(1)}, bf16[8,32,256]{2,1,0:T(8,128)(2,1)}, u32[]{:S(2)}) copy-start(bf16[8,32,256]{2,1,0:T(8,128)(2,1)} %param.14) | copy-start | bytes 393220
  5.0 1.8 %collective-permute-start = (bf16[17,32,256]{2,1,0:T(8,128)(2,1)S(1)}, bf16[17,32,256]{2,1,0:T(8,128)(2,1)S(1)}, u32[]{:S(2)}, u32[]{:S(2)}) collective-permute-start(bf16[17,32,256]{2,1,0:T(8,128)(2,1)S(1)} %get-tuple-element.58.payload_ref), channel_id=1, source_target_pairs={{0,1},{1,0},{2,3},{3,2},{4,5},{5,4},{6,7},{7,6},{8,9},{9,8},{10,11... | collective-permute-start | bytes 835592 | tf_op jit(solution)/shard_map/ppermute | solution.py:484
  6.9 8.8 %collective-permute-start.1 = (bf16[6,32,256]{2,1,0:T(8,128)(2,1)S(1)}, bf16[6,32,256]{2,1,0:T(8,128)(2,1)S(1)}, u32[]{:S(2)}, u32[]{:S(2)}) collective-permute-start(bf16[6,32,256]{2,1,0:T(8,128)(2,1)S(1)} %pad_maximum_fusion.2), channel_id=1, source_target_pairs={{0,9},{1,8},{2,11},{3,10},{4,13},{5,12},{6,15},{7,14},{8,1},{9,0},... | collective-permute-start | bytes 294920 | tf_op jit(solution)/shard_map/ppermute | solution.py:484
  11.3 10.2 %collective-permute-start.2 = (bf16[8,64,256]{2,1,0:T(8,128)(2,1)S(1)}, bf16[8,64,256]{2,1,0:T(8,128)(2,1)S(1)}, u32[]{:S(2)}, u32[]{:S(2)}) collective-permute-start(bf16[8,64,256]{2,1,0:T(8,128)(2,1)S(1)} %get-tuple-element.64.field_ref), channel_id=1, source_target_pairs={{1,0},{2,1},{3,2},{4,3},{5,4},{6,5},{7,6},{8,7},{9,8},{10,9},{11,1... | collective-permute-start | bytes 786440 | tf_op jit(solution)/shard_map/ppermute | solution.py:487
  15.8 5.8 %collective-permute-start.3 = (bf16[6,32,256]{2,1,0:T(8,128)(2,1)S(1)}, bf16[6,32,256]{2,1,0:T(8,128)(2,1)S(1)}, u32[]{:S(2)}, u32[]{:S(2)}) collective-permute-start(bf16[6,32,256]{2,1,0:T(8,128)(2,1)S(1)} %pad_maximum_fusion.4), channel_id=1, source_target_pairs={{0,3},{1,2},{2,1},{3,0},{4,7},{5,6},{6,5},{7,4},{8,11},{9,10},{10,... | collective-permute-start | bytes 294920 | tf_op jit(solution)/shard_map/ppermute | solution.py:484
  17.4 5.4 %collective-permute-start.5 = (bf16[8,32,256]{2,1,0:T(8,128)(2,1)S(1)}, bf16[8,32,256]{2,1,0:T(8,128)(2,1)S(1)}, u32[]{:S(2)}, u32[]{:S(2)}) collective-permute-start(bf16[8,32,256]{2,1,0:T(8,128)(2,1)S(1)} %get-tuple-element.77), channel_id=1, source_target_pairs={{0,1},{1,2},{2,3},{3,4},{4,5},{5,6},{6,7},{7,8},{8,9},{9,10},{10,1... | collective-permute-start | bytes 393224 | tf_op jit(solution)/shard_map/ppermute | solution.py:487
  21.6 6.0 %collective-permute-start.4 = (bf16[9,32,256]{2,1,0:T(8,128)(2,1)S(1)}, bf16[9,32,256]{2,1,0:T(8,128)(2,1)S(1)}, u32[]{:S(2)}, u32[]{:S(2)}) collective-permute-start(bf16[9,32,256]{2,1,0:T(8,128)(2,1)S(1)} %constant_dynamic-update-slice_fusion), channel_id=1, source_target_pairs={{0,5},{1,4},{2,7},{3,6},{4,1},{5,0},{6,3},{7,2},{8,13},{9,12},{10,... | collective-permute-start | bytes 442376 | tf_op jit(solution)/shard_map/ppermute | solution.py:484
  28.6 1.4 %collective-permute-start.6 = (bf16[9,32,256]{2,1,0:T(8,128)(2,1)S(1)}, bf16[9,32,256]{2,1,0:T(8,128)(2,1)S(1)}, u32[]{:S(2)}, u32[]{:S(2)}) collective-permute-start(bf16[9,32,256]{2,1,0:T(8,128)(2,1)S(1)} %get-tuple-element.81.payload_ref), channel_id=1, source_target_pairs={{0,1},{1,0},{2,3},{3,2},{4,5},{5,4},{6,7},{7,6},{8,9},{9,8},{10,11... | collective-permute-start | bytes 442376 | tf_op jit(solution)/shard_map/ppermute | solution.py:484
  30.2 7.8 %collective-permute-start.7 = (bf16[6,32,256]{2,1,0:T(8,128)(2,1)S(1)}, bf16[6,32,256]{2,1,0:T(8,128)(2,1)S(1)}, u32[]{:S(2)}, u32[]{:S(2)}) collective-permute-start(bf16[6,32,256]{2,1,0:T(8,128)(2,1)S(1)} %pad_maximum_fusion.5), channel_id=1, source_target_pairs={{0,9},{1,8},{2,11},{3,10},{4,13},{5,12},{6,15},{7,14},{8,1},{9,0},... | collective-permute-start | bytes 294920 | tf_op jit(solution)/shard_map/ppermute | solution.py:484
  31.9 11.3 %collective-permute-start.8 = (bf16[8,64,256]{2,1,0:T(8,128)(2,1)S(1)}, bf16[8,64,256]{2,1,0:T(8,128)(2,1)S(1)}, u32[]{:S(2)}, u32[]{:S(2)}) collective-permute-start(bf16[8,64,256]{2,1,0:T(8,128)(2,1)S(1)} %get-tuple-element.88.field_ref), channel_id=1, source_target_pairs={{1,0},{2,1},{3,2},{4,3},{5,4},{6,5},{7,6},{8,7},{9,8},{10,9},{11,1... | collective-permute-start | bytes 786440 | tf_op jit(solution)/shard_map/ppermute | solution.py:487
  38.1 5.1 %collective-permute-start.9 = (bf16[6,32,256]{2,1,0:T(8,128)(2,1)S(1)}, bf16[6,32,256]{2,1,0:T(8,128)(2,1)S(1)}, u32[]{:S(2)}, u32[]{:S(2)}) collective-permute-start(bf16[6,32,256]{2,1,0:T(8,128)(2,1)S(1)} %pad_maximum_fusion.7), channel_id=1, source_target_pairs={{0,3},{1,2},{2,1},{3,0},{4,7},{5,6},{6,5},{7,4},{8,11},{9,10},{10,... | collective-permute-start | bytes 294920 | tf_op jit(solution)/shard_map/ppermute | solution.py:484
  40.2 3.8 %collective-permute-start.11 = (bf16[8,32,256]{2,1,0:T(8,128)(2,1)S(1)}, bf16[8,32,256]{2,1,0:T(8,128)(2,1)S(1)}, u32[]{:S(2)}, u32[]{:S(2)}) collective-permute-start(bf16[8,32,256]{2,1,0:T(8,128)(2,1)S(1)} %get-tuple-element.97), channel_id=1, source_target_pairs={{0,1},{1,2},{2,3},{3,4},{4,5},{5,6},{6,7},{7,8},{8,9},{9,10},{10,1... | collective-permute-start | bytes 393224 | tf_op jit(solution)/shard_map/ppermute | solution.py:487
  43.2 5.9 %collective-permute-start.10 = (bf16[9,32,256]{2,1,0:T(8,128)(2,1)S(1)}, bf16[9,32,256]{2,1,0:T(8,128)(2,1)S(1)}, u32[]{:S(2)}, u32[]{:S(2)}) collective-permute-start(bf16[9,32,256]{2,1,0:T(8,128)(2,1)S(1)} %constant_dynamic-update-slice_fusion.5), channel_id=1, source_target_pairs={{0,5},{1,4},{2,7},{3,6},{4,1},{5,0},{6,3},{7,2},{8,13},{9,12},{10,... | collective-permute-start | bytes 442376 | tf_op jit(solution)/shard_map/ppermute | solution.py:484
  50.5 1.2 %collective-permute-start.12 = (f32[48,128]{1,0:T(8,128)S(1)}, f32[48,128]{1,0:T(8,128)S(1)}, u32[]{:S(2)}, u32[]{:S(2)}) collective-permute-start(f32[48,128]{1,0:T(8,128)S(1)} %get-tuple-element.103), channel_id=1, source_target_pairs={{0,1},{1,0},{2,3},{3,2},{4,5},{5,4},{6,7},{7,6},{8,9},{9,8},{10,11... | collective-permute-start | bytes 73736 | tf_op jit(solution)/shard_map/ppermute | solution.py:484
  51.7 4.2 %collective-permute-start.13 = (f32[48,128]{1,0:T(8,128)S(1)}, f32[48,128]{1,0:T(8,128)S(1)}, u32[]{:S(2)}, u32[]{:S(2)}) collective-permute-start(f32[48,128]{1,0:T(8,128)S(1)} %add.37), channel_id=1, source_target_pairs={{0,9},{1,8},{2,11},{3,10},{4,13},{5,12},{6,15},{7,14},{8,1},{9,0},... | collective-permute-start | bytes 73736 | tf_op jit(solution)/shard_map/ppermute | solution.py:484
  55.9 3.5 %collective-permute-start.14 = (f32[48,128]{1,0:T(8,128)S(1)}, f32[48,128]{1,0:T(8,128)S(1)}, u32[]{:S(2)}, u32[]{:S(2)}) collective-permute-start(f32[48,128]{1,0:T(8,128)S(1)} %add.38), channel_id=1, source_target_pairs={{0,3},{1,2},{2,1},{3,0},{4,7},{5,6},{6,5},{7,4},{8,11},{9,10},{10,... | collective-permute-start | bytes 73736 | tf_op jit(solution)/shard_map/ppermute | solution.py:484
  59.4 3.3 %collective-permute-start.15 = (f32[48,128]{1,0:T(8,128)S(1)}, f32[48,128]{1,0:T(8,128)S(1)}, u32[]{:S(2)}, u32[]{:S(2)}) collective-permute-start(f32[48,128]{1,0:T(8,128)S(1)} %add.39.kept_ref), channel_id=1, source_target_pairs={{0,5},{1,4},{2,7},{3,6},{4,1},{5,0},{6,3},{7,2},{8,13},{9,12},{10,... | collective-permute-start | bytes 73736 | tf_op jit(solution)/shard_map/ppermute | solution.py:484

commit v7 on v6

--- a/solution.py
+++ b/solution.py
@@ -56,6 +56,18 @@
 
 def join_rows(x):
     return x[:R] + x[R:]
+
+
+def split_nt(x, high, low):
+    return join_rows(dot_nt(x, high)) + dot_nt(x[:R], low)
+
+
+def stack(*halves):
+    zero = jnp.zeros((R, halves[0 if halves[0] is not None else 2].shape[1]), bf16)
+    return (
+        jnp.concatenate([zero if x is None else x[:R] for x in halves], axis=0),
+        jnp.concatenate([zero if x is None else x[R:] for x in halves], axis=0),
+    )
 
 
 def lane_group(shape):
@@ -192,7 +204,7 @@
             payload_ref[1 + d] = (value - high.astype(f32)).astype(bf16)
 
 
-def keep_one_kernel(coupled_ref, payload_ref, basis_ref, right_ref, kept_ref, cross_ref, corner_ref):
+def keep_one_kernel(coupled_ref, payload_ref, basis_ref, field_ref, kept_ref, cross_ref, corner_ref):
     devices = coupled_ref.shape[0] // 2
     proj = payload_ref[0]
     for d in range(devices // 2):
@@ -205,10 +217,9 @@
     cross_ref[0] = high
     cross_ref[1] = (cross - high.astype(f32)).astype(bf16)
     corner = jnp.zeros((R, 4 * R), f32)
-    zero = jnp.zeros((R, PANEL), f32)
-    for c in range(right_ref.shape[1] // PANEL):
-        right = right_ref[:, c * PANEL : (c + 1) * PANEL]
-        corner = corner + exact_nt(right, jnp.concatenate([zero, zero, right, zero], axis=0))
+    for c in range(field_ref.shape[0]):
+        right = field_ref[c]
+        corner = corner + split_nt(right, *stack(None, None, right, None))
     corner_ref[...] = corner
 
 
@@ -241,7 +252,7 @@
     next_ref[...] = total[clusters : 2 * clusters].astype(bf16)
 
 
-def near_rows_kernel(pairs_ref, count_ref, blocks_ref, field_ref, after_ref, begun_ref, back_ref, basis_ref,
+def near_rows(pairs_ref, count_ref, blocks_ref, field_ref, after_ref, begun_ref, back_ref, basis_ref,
                      out_ref, proj_ref, window, total):
     clusters = field_ref.shape[0]
     window[:clusters] = field_ref[...]
@@ -259,13 +270,22 @@
     out_ref[...] = near
     split = jnp.concatenate([split_rows(near[c]) for c in range(clusters)], axis=0)
     proj_ref[...] = project(split, basis_ref[...])
+    return split
+
+
+def rows_one_kernel(*refs):
+    near_rows(*refs)
 
 
 def rows_two_kernel(pairs_ref, count_ref, blocks_ref, field_ref, after_ref, begun_ref, back_ref, basis_ref,
-                    right_ref, image_ref, out_ref, proj_ref, gram_ref, window, total):
-    near_rows_kernel(pairs_ref, count_ref, blocks_ref, field_ref, after_ref, begun_ref, back_ref, basis_ref,
-                     out_ref, proj_ref, window, total)
-    gram_two(right_ref, image_ref, out_ref, gram_ref)
+                    right_ref, out_ref, proj_ref, gram_ref, window, total):
+    split = near_rows(pairs_ref, count_ref, blocks_ref, field_ref, after_ref, begun_ref, back_ref, basis_ref,
+                      out_ref, proj_ref, window, total)
+    gram = jnp.zeros((R, 4 * R), f32)
+    for c in range(field_ref.shape[0]):
+        near = split[c * 2 * R : (c + 1) * 2 * R]
+        gram = gram + split_nt(near, *stack(right_ref[c], field_ref[c], near, None))
+    gram_ref[...] = gram
 
 
 def merge_kernel(coupled_ref, out_ref, turned_ref):
@@ -319,19 +339,8 @@
 
 def gram_one_kernel(corner_ref, right_ref, image_ref, gram_ref):
     gram = corner_ref[...]
-    zero = jnp.zeros((R, PANEL), f32)
     for c in range(image_ref.shape[0]):
-        right, image = right_ref[:, c * PANEL : (c + 1) * PANEL], image_ref[c]
-        gram = gram + exact_nt(image, jnp.concatenate([right, image, zero, zero], axis=0))
-    gram_ref[...] = gram
-
-
-def gram_two(right_ref, image_ref, near_ref, gram_ref):
-    gram = jnp.zeros((R, 4 * R), f32)
-    zero = jnp.zeros((R, PANEL), f32)
-    for c in range(image_ref.shape[0]):
-        right, near = right_ref[:, c * PANEL : (c + 1) * PANEL], near_ref[c]
-        gram = gram + exact_nt(near, jnp.concatenate([right, image_ref[c], near, zero], axis=0))
+        gram = gram + split_nt(image_ref[c], *stack(right_ref[c], image_ref[c], None, None))
     gram_ref[...] = gram
 
 
@@ -340,10 +349,10 @@
     sums = far_sums(place, merged_ref, low_ref, high_ref, kept_ref, got_ref)
     sums_ref[...] = sums
     half = near_proj_ref[...] + 0.5 * across_clusters(sums, cross_ref)
-    sums = join_rows(sums.astype(f32))
     known = jnp.concatenate([right_proj_ref[...], image_proj_ref[...], half, jnp.zeros_like(half)], axis=0)
-    added = exact_nt(sums, known)
-    mirror = exact_nt(half, jnp.concatenate([jnp.zeros_like(sums)] * 2 + [sums, jnp.zeros_like(sums)], axis=0))
+    high = known.astype(bf16)
+    added = split_nt(sums, high, (known - high.astype(f32)).astype(bf16))
+    mirror = jnp.where(lane_group(added.shape) == 2, jnp.concatenate([added[:, 2 * R : 3 * R].T] * 4, axis=1), 0.0)
     late = gram_ref[...] + added + mirror
     lanes = lane_group(late.shape)
     out_ref[:R] = jnp.where(lanes == 3, pltpu.roll(late, 3 * R, 1), early_ref[...])
@@ -522,6 +531,8 @@
         placed=[SMEM] + [VMEM] * 5,
     )
 
+    right_field = field
+
     def exchange(make_field, beside, keep, payload, merged=None):
         first = merged is None
         for t, b in enumerate(order):
@@ -546,7 +557,7 @@
                 )
                 back = shift(following, 1)
             if t == 1:
-                made, got = beside(image, corner, got)
+                made, got = beside(field, corner, got)
             if t == len(order) - 2:
                 after, got = barrier((after, got))
             got_gathered, got_sums = got[:held], got[held:]
@@ -554,9 +565,9 @@
                 gathered = jnp.concatenate([gathered, got_gathered], axis=0)
                 for piece in range(0, got_sums.shape[0], sums.shape[0]):
                     sums = sums + got_sums[piece : piece + sums.shape[0]].astype(f32)
-        kernel, ins, outs = near_rows_kernel, (near_blocks, field, after, own, back, basis), (panels, rank_wide)
+        kernel, ins, outs = rows_one_kernel, (near_blocks, field, after, own, back, basis), (panels, rank_wide)
         if not first:
-            kernel, ins, outs = rows_two_kernel, ins + (right_side, image), outs + (sds((R, 4 * R), f32),)
+            kernel, ins, outs = rows_two_kernel, ins + (right_field,), outs + (sds((R, 4 * R), f32),)
         near, near_proj, *gram = call(
             kernel, outs, (near_pairs, near_count) + ins, [SMEM] * 2 + [VMEM] * len(ins),
             [pltpu.VMEM((2 * clusters, 2 * R, PANEL), bf16), pltpu.VMEM((clusters + 1, R, PANEL), f32)],
@@ -572,7 +583,7 @@
     def keep_one(payload):
         return call(
             keep_one_kernel, (kept_out, sds((2, clusters * K, clusters * K), bf16), sds((R, 4 * R), f32)),
-            (coupled, payload, basis, right_side), [VMEM] * 4,
+            (coupled, payload, basis, right_field), [VMEM] * 4,
         )
 
     def merging(image, corner, got):
@@ -581,7 +592,7 @@
 
     def multiplying(image, corner, got):
         ready, got = barrier((image, got))
-        return call(gram_one_kernel, sds((R, 4 * R), f32), (corner, right_side, ready), [VMEM] * 3), got
+        return call(gram_one_kernel, sds((R, 4 * R), f32), (corner, right_field, ready), [VMEM] * 3), got
 
     unused, near, merged, unused, cross, corner, parts = exchange(first_field, merging, keep_one, payload)
     far, image_proj, payload = call(

time: 67.5 us -> 67.3 us (level)
  starting transfers between devices: 22.9 us -> 26.2 us
  waiting for transfers between devices: 14.5 us -> 12.2 us
  Pallas kernels: 27.7 us -> 26.5 us
    ppermute x12, starting transfers between devices: 15.8 us -> 19.1 us  [across(): return lax.ppermute(x, 'leaf', [(i, i ^ b) for i in range(devices)])]
    ppermute x12, waiting for transfers between devices: 14.5 us -> 12.2 us  [across(): return lax.ppermute(x, 'leaf', [(i, i ^ b) for i in range(devices)])]
    pallas_call x14, Pallas kernels: 27.7 us -> 26.5 us  [call(): pl.pallas_call(kernel, out_shape=outs, in_specs=[spec(s) for s in spaces]...]
  transfers between devices with their start and end apart: 16 -> 16, of which waited for: 11 -> 12; matrix products, arithmetic and copies ran while one was open for 0% -> 0% of each run, Pallas kernels for 25% -> 23%
where the time goes in v7:
time: 67.3 us; the launch traced here: 66.8 us
  Pallas kernels  26.5 us (39%)
  starting transfers between devices  26.2 us (39%)
  waiting for transfers between devices  12.2 us (18%)
  between operations  1.61 us (2%)
    pallas_call x14, Pallas kernels, call(): pl.pallas_call(kernel, out_shape=outs, in_specs=[spec(s) for s in spaces]...  26.5 us
    ppermute x12, starting transfers between devices, across(): return lax.ppermute(x, 'leaf', [(i, i ^ b) for i in range(devices)])  19.1 us
    ppermute x12, waiting for transfers between devices, across(): return lax.ppermute(x, 'leaf', [(i, i ^ b) for i in range(devices)])  12.2 us
    ppermute x4, starting transfers between devices, shift(): lax.ppermute(x, 'leaf', [(i, i + by) for i in range(devices) if 0 <= i +...  7.1 us
  transfers between devices with their start and end apart: 16, of which 12 were waited for; matrix products, arithmetic and copies ran while one was open for 0% of the time, Pallas kernels for 23%

profile of v7, /device:TPU:0, one launch (start us, length us, event | category | flops | bytes accessed | tf_op | source)
XLA Modules:
  0.0 66.8 jit_solution(17117120365037382681)
XLA Ops:
  0.6 4.3 %shard_map.103 = (s32[2,64]{1,0:T(2,128)S(1)}, bf16[64,256,256]{2,1,0:T(8,128)(2,1)S(1)}, bf16[8,64,256]{2,1,0:T(8,128)(2,1)S(1)}, f32[32,256]{1,0:T(8,128)S(1)}...) custom-call(s32[1]{0:T(128)} %bitcast.me_ref, s32[2,128]{1,0:T(2,128)} %pairs_hbm.1, s32[128]{0:T(128)} %slots_hbm.1, ...), custom_call_target="tpu_custom_call" | custom-call | flops 100000000 | bytes 1000000 | tf_op jit(solution)/shard_map/pallas_call | solution.py:28
  5.5 0.9 %shard_map.104 = (f32[8,32,256]{2,1,0:T(8,128)S(1)}, bf16[2,256,256]{2,1,0:T(8,128)(2,1)S(1)}, f32[32,128]{1,0:T(8,128)S(1)}) custom-call(bf16[32,256,256]{2,1,0:T(8,128)(2,1)S(1)} %get-tuple-element.70.coupled_ref, bf16[17,32,256]{2,1,0:T(8,128)(2,1)S(1)} %get-tuple-element.58.payload_ref, bf16[256,256]{1,0:T(8,128)(2,1)S(1)} %bitcast.4, ...), custom_call_target="tpu_custom_call" | custom-call | flops 100000000 | bytes 1000000 | tf_op jit(solution)/shard_map/pallas_call | solution.py:28
  6.8 3.8 %collective-permute-start.1 = (bf16[6,32,256]{2,1,0:T(8,128)(2,1)S(1)}, bf16[6,32,256]{2,1,0:T(8,128)(2,1)S(1)}, u32[]{:S(2)}, u32[]{:S(2)}) collective-permute-start(bf16[6,32,256]{2,1,0:T(8,128)(2,1)S(1)} %pad_maximum_fusion.2), channel_id=1, source_target_pairs={{0,9},{1,8},{2,11},{3,10},{4,13},{5,12},{6,15},{7,14},{8,1},{9,0},... | collective-permute-start | bytes 294920 | tf_op jit(solution)/shard_map/ppermute | solution.py:493
  11.2 1.3 %collective-permute-start.2 = (bf16[8,64,256]{2,1,0:T(8,128)(2,1)S(1)}, bf16[8,64,256]{2,1,0:T(8,128)(2,1)S(1)}, u32[]{:S(2)}, u32[]{:S(2)}) collective-permute-start(bf16[8,64,256]{2,1,0:T(8,128)(2,1)S(1)} %get-tuple-element.64.field_ref.refs_3_.right_ref), channel_id=1, source_target_pairs={{1,0},{2,1},{3,2},{4,3},{5,4},{6,5},{7,6},{8,7},{9,8},{10,9},{11,1... | collective-permute-start | bytes 786440 | tf_op jit(solution)/shard_map/ppermute | solution.py:496
  12.5 2.4 %shard_map.105 = (f32[8,32,256]{2,1,0:T(8,128)S(1)}, bf16[8,32,256]{2,1,0:T(8,128)(2,1)S(1)}) custom-call(s32[2,64]{1,0:T(2,128)S(1)} %get-tuple-element.65.pairs_ref.refs_0_, s32[1]{0:T(128)S(6)} %copy.19.count_ref.refs_1_, bf16[64,256,256]{2,1,0:T(8,128)(2,1)S(1)} %get-tuple-element.66.blocks_ref.refs_2_, ...), custom_call_target="tpu_custom_call" | custom-call | flops 100000000 | bytes 12582912 | tf_op jit(solution)/shard_map/pallas_call | solution.py:28
  15.6 1.8 %collective-permute-start.3 = (bf16[6,32,256]{2,1,0:T(8,128)(2,1)S(1)}, bf16[6,32,256]{2,1,0:T(8,128)(2,1)S(1)}, u32[]{:S(2)}, u32[]{:S(2)}) collective-permute-start(bf16[6,32,256]{2,1,0:T(8,128)(2,1)S(1)} %pad_maximum_fusion.4), channel_id=1, source_target_pairs={{0,3},{1,2},{2,1},{3,0},{4,7},{5,6},{6,5},{7,4},{8,11},{9,10},{10,... | collective-permute-start | bytes 294920 | tf_op jit(solution)/shard_map/ppermute | solution.py:493
  17.4 2.3 %collective-permute-start.5 = (bf16[8,32,256]{2,1,0:T(8,128)(2,1)S(1)}, bf16[8,32,256]{2,1,0:T(8,128)(2,1)S(1)}, u32[]{:S(2)}, u32[]{:S(2)}) collective-permute-start(bf16[8,32,256]{2,1,0:T(8,128)(2,1)S(1)} %get-tuple-element.77), channel_id=1, source_target_pairs={{0,1},{1,2},{2,3},{3,4},{4,5},{5,6},{6,7},{7,8},{8,9},{9,10},{10,1... | collective-permute-start | bytes 393224 | tf_op jit(solution)/shard_map/ppermute | solution.py:496
  19.7 1.1 %shard_map.106 = (bf16[16,256,256]{2,1,0:T(8,128)(2,1)S(1)}, bf16[16,256,256]{2,1,0:T(8,128)(2,1)S(1)}) custom-call(bf16[32,256,256]{2,1,0:T(8,128)(2,1)S(1)} %get-tuple-element.70.coupled_ref), custom_call_target="tpu_custom_call" | custom-call | flops 100000000 | bytes 1000000 | tf_op jit(solution)/shard_map/pallas_call | solution.py:28
  20.8 0.7 %collective-permute-done.3 = bf16[6,32,256]{2,1,0:T(8,128)(2,1)S(1)} collective-permute-done((bf16[6,32,256]{2,1,0:T(8,128)(2,1)S(1)}, bf16[6,32,256]{2,1,0:T(8,128)(2,1)S(1)}, u32[]{:S(2)}, u32[]{:S(2)}) %collective-permute-start.3) | collective-permute-done | bytes 98336 | tf_op jit(solution)/shard_map/ppermute | solution.py:493
  21.6 1.3 %collective-permute-start.4 = (bf16[9,32,256]{2,1,0:T(8,128)(2,1)S(1)}, bf16[9,32,256]{2,1,0:T(8,128)(2,1)S(1)}, u32[]{:S(2)}, u32[]{:S(2)}) collective-permute-start(bf16[9,32,256]{2,1,0:T(8,128)(2,1)S(1)} %constant_dynamic-update-slice_fusion), channel_id=1, source_target_pairs={{0,5},{1,4},{2,7},{3,6},{4,1},{5,0},{6,3},{7,2},{8,13},{9,12},{10,... | collective-permute-start | bytes 442376 | tf_op jit(solution)/shard_map/ppermute | solution.py:493
  22.9 3.7 %shard_map.107 = (f32[8,32,256]{2,1,0:T(8,128)S(1)}, f32[32,256]{1,0:T(8,128)S(1)}) custom-call(s32[2,64]{1,0:T(2,128)S(1)} %get-tuple-element.65.pairs_ref.refs_0_, s32[1]{0:T(128)S(6)} %copy.19.count_ref.refs_1_, bf16[64,256,256]{2,1,0:T(8,128)(2,1)S(1)} %get-tuple-element.66.blocks_ref.refs_2_, ...), custom_call_target="tpu_custom_call" | custom-call | flops 100000000 | bytes 12582912 | tf_op jit(solution)/shard_map/pallas_call | solution.py:28
  26.6 1.0 %collective-permute-done.4 = bf16[9,32,256]{2,1,0:T(8,128)(2,1)S(1)} collective-permute-done((bf16[9,32,256]{2,1,0:T(8,128)(2,1)S(1)}, bf16[9,32,256]{2,1,0:T(8,128)(2,1)S(1)}, u32[]{:S(2)}, u32[]{:S(2)}) %collective-permute-start.4) | collective-permute-done | bytes 147488 | tf_op jit(solution)/shard_map/ppermute | solution.py:493
  27.6 1.1 %shard_map.108 = (bf16[64,256]{1,0:T(8,128)(2,1)S(1)}, f32[32,256]{1,0:T(8,128)S(1)}, bf16[9,32,256]{2,1,0:T(8,128)(2,1)S(1)}) custom-call(bf16[16,256,256]{2,1,0:T(8,128)(2,1)S(1)} %get-tuple-element.73.merged_ref, bf16[8,32,256]{2,1,0:T(8,128)(2,1)S(1)} %pad_maximum_fusion.low_ref, bf16[8,32,256]{2,1,0:T(8,128)(2,1)S(1)} %slice.138.high_ref, ...), custom_call_target="tpu_custom_call" | custom-call | flops 100000000 | bytes 1000000 | tf_op jit(solution)/shard_map/pallas_call | solution.py:28
  29.1 1.0 %collective-permute-done.6 = bf16[9,32,256]{2,1,0:T(8,128)(2,1)S(1)} collective-permute-done((bf16[9,32,256]{2,1,0:T(8,128)(2,1)S(1)}, bf16[9,32,256]{2,1,0:T(8,128)(2,1)S(1)}, u32[]{:S(2)}, u32[]{:S(2)}) %collective-permute-start.6) | collective-permute-done | bytes 147488 | tf_op jit(solution)/shard_map/ppermute | solution.py:493
  30.1 2.9 %collective-permute-start.7 = (bf16[6,32,256]{2,1,0:T(8,128)(2,1)S(1)}, bf16[6,32,256]{2,1,0:T(8,128)(2,1)S(1)}, u32[]{:S(2)}, u32[]{:S(2)}) collective-permute-start(bf16[6,32,256]{2,1,0:T(8,128)(2,1)S(1)} %pad_maximum_fusion.5), channel_id=1, source_target_pairs={{0,9},{1,8},{2,11},{3,10},{4,13},{5,12},{6,15},{7,14},{8,1},{9,0},... | collective-permute-start | bytes 294920 | tf_op jit(solution)/shard_map/ppermute | solution.py:493
  33.3 1.3 %collective-permute-start.8 = (bf16[8,64,256]{2,1,0:T(8,128)(2,1)S(1)}, bf16[8,64,256]{2,1,0:T(8,128)(2,1)S(1)}, u32[]{:S(2)}, u32[]{:S(2)}) collective-permute-start(bf16[8,64,256]{2,1,0:T(8,128)(2,1)S(1)} %get-tuple-element.92.field_ref.image_ref), channel_id=1, source_target_pairs={{1,0},{2,1},{3,2},{4,3},{5,4},{6,5},{7,6},{8,7},{9,8},{10,9},{11,1... | collective-permute-start | bytes 786440 | tf_op jit(solution)/shard_map/ppermute | solution.py:496
  34.6 2.4 %shard_map.111 = (f32[8,32,256]{2,1,0:T(8,128)S(1)}, bf16[8,32,256]{2,1,0:T(8,128)(2,1)S(1)}) custom-call(s32[2,64]{1,0:T(2,128)S(1)} %get-tuple-element.65.pairs_ref.refs_0_, s32[1]{0:T(128)S(6)} %copy.19.count_ref.refs_1_, bf16[64,256,256]{2,1,0:T(8,128)(2,1)S(1)} %get-tuple-element.66.blocks_ref.refs_2_, ...), custom_call_target="tpu_custom_call" | custom-call | flops 100000000 | bytes 12582912 | tf_op jit(solution)/shard_map/pallas_call | solution.py:28
  37.0 1.0 %collective-permute-done.7 = bf16[6,32,256]{2,1,0:T(8,128)(2,1)S(1)} collective-permute-done((bf16[6,32,256]{2,1,0:T(8,128)(2,1)S(1)}, bf16[6,32,256]{2,1,0:T(8,128)(2,1)S(1)}, u32[]{:S(2)}, u32[]{:S(2)}) %collective-permute-start.7) | collective-permute-done | bytes 98336 | tf_op jit(solution)/shard_map/ppermute | solution.py:493
  38.1 2.1 %collective-permute-start.9 = (bf16[6,32,256]{2,1,0:T(8,128)(2,1)S(1)}, bf16[6,32,256]{2,1,0:T(8,128)(2,1)S(1)}, u32[]{:S(2)}, u32[]{:S(2)}) collective-permute-start(bf16[6,32,256]{2,1,0:T(8,128)(2,1)S(1)} %pad_maximum_fusion.7), channel_id=1, source_target_pairs={{0,3},{1,2},{2,1},{3,0},{4,7},{5,6},{6,5},{7,4},{8,11},{9,10},{10,... | collective-permute-start | bytes 294920 | tf_op jit(solution)/shard_map/ppermute | solution.py:493
  40.2 2.2 %collective-permute-start.11 = (bf16[8,32,256]{2,1,0:T(8,128)(2,1)S(1)}, bf16[8,32,256]{2,1,0:T(8,128)(2,1)S(1)}, u32[]{:S(2)}, u32[]{:S(2)}) collective-permute-start(bf16[8,32,256]{2,1,0:T(8,128)(2,1)S(1)} %get-tuple-element.96), channel_id=1, source_target_pairs={{0,1},{1,2},{2,3},{3,4},{4,5},{5,6},{6,7},{7,8},{8,9},{9,10},{10,1... | collective-permute-start | bytes 393224 | tf_op jit(solution)/shard_map/ppermute | solution.py:496
  43.3 0.7 %collective-permute-start.10 = (bf16[9,32,256]{2,1,0:T(8,128)(2,1)S(1)}, bf16[9,32,256]{2,1,0:T(8,128)(2,1)S(1)}, u32[]{:S(2)}, u32[]{:S(2)}) collective-permute-start(bf16[9,32,256]{2,1,0:T(8,128)(2,1)S(1)} %constant_dynamic-update-slice_fusion.5), channel_id=1, source_target_pairs={{0,5},{1,4},{2,7},{3,6},{4,1},{5,0},{6,3},{7,2},{8,13},{9,12},{10,... | collective-permute-start | bytes 442376 | tf_op jit(solution)/shard_map/ppermute | solution.py:493
  44.0 3.9 %shard_map.113 = (f32[8,32,256]{2,1,0:T(8,128)S(1)}, f32[32,256]{1,0:T(8,128)S(1)}, f32[32,128]{1,0:T(8,128)S(1)}) custom-call(s32[2,64]{1,0:T(2,128)S(1)} %get-tuple-element.65.pairs_ref.refs_0_, s32[1]{0:T(128)S(6)} %copy.19.count_ref.refs_1_, bf16[64,256,256]{2,1,0:T(8,128)(2,1)S(1)} %get-tuple-element.66.blocks_ref.refs_2_, ...), custom_call_target="tpu_custom_call" | custom-call | flops 100000000 | bytes 12582912 | tf_op jit(solution)/shard_map/pallas_call | solution.py:28
  47.9 1.3 %collective-permute-done.10 = bf16[9,32,256]{2,1,0:T(8,128)(2,1)S(1)} collective-permute-done((bf16[9,32,256]{2,1,0:T(8,128)(2,1)S(1)}, bf16[9,32,256]{2,1,0:T(8,128)(2,1)S(1)}, u32[]{:S(2)}, u32[]{:S(2)}) %collective-permute-start.10) | collective-permute-done | bytes 147488 | tf_op jit(solution)/shard_map/ppermute | solution.py:493
  49.2 1.2 %shard_map.114 = (bf16[64,256]{1,0:T(8,128)(2,1)S(1)}, f32[48,128]{1,0:T(8,128)S(1)}) custom-call(bf16[16,256,256]{2,1,0:T(8,128)(2,1)S(1)} %get-tuple-element.73.merged_ref, bf16[8,32,256]{2,1,0:T(8,128)(2,1)S(1)} %pad_maximum_fusion.1.low_ref, bf16[8,32,256]{2,1,0:T(8,128)(2,1)S(1)} %slice.146.high_ref, f32[1,32,256]{2,1,0:T(8,128)S(1)} %slice.147.kept_ref, ...), custom_call_target="tpu_custom_call" | custom-call | flops 100000000 | bytes 1000000 | tf_op jit(solution)/shard_map/pallas_call | solution.py:28
  50.5 1.1 %collective-permute-done.12 = f32[48,128]{1,0:T(8,128)S(1)} collective-permute-done((f32[48,128]{1,0:T(8,128)S(1)}, f32[48,128]{1,0:T(8,128)S(1)}, u32[]{:S(2)}, u32[]{:S(2)}) %collective-permute-start.12) | collective-permute-done | bytes 24608 | tf_op jit(solution)/shard_map/ppermute | solution.py:493
  51.6 2.5 %collective-permute-start.13 = (f32[48,128]{1,0:T(8,128)S(1)}, f32[48,128]{1,0:T(8,128)S(1)}, u32[]{:S(2)}, u32[]{:S(2)}) collective-permute-start(f32[48,128]{1,0:T(8,128)S(1)} %add.37), channel_id=1, source_target_pairs={{0,9},{1,8},{2,11},{3,10},{4,13},{5,12},{6,15},{7,14},{8,1},{9,0},... | collective-permute-start | bytes 73736 | tf_op jit(solution)/shard_map/ppermute | solution.py:493
  54.3 1.4 %collective-permute-done.13 = f32[48,128]{1,0:T(8,128)S(1)} collective-permute-done((f32[48,128]{1,0:T(8,128)S(1)}, f32[48,128]{1,0:T(8,128)S(1)}, u32[]{:S(2)}, u32[]{:S(2)}) %collective-permute-start.13) | collective-permute-done | bytes 24608 | tf_op jit(solution)/shard_map/ppermute | solution.py:493
  55.8 1.8 %collective-permute-start.14 = (f32[48,128]{1,0:T(8,128)S(1)}, f32[48,128]{1,0:T(8,128)S(1)}, u32[]{:S(2)}, u32[]{:S(2)}) collective-permute-start(f32[48,128]{1,0:T(8,128)S(1)} %add.38), channel_id=1, source_target_pairs={{0,3},{1,2},{2,1},{3,0},{4,7},{5,6},{6,5},{7,4},{8,11},{9,10},{10,... | collective-permute-start | bytes 73736 | tf_op jit(solution)/shard_map/ppermute | solution.py:493
  57.5 1.5 %collective-permute-done.14 = f32[48,128]{1,0:T(8,128)S(1)} collective-permute-done((f32[48,128]{1,0:T(8,128)S(1)}, f32[48,128]{1,0:T(8,128)S(1)}, u32[]{:S(2)}, u32[]{:S(2)}) %collective-permute-start.14) | collective-permute-done | bytes 24608 | tf_op jit(solution)/shard_map/ppermute | solution.py:493
  59.1 1.4 %collective-permute-start.15 = (f32[48,128]{1,0:T(8,128)S(1)}, f32[48,128]{1,0:T(8,128)S(1)}, u32[]{:S(2)}, u32[]{:S(2)}) collective-permute-start(f32[48,128]{1,0:T(8,128)S(1)} %add.39.kept_ref), channel_id=1, source_target_pairs={{0,5},{1,4},{2,7},{3,6},{4,1},{5,0},{6,3},{7,2},{8,13},{9,12},{10,... | collective-permute-start | bytes 73736 | tf_op jit(solution)/shard_map/ppermute | solution.py:493
  60.5 1.8 %collective-permute-done.15.got_ref = f32[48,128]{1,0:T(8,128)S(1)} collective-permute-done((f32[48,128]{1,0:T(8,128)S(1)}, f32[48,128]{1,0:T(8,128)S(1)}, u32[]{:S(2)}, u32[]{:S(2)}) %collective-permute-start.15) | collective-permute-done | bytes 24608 | tf_op jit(solution)/shard_map/ppermute | solution.py:493
  62.3 4.5 %shard_map.116 = (f32[32,2048]{1,0:T(8,128)}, f32[32,2048]{1,0:T(8,128)}, f32[32,64]{1,0:T(8,128)}) custom-call(f32[48,128]{1,0:T(8,128)S(1)} %add.39.kept_ref, f32[48,128]{1,0:T(8,128)S(1)} %collective-permute-done.15.got_ref, f32[32,2048]{1,0:T(8,128)S(1)} %copy-done.1, f32[8,32,256]{2,1,0:T(8,128)S(1)} %get-tuple-element.108.image_ref, ...), custom_call_target="tpu_custom_call" | custom-call | flops 100000000 | bytes 1000000 | tf_op jit(solution)/shard_map/pallas_call | solution.py:28
  (53 shorter events, 3.6 us)
Async XLA Ops:
  0.6 4.9 %copy-start = (bf16[8,32,256]{2,1,0:T(8,128)(2,1)S(1)}, bf16[8,32,256]{2,1,0:T(8,128)(2,1)}, u32[]{:S(2)}) copy-start(bf16[8,32,256]{2,1,0:T(8,128)(2,1)} %param.14) | copy-start | bytes 393220
  5.0 1.7 %collective-permute-start = (bf16[17,32,256]{2,1,0:T(8,128)(2,1)S(1)}, bf16[17,32,256]{2,1,0:T(8,128)(2,1)S(1)}, u32[]{:S(2)}, u32[]{:S(2)}) collective-permute-start(bf16[17,32,256]{2,1,0:T(8,128)(2,1)S(1)} %get-tuple-element.58.payload_ref), channel_id=1, source_target_pairs={{0,1},{1,0},{2,3},{3,2},{4,5},{5,4},{6,7},{7,6},{8,9},{9,8},{10,11... | collective-permute-start | bytes 835592 | tf_op jit(solution)/shard_map/ppermute | solution.py:493
  6.8 8.7 %collective-permute-start.1 = (bf16[6,32,256]{2,1,0:T(8,128)(2,1)S(1)}, bf16[6,32,256]{2,1,0:T(8,128)(2,1)S(1)}, u32[]{:S(2)}, u32[]{:S(2)}) collective-permute-start(bf16[6,32,256]{2,1,0:T(8,128)(2,1)S(1)} %pad_maximum_fusion.2), channel_id=1, source_target_pairs={{0,9},{1,8},{2,11},{3,10},{4,13},{5,12},{6,15},{7,14},{8,1},{9,0},... | collective-permute-start | bytes 294920 | tf_op jit(solution)/shard_map/ppermute | solution.py:493
  11.2 10.3 %collective-permute-start.2 = (bf16[8,64,256]{2,1,0:T(8,128)(2,1)S(1)}, bf16[8,64,256]{2,1,0:T(8,128)(2,1)S(1)}, u32[]{:S(2)}, u32[]{:S(2)}) collective-permute-start(bf16[8,64,256]{2,1,0:T(8,128)(2,1)S(1)} %get-tuple-element.64.field_ref.refs_3_.right_ref), channel_id=1, source_target_pairs={{1,0},{2,1},{3,2},{4,3},{5,4},{6,5},{7,6},{8,7},{9,8},{10,9},{11,1... | collective-permute-start | bytes 786440 | tf_op jit(solution)/shard_map/ppermute | solution.py:496
  15.6 5.9 %collective-permute-start.3 = (bf16[6,32,256]{2,1,0:T(8,128)(2,1)S(1)}, bf16[6,32,256]{2,1,0:T(8,128)(2,1)S(1)}, u32[]{:S(2)}, u32[]{:S(2)}) collective-permute-start(bf16[6,32,256]{2,1,0:T(8,128)(2,1)S(1)} %pad_maximum_fusion.4), channel_id=1, source_target_pairs={{0,3},{1,2},{2,1},{3,0},{4,7},{5,6},{6,5},{7,4},{8,11},{9,10},{10,... | collective-permute-start | bytes 294920 | tf_op jit(solution)/shard_map/ppermute | solution.py:493
  17.4 5.5 %collective-permute-start.5 = (bf16[8,32,256]{2,1,0:T(8,128)(2,1)S(1)}, bf16[8,32,256]{2,1,0:T(8,128)(2,1)S(1)}, u32[]{:S(2)}, u32[]{:S(2)}) collective-permute-start(bf16[8,32,256]{2,1,0:T(8,128)(2,1)S(1)} %get-tuple-element.77), channel_id=1, source_target_pairs={{0,1},{1,2},{2,3},{3,4},{4,5},{5,6},{6,7},{7,8},{8,9},{9,10},{10,1... | collective-permute-start | bytes 393224 | tf_op jit(solution)/shard_map/ppermute | solution.py:496
  21.6 6.0 %collective-permute-start.4 = (bf16[9,32,256]{2,1,0:T(8,128)(2,1)S(1)}, bf16[9,32,256]{2,1,0:T(8,128)(2,1)S(1)}, u32[]{:S(2)}, u32[]{:S(2)}) collective-permute-start(bf16[9,32,256]{2,1,0:T(8,128)(2,1)S(1)} %constant_dynamic-update-slice_fusion), channel_id=1, source_target_pairs={{0,5},{1,4},{2,7},{3,6},{4,1},{5,0},{6,3},{7,2},{8,13},{9,12},{10,... | collective-permute-start | bytes 442376 | tf_op jit(solution)/shard_map/ppermute | solution.py:493
  28.6 1.4 %collective-permute-start.6 = (bf16[9,32,256]{2,1,0:T(8,128)(2,1)S(1)}, bf16[9,32,256]{2,1,0:T(8,128)(2,1)S(1)}, u32[]{:S(2)}, u32[]{:S(2)}) collective-permute-start(bf16[9,32,256]{2,1,0:T(8,128)(2,1)S(1)} %get-tuple-element.81.payload_ref), channel_id=1, source_target_pairs={{0,1},{1,0},{2,3},{3,2},{4,5},{5,4},{6,7},{7,6},{8,9},{9,8},{10,11... | collective-permute-start | bytes 442376 | tf_op jit(solution)/shard_map/ppermute | solution.py:493
  30.1 7.9 %collective-permute-start.7 = (bf16[6,32,256]{2,1,0:T(8,128)(2,1)S(1)}, bf16[6,32,256]{2,1,0:T(8,128)(2,1)S(1)}, u32[]{:S(2)}, u32[]{:S(2)}) collective-permute-start(bf16[6,32,256]{2,1,0:T(8,128)(2,1)S(1)} %pad_maximum_fusion.5), channel_id=1, source_target_pairs={{0,9},{1,8},{2,11},{3,10},{4,13},{5,12},{6,15},{7,14},{8,1},{9,0},... | collective-permute-start | bytes 294920 | tf_op jit(solution)/shard_map/ppermute | solution.py:493
  33.3 10.0 %collective-permute-start.8 = (bf16[8,64,256]{2,1,0:T(8,128)(2,1)S(1)}, bf16[8,64,256]{2,1,0:T(8,128)(2,1)S(1)}, u32[]{:S(2)}, u32[]{:S(2)}) collective-permute-start(bf16[8,64,256]{2,1,0:T(8,128)(2,1)S(1)} %get-tuple-element.92.field_ref.image_ref), channel_id=1, source_target_pairs={{1,0},{2,1},{3,2},{4,3},{5,4},{6,5},{7,6},{8,7},{9,8},{10,9},{11,1... | collective-permute-start | bytes 786440 | tf_op jit(solution)/shard_map/ppermute | solution.py:496
  38.1 5.1 %collective-permute-start.9 = (bf16[6,32,256]{2,1,0:T(8,128)(2,1)S(1)}, bf16[6,32,256]{2,1,0:T(8,128)(2,1)S(1)}, u32[]{:S(2)}, u32[]{:S(2)}) collective-permute-start(bf16[6,32,256]{2,1,0:T(8,128)(2,1)S(1)} %pad_maximum_fusion.7), channel_id=1, source_target_pairs={{0,3},{1,2},{2,1},{3,0},{4,7},{5,6},{6,5},{7,4},{8,11},{9,10},{10,... | collective-permute-start | bytes 294920 | tf_op jit(solution)/shard_map/ppermute | solution.py:493
  40.2 3.8 %collective-permute-start.11 = (bf16[8,32,256]{2,1,0:T(8,128)(2,1)S(1)}, bf16[8,32,256]{2,1,0:T(8,128)(2,1)S(1)}, u32[]{:S(2)}, u32[]{:S(2)}) collective-permute-start(bf16[8,32,256]{2,1,0:T(8,128)(2,1)S(1)} %get-tuple-element.96), channel_id=1, source_target_pairs={{0,1},{1,2},{2,3},{3,4},{4,5},{5,6},{6,7},{7,8},{8,9},{9,10},{10,1... | collective-permute-start | bytes 393224 | tf_op jit(solution)/shard_map/ppermute | solution.py:496
  43.3 5.9 %collective-permute-start.10 = (bf16[9,32,256]{2,1,0:T(8,128)(2,1)S(1)}, bf16[9,32,256]{2,1,0:T(8,128)(2,1)S(1)}, u32[]{:S(2)}, u32[]{:S(2)}) collective-permute-start(bf16[9,32,256]{2,1,0:T(8,128)(2,1)S(1)} %constant_dynamic-update-slice_fusion.5), channel_id=1, source_target_pairs={{0,5},{1,4},{2,7},{3,6},{4,1},{5,0},{6,3},{7,2},{8,13},{9,12},{10,... | collective-permute-start | bytes 442376 | tf_op jit(solution)/shard_map/ppermute | solution.py:493
  47.9 14.4 %copy-start.1 = (f32[32,2048]{1,0:T(8,128)S(1)}, f32[32,2048]{1,0:T(8,128)}, u32[]{:S(2)}) copy-start(f32[32,2048]{1,0:T(8,128)} %right_ref.1) | copy-start | bytes 786436
  50.4 1.2 %collective-permute-start.12 = (f32[48,128]{1,0:T(8,128)S(1)}, f32[48,128]{1,0:T(8,128)S(1)}, u32[]{:S(2)}, u32[]{:S(2)}) collective-permute-start(f32[48,128]{1,0:T(8,128)S(1)} %get-tuple-element.102), channel_id=1, source_target_pairs={{0,1},{1,0},{2,3},{3,2},{4,5},{5,4},{6,7},{7,6},{8,9},{9,8},{10,11... | collective-permute-start | bytes 73736 | tf_op jit(solution)/shard_map/ppermute | solution.py:493
  51.6 4.2 %collective-permute-start.13 = (f32[48,128]{1,0:T(8,128)S(1)}, f32[48,128]{1,0:T(8,128)S(1)}, u32[]{:S(2)}, u32[]{:S(2)}) collective-permute-start(f32[48,128]{1,0:T(8,128)S(1)} %add.37), channel_id=1, source_target_pairs={{0,9},{1,8},{2,11},{3,10},{4,13},{5,12},{6,15},{7,14},{8,1},{9,0},... | collective-permute-start | bytes 73736 | tf_op jit(solution)/shard_map/ppermute | solution.py:493
  55.8 3.3 %collective-permute-start.14 = (f32[48,128]{1,0:T(8,128)S(1)}, f32[48,128]{1,0:T(8,128)S(1)}, u32[]{:S(2)}, u32[]{:S(2)}) collective-permute-start(f32[48,128]{1,0:T(8,128)S(1)} %add.38), channel_id=1, source_target_pairs={{0,3},{1,2},{2,1},{3,0},{4,7},{5,6},{6,5},{7,4},{8,11},{9,10},{10,... | collective-permute-start | bytes 73736 | tf_op jit(solution)/shard_map/ppermute | solution.py:493
  59.1 3.3 %collective-permute-start.15 = (f32[48,128]{1,0:T(8,128)S(1)}, f32[48,128]{1,0:T(8,128)S(1)}, u32[]{:S(2)}, u32[]{:S(2)}) collective-permute-start(f32[48,128]{1,0:T(8,128)S(1)} %add.39.kept_ref), channel_id=1, source_target_pairs={{0,5},{1,4},{2,7},{3,6},{4,1},{5,0},{6,3},{7,2},{8,13},{9,12},{10,... | collective-permute-start | bytes 73736 | tf_op jit(solution)/shard_map/ppermute | solution.py:493

commit v8 on v7

--- a/solution.py
+++ b/solution.py
@@ -229,13 +229,13 @@
         kept_ref[d] = dot(proj, turned_ref[d])
 
 
-def near_loop(count_ref, one):
+def near_loop(count_ref, one, many=GROUP):
     def group(g, carry):
-        for u in range(GROUP):
-            one(g * GROUP + u)
+        for u in range(many):
+            one(g * many + u)
         return carry
 
-    lax.fori_loop(0, (count_ref[0] + GROUP - 1) // GROUP, group, 0)
+    lax.fori_loop(0, (count_ref[0] + many - 1) // many, group, 0)
 
 
 def near_cols_kernel(pairs_ref, count_ref, blocks_ref, field_ref, own_ref, next_ref, total):
@@ -265,7 +265,7 @@
         j = pairs_ref[1, s]
         total[i] = total[i] + join_rows(dot_nt(window[j], blocks_ref[s]))
 
-    near_loop(count_ref, one)
+    near_loop(count_ref, one, blocks_ref.shape[0])
     near = total[:clusters]
     out_ref[...] = near
     split = jnp.concatenate([split_rows(near[c]) for c in range(clusters)], axis=0)

time: 67.3 us -> 67.1 us (level)
  Pallas kernels: 26.5 us -> 24.6 us
  starting transfers between devices: 26.2 us -> 27.8 us
    pallas_call x14, Pallas kernels: 26.5 us -> 24.6 us  [call(): pl.pallas_call(kernel, out_shape=outs, in_specs=[spec(s) for s in spaces]...]
    ppermute x12, starting transfers between devices: 19.1 us -> 20.7 us  [across(): return lax.ppermute(x, 'leaf', [(i, i ^ b) for i in range(devices)])]
  transfers between devices with their start and end apart: 16 -> 16, of which waited for: 12 -> 12; matrix products, arithmetic and copies ran while one was open for 0% -> 0% of each run, Pallas kernels for 23% -> 20%
where the time goes in v8:
time: 67.1 us; the launch traced here: 66.9 us
  starting transfers between devices  27.8 us (41%)
  Pallas kernels  24.6 us (37%)
  waiting for transfers between devices  12.5 us (19%)
  between operations  1.61 us (2%)
    pallas_call x14, Pallas kernels, call(): pl.pallas_call(kernel, out_shape=outs, in_specs=[spec(s) for s in spaces]...  24.6 us
    ppermute x12, starting transfers between devices, across(): return lax.ppermute(x, 'leaf', [(i, i ^ b) for i in range(devices)])  20.7 us
    ppermute x12, waiting for transfers between devices, across(): return lax.ppermute(x, 'leaf', [(i, i ^ b) for i in range(devices)])  12.5 us
    ppermute x4, starting transfers between devices, shift(): lax.ppermute(x, 'leaf', [(i, i + by) for i in range(devices) if 0 <= i +...  7.15 us
  transfers between devices with their start and end apart: 16, of which 12 were waited for; matrix products, arithmetic and copies ran while one was open for 0% of the time, Pallas kernels for 20%

profile of v8, /device:TPU:0, one launch (start us, length us, event | category | flops | bytes accessed | tf_op | source)
XLA Modules:
  0.0 66.9 jit_solution(14377406237597082804)
XLA Ops:
  0.6 4.3 %shard_map.103 = (s32[2,64]{1,0:T(2,128)S(1)}, bf16[64,256,256]{2,1,0:T(8,128)(2,1)S(1)}, bf16[8,64,256]{2,1,0:T(8,128)(2,1)S(1)}, f32[32,256]{1,0:T(8,128)S(1)}...) custom-call(s32[1]{0:T(128)} %bitcast.me_ref, s32[2,128]{1,0:T(2,128)} %pairs_hbm.1, s32[128]{0:T(128)} %slots_hbm.1, ...), custom_call_target="tpu_custom_call" | custom-call | flops 100000000 | bytes 1000000 | tf_op jit(solution)/shard_map/pallas_call | solution.py:28
  5.5 0.9 %shard_map.104 = (f32[8,32,256]{2,1,0:T(8,128)S(1)}, bf16[2,256,256]{2,1,0:T(8,128)(2,1)S(1)}, f32[32,128]{1,0:T(8,128)S(1)}) custom-call(bf16[32,256,256]{2,1,0:T(8,128)(2,1)S(1)} %get-tuple-element.70.coupled_ref, bf16[17,32,256]{2,1,0:T(8,128)(2,1)S(1)} %get-tuple-element.58.payload_ref, bf16[256,256]{1,0:T(8,128)(2,1)S(1)} %bitcast.4, ...), custom_call_target="tpu_custom_call" | custom-call | flops 100000000 | bytes 1000000 | tf_op jit(solution)/shard_map/pallas_call | solution.py:28
  6.8 3.8 %collective-permute-start.1 = (bf16[6,32,256]{2,1,0:T(8,128)(2,1)S(1)}, bf16[6,32,256]{2,1,0:T(8,128)(2,1)S(1)}, u32[]{:S(2)}, u32[]{:S(2)}) collective-permute-start(bf16[6,32,256]{2,1,0:T(8,128)(2,1)S(1)} %pad_maximum_fusion.2), channel_id=1, source_target_pairs={{0,9},{1,8},{2,11},{3,10},{4,13},{5,12},{6,15},{7,14},{8,1},{9,0},... | collective-permute-start | bytes 294920 | tf_op jit(solution)/shard_map/ppermute | solution.py:493
  11.2 1.3 %collective-permute-start.2 = (bf16[8,64,256]{2,1,0:T(8,128)(2,1)S(1)}, bf16[8,64,256]{2,1,0:T(8,128)(2,1)S(1)}, u32[]{:S(2)}, u32[]{:S(2)}) collective-permute-start(bf16[8,64,256]{2,1,0:T(8,128)(2,1)S(1)} %get-tuple-element.64.field_ref.refs_3_.right_ref), channel_id=1, source_target_pairs={{1,0},{2,1},{3,2},{4,3},{5,4},{6,5},{7,6},{8,7},{9,8},{10,9},{11,1... | collective-permute-start | bytes 786440 | tf_op jit(solution)/shard_map/ppermute | solution.py:496
  12.5 1.5 %shard_map.105 = (f32[8,32,256]{2,1,0:T(8,128)S(1)}, bf16[8,32,256]{2,1,0:T(8,128)(2,1)S(1)}) custom-call(s32[2,64]{1,0:T(2,128)S(1)} %get-tuple-element.65.pairs_ref.refs_0_, s32[1]{0:T(128)S(6)} %copy.19.count_ref.refs_1_, bf16[64,256,256]{2,1,0:T(8,128)(2,1)S(1)} %get-tuple-element.66.blocks_ref.refs_2_, ...), custom_call_target="tpu_custom_call" | custom-call | flops 100000000 | bytes 12582912 | tf_op jit(solution)/shard_map/pallas_call | solution.py:28
  14.0 1.5 %collective-permute-done.1 = bf16[6,32,256]{2,1,0:T(8,128)(2,1)S(1)} collective-permute-done((bf16[6,32,256]{2,1,0:T(8,128)(2,1)S(1)}, bf16[6,32,256]{2,1,0:T(8,128)(2,1)S(1)}, u32[]{:S(2)}, u32[]{:S(2)}) %collective-permute-start.1) | collective-permute-done | bytes 98336 | tf_op jit(solution)/shard_map/ppermute | solution.py:493
  15.6 1.8 %collective-permute-start.3 = (bf16[6,32,256]{2,1,0:T(8,128)(2,1)S(1)}, bf16[6,32,256]{2,1,0:T(8,128)(2,1)S(1)}, u32[]{:S(2)}, u32[]{:S(2)}) collective-permute-start(bf16[6,32,256]{2,1,0:T(8,128)(2,1)S(1)} %pad_maximum_fusion.4), channel_id=1, source_target_pairs={{0,3},{1,2},{2,1},{3,0},{4,7},{5,6},{6,5},{7,4},{8,11},{9,10},{10,... | collective-permute-start | bytes 294920 | tf_op jit(solution)/shard_map/ppermute | solution.py:493
  17.4 2.3 %collective-permute-start.5 = (bf16[8,32,256]{2,1,0:T(8,128)(2,1)S(1)}, bf16[8,32,256]{2,1,0:T(8,128)(2,1)S(1)}, u32[]{:S(2)}, u32[]{:S(2)}) collective-permute-start(bf16[8,32,256]{2,1,0:T(8,128)(2,1)S(1)} %get-tuple-element.77), channel_id=1, source_target_pairs={{0,1},{1,2},{2,3},{3,4},{4,5},{5,6},{6,7},{7,8},{8,9},{9,10},{10,1... | collective-permute-start | bytes 393224 | tf_op jit(solution)/shard_map/ppermute | solution.py:496
  19.7 1.1 %shard_map.106 = (bf16[16,256,256]{2,1,0:T(8,128)(2,1)S(1)}, bf16[16,256,256]{2,1,0:T(8,128)(2,1)S(1)}) custom-call(bf16[32,256,256]{2,1,0:T(8,128)(2,1)S(1)} %get-tuple-element.70.coupled_ref), custom_call_target="tpu_custom_call" | custom-call | flops 100000000 | bytes 1000000 | tf_op jit(solution)/shard_map/pallas_call | solution.py:28
  20.9 0.6 collective-permute-done.3
  21.6 1.3 %collective-permute-start.4 = (bf16[9,32,256]{2,1,0:T(8,128)(2,1)S(1)}, bf16[9,32,256]{2,1,0:T(8,128)(2,1)S(1)}, u32[]{:S(2)}, u32[]{:S(2)}) collective-permute-start(bf16[9,32,256]{2,1,0:T(8,128)(2,1)S(1)} %constant_dynamic-update-slice_fusion), channel_id=1, source_target_pairs={{0,5},{1,4},{2,7},{3,6},{4,1},{5,0},{6,3},{7,2},{8,13},{9,12},{10,... | collective-permute-start | bytes 442376 | tf_op jit(solution)/shard_map/ppermute | solution.py:493
  22.9 3.6 %shard_map.107 = (f32[8,32,256]{2,1,0:T(8,128)S(1)}, f32[32,256]{1,0:T(8,128)S(1)}) custom-call(s32[2,64]{1,0:T(2,128)S(1)} %get-tuple-element.65.pairs_ref.refs_0_, s32[1]{0:T(128)S(6)} %copy.19.count_ref.refs_1_, bf16[64,256,256]{2,1,0:T(8,128)(2,1)S(1)} %get-tuple-element.66.blocks_ref.refs_2_, ...), custom_call_target="tpu_custom_call" | custom-call | flops 100000000 | bytes 12582912 | tf_op jit(solution)/shard_map/pallas_call | solution.py:28
  26.5 1.0 %collective-permute-done.4 = bf16[9,32,256]{2,1,0:T(8,128)(2,1)S(1)} collective-permute-done((bf16[9,32,256]{2,1,0:T(8,128)(2,1)S(1)}, bf16[9,32,256]{2,1,0:T(8,128)(2,1)S(1)}, u32[]{:S(2)}, u32[]{:S(2)}) %collective-permute-start.4) | collective-permute-done | bytes 147488 | tf_op jit(solution)/shard_map/ppermute | solution.py:493
  27.5 1.1 %shard_map.108 = (bf16[64,256]{1,0:T(8,128)(2,1)S(1)}, f32[32,256]{1,0:T(8,128)S(1)}, bf16[9,32,256]{2,1,0:T(8,128)(2,1)S(1)}) custom-call(bf16[16,256,256]{2,1,0:T(8,128)(2,1)S(1)} %get-tuple-element.73.merged_ref, bf16[8,32,256]{2,1,0:T(8,128)(2,1)S(1)} %pad_maximum_fusion.low_ref, bf16[8,32,256]{2,1,0:T(8,128)(2,1)S(1)} %slice.138.high_ref, ...), custom_call_target="tpu_custom_call" | custom-call | flops 100000000 | bytes 1000000 | tf_op jit(solution)/shard_map/pallas_call | solution.py:28
  29.1 1.0 %collective-permute-done.6 = bf16[9,32,256]{2,1,0:T(8,128)(2,1)S(1)} collective-permute-done((bf16[9,32,256]{2,1,0:T(8,128)(2,1)S(1)}, bf16[9,32,256]{2,1,0:T(8,128)(2,1)S(1)}, u32[]{:S(2)}, u32[]{:S(2)}) %collective-permute-start.6) | collective-permute-done | bytes 147488 | tf_op jit(solution)/shard_map/ppermute | solution.py:493
  30.1 2.8 %collective-permute-start.7 = (bf16[6,32,256]{2,1,0:T(8,128)(2,1)S(1)}, bf16[6,32,256]{2,1,0:T(8,128)(2,1)S(1)}, u32[]{:S(2)}, u32[]{:S(2)}) collective-permute-start(bf16[6,32,256]{2,1,0:T(8,128)(2,1)S(1)} %pad_maximum_fusion.5), channel_id=1, source_target_pairs={{0,9},{1,8},{2,11},{3,10},{4,13},{5,12},{6,15},{7,14},{8,1},{9,0},... | collective-permute-start | bytes 294920 | tf_op jit(solution)/shard_map/ppermute | solution.py:493
  33.1 1.3 %collective-permute-start.8 = (bf16[8,64,256]{2,1,0:T(8,128)(2,1)S(1)}, bf16[8,64,256]{2,1,0:T(8,128)(2,1)S(1)}, u32[]{:S(2)}, u32[]{:S(2)}) collective-permute-start(bf16[8,64,256]{2,1,0:T(8,128)(2,1)S(1)} %get-tuple-element.92.field_ref.image_ref), channel_id=1, source_target_pairs={{1,0},{2,1},{3,2},{4,3},{5,4},{6,5},{7,6},{8,7},{9,8},{10,9},{11,1... | collective-permute-start | bytes 786440 | tf_op jit(solution)/shard_map/ppermute | solution.py:496
  34.4 1.5 %shard_map.111 = (f32[8,32,256]{2,1,0:T(8,128)S(1)}, bf16[8,32,256]{2,1,0:T(8,128)(2,1)S(1)}) custom-call(s32[2,64]{1,0:T(2,128)S(1)} %get-tuple-element.65.pairs_ref.refs_0_, s32[1]{0:T(128)S(6)} %copy.19.count_ref.refs_1_, bf16[64,256,256]{2,1,0:T(8,128)(2,1)S(1)} %get-tuple-element.66.blocks_ref.refs_2_, ...), custom_call_target="tpu_custom_call" | custom-call | flops 100000000 | bytes 12582912 | tf_op jit(solution)/shard_map/pallas_call | solution.py:28
  36.0 1.9 %collective-permute-done.7 = bf16[6,32,256]{2,1,0:T(8,128)(2,1)S(1)} collective-permute-done((bf16[6,32,256]{2,1,0:T(8,128)(2,1)S(1)}, bf16[6,32,256]{2,1,0:T(8,128)(2,1)S(1)}, u32[]{:S(2)}, u32[]{:S(2)}) %collective-permute-start.7) | collective-permute-done | bytes 98336 | tf_op jit(solution)/shard_map/ppermute | solution.py:493
  38.0 2.3 %collective-permute-start.9 = (bf16[6,32,256]{2,1,0:T(8,128)(2,1)S(1)}, bf16[6,32,256]{2,1,0:T(8,128)(2,1)S(1)}, u32[]{:S(2)}, u32[]{:S(2)}) collective-permute-start(bf16[6,32,256]{2,1,0:T(8,128)(2,1)S(1)} %pad_maximum_fusion.7), channel_id=1, source_target_pairs={{0,3},{1,2},{2,1},{3,0},{4,7},{5,6},{6,5},{7,4},{8,11},{9,10},{10,... | collective-permute-start | bytes 294920 | tf_op jit(solution)/shard_map/ppermute | solution.py:493
  40.2 2.3 %collective-permute-start.11 = (bf16[8,32,256]{2,1,0:T(8,128)(2,1)S(1)}, bf16[8,32,256]{2,1,0:T(8,128)(2,1)S(1)}, u32[]{:S(2)}, u32[]{:S(2)}) collective-permute-start(bf16[8,32,256]{2,1,0:T(8,128)(2,1)S(1)} %get-tuple-element.96), channel_id=1, source_target_pairs={{0,1},{1,2},{2,3},{3,4},{4,5},{5,6},{6,7},{7,8},{8,9},{9,10},{10,1... | collective-permute-start | bytes 393224 | tf_op jit(solution)/shard_map/ppermute | solution.py:496
  43.3 1.8 %collective-permute-start.10 = (bf16[9,32,256]{2,1,0:T(8,128)(2,1)S(1)}, bf16[9,32,256]{2,1,0:T(8,128)(2,1)S(1)}, u32[]{:S(2)}, u32[]{:S(2)}) collective-permute-start(bf16[9,32,256]{2,1,0:T(8,128)(2,1)S(1)} %constant_dynamic-update-slice_fusion.5), channel_id=1, source_target_pairs={{0,5},{1,4},{2,7},{3,6},{4,1},{5,0},{6,3},{7,2},{8,13},{9,12},{10,... | collective-permute-start | bytes 442376 | tf_op jit(solution)/shard_map/ppermute | solution.py:493
  45.1 3.9 %shard_map.113 = (f32[8,32,256]{2,1,0:T(8,128)S(1)}, f32[32,256]{1,0:T(8,128)S(1)}, f32[32,128]{1,0:T(8,128)S(1)}) custom-call(s32[2,64]{1,0:T(2,128)S(1)} %get-tuple-element.65.pairs_ref.refs_0_, s32[1]{0:T(128)S(6)} %copy.19.count_ref.refs_1_, bf16[64,256,256]{2,1,0:T(8,128)(2,1)S(1)} %get-tuple-element.66.blocks_ref.refs_2_, ...), custom_call_target="tpu_custom_call" | custom-call | flops 100000000 | bytes 12582912 | tf_op jit(solution)/shard_map/pallas_call | solution.py:28
  49.2 1.2 %shard_map.114 = (bf16[64,256]{1,0:T(8,128)(2,1)S(1)}, f32[48,128]{1,0:T(8,128)S(1)}) custom-call(bf16[16,256,256]{2,1,0:T(8,128)(2,1)S(1)} %get-tuple-element.73.merged_ref, bf16[8,32,256]{2,1,0:T(8,128)(2,1)S(1)} %pad_maximum_fusion.1.low_ref, bf16[8,32,256]{2,1,0:T(8,128)(2,1)S(1)} %slice.146.high_ref, f32[1,32,256]{2,1,0:T(8,128)S(1)} %slice.147.kept_ref, ...), custom_call_target="tpu_custom_call" | custom-call | flops 100000000 | bytes 1000000 | tf_op jit(solution)/shard_map/pallas_call | solution.py:28
  50.5 1.1 %collective-permute-done.12 = f32[48,128]{1,0:T(8,128)S(1)} collective-permute-done((f32[48,128]{1,0:T(8,128)S(1)}, f32[48,128]{1,0:T(8,128)S(1)}, u32[]{:S(2)}, u32[]{:S(2)}) %collective-permute-start.12) | collective-permute-done | bytes 24608 | tf_op jit(solution)/shard_map/ppermute | solution.py:493
  51.6 2.5 %collective-permute-start.13 = (f32[48,128]{1,0:T(8,128)S(1)}, f32[48,128]{1,0:T(8,128)S(1)}, u32[]{:S(2)}, u32[]{:S(2)}) collective-permute-start(f32[48,128]{1,0:T(8,128)S(1)} %add.37), channel_id=1, source_target_pairs={{0,9},{1,8},{2,11},{3,10},{4,13},{5,12},{6,15},{7,14},{8,1},{9,0},... | collective-permute-start | bytes 73736 | tf_op jit(solution)/shard_map/ppermute | solution.py:493
  54.4 1.4 %collective-permute-done.13 = f32[48,128]{1,0:T(8,128)S(1)} collective-permute-done((f32[48,128]{1,0:T(8,128)S(1)}, f32[48,128]{1,0:T(8,128)S(1)}, u32[]{:S(2)}, u32[]{:S(2)}) %collective-permute-start.13) | collective-permute-done | bytes 24608 | tf_op jit(solution)/shard_map/ppermute | solution.py:493
  55.8 1.7 %collective-permute-start.14 = (f32[48,128]{1,0:T(8,128)S(1)}, f32[48,128]{1,0:T(8,128)S(1)}, u32[]{:S(2)}, u32[]{:S(2)}) collective-permute-start(f32[48,128]{1,0:T(8,128)S(1)} %add.38), channel_id=1, source_target_pairs={{0,3},{1,2},{2,1},{3,0},{4,7},{5,6},{6,5},{7,4},{8,11},{9,10},{10,... | collective-permute-start | bytes 73736 | tf_op jit(solution)/shard_map/ppermute | solution.py:493
  57.5 1.5 %collective-permute-done.14 = f32[48,128]{1,0:T(8,128)S(1)} collective-permute-done((f32[48,128]{1,0:T(8,128)S(1)}, f32[48,128]{1,0:T(8,128)S(1)}, u32[]{:S(2)}, u32[]{:S(2)}) %collective-permute-start.14) | collective-permute-done | bytes 24608 | tf_op jit(solution)/shard_map/ppermute | solution.py:493
  59.0 1.9 %collective-permute-start.15 = (f32[48,128]{1,0:T(8,128)S(1)}, f32[48,128]{1,0:T(8,128)S(1)}, u32[]{:S(2)}, u32[]{:S(2)}) collective-permute-start(f32[48,128]{1,0:T(8,128)S(1)} %add.39.kept_ref), channel_id=1, source_target_pairs={{0,5},{1,4},{2,7},{3,6},{4,1},{5,0},{6,3},{7,2},{8,13},{9,12},{10,... | collective-permute-start | bytes 73736 | tf_op jit(solution)/shard_map/ppermute | solution.py:493
  60.9 1.5 %collective-permute-done.15.got_ref = f32[48,128]{1,0:T(8,128)S(1)} collective-permute-done((f32[48,128]{1,0:T(8,128)S(1)}, f32[48,128]{1,0:T(8,128)S(1)}, u32[]{:S(2)}, u32[]{:S(2)}) %collective-permute-start.15) | collective-permute-done | bytes 24608 | tf_op jit(solution)/shard_map/ppermute | solution.py:493
  62.4 4.5 %shard_map.116 = (f32[32,2048]{1,0:T(8,128)}, f32[32,2048]{1,0:T(8,128)}, f32[32,64]{1,0:T(8,128)}) custom-call(f32[48,128]{1,0:T(8,128)S(1)} %add.39.kept_ref, f32[48,128]{1,0:T(8,128)S(1)} %collective-permute-done.15.got_ref, f32[32,2048]{1,0:T(8,128)S(1)} %copy-done.1, f32[8,32,256]{2,1,0:T(8,128)S(1)} %get-tuple-element.108.image_ref, ...), custom_call_target="tpu_custom_call" | custom-call | flops 100000000 | bytes 1000000 | tf_op jit(solution)/shard_map/pallas_call | solution.py:28
  (53 shorter events, 3.1 us)
Async XLA Ops:
  0.6 4.9 %copy-start = (bf16[8,32,256]{2,1,0:T(8,128)(2,1)S(1)}, bf16[8,32,256]{2,1,0:T(8,128)(2,1)}, u32[]{:S(2)}) copy-start(bf16[8,32,256]{2,1,0:T(8,128)(2,1)} %param.14) | copy-start | bytes 393220
  5.0 1.7 %collective-permute-start = (bf16[17,32,256]{2,1,0:T(8,128)(2,1)S(1)}, bf16[17,32,256]{2,1,0:T(8,128)(2,1)S(1)}, u32[]{:S(2)}, u32[]{:S(2)}) collective-permute-start(bf16[17,32,256]{2,1,0:T(8,128)(2,1)S(1)} %get-tuple-element.58.payload_ref), channel_id=1, source_target_pairs={{0,1},{1,0},{2,3},{3,2},{4,5},{5,4},{6,7},{7,6},{8,9},{9,8},{10,11... | collective-permute-start | bytes 835592 | tf_op jit(solution)/shard_map/ppermute | solution.py:493
  6.8 8.7 %collective-permute-start.1 = (bf16[6,32,256]{2,1,0:T(8,128)(2,1)S(1)}, bf16[6,32,256]{2,1,0:T(8,128)(2,1)S(1)}, u32[]{:S(2)}, u32[]{:S(2)}) collective-permute-start(bf16[6,32,256]{2,1,0:T(8,128)(2,1)S(1)} %pad_maximum_fusion.2), channel_id=1, source_target_pairs={{0,9},{1,8},{2,11},{3,10},{4,13},{5,12},{6,15},{7,14},{8,1},{9,0},... | collective-permute-start | bytes 294920 | tf_op jit(solution)/shard_map/ppermute | solution.py:493
  11.2 10.3 %collective-permute-start.2 = (bf16[8,64,256]{2,1,0:T(8,128)(2,1)S(1)}, bf16[8,64,256]{2,1,0:T(8,128)(2,1)S(1)}, u32[]{:S(2)}, u32[]{:S(2)}) collective-permute-start(bf16[8,64,256]{2,1,0:T(8,128)(2,1)S(1)} %get-tuple-element.64.field_ref.refs_3_.right_ref), channel_id=1, source_target_pairs={{1,0},{2,1},{3,2},{4,3},{5,4},{6,5},{7,6},{8,7},{9,8},{10,9},{11,1... | collective-permute-start | bytes 786440 | tf_op jit(solution)/shard_map/ppermute | solution.py:496
  15.6 5.9 %collective-permute-start.3 = (bf16[6,32,256]{2,1,0:T(8,128)(2,1)S(1)}, bf16[6,32,256]{2,1,0:T(8,128)(2,1)S(1)}, u32[]{:S(2)}, u32[]{:S(2)}) collective-permute-start(bf16[6,32,256]{2,1,0:T(8,128)(2,1)S(1)} %pad_maximum_fusion.4), channel_id=1, source_target_pairs={{0,3},{1,2},{2,1},{3,0},{4,7},{5,6},{6,5},{7,4},{8,11},{9,10},{10,... | collective-permute-start | bytes 294920 | tf_op jit(solution)/shard_map/ppermute | solution.py:493
  17.4 5.5 %collective-permute-start.5 = (bf16[8,32,256]{2,1,0:T(8,128)(2,1)S(1)}, bf16[8,32,256]{2,1,0:T(8,128)(2,1)S(1)}, u32[]{:S(2)}, u32[]{:S(2)}) collective-permute-start(bf16[8,32,256]{2,1,0:T(8,128)(2,1)S(1)} %get-tuple-element.77), channel_id=1, source_target_pairs={{0,1},{1,2},{2,3},{3,4},{4,5},{5,6},{6,7},{7,8},{8,9},{9,10},{10,1... | collective-permute-start | bytes 393224 | tf_op jit(solution)/shard_map/ppermute | solution.py:496
  21.6 6.0 %collective-permute-start.4 = (bf16[9,32,256]{2,1,0:T(8,128)(2,1)S(1)}, bf16[9,32,256]{2,1,0:T(8,128)(2,1)S(1)}, u32[]{:S(2)}, u32[]{:S(2)}) collective-permute-start(bf16[9,32,256]{2,1,0:T(8,128)(2,1)S(1)} %constant_dynamic-update-slice_fusion), channel_id=1, source_target_pairs={{0,5},{1,4},{2,7},{3,6},{4,1},{5,0},{6,3},{7,2},{8,13},{9,12},{10,... | collective-permute-start | bytes 442376 | tf_op jit(solution)/shard_map/ppermute | solution.py:493
  28.6 1.4 %collective-permute-start.6 = (bf16[9,32,256]{2,1,0:T(8,128)(2,1)S(1)}, bf16[9,32,256]{2,1,0:T(8,128)(2,1)S(1)}, u32[]{:S(2)}, u32[]{:S(2)}) collective-permute-start(bf16[9,32,256]{2,1,0:T(8,128)(2,1)S(1)} %get-tuple-element.81.payload_ref), channel_id=1, source_target_pairs={{0,1},{1,0},{2,3},{3,2},{4,5},{5,4},{6,7},{7,6},{8,9},{9,8},{10,11... | collective-permute-start | bytes 442376 | tf_op jit(solution)/shard_map/ppermute | solution.py:493
  30.1 7.8 %collective-permute-start.7 = (bf16[6,32,256]{2,1,0:T(8,128)(2,1)S(1)}, bf16[6,32,256]{2,1,0:T(8,128)(2,1)S(1)}, u32[]{:S(2)}, u32[]{:S(2)}) collective-permute-start(bf16[6,32,256]{2,1,0:T(8,128)(2,1)S(1)} %pad_maximum_fusion.5), channel_id=1, source_target_pairs={{0,9},{1,8},{2,11},{3,10},{4,13},{5,12},{6,15},{7,14},{8,1},{9,0},... | collective-permute-start | bytes 294920 | tf_op jit(solution)/shard_map/ppermute | solution.py:493
  33.1 10.1 %collective-permute-start.8 = (bf16[8,64,256]{2,1,0:T(8,128)(2,1)S(1)}, bf16[8,64,256]{2,1,0:T(8,128)(2,1)S(1)}, u32[]{:S(2)}, u32[]{:S(2)}) collective-permute-start(bf16[8,64,256]{2,1,0:T(8,128)(2,1)S(1)} %get-tuple-element.92.field_ref.image_ref), channel_id=1, source_target_pairs={{1,0},{2,1},{3,2},{4,3},{5,4},{6,5},{7,6},{8,7},{9,8},{10,9},{11,1... | collective-permute-start | bytes 786440 | tf_op jit(solution)/shard_map/ppermute | solution.py:496
  38.0 5.3 %collective-permute-start.9 = (bf16[6,32,256]{2,1,0:T(8,128)(2,1)S(1)}, bf16[6,32,256]{2,1,0:T(8,128)(2,1)S(1)}, u32[]{:S(2)}, u32[]{:S(2)}) collective-permute-start(bf16[6,32,256]{2,1,0:T(8,128)(2,1)S(1)} %pad_maximum_fusion.7), channel_id=1, source_target_pairs={{0,3},{1,2},{2,1},{3,0},{4,7},{5,6},{6,5},{7,4},{8,11},{9,10},{10,... | collective-permute-start | bytes 294920 | tf_op jit(solution)/shard_map/ppermute | solution.py:493
  40.2 4.8 %collective-permute-start.11 = (bf16[8,32,256]{2,1,0:T(8,128)(2,1)S(1)}, bf16[8,32,256]{2,1,0:T(8,128)(2,1)S(1)}, u32[]{:S(2)}, u32[]{:S(2)}) collective-permute-start(bf16[8,32,256]{2,1,0:T(8,128)(2,1)S(1)} %get-tuple-element.96), channel_id=1, source_target_pairs={{0,1},{1,2},{2,3},{3,4},{4,5},{5,6},{6,7},{7,8},{8,9},{9,10},{10,1... | collective-permute-start | bytes 393224 | tf_op jit(solution)/shard_map/ppermute | solution.py:496
  43.3 5.9 %collective-permute-start.10 = (bf16[9,32,256]{2,1,0:T(8,128)(2,1)S(1)}, bf16[9,32,256]{2,1,0:T(8,128)(2,1)S(1)}, u32[]{:S(2)}, u32[]{:S(2)}) collective-permute-start(bf16[9,32,256]{2,1,0:T(8,128)(2,1)S(1)} %constant_dynamic-update-slice_fusion.5), channel_id=1, source_target_pairs={{0,5},{1,4},{2,7},{3,6},{4,1},{5,0},{6,3},{7,2},{8,13},{9,12},{10,... | collective-permute-start | bytes 442376 | tf_op jit(solution)/shard_map/ppermute | solution.py:493
  49.0 13.4 %copy-start.1 = (f32[32,2048]{1,0:T(8,128)S(1)}, f32[32,2048]{1,0:T(8,128)}, u32[]{:S(2)}) copy-start(f32[32,2048]{1,0:T(8,128)} %right_ref.1) | copy-start | bytes 786436
  50.4 1.2 %collective-permute-start.12 = (f32[48,128]{1,0:T(8,128)S(1)}, f32[48,128]{1,0:T(8,128)S(1)}, u32[]{:S(2)}, u32[]{:S(2)}) collective-permute-start(f32[48,128]{1,0:T(8,128)S(1)} %get-tuple-element.102), channel_id=1, source_target_pairs={{0,1},{1,0},{2,3},{3,2},{4,5},{5,4},{6,7},{7,6},{8,9},{9,8},{10,11... | collective-permute-start | bytes 73736 | tf_op jit(solution)/shard_map/ppermute | solution.py:493
  51.6 4.2 %collective-permute-start.13 = (f32[48,128]{1,0:T(8,128)S(1)}, f32[48,128]{1,0:T(8,128)S(1)}, u32[]{:S(2)}, u32[]{:S(2)}) collective-permute-start(f32[48,128]{1,0:T(8,128)S(1)} %add.37), channel_id=1, source_target_pairs={{0,9},{1,8},{2,11},{3,10},{4,13},{5,12},{6,15},{7,14},{8,1},{9,0},... | collective-permute-start | bytes 73736 | tf_op jit(solution)/shard_map/ppermute | solution.py:493
  55.8 3.3 %collective-permute-start.14 = (f32[48,128]{1,0:T(8,128)S(1)}, f32[48,128]{1,0:T(8,128)S(1)}, u32[]{:S(2)}, u32[]{:S(2)}) collective-permute-start(f32[48,128]{1,0:T(8,128)S(1)} %add.38), channel_id=1, source_target_pairs={{0,3},{1,2},{2,1},{3,0},{4,7},{5,6},{6,5},{7,4},{8,11},{9,10},{10,... | collective-permute-start | bytes 73736 | tf_op jit(solution)/shard_map/ppermute | solution.py:493
  59.0 3.4 %collective-permute-start.15 = (f32[48,128]{1,0:T(8,128)S(1)}, f32[48,128]{1,0:T(8,128)S(1)}, u32[]{:S(2)}, u32[]{:S(2)}) collective-permute-start(f32[48,128]{1,0:T(8,128)S(1)} %add.39.kept_ref), channel_id=1, source_target_pairs={{0,5},{1,4},{2,7},{3,6},{4,1},{5,0},{6,3},{7,2},{8,13},{9,12},{10,... | collective-permute-start | bytes 73736 | tf_op jit(solution)/shard_map/ppermute | solution.py:493

commit v9 on v8

--- a/solution.py
+++ b/solution.py
@@ -140,11 +140,11 @@
         out_ref[where, here, :] = out_ref[where, here, :] + block
 
     def some(step, carry):
-        for u in range(16):
-            one(step * 16 + u)
+        for u in range(32):
+            one(step * 32 + u)
         return carry
 
-    lax.fori_loop(0, pairs // 16, some, 0)
+    lax.fori_loop(0, pairs // 32, some, 0)
 
 
 def open_kernel(me_ref, pairs_hbm, slots_hbm, coupling_hbm, right_hbm, basis_hbm, near_hbm, blocks_hbm,
@@ -375,25 +375,27 @@
     columns = [[lane(x, k + j) for x in wide[block:]] for j in range(4)]
     m = [[columns[j][0][at + i : at + i + 1] for j in range(4)] for i in range(4)]
     scale = 1.0 / (m[0][0] * m[1][1] - m[0][1] * m[1][0])
-    first = {j: (m[1][1] * m[0][j] - m[0][1] * m[1][j]) * scale for j in (2, 3)}
-    second = {j: (m[0][0] * m[1][j] - m[1][0] * m[0][j]) * scale for j in (2, 3)}
-    s = {(i, j): m[i][j] - (m[i][0] * first[j] + m[i][1] * second[j]) for i in (2, 3) for j in (2, 3)}
+    upper = {j: m[1][1] * m[0][j] - m[0][1] * m[1][j] for j in (2, 3)}
+    under = {j: m[0][0] * m[1][j] - m[1][0] * m[0][j] for j in (2, 3)}
+    s = {
+        (i, j): m[i][j] - (m[i][0] * upper[j] + m[i][1] * under[j]) * scale for i in (2, 3) for j in (2, 3)
+    }
     after = 1.0 / (s[2, 2] * s[3, 3] - s[2, 3] * s[3, 2])
     ratio, last_ratio = m[1][0] / m[0][0], s[3, 2] / s[2, 2]
     for part in both:
         p = [part[block][at + i : at + i + 1] for i in range(4)]
-        y0 = (m[1][1] * p[0] - m[0][1] * p[1]) * scale
-        y1 = (m[0][0] * p[1] - m[1][0] * p[0]) * scale
-        r2 = p[2] - (m[2][0] * y0 + m[2][1] * y1)
-        r3 = p[3] - (m[3][0] * y0 + m[3][1] * y1)
-        x2 = (s[3, 3] * r2 - s[2, 3] * r3) * after
-        x3 = (s[2, 2] * r3 - s[3, 2] * r2) * after
-        x0 = y0 - (first[2] * x2 + first[3] * x3)
-        x1 = y1 - (second[2] * x2 + second[3] * x3)
+        y0, y1 = m[1][1] * p[0] - m[0][1] * p[1], m[0][0] * p[1] - m[1][0] * p[0]
+        r2 = p[2] - (m[2][0] * y0 + m[2][1] * y1) * scale
+        r3 = p[3] - (m[3][0] * y0 + m[3][1] * y1) * scale
+        y0, y1 = y0 * scale, y1 * scale
+        x2, x3 = s[3, 3] * r2 - s[2, 3] * r3, s[2, 2] * r3 - s[3, 2] * r2
+        x0 = (upper[2] * x2 + upper[3] * x3) * scale
+        x1 = (under[2] * x2 + under[3] * x3) * scale
         own = [p[0], p[1] - ratio * p[0], r2, r3 - last_ratio * r2]
         for i in range(block, len(wide)):
             c = [column[i - block] for column in columns]
-            rest = part[i] - ((c[0] * x0 + c[1] * x1) + (c[2] * x2 + c[3] * x3))
+            begun = part[i] - (c[0] * y0 + c[1] * y1)
+            rest = begun - ((c[2] * x2 + c[3] * x3) - (c[0] * x0 + c[1] * x1)) * after
             if i == block:
                 rest = jnp.where(rows > at + 3, rest, part[i])
                 for t in range(1, 4):

time: 67.1 us -> 67 us (level)
  starting transfers between devices: 27.8 us -> 25.9 us
  Pallas kernels: 24.6 us -> 26.4 us
    ppermute x12, starting transfers between devices: 20.7 us -> 18.8 us  [across(): return lax.ppermute(x, 'leaf', [(i, i ^ b) for i in range(devices)])]
    pallas_call x14, Pallas kernels: 24.6 us -> 26.4 us  [call(): pl.pallas_call(kernel, out_shape=outs, in_specs=[spec(s) for s in spaces]...]
  transfers between devices with their start and end apart: 16 -> 16, of which waited for: 12 -> 12; matrix products, arithmetic and copies ran while one was open for 0% -> 0% of each run, Pallas kernels for 20% -> 23%
where the time goes in v9:
time: 67 us; the launch traced here: 66.8 us
  Pallas kernels  26.4 us (39%)
  starting transfers between devices  25.9 us (39%)
  waiting for transfers between devices  12.5 us (19%)
  between operations  1.61 us (2%)
    pallas_call x14, Pallas kernels, call(): pl.pallas_call(kernel, out_shape=outs, in_specs=[spec(s) for s in spaces]...  26.4 us
    ppermute x12, starting transfers between devices, across(): return lax.ppermute(x, 'leaf', [(i, i ^ b) for i in range(devices)])  18.8 us
    ppermute x12, waiting for transfers between devices, across(): return lax.ppermute(x, 'leaf', [(i, i ^ b) for i in range(devices)])  12.5 us
    ppermute x4, starting transfers between devices, shift(): lax.ppermute(x, 'leaf', [(i, i + by) for i in range(devices) if 0 <= i +...  7.15 us
  transfers between devices with their start and end apart: 16, of which 12 were waited for; matrix products, arithmetic and copies ran while one was open for 0% of the time, Pallas kernels for 23%

profile of v9, /device:TPU:0, one launch (start us, length us, event | category | flops | bytes accessed | tf_op | source)
XLA Modules:
  0.0 66.8 jit_solution(7963637661925901671)
XLA Ops:
  0.6 4.3 %shard_map.103 = (s32[2,64]{1,0:T(2,128)S(1)}, bf16[64,256,256]{2,1,0:T(8,128)(2,1)S(1)}, bf16[8,64,256]{2,1,0:T(8,128)(2,1)S(1)}, f32[32,256]{1,0:T(8,128)S(1)}...) custom-call(s32[1]{0:T(128)} %bitcast.me_ref, s32[2,128]{1,0:T(2,128)} %pairs_hbm.1, s32[128]{0:T(128)} %slots_hbm.1, ...), custom_call_target="tpu_custom_call" | custom-call | flops 100000000 | bytes 1000000 | tf_op jit(solution)/shard_map/pallas_call | solution.py:28
  5.5 0.9 %shard_map.104 = (f32[8,32,256]{2,1,0:T(8,128)S(1)}, bf16[2,256,256]{2,1,0:T(8,128)(2,1)S(1)}, f32[32,128]{1,0:T(8,128)S(1)}) custom-call(bf16[32,256,256]{2,1,0:T(8,128)(2,1)S(1)} %get-tuple-element.70.coupled_ref, bf16[17,32,256]{2,1,0:T(8,128)(2,1)S(1)} %get-tuple-element.58.payload_ref, bf16[256,256]{1,0:T(8,128)(2,1)S(1)} %bitcast.4, ...), custom_call_target="tpu_custom_call" | custom-call | flops 100000000 | bytes 1000000 | tf_op jit(solution)/shard_map/pallas_call | solution.py:28
  6.8 3.8 %collective-permute-start.1 = (bf16[6,32,256]{2,1,0:T(8,128)(2,1)S(1)}, bf16[6,32,256]{2,1,0:T(8,128)(2,1)S(1)}, u32[]{:S(2)}, u32[]{:S(2)}) collective-permute-start(bf16[6,32,256]{2,1,0:T(8,128)(2,1)S(1)} %pad_maximum_fusion.2), channel_id=1, source_target_pairs={{0,9},{1,8},{2,11},{3,10},{4,13},{5,12},{6,15},{7,14},{8,1},{9,0},... | collective-permute-start | bytes 294920 | tf_op jit(solution)/shard_map/ppermute | solution.py:495
  11.2 1.3 %collective-permute-start.2 = (bf16[8,64,256]{2,1,0:T(8,128)(2,1)S(1)}, bf16[8,64,256]{2,1,0:T(8,128)(2,1)S(1)}, u32[]{:S(2)}, u32[]{:S(2)}) collective-permute-start(bf16[8,64,256]{2,1,0:T(8,128)(2,1)S(1)} %get-tuple-element.64.field_ref.refs_3_.right_ref), channel_id=1, source_target_pairs={{1,0},{2,1},{3,2},{4,3},{5,4},{6,5},{7,6},{8,7},{9,8},{10,9},{11,1... | collective-permute-start | bytes 786440 | tf_op jit(solution)/shard_map/ppermute | solution.py:498
  12.5 2.4 %shard_map.105 = (f32[8,32,256]{2,1,0:T(8,128)S(1)}, bf16[8,32,256]{2,1,0:T(8,128)(2,1)S(1)}) custom-call(s32[2,64]{1,0:T(2,128)S(1)} %get-tuple-element.65.pairs_ref.refs_0_, s32[1]{0:T(128)S(6)} %copy.19.count_ref.refs_1_, bf16[64,256,256]{2,1,0:T(8,128)(2,1)S(1)} %get-tuple-element.66.blocks_ref.refs_2_, ...), custom_call_target="tpu_custom_call" | custom-call | flops 100000000 | bytes 12582912 | tf_op jit(solution)/shard_map/pallas_call | solution.py:28
  14.9 0.6 collective-permute-done.1
  15.6 1.8 %collective-permute-start.3 = (bf16[6,32,256]{2,1,0:T(8,128)(2,1)S(1)}, bf16[6,32,256]{2,1,0:T(8,128)(2,1)S(1)}, u32[]{:S(2)}, u32[]{:S(2)}) collective-permute-start(bf16[6,32,256]{2,1,0:T(8,128)(2,1)S(1)} %pad_maximum_fusion.4), channel_id=1, source_target_pairs={{0,3},{1,2},{2,1},{3,0},{4,7},{5,6},{6,5},{7,4},{8,11},{9,10},{10,... | collective-permute-start | bytes 294920 | tf_op jit(solution)/shard_map/ppermute | solution.py:495
  17.4 2.3 %collective-permute-start.5 = (bf16[8,32,256]{2,1,0:T(8,128)(2,1)S(1)}, bf16[8,32,256]{2,1,0:T(8,128)(2,1)S(1)}, u32[]{:S(2)}, u32[]{:S(2)}) collective-permute-start(bf16[8,32,256]{2,1,0:T(8,128)(2,1)S(1)} %get-tuple-element.77), channel_id=1, source_target_pairs={{0,1},{1,2},{2,3},{3,4},{4,5},{5,6},{6,7},{7,8},{8,9},{9,10},{10,1... | collective-permute-start | bytes 393224 | tf_op jit(solution)/shard_map/ppermute | solution.py:498
  19.7 1.1 %shard_map.106 = (bf16[16,256,256]{2,1,0:T(8,128)(2,1)S(1)}, bf16[16,256,256]{2,1,0:T(8,128)(2,1)S(1)}) custom-call(bf16[32,256,256]{2,1,0:T(8,128)(2,1)S(1)} %get-tuple-element.70.coupled_ref), custom_call_target="tpu_custom_call" | custom-call | flops 100000000 | bytes 1000000 | tf_op jit(solution)/shard_map/pallas_call | solution.py:28
  20.9 0.6 collective-permute-done.3
  21.6 1.4 %collective-permute-start.4 = (bf16[9,32,256]{2,1,0:T(8,128)(2,1)S(1)}, bf16[9,32,256]{2,1,0:T(8,128)(2,1)S(1)}, u32[]{:S(2)}, u32[]{:S(2)}) collective-permute-start(bf16[9,32,256]{2,1,0:T(8,128)(2,1)S(1)} %constant_dynamic-update-slice_fusion), channel_id=1, source_target_pairs={{0,5},{1,4},{2,7},{3,6},{4,1},{5,0},{6,3},{7,2},{8,13},{9,12},{10,... | collective-permute-start | bytes 442376 | tf_op jit(solution)/shard_map/ppermute | solution.py:495
  22.9 3.5 %shard_map.107 = (f32[8,32,256]{2,1,0:T(8,128)S(1)}, f32[32,256]{1,0:T(8,128)S(1)}) custom-call(s32[2,64]{1,0:T(2,128)S(1)} %get-tuple-element.65.pairs_ref.refs_0_, s32[1]{0:T(128)S(6)} %copy.19.count_ref.refs_1_, bf16[64,256,256]{2,1,0:T(8,128)(2,1)S(1)} %get-tuple-element.66.blocks_ref.refs_2_, ...), custom_call_target="tpu_custom_call" | custom-call | flops 100000000 | bytes 12582912 | tf_op jit(solution)/shard_map/pallas_call | solution.py:28
  26.5 1.0 %collective-permute-done.4 = bf16[9,32,256]{2,1,0:T(8,128)(2,1)S(1)} collective-permute-done((bf16[9,32,256]{2,1,0:T(8,128)(2,1)S(1)}, bf16[9,32,256]{2,1,0:T(8,128)(2,1)S(1)}, u32[]{:S(2)}, u32[]{:S(2)}) %collective-permute-start.4) | collective-permute-done | bytes 147488 | tf_op jit(solution)/shard_map/ppermute | solution.py:495
  27.5 1.1 %shard_map.108 = (bf16[64,256]{1,0:T(8,128)(2,1)S(1)}, f32[32,256]{1,0:T(8,128)S(1)}, bf16[9,32,256]{2,1,0:T(8,128)(2,1)S(1)}) custom-call(bf16[16,256,256]{2,1,0:T(8,128)(2,1)S(1)} %get-tuple-element.73.merged_ref, bf16[8,32,256]{2,1,0:T(8,128)(2,1)S(1)} %pad_maximum_fusion.low_ref, bf16[8,32,256]{2,1,0:T(8,128)(2,1)S(1)} %slice.138.high_ref, ...), custom_call_target="tpu_custom_call" | custom-call | flops 100000000 | bytes 1000000 | tf_op jit(solution)/shard_map/pallas_call | solution.py:28
  29.1 1.0 %collective-permute-done.6 = bf16[9,32,256]{2,1,0:T(8,128)(2,1)S(1)} collective-permute-done((bf16[9,32,256]{2,1,0:T(8,128)(2,1)S(1)}, bf16[9,32,256]{2,1,0:T(8,128)(2,1)S(1)}, u32[]{:S(2)}, u32[]{:S(2)}) %collective-permute-start.6) | collective-permute-done | bytes 147488 | tf_op jit(solution)/shard_map/ppermute | solution.py:495
  30.1 1.9 %collective-permute-start.7 = (bf16[6,32,256]{2,1,0:T(8,128)(2,1)S(1)}, bf16[6,32,256]{2,1,0:T(8,128)(2,1)S(1)}, u32[]{:S(2)}, u32[]{:S(2)}) collective-permute-start(bf16[6,32,256]{2,1,0:T(8,128)(2,1)S(1)} %pad_maximum_fusion.5), channel_id=1, source_target_pairs={{0,9},{1,8},{2,11},{3,10},{4,13},{5,12},{6,15},{7,14},{8,1},{9,0},... | collective-permute-start | bytes 294920 | tf_op jit(solution)/shard_map/ppermute | solution.py:495
  32.3 1.3 %collective-permute-start.8 = (bf16[8,64,256]{2,1,0:T(8,128)(2,1)S(1)}, bf16[8,64,256]{2,1,0:T(8,128)(2,1)S(1)}, u32[]{:S(2)}, u32[]{:S(2)}) collective-permute-start(bf16[8,64,256]{2,1,0:T(8,128)(2,1)S(1)} %get-tuple-element.92.field_ref.image_ref), channel_id=1, source_target_pairs={{1,0},{2,1},{3,2},{4,3},{5,4},{6,5},{7,6},{8,7},{9,8},{10,9},{11,1... | collective-permute-start | bytes 786440 | tf_op jit(solution)/shard_map/ppermute | solution.py:498
  33.6 2.4 %shard_map.111 = (f32[8,32,256]{2,1,0:T(8,128)S(1)}, bf16[8,32,256]{2,1,0:T(8,128)(2,1)S(1)}) custom-call(s32[2,64]{1,0:T(2,128)S(1)} %get-tuple-element.65.pairs_ref.refs_0_, s32[1]{0:T(128)S(6)} %copy.19.count_ref.refs_1_, bf16[64,256,256]{2,1,0:T(8,128)(2,1)S(1)} %get-tuple-element.66.blocks_ref.refs_2_, ...), custom_call_target="tpu_custom_call" | custom-call | flops 100000000 | bytes 12582912 | tf_op jit(solution)/shard_map/pallas_call | solution.py:28
  36.0 2.0 %collective-permute-done.7 = bf16[6,32,256]{2,1,0:T(8,128)(2,1)S(1)} collective-permute-done((bf16[6,32,256]{2,1,0:T(8,128)(2,1)S(1)}, bf16[6,32,256]{2,1,0:T(8,128)(2,1)S(1)}, u32[]{:S(2)}, u32[]{:S(2)}) %collective-permute-start.7) | collective-permute-done | bytes 98336 | tf_op jit(solution)/shard_map/ppermute | solution.py:495
  38.0 2.2 %collective-permute-start.9 = (bf16[6,32,256]{2,1,0:T(8,128)(2,1)S(1)}, bf16[6,32,256]{2,1,0:T(8,128)(2,1)S(1)}, u32[]{:S(2)}, u32[]{:S(2)}) collective-permute-start(bf16[6,32,256]{2,1,0:T(8,128)(2,1)S(1)} %pad_maximum_fusion.7), channel_id=1, source_target_pairs={{0,3},{1,2},{2,1},{3,0},{4,7},{5,6},{6,5},{7,4},{8,11},{9,10},{10,... | collective-permute-start | bytes 294920 | tf_op jit(solution)/shard_map/ppermute | solution.py:495
  40.2 2.3 %collective-permute-start.11 = (bf16[8,32,256]{2,1,0:T(8,128)(2,1)S(1)}, bf16[8,32,256]{2,1,0:T(8,128)(2,1)S(1)}, u32[]{:S(2)}, u32[]{:S(2)}) collective-permute-start(bf16[8,32,256]{2,1,0:T(8,128)(2,1)S(1)} %get-tuple-element.96), channel_id=1, source_target_pairs={{0,1},{1,2},{2,3},{3,4},{4,5},{5,6},{6,7},{7,8},{8,9},{9,10},{10,1... | collective-permute-start | bytes 393224 | tf_op jit(solution)/shard_map/ppermute | solution.py:498
  43.3 1.8 %collective-permute-start.10 = (bf16[9,32,256]{2,1,0:T(8,128)(2,1)S(1)}, bf16[9,32,256]{2,1,0:T(8,128)(2,1)S(1)}, u32[]{:S(2)}, u32[]{:S(2)}) collective-permute-start(bf16[9,32,256]{2,1,0:T(8,128)(2,1)S(1)} %constant_dynamic-update-slice_fusion.5), channel_id=1, source_target_pairs={{0,5},{1,4},{2,7},{3,6},{4,1},{5,0},{6,3},{7,2},{8,13},{9,12},{10,... | collective-permute-start | bytes 442376 | tf_op jit(solution)/shard_map/ppermute | solution.py:495
  45.1 3.9 %shard_map.113 = (f32[8,32,256]{2,1,0:T(8,128)S(1)}, f32[32,256]{1,0:T(8,128)S(1)}, f32[32,128]{1,0:T(8,128)S(1)}) custom-call(s32[2,64]{1,0:T(2,128)S(1)} %get-tuple-element.65.pairs_ref.refs_0_, s32[1]{0:T(128)S(6)} %copy.19.count_ref.refs_1_, bf16[64,256,256]{2,1,0:T(8,128)(2,1)S(1)} %get-tuple-element.66.blocks_ref.refs_2_, ...), custom_call_target="tpu_custom_call" | custom-call | flops 100000000 | bytes 12582912 | tf_op jit(solution)/shard_map/pallas_call | solution.py:28
  49.2 1.2 %shard_map.114 = (bf16[64,256]{1,0:T(8,128)(2,1)S(1)}, f32[48,128]{1,0:T(8,128)S(1)}) custom-call(bf16[16,256,256]{2,1,0:T(8,128)(2,1)S(1)} %get-tuple-element.73.merged_ref, bf16[8,32,256]{2,1,0:T(8,128)(2,1)S(1)} %pad_maximum_fusion.1.low_ref, bf16[8,32,256]{2,1,0:T(8,128)(2,1)S(1)} %slice.146.high_ref, f32[1,32,256]{2,1,0:T(8,128)S(1)} %slice.147.kept_ref, ...), custom_call_target="tpu_custom_call" | custom-call | flops 100000000 | bytes 1000000 | tf_op jit(solution)/shard_map/pallas_call | solution.py:28
  50.5 1.1 %collective-permute-done.12 = f32[48,128]{1,0:T(8,128)S(1)} collective-permute-done((f32[48,128]{1,0:T(8,128)S(1)}, f32[48,128]{1,0:T(8,128)S(1)}, u32[]{:S(2)}, u32[]{:S(2)}) %collective-permute-start.12) | collective-permute-done | bytes 24608 | tf_op jit(solution)/shard_map/ppermute | solution.py:495
  51.6 1.6 %collective-permute-start.13 = (f32[48,128]{1,0:T(8,128)S(1)}, f32[48,128]{1,0:T(8,128)S(1)}, u32[]{:S(2)}, u32[]{:S(2)}) collective-permute-start(f32[48,128]{1,0:T(8,128)S(1)} %add.37), channel_id=1, source_target_pairs={{0,9},{1,8},{2,11},{3,10},{4,13},{5,12},{6,15},{7,14},{8,1},{9,0},... | collective-permute-start | bytes 73736 | tf_op jit(solution)/shard_map/ppermute | solution.py:495
  53.5 2.3 %collective-permute-done.13 = f32[48,128]{1,0:T(8,128)S(1)} collective-permute-done((f32[48,128]{1,0:T(8,128)S(1)}, f32[48,128]{1,0:T(8,128)S(1)}, u32[]{:S(2)}, u32[]{:S(2)}) %collective-permute-start.13) | collective-permute-done | bytes 24608 | tf_op jit(solution)/shard_map/ppermute | solution.py:495
  55.8 1.7 %collective-permute-start.14 = (f32[48,128]{1,0:T(8,128)S(1)}, f32[48,128]{1,0:T(8,128)S(1)}, u32[]{:S(2)}, u32[]{:S(2)}) collective-permute-start(f32[48,128]{1,0:T(8,128)S(1)} %add.38), channel_id=1, source_target_pairs={{0,3},{1,2},{2,1},{3,0},{4,7},{5,6},{6,5},{7,4},{8,11},{9,10},{10,... | collective-permute-start | bytes 73736 | tf_op jit(solution)/shard_map/ppermute | solution.py:495
  57.5 1.5 %collective-permute-done.14 = f32[48,128]{1,0:T(8,128)S(1)} collective-permute-done((f32[48,128]{1,0:T(8,128)S(1)}, f32[48,128]{1,0:T(8,128)S(1)}, u32[]{:S(2)}, u32[]{:S(2)}) %collective-permute-start.14) | collective-permute-done | bytes 24608 | tf_op jit(solution)/shard_map/ppermute | solution.py:495
  59.0 1.8 %collective-permute-start.15 = (f32[48,128]{1,0:T(8,128)S(1)}, f32[48,128]{1,0:T(8,128)S(1)}, u32[]{:S(2)}, u32[]{:S(2)}) collective-permute-start(f32[48,128]{1,0:T(8,128)S(1)} %add.39.kept_ref), channel_id=1, source_target_pairs={{0,5},{1,4},{2,7},{3,6},{4,1},{5,0},{6,3},{7,2},{8,13},{9,12},{10,... | collective-permute-start | bytes 73736 | tf_op jit(solution)/shard_map/ppermute | solution.py:495
  60.8 1.5 %collective-permute-done.15.got_ref = f32[48,128]{1,0:T(8,128)S(1)} collective-permute-done((f32[48,128]{1,0:T(8,128)S(1)}, f32[48,128]{1,0:T(8,128)S(1)}, u32[]{:S(2)}, u32[]{:S(2)}) %collective-permute-start.15) | collective-permute-done | bytes 24608 | tf_op jit(solution)/shard_map/ppermute | solution.py:495
  62.3 4.5 %shard_map.116 = (f32[32,2048]{1,0:T(8,128)}, f32[32,2048]{1,0:T(8,128)}, f32[32,64]{1,0:T(8,128)}) custom-call(f32[48,128]{1,0:T(8,128)S(1)} %add.39.kept_ref, f32[48,128]{1,0:T(8,128)S(1)} %collective-permute-done.15.got_ref, f32[32,2048]{1,0:T(8,128)S(1)} %copy-done.1, f32[8,32,256]{2,1,0:T(8,128)S(1)} %get-tuple-element.108.image_ref, ...), custom_call_target="tpu_custom_call" | custom-call | flops 100000000 | bytes 1000000 | tf_op jit(solution)/shard_map/pallas_call | solution.py:28
  (53 shorter events, 3.1 us)
Async XLA Ops:
  0.6 4.9 %copy-start = (bf16[8,32,256]{2,1,0:T(8,128)(2,1)S(1)}, bf16[8,32,256]{2,1,0:T(8,128)(2,1)}, u32[]{:S(2)}) copy-start(bf16[8,32,256]{2,1,0:T(8,128)(2,1)} %param.14) | copy-start | bytes 393220
  5.0 1.7 %collective-permute-start = (bf16[17,32,256]{2,1,0:T(8,128)(2,1)S(1)}, bf16[17,32,256]{2,1,0:T(8,128)(2,1)S(1)}, u32[]{:S(2)}, u32[]{:S(2)}) collective-permute-start(bf16[17,32,256]{2,1,0:T(8,128)(2,1)S(1)} %get-tuple-element.58.payload_ref), channel_id=1, source_target_pairs={{0,1},{1,0},{2,3},{3,2},{4,5},{5,4},{6,7},{7,6},{8,9},{9,8},{10,11... | collective-permute-start | bytes 835592 | tf_op jit(solution)/shard_map/ppermute | solution.py:495
  6.8 8.7 %collective-permute-start.1 = (bf16[6,32,256]{2,1,0:T(8,128)(2,1)S(1)}, bf16[6,32,256]{2,1,0:T(8,128)(2,1)S(1)}, u32[]{:S(2)}, u32[]{:S(2)}) collective-permute-start(bf16[6,32,256]{2,1,0:T(8,128)(2,1)S(1)} %pad_maximum_fusion.2), channel_id=1, source_target_pairs={{0,9},{1,8},{2,11},{3,10},{4,13},{5,12},{6,15},{7,14},{8,1},{9,0},... | collective-permute-start | bytes 294920 | tf_op jit(solution)/shard_map/ppermute | solution.py:495
  11.2 10.3 %collective-permute-start.2 = (bf16[8,64,256]{2,1,0:T(8,128)(2,1)S(1)}, bf16[8,64,256]{2,1,0:T(8,128)(2,1)S(1)}, u32[]{:S(2)}, u32[]{:S(2)}) collective-permute-start(bf16[8,64,256]{2,1,0:T(8,128)(2,1)S(1)} %get-tuple-element.64.field_ref.refs_3_.right_ref), channel_id=1, source_target_pairs={{1,0},{2,1},{3,2},{4,3},{5,4},{6,5},{7,6},{8,7},{9,8},{10,9},{11,1... | collective-permute-start | bytes 786440 | tf_op jit(solution)/shard_map/ppermute | solution.py:498
  15.6 5.9 %collective-permute-start.3 = (bf16[6,32,256]{2,1,0:T(8,128)(2,1)S(1)}, bf16[6,32,256]{2,1,0:T(8,128)(2,1)S(1)}, u32[]{:S(2)}, u32[]{:S(2)}) collective-permute-start(bf16[6,32,256]{2,1,0:T(8,128)(2,1)S(1)} %pad_maximum_fusion.4), channel_id=1, source_target_pairs={{0,3},{1,2},{2,1},{3,0},{4,7},{5,6},{6,5},{7,4},{8,11},{9,10},{10,... | collective-permute-start | bytes 294920 | tf_op jit(solution)/shard_map/ppermute | solution.py:495
  17.4 5.5 %collective-permute-start.5 = (bf16[8,32,256]{2,1,0:T(8,128)(2,1)S(1)}, bf16[8,32,256]{2,1,0:T(8,128)(2,1)S(1)}, u32[]{:S(2)}, u32[]{:S(2)}) collective-permute-start(bf16[8,32,256]{2,1,0:T(8,128)(2,1)S(1)} %get-tuple-element.77), channel_id=1, source_target_pairs={{0,1},{1,2},{2,3},{3,4},{4,5},{5,6},{6,7},{7,8},{8,9},{9,10},{10,1... | collective-permute-start | bytes 393224 | tf_op jit(solution)/shard_map/ppermute | solution.py:498
  21.6 6.0 %collective-permute-start.4 = (bf16[9,32,256]{2,1,0:T(8,128)(2,1)S(1)}, bf16[9,32,256]{2,1,0:T(8,128)(2,1)S(1)}, u32[]{:S(2)}, u32[]{:S(2)}) collective-permute-start(bf16[9,32,256]{2,1,0:T(8,128)(2,1)S(1)} %constant_dynamic-update-slice_fusion), channel_id=1, source_target_pairs={{0,5},{1,4},{2,7},{3,6},{4,1},{5,0},{6,3},{7,2},{8,13},{9,12},{10,... | collective-permute-start | bytes 442376 | tf_op jit(solution)/shard_map/ppermute | solution.py:495
  28.6 1.4 %collective-permute-start.6 = (bf16[9,32,256]{2,1,0:T(8,128)(2,1)S(1)}, bf16[9,32,256]{2,1,0:T(8,128)(2,1)S(1)}, u32[]{:S(2)}, u32[]{:S(2)}) collective-permute-start(bf16[9,32,256]{2,1,0:T(8,128)(2,1)S(1)} %get-tuple-element.81.payload_ref), channel_id=1, source_target_pairs={{0,1},{1,0},{2,3},{3,2},{4,5},{5,4},{6,7},{7,6},{8,9},{9,8},{10,11... | collective-permute-start | bytes 442376 | tf_op jit(solution)/shard_map/ppermute | solution.py:495
  30.1 7.8 %collective-permute-start.7 = (bf16[6,32,256]{2,1,0:T(8,128)(2,1)S(1)}, bf16[6,32,256]{2,1,0:T(8,128)(2,1)S(1)}, u32[]{:S(2)}, u32[]{:S(2)}) collective-permute-start(bf16[6,32,256]{2,1,0:T(8,128)(2,1)S(1)} %pad_maximum_fusion.5), channel_id=1, source_target_pairs={{0,9},{1,8},{2,11},{3,10},{4,13},{5,12},{6,15},{7,14},{8,1},{9,0},... | collective-permute-start | bytes 294920 | tf_op jit(solution)/shard_map/ppermute | solution.py:495
  32.3 10.9 %collective-permute-start.8 = (bf16[8,64,256]{2,1,0:T(8,128)(2,1)S(1)}, bf16[8,64,256]{2,1,0:T(8,128)(2,1)S(1)}, u32[]{:S(2)}, u32[]{:S(2)}) collective-permute-start(bf16[8,64,256]{2,1,0:T(8,128)(2,1)S(1)} %get-tuple-element.92.field_ref.image_ref), channel_id=1, source_target_pairs={{1,0},{2,1},{3,2},{4,3},{5,4},{6,5},{7,6},{8,7},{9,8},{10,9},{11,1... | collective-permute-start | bytes 786440 | tf_op jit(solution)/shard_map/ppermute | solution.py:498
  38.0 5.2 %collective-permute-start.9 = (bf16[6,32,256]{2,1,0:T(8,128)(2,1)S(1)}, bf16[6,32,256]{2,1,0:T(8,128)(2,1)S(1)}, u32[]{:S(2)}, u32[]{:S(2)}) collective-permute-start(bf16[6,32,256]{2,1,0:T(8,128)(2,1)S(1)} %pad_maximum_fusion.7), channel_id=1, source_target_pairs={{0,3},{1,2},{2,1},{3,0},{4,7},{5,6},{6,5},{7,4},{8,11},{9,10},{10,... | collective-permute-start | bytes 294920 | tf_op jit(solution)/shard_map/ppermute | solution.py:495
  40.2 4.8 %collective-permute-start.11 = (bf16[8,32,256]{2,1,0:T(8,128)(2,1)S(1)}, bf16[8,32,256]{2,1,0:T(8,128)(2,1)S(1)}, u32[]{:S(2)}, u32[]{:S(2)}) collective-permute-start(bf16[8,32,256]{2,1,0:T(8,128)(2,1)S(1)} %get-tuple-element.96), channel_id=1, source_target_pairs={{0,1},{1,2},{2,3},{3,4},{4,5},{5,6},{6,7},{7,8},{8,9},{9,10},{10,1... | collective-permute-start | bytes 393224 | tf_op jit(solution)/shard_map/ppermute | solution.py:498
  43.3 5.9 %collective-permute-start.10 = (bf16[9,32,256]{2,1,0:T(8,128)(2,1)S(1)}, bf16[9,32,256]{2,1,0:T(8,128)(2,1)S(1)}, u32[]{:S(2)}, u32[]{:S(2)}) collective-permute-start(bf16[9,32,256]{2,1,0:T(8,128)(2,1)S(1)} %constant_dynamic-update-slice_fusion.5), channel_id=1, source_target_pairs={{0,5},{1,4},{2,7},{3,6},{4,1},{5,0},{6,3},{7,2},{8,13},{9,12},{10,... | collective-permute-start | bytes 442376 | tf_op jit(solution)/shard_map/ppermute | solution.py:495
  49.0 13.4 %copy-start.1 = (f32[32,2048]{1,0:T(8,128)S(1)}, f32[32,2048]{1,0:T(8,128)}, u32[]{:S(2)}) copy-start(f32[32,2048]{1,0:T(8,128)} %right_ref.1) | copy-start | bytes 786436
  50.4 1.2 %collective-permute-start.12 = (f32[48,128]{1,0:T(8,128)S(1)}, f32[48,128]{1,0:T(8,128)S(1)}, u32[]{:S(2)}, u32[]{:S(2)}) collective-permute-start(f32[48,128]{1,0:T(8,128)S(1)} %get-tuple-element.102), channel_id=1, source_target_pairs={{0,1},{1,0},{2,3},{3,2},{4,5},{5,4},{6,7},{7,6},{8,9},{9,8},{10,11... | collective-permute-start | bytes 73736 | tf_op jit(solution)/shard_map/ppermute | solution.py:495
  51.6 4.2 %collective-permute-start.13 = (f32[48,128]{1,0:T(8,128)S(1)}, f32[48,128]{1,0:T(8,128)S(1)}, u32[]{:S(2)}, u32[]{:S(2)}) collective-permute-start(f32[48,128]{1,0:T(8,128)S(1)} %add.37), channel_id=1, source_target_pairs={{0,9},{1,8},{2,11},{3,10},{4,13},{5,12},{6,15},{7,14},{8,1},{9,0},... | collective-permute-start | bytes 73736 | tf_op jit(solution)/shard_map/ppermute | solution.py:495
  55.8 3.3 %collective-permute-start.14 = (f32[48,128]{1,0:T(8,128)S(1)}, f32[48,128]{1,0:T(8,128)S(1)}, u32[]{:S(2)}, u32[]{:S(2)}) collective-permute-start(f32[48,128]{1,0:T(8,128)S(1)} %add.38), channel_id=1, source_target_pairs={{0,3},{1,2},{2,1},{3,0},{4,7},{5,6},{6,5},{7,4},{8,11},{9,10},{10,... | collective-permute-start | bytes 73736 | tf_op jit(solution)/shard_map/ppermute | solution.py:495
  59.0 3.3 %collective-permute-start.15 = (f32[48,128]{1,0:T(8,128)S(1)}, f32[48,128]{1,0:T(8,128)S(1)}, u32[]{:S(2)}, u32[]{:S(2)}) collective-permute-start(f32[48,128]{1,0:T(8,128)S(1)} %add.39.kept_ref), channel_id=1, source_target_pairs={{0,5},{1,4},{2,7},{3,6},{4,1},{5,0},{6,3},{7,2},{8,13},{9,12},{10,... | collective-permute-start | bytes 73736 | tf_op jit(solution)/shard_map/ppermute | solution.py:495
